TPU v7x, 32 devices: a whole 2x2x4 slice. The times are simulated.
32 devices in a mesh: ew: 8 (over z, x), ns: 4 (over y, core).
Axes of the slice: x: 2, y: 2, z: 4, core: 2. Of those that a mesh axis runs over, the one named last changes fastest.
Arguments:
- temp: float32 [32, 64, 1024], P(None, 'ns', 'ew'), may hold values from -6 to 6
- salt: float32 [32, 64, 1024], P(None, 'ns', 'ew'), may hold values from -6 to 6
- u_east: float32 [32, 64, 1024], P(None, 'ns', 'ew'), may hold values from -0.25 to 0.25
- v_north: float32 [32, 64, 1024], P(None, 'ns', 'ew'), may hold values from -0.25 to 0.25
- wet: int32 [32, 64, 1024], P(None, 'ns', 'ew'), may hold values 0 or 1
- cot_temp: float32 [32, 64, 1024], P(None, 'ns', 'ew'), may hold values from -6 to 6
- cot_salt: float32 [32, 64, 1024], P(None, 'ns', 'ew'), may hold values from -6 to 6
Outputs:
- temp_final: float32 [32, 64, 1024], P(None, 'ns', 'ew')
- salt_final: float32 [32, 64, 1024], P(None, 'ns', 'ew')
- grad_temp: float32 [32, 64, 1024], P(None, 'ns', 'ew')
- grad_salt: float32 [32, 64, 1024], P(None, 'ns', 'ew')
All inputs are finite; a program needn't handle non-finite values. No bound on the sum of `wet` on one device may be relied on, other than what follows from the above.
Results may differ from a plain program's by a relative error of at most 0.00002.
Values sent between devices are 32-bit elements; how exact they have to be, the bound alone decides.
No kernel may reach another device: no remote copies, remote signals or barrier semaphores. Data moves between devices by JAX's collectives and lax.ppermute only.
A program may use at most 64 MiB of HBM per device.

v0:
```python
import jax
import jax.numpy as jnp
from jax import lax
from jax.sharding import PartitionSpec as P

horizontal_mix = 0.05
vertical_mix = 0.2


def padded_2(cells, sides, width, closed):
    for axis, dim in sides:
        count = lax.axis_size(axis)
        ends = count if closed else count - 1
        head = lax.slice_in_dim(cells, 0, width, axis=dim)
        tail = lax.slice_in_dim(cells, cells.shape[dim] - width, cells.shape[dim], axis=dim)
        cells = jnp.concatenate(
            [
                lax.ppermute(tail, axis, [(i, (i + 1) % count) for i in range(ends)]),
                cells,
                lax.ppermute(head, axis, [((i + 1) % count, i) for i in range(ends)]),
            ],
            axis=dim,
        )
    return cells


def window_of(array, start, stop, axis):
    return lax.slice_in_dim(array, start, array.shape[axis] + stop, 1, axis)


def coefficients(speed):
    magnitude = jnp.abs(speed)
    return (
        (-speed - magnitude) / 12.0,
        (7.0 * speed + 3.0 * magnitude) / 12.0 + horizontal_mix,
        (7.0 * speed - 3.0 * magnitude) / 12.0 - horizontal_mix,
        (-speed + magnitude) / 12.0,
    )


def face_change(field, speed, wetness, axis):
    far_left = window_of(field, 0, -3, axis)
    left = window_of(field, 1, -2, axis)
    right = window_of(field, 2, -1, axis)
    far_right = window_of(field, 3, 0, axis)
    weights = coefficients(window_of(speed, 1, -2, axis))
    open_face = window_of(wetness, 1, -2, axis) * window_of(wetness, 2, -1, axis)
    flux = open_face * (
        weights[0] * far_left + weights[1] * left + weights[2] * right + weights[3] * far_right
    )
    return window_of(flux, 0, -1, axis) - window_of(flux, 1, 0, axis)


def face_adjoint(field, speed, wetness, axis):
    weighted = wetness * field
    jump = window_of(weighted, 1, 0, axis) - window_of(weighted, 0, -1, axis)
    open_face = window_of(wetness, 0, -1, axis) * window_of(wetness, 1, 0, axis)
    weights = coefficients(window_of(speed, 0, -1, axis))
    scaled = open_face * jump
    return (
        window_of(weights[0] * scaled, 3, 0, axis)
        + window_of(weights[1] * scaled, 2, -1, axis)
        + window_of(weights[2] * scaled, 1, -2, axis)
        + window_of(weights[3] * scaled, 0, -3, axis)
    )


def vertical_change(field, wetness):
    open_face = wetness[:, :-1] * wetness[:, 1:]
    flux = vertical_mix * open_face * (field[:, :-1] - field[:, 1:])
    return jnp.pad(flux, ((0, 0), (1, 0), (0, 0), (0, 0))) - jnp.pad(
        flux, ((0, 0), (0, 1), (0, 0), (0, 0))
    )


def vertical_adjoint(field, wetness):
    weighted = wetness * field
    open_face = wetness[:, :-1] * wetness[:, 1:]
    flux = vertical_mix * open_face * (weighted[:, 1:] - weighted[:, :-1])
    return jnp.pad(flux, ((0, 0), (0, 1), (0, 0), (0, 0))) - jnp.pad(
        flux, ((0, 0), (1, 0), (0, 0), (0, 0))
    )


def advance(padded, flow_wide):
    east_speed = flow_wide[0:1]
    north_speed = flow_wide[1:2]
    wetness = flow_wide[2:3]
    change_x = face_change(
        window_of(padded, 2, -2, 2),
        window_of(east_speed, 2, -2, 2),
        window_of(wetness, 2, -2, 2),
        3,
    )
    change_y = face_change(
        window_of(padded, 2, -2, 3),
        window_of(north_speed, 2, -2, 3),
        window_of(wetness, 2, -2, 3),
        2,
    )
    inner = window_of(window_of(padded, 2, -2, 2), 2, -2, 3)
    inner_wet = window_of(window_of(wetness, 2, -2, 2), 2, -2, 3)
    change_z = vertical_change(inner, inner_wet)
    return inner + inner_wet * (change_x + change_y + change_z)


def retreat(padded, flow_wide):
    east_speed = flow_wide[0:1]
    north_speed = flow_wide[1:2]
    wetness = flow_wide[2:3]
    back_x = face_adjoint(
        window_of(padded, 2, -2, 2),
        window_of(east_speed, 2, -2, 2),
        window_of(wetness, 2, -2, 2),
        3,
    )
    back_y = face_adjoint(
        window_of(padded, 2, -2, 3),
        window_of(north_speed, 2, -2, 3),
        window_of(wetness, 2, -2, 3),
        2,
    )
    inner = window_of(window_of(padded, 2, -2, 2), 2, -2, 3)
    inner_wet = window_of(window_of(wetness, 2, -2, 2), 2, -2, 3)
    back_z = vertical_adjoint(inner, inner_wet)
    return inner + back_x + back_y + back_z


def widen_state(field, width):
    across = padded_2(field, (("ew", 3),), width, True)
    return padded_2(across, (("ns", 2),), width, False)


def widen_flow(field, width):
    across = padded_2(field, (("ew", 3),), width, True)
    return padded_2(across, (("ns", 2),), width, False)


def evolve(field, flow_wide, stepper):
    for turn in range(2):
        field = stepper(widen_state(field, 2), flow_wide)
    return field


def local(temp, salt, u_east, v_north, wet, cot_temp, cot_salt):
    reach = 2
    flow_wide = widen_flow(jnp.stack([u_east, v_north, wet.astype(jnp.float32)]), reach)
    tracers = evolve(jnp.stack([temp, salt]), flow_wide, advance)
    sensitivity = evolve(jnp.stack([cot_temp, cot_salt]), flow_wide, retreat)
    return (tracers[0], tracers[1], sensitivity[0], sensitivity[1])


def solution(mesh):
    in_specs = (
        P(None, "ns", "ew"),
        P(None, "ns", "ew"),
        P(None, "ns", "ew"),
        P(None, "ns", "ew"),
        P(None, "ns", "ew"),
        P(None, "ns", "ew"),
        P(None, "ns", "ew"),
    )
    out_specs = (P(None, "ns", "ew"), P(None, "ns", "ew"), P(None, "ns", "ew"), P(None, "ns", "ew"))
    return jax.shard_map(local, mesh=mesh, in_specs=in_specs, out_specs=out_specs, check_vma=False)
```

profile of v0, /device:TPU:1, one launch (start us, length us, event | category | flops | bytes accessed | tf_op | source)
XLA Modules:
  0.0 160.1 jit_solution(598377724132125750)
XLA Ops:
  0.6 1.7 %fusion.77 = (f32[32,16,128]{2,1,0:T(8,128)}, f32[1,32,16,128]{3,2,1,0:T(8,128)S(1)}) fusion(s32[32,16,128]{2,1,0:T(8,128)} %param.11), kind=kLoop, calls=%fused_computation.200 | loop fusion | flops 65536 | bytes 786432 | tf_op jit(solution)/shard_map/convert_element_type | solution.py:147
  4.7 2.0 %collective-permute-start = (f32[3,32,16,2]{1,2,3,0:T(8,128)}, f32[3,32,16,2]{1,2,3,0:T(8,128)}, u32[]{:S(2)}, u32[]{:S(2)}) collective-permute-start(f32[3,32,16,2]{1,2,3,0:T(8,128)} %copy.86), channel_id=1, source_target_pairs={{0,4},{4,8},{8,12},{12,16},{16,20},{20,24},{24,28},{28,0},{1,5},{5... | collective-permute-start | bytes 36872 | tf_op jit(solution)/shard_map/ppermute | solution.py:18
  7.8 3.0 %collective-permute-start.1 = (f32[3,32,16,2]{1,2,3,0:T(8,128)}, f32[3,32,16,2]{1,2,3,0:T(8,128)}, u32[]{:S(2)}, u32[]{:S(2)}) collective-permute-start(f32[3,32,16,2]{1,2,3,0:T(8,128)} %copy.87), channel_id=1, source_target_pairs={{4,0},{8,4},{12,8},{16,12},{20,16},{24,20},{28,24},{0,28},{5,1},{9... | collective-permute-start | bytes 36872 | tf_op jit(solution)/shard_map/ppermute | solution.py:20
  10.8 1.1 fusion.24
  12.8 3.6 %collective-permute-start.3 = (f32[2,32,16,2]{3,2,1,0:T(8,128)S(1)}, f32[2,32,16,2]{3,2,1,0:T(8,128)S(1)}, u32[]{:S(2)}, u32[]{:S(2)}) collective-permute-start(f32[2,32,16,2]{3,2,1,0:T(8,128)S(1)} %get-tuple-element.63), channel_id=1, source_target_pairs={{4,0},{8,4},{12,8},{16,12},{20,16},{24,20},{28,24},{0,28},{5,1},{9... | collective-permute-start | bytes 24584 | tf_op jit(solution)/shard_map/ppermute | solution.py:20
  17.4 27.9 %collective-permute-done.2 = f32[2,32,16,2]{3,2,1,0:T(8,128)S(1)} collective-permute-done((f32[2,32,16,2]{3,2,1,0:T(8,128)S(1)}, f32[2,32,16,2]{3,2,1,0:T(8,128)S(1)}, u32[]{:S(2)}, u32[]{:S(2)}) %collective-permute-start.2) | collective-permute-done | bytes 8224 | tf_op jit(solution)/shard_map/ppermute | solution.py:18
  45.2 5.0 %collective-permute-start.13 = (f32[2,32,16,2]{3,2,1,0:T(8,128)}, f32[2,32,16,2]{3,2,1,0:T(8,128)}, u32[]{:S(2)}, u32[]{:S(2)}) collective-permute-start(f32[2,32,16,2]{3,2,1,0:T(8,128)} %get-tuple-element.52), channel_id=1, source_target_pairs={{4,0},{8,4},{12,8},{16,12},{20,16},{24,20},{28,24},{0,28},{5,1},{9... | collective-permute-start | bytes 24584 | tf_op jit(solution)/shard_map/ppermute | solution.py:20
  51.3 4.6 %collective-permute-start.6 = (f32[2,32,2,132]{3,2,1,0:T(2,128)}, f32[2,32,2,132]{3,2,1,0:T(2,128)}, u32[]{:S(2)}, u32[]{:S(2)}) collective-permute-start(f32[2,32,2,132]{3,2,1,0:T(2,128)} %get-tuple-element.39), channel_id=1, source_target_pairs={{0,1},{1,2},{2,3},{4,5},{5,6},{6,7},{8,9},{9,10},{10,11},{12,13},{... | collective-permute-start | bytes 202760 | tf_op jit(solution)/shard_map/ppermute | solution.py:18
  56.4 1.9 %collective-permute-start.7 = (f32[2,32,2,132]{3,2,1,0:T(2,128)S(1)}, f32[2,32,2,132]{3,2,1,0:T(2,128)}, u32[]{:S(2)}, u32[]{:S(2)}) collective-permute-start(f32[2,32,2,132]{3,2,1,0:T(2,128)S(1)} %get-tuple-element.40), channel_id=1, source_target_pairs={{1,0},{2,1},{3,2},{5,4},{6,5},{7,6},{9,8},{10,9},{11,10},{13,12},{... | collective-permute-start | bytes 202760 | tf_op jit(solution)/shard_map/ppermute | solution.py:20
  58.3 2.1 %copy.63 = f32[3,32,16,2]{3,2,1,0:T(8,128)} copy(f32[3,32,16,2]{1,2,3,0:T(8,128)} %collective-permute-done) | data formatting | bytes 24576 | tf_op jit(solution)/shard_map/ppermute | solution.py:18
  60.4 2.0 %copy.65 = f32[3,32,16,2]{3,2,1,0:T(8,128)} copy(f32[3,32,16,2]{1,2,3,0:T(8,128)} %collective-permute-done.1) | data formatting | bytes 24576 | tf_op jit(solution)/shard_map/ppermute | solution.py:20
  62.4 2.2 %pad_maximum_fusion = f32[3,32,16,132]{3,2,1,0:T(8,128)S(1)} fusion(f32[3,32,16,2]{3,2,1,0:T(8,128)} %copy.65, f32[1,32,16,128]{3,2,1,0:T(8,128)S(1)} %get-tuple-element.67, f32[1,32,16,128]{3,2,1,0:T(8,128)} %bitcast.85, f32[1,32,16,128]{3,2,1,0:T(8,128)} %bitcast.88, f32[3,32,16,2]{3,2,1,0:T(8,128)} %copy.63), kind=kLoop, calls=%fused_computation | loop fusion | flops 811008 | bytes 1622016 | tf_op jit(solution)/shard_map/concatenate | solution.py:16
  66.8 3.6 %collective-permute-start.4 = (f32[3,32,2,132]{3,2,1,0:T(2,128)S(1)}, f32[3,32,2,132]{3,2,1,0:T(2,128)S(1)}, u32[]{:S(2)}, u32[]{:S(2)}) collective-permute-start(f32[3,32,2,132]{3,2,1,0:T(2,128)S(1)} %get-tuple-element.36), channel_id=1, source_target_pairs={{0,1},{1,2},{2,3},{4,5},{5,6},{6,7},{8,9},{9,10},{10,11},{12,13},{... | collective-permute-start | bytes 304136 | tf_op jit(solution)/shard_map/ppermute | solution.py:18
  70.5 1.9 %collective-permute-start.5 = (f32[3,32,2,132]{3,2,1,0:T(2,128)S(1)}, f32[3,32,2,132]{3,2,1,0:T(2,128)S(1)}, u32[]{:S(2)}, u32[]{:S(2)}) collective-permute-start(f32[3,32,2,132]{3,2,1,0:T(2,128)S(1)} %get-tuple-element.35), channel_id=1, source_target_pairs={{1,0},{2,1},{3,2},{5,4},{6,5},{7,6},{9,8},{10,9},{11,10},{13,12},{... | collective-permute-start | bytes 304136 | tf_op jit(solution)/shard_map/ppermute | solution.py:20
  72.4 1.7 %broadcast_multiply_fusion.1 = (f32[2,32,16,132]{3,2,1,0:T(8,128)S(1)}, f32[2,32,16,132]{3,2,1,0:T(8,128)S(1)}) fusion(f32[32,16,132]{2,1,0:T(8,128)S(1)} %slice_bitcast_fusion, f32[2,32,16,2]{3,2,1,0:T(8,128)} %collective-permute-done.13, f32[1,32,16,128]{3,2,1,0:T(8,128)S(1)} %bitcast.75, f32[1,32,16,128]{3,2,1,0:T(8,128)S(1)} %bitcast.80, ...), kind=kLoop, calls=%fused_computation.142 | loop fusion | flops 540672 | bytes 1892352 | tf_op jit(solution)/shard_map/mul | solution.py:55
  74.2 3.6 %collective-permute-start.14 = (f32[2,32,2,132]{3,2,1,0:T(2,128)S(1)}, f32[2,32,2,132]{3,2,1,0:T(2,128)S(1)}, u32[]{:S(2)}, u32[]{:S(2)}) collective-permute-start(f32[2,32,2,132]{3,2,1,0:T(2,128)S(1)} %get-tuple-element.43), channel_id=1, source_target_pairs={{0,1},{1,2},{2,3},{4,5},{5,6},{6,7},{8,9},{9,10},{10,11},{12,13},{... | collective-permute-start | bytes 202760 | tf_op jit(solution)/shard_map/ppermute | solution.py:18
  79.8 2.1 %collective-permute-start.15 = (f32[2,32,2,132]{3,2,1,0:T(2,128)S(1)}, f32[2,32,2,132]{3,2,1,0:T(2,128)S(1)}, u32[]{:S(2)}, u32[]{:S(2)}) collective-permute-start(f32[2,32,2,132]{3,2,1,0:T(2,128)S(1)} %get-tuple-element.44), channel_id=1, source_target_pairs={{1,0},{2,1},{3,2},{5,4},{6,5},{7,6},{9,8},{10,9},{11,10},{13,12},{... | collective-permute-start | bytes 202760 | tf_op jit(solution)/shard_map/ppermute | solution.py:20
  82.0 2.1 %maximum_maximum_fusion = (f32[2,32,18,132]{3,2,1,0:T(8,128)S(1)}, f32[2,32,18,132]{3,2,1,0:T(8,128)S(1)}) fusion(f32[2,32,16,2]{3,2,1,0:T(8,128)S(1)} %copy-done.11, f32[1,32,16,128]{3,2,1,0:T(8,128)S(1)} %bitcast.66, f32[1,32,16,128]{3,2,1,0:T(8,128)S(1)} %bitcast.72, f32[2,32,16,2]{3,2,1,0:T(8,128)S(1)} %copy-done.9, ...), kind=kLoop, calls=%fused_computation.1 | loop fusion | flops 1216512 | bytes 1892352 | tf_op jit(solution)/shard_map/concatenate | solution.py:16
  89.0 4.1 %collective-permute-start.9 = (f32[2,32,16,2]{3,2,1,0:T(8,128)S(1)}, f32[2,32,16,2]{3,2,1,0:T(8,128)S(1)}, u32[]{:S(2)}, u32[]{:S(2)}) collective-permute-start(f32[2,32,16,2]{3,2,1,0:T(8,128)S(1)} %get-tuple-element.56), channel_id=1, source_target_pairs={{4,0},{8,4},{12,8},{16,12},{20,16},{24,20},{28,24},{0,28},{5,1},{9... | collective-permute-start | bytes 24584 | tf_op jit(solution)/shard_map/ppermute | solution.py:20
  93.2 1.5 fusion.15
  96.4 13.9 %collective-permute-done.8 = f32[2,32,16,2]{3,2,1,0:T(8,128)S(1)} collective-permute-done((f32[2,32,16,2]{3,2,1,0:T(8,128)S(1)}, f32[2,32,16,2]{3,2,1,0:T(8,128)S(1)}, u32[]{:S(2)}, u32[]{:S(2)}) %collective-permute-start.8) | collective-permute-done | bytes 8224 | tf_op jit(solution)/shard_map/ppermute | solution.py:18
  110.3 2.2 %collective-permute-done.9 = f32[2,32,16,2]{3,2,1,0:T(8,128)S(1)} collective-permute-done((f32[2,32,16,2]{3,2,1,0:T(8,128)S(1)}, f32[2,32,16,2]{3,2,1,0:T(8,128)S(1)}, u32[]{:S(2)}, u32[]{:S(2)}) %collective-permute-start.9) | collective-permute-done | bytes 8224 | tf_op jit(solution)/shard_map/ppermute | solution.py:20
  113.0 4.0 %collective-permute-start.10 = (f32[2,32,2,132]{3,2,1,0:T(2,128)S(1)}, f32[2,32,2,132]{3,2,1,0:T(2,128)S(1)}, u32[]{:S(2)}, u32[]{:S(2)}) collective-permute-start(f32[2,32,2,132]{3,2,1,0:T(2,128)S(1)} %get-tuple-element.32), channel_id=1, source_target_pairs={{0,1},{1,2},{2,3},{4,5},{5,6},{6,7},{8,9},{9,10},{10,11},{12,13},{... | collective-permute-start | bytes 202760 | tf_op jit(solution)/shard_map/ppermute | solution.py:18
  117.0 1.9 %collective-permute-start.11 = (f32[2,32,2,132]{3,2,1,0:T(2,128)S(1)}, f32[2,32,2,132]{3,2,1,0:T(2,128)S(1)}, u32[]{:S(2)}, u32[]{:S(2)}) collective-permute-start(f32[2,32,2,132]{3,2,1,0:T(2,128)S(1)} %get-tuple-element.33), channel_id=1, source_target_pairs={{1,0},{2,1},{3,2},{5,4},{6,5},{7,6},{9,8},{10,9},{11,10},{13,12},{... | collective-permute-start | bytes 202760 | tf_op jit(solution)/shard_map/ppermute | solution.py:20
  119.0 1.2 fusion.4
  120.1 3.2 %collective-permute-done.11 = f32[2,32,2,132]{3,2,1,0:T(2,128)S(1)} collective-permute-done((f32[2,32,2,132]{3,2,1,0:T(2,128)S(1)}, f32[2,32,2,132]{3,2,1,0:T(2,128)S(1)}, u32[]{:S(2)}, u32[]{:S(2)}) %collective-permute-start.11) | collective-permute-done | bytes 67616 | tf_op jit(solution)/shard_map/ppermute | solution.py:20
  126.6 4.1 %collective-permute-start.17 = (f32[2,32,16,2]{3,2,1,0:T(8,128)S(1)}, f32[2,32,16,2]{3,2,1,0:T(8,128)S(1)}, u32[]{:S(2)}, u32[]{:S(2)}) collective-permute-start(f32[2,32,16,2]{3,2,1,0:T(8,128)S(1)} %get-tuple-element.50), channel_id=1, source_target_pairs={{4,0},{8,4},{12,8},{16,12},{20,16},{24,20},{28,24},{0,28},{5,1},{9... | collective-permute-start | bytes 24584 | tf_op jit(solution)/shard_map/ppermute | solution.py:20
  130.8 16.1 %collective-permute-done.16 = f32[2,32,16,2]{3,2,1,0:T(8,128)S(1)} collective-permute-done((f32[2,32,16,2]{3,2,1,0:T(8,128)S(1)}, f32[2,32,16,2]{3,2,1,0:T(8,128)S(1)}, u32[]{:S(2)}, u32[]{:S(2)}) %collective-permute-start.16) | collective-permute-done | bytes 8224 | tf_op jit(solution)/shard_map/ppermute | solution.py:18
  146.9 2.2 %collective-permute-done.17 = f32[2,32,16,2]{3,2,1,0:T(8,128)S(1)} collective-permute-done((f32[2,32,16,2]{3,2,1,0:T(8,128)S(1)}, f32[2,32,16,2]{3,2,1,0:T(8,128)S(1)}, u32[]{:S(2)}, u32[]{:S(2)}) %collective-permute-start.17) | collective-permute-done | bytes 8224 | tf_op jit(solution)/shard_map/ppermute | solution.py:20
  149.7 1.9 %collective-permute-start.18 = (f32[2,32,2,132]{3,2,1,0:T(2,128)S(1)}, f32[2,32,2,132]{3,2,1,0:T(2,128)S(1)}, u32[]{:S(2)}, u32[]{:S(2)}) collective-permute-start(f32[2,32,2,132]{3,2,1,0:T(2,128)S(1)} %get-tuple-element.41), channel_id=1, source_target_pairs={{0,1},{1,2},{2,3},{4,5},{5,6},{6,7},{8,9},{9,10},{10,11},{12,13},{... | collective-permute-start | bytes 202760 | tf_op jit(solution)/shard_map/ppermute | solution.py:18
  151.6 2.4 %collective-permute-start.19 = (f32[2,32,2,132]{3,2,1,0:T(2,128)S(1)}, f32[2,32,2,132]{3,2,1,0:T(2,128)S(1)}, u32[]{:S(2)}, u32[]{:S(2)}) collective-permute-start(f32[2,32,2,132]{3,2,1,0:T(2,128)S(1)} %get-tuple-element.42), channel_id=1, source_target_pairs={{1,0},{2,1},{3,2},{5,4},{6,5},{7,6},{9,8},{10,9},{11,10},{13,12},{... | collective-permute-start | bytes 202760 | tf_op jit(solution)/shard_map/ppermute | solution.py:20
  154.4 3.5 %collective-permute-done.19 = f32[2,32,2,132]{3,2,1,0:T(2,128)S(1)} collective-permute-done((f32[2,32,2,132]{3,2,1,0:T(2,128)S(1)}, f32[2,32,2,132]{3,2,1,0:T(2,128)S(1)}, u32[]{:S(2)}, u32[]{:S(2)}) %collective-permute-start.19) | collective-permute-done | bytes 67616 | tf_op jit(solution)/shard_map/ppermute | solution.py:20
  (111 shorter events, 24.2 us)
Async XLA Ops:
  3.7 7.2 %copy-start.4 = (f32[32,16,128]{2,1,0:T(8,128)S(1)}, f32[32,16,128]{2,1,0:T(8,128)}, u32[]{:S(2)}) copy-start(f32[32,16,128]{2,1,0:T(8,128)} %param.13) | copy-start | bytes 786436
  3.7 7.2 %copy-start.5 = (f32[32,16,128]{2,1,0:T(8,128)S(1)}, f32[32,16,128]{2,1,0:T(8,128)}, u32[]{:S(2)}) copy-start(f32[32,16,128]{2,1,0:T(8,128)} %param.12) | copy-start | bytes 786436
  3.7 8.3 %copy-start = (f32[32,16,128]{2,1,0:T(8,128)S(1)}, f32[32,16,128]{2,1,0:T(8,128)}, u32[]{:S(2)}) copy-start(f32[32,16,128]{2,1,0:T(8,128)} %param.8) | copy-start | bytes 786436
  3.7 8.3 %copy-start.1 = (f32[32,16,128]{2,1,0:T(8,128)S(1)}, f32[32,16,128]{2,1,0:T(8,128)}, u32[]{:S(2)}) copy-start(f32[32,16,128]{2,1,0:T(8,128)} %param.7) | copy-start | bytes 786436
  4.7 51.6 %collective-permute-start = (f32[3,32,16,2]{1,2,3,0:T(8,128)}, f32[3,32,16,2]{1,2,3,0:T(8,128)}, u32[]{:S(2)}, u32[]{:S(2)}) collective-permute-start(f32[3,32,16,2]{1,2,3,0:T(8,128)} %copy.86), channel_id=1, source_target_pairs={{0,4},{4,8},{8,12},{12,16},{16,20},{20,24},{24,28},{28,0},{1,5},{5... | collective-permute-start | bytes 36872 | tf_op jit(solution)/shard_map/ppermute | solution.py:18
  7.8 52.6 %collective-permute-start.1 = (f32[3,32,16,2]{1,2,3,0:T(8,128)}, f32[3,32,16,2]{1,2,3,0:T(8,128)}, u32[]{:S(2)}, u32[]{:S(2)}) collective-permute-start(f32[3,32,16,2]{1,2,3,0:T(8,128)} %copy.87), channel_id=1, source_target_pairs={{4,0},{8,4},{12,8},{16,12},{20,16},{24,20},{28,24},{0,28},{5,1},{9... | collective-permute-start | bytes 36872 | tf_op jit(solution)/shard_map/ppermute | solution.py:20
  12.0 58.5 %collective-permute-start.12 = (f32[2,32,16,2]{3,2,1,0:T(8,128)}, f32[2,32,16,2]{3,2,1,0:T(8,128)}, u32[]{:S(2)}, u32[]{:S(2)}) collective-permute-start(f32[2,32,16,2]{3,2,1,0:T(8,128)} %get-tuple-element.51), channel_id=1, source_target_pairs={{0,4},{4,8},{8,12},{12,16},{16,20},{20,24},{24,28},{28,0},{1,5},{5... | collective-permute-start | bytes 24584 | tf_op jit(solution)/shard_map/ppermute | solution.py:18
  12.2 33.1 %collective-permute-start.2 = (f32[2,32,16,2]{3,2,1,0:T(8,128)S(1)}, f32[2,32,16,2]{3,2,1,0:T(8,128)S(1)}, u32[]{:S(2)}, u32[]{:S(2)}) collective-permute-start(f32[2,32,16,2]{3,2,1,0:T(8,128)S(1)} %get-tuple-element.62), channel_id=1, source_target_pairs={{0,4},{4,8},{8,12},{12,16},{16,20},{20,24},{24,28},{28,0},{1,5},{5... | collective-permute-start | bytes 24584 | tf_op jit(solution)/shard_map/ppermute | solution.py:18
  12.8 37.4 %collective-permute-start.3 = (f32[2,32,16,2]{3,2,1,0:T(8,128)S(1)}, f32[2,32,16,2]{3,2,1,0:T(8,128)S(1)}, u32[]{:S(2)}, u32[]{:S(2)}) collective-permute-start(f32[2,32,16,2]{3,2,1,0:T(8,128)S(1)} %get-tuple-element.63), channel_id=1, source_target_pairs={{4,0},{8,4},{12,8},{16,12},{20,16},{24,20},{28,24},{0,28},{5,1},{9... | collective-permute-start | bytes 24584 | tf_op jit(solution)/shard_map/ppermute | solution.py:20
  16.5 34.9 %copy-start.6 = (f32[31,16,128]{2,1,0:T(8,128)}, f32[31,16,128]{2,1,0:T(8,128)S(1)}, u32[]{:S(2)}) copy-start(f32[31,16,128]{2,1,0:T(8,128)S(1)} %fusion.69) | copy-start | bytes 761860
  45.2 11.1 %copy-start.8 = (f32[2,32,16,2]{3,2,1,0:T(8,128)}, f32[2,32,16,2]{3,2,1,0:T(8,128)S(1)}, u32[]{:S(2)}) copy-start(f32[2,32,16,2]{3,2,1,0:T(8,128)S(1)} %collective-permute-done.2) | copy-start | bytes 24580
  45.2 27.2 %collective-permute-start.13 = (f32[2,32,16,2]{3,2,1,0:T(8,128)}, f32[2,32,16,2]{3,2,1,0:T(8,128)}, u32[]{:S(2)}, u32[]{:S(2)}) collective-permute-start(f32[2,32,16,2]{3,2,1,0:T(8,128)} %get-tuple-element.52), channel_id=1, source_target_pairs={{4,0},{8,4},{12,8},{16,12},{20,16},{24,20},{28,24},{0,28},{5,1},{9... | collective-permute-start | bytes 24584 | tf_op jit(solution)/shard_map/ppermute | solution.py:20
  50.2 6.1 %copy-start.10 = (f32[2,32,16,2]{3,2,1,0:T(8,128)}, f32[2,32,16,2]{3,2,1,0:T(8,128)S(1)}, u32[]{:S(2)}) copy-start(f32[2,32,16,2]{3,2,1,0:T(8,128)S(1)} %collective-permute-done.3) | copy-start | bytes 24580
  51.3 28.5 %collective-permute-start.6 = (f32[2,32,2,132]{3,2,1,0:T(2,128)}, f32[2,32,2,132]{3,2,1,0:T(2,128)}, u32[]{:S(2)}, u32[]{:S(2)}) collective-permute-start(f32[2,32,2,132]{3,2,1,0:T(2,128)} %get-tuple-element.39), channel_id=1, source_target_pairs={{0,1},{1,2},{2,3},{4,5},{5,6},{6,7},{8,9},{9,10},{10,11},{12,13},{... | collective-permute-start | bytes 202760 | tf_op jit(solution)/shard_map/ppermute | solution.py:18
  56.4 25.6 %collective-permute-start.7 = (f32[2,32,2,132]{3,2,1,0:T(2,128)S(1)}, f32[2,32,2,132]{3,2,1,0:T(2,128)}, u32[]{:S(2)}, u32[]{:S(2)}) collective-permute-start(f32[2,32,2,132]{3,2,1,0:T(2,128)S(1)} %get-tuple-element.40), channel_id=1, source_target_pairs={{1,0},{2,1},{3,2},{5,4},{6,5},{7,6},{9,8},{10,9},{11,10},{13,12},{... | collective-permute-start | bytes 202760 | tf_op jit(solution)/shard_map/ppermute | solution.py:20
  64.8 1.4 copy-start.3
  64.8 1.4 copy-start.13
  64.9 1.5 copy-start.14
  66.8 17.2 %collective-permute-start.4 = (f32[3,32,2,132]{3,2,1,0:T(2,128)S(1)}, f32[3,32,2,132]{3,2,1,0:T(2,128)S(1)}, u32[]{:S(2)}, u32[]{:S(2)}) collective-permute-start(f32[3,32,2,132]{3,2,1,0:T(2,128)S(1)} %get-tuple-element.36), channel_id=1, source_target_pairs={{0,1},{1,2},{2,3},{4,5},{5,6},{6,7},{8,9},{9,10},{10,11},{12,13},{... | collective-permute-start | bytes 304136 | tf_op jit(solution)/shard_map/ppermute | solution.py:18
  70.5 14.6 %collective-permute-start.5 = (f32[3,32,2,132]{3,2,1,0:T(2,128)S(1)}, f32[3,32,2,132]{3,2,1,0:T(2,128)S(1)}, u32[]{:S(2)}, u32[]{:S(2)}) collective-permute-start(f32[3,32,2,132]{3,2,1,0:T(2,128)S(1)} %get-tuple-element.35), channel_id=1, source_target_pairs={{1,0},{2,1},{3,2},{5,4},{6,5},{7,6},{9,8},{10,9},{11,10},{13,12},{... | collective-permute-start | bytes 304136 | tf_op jit(solution)/shard_map/ppermute | solution.py:20
  74.2 18.9 %collective-permute-start.14 = (f32[2,32,2,132]{3,2,1,0:T(2,128)S(1)}, f32[2,32,2,132]{3,2,1,0:T(2,128)S(1)}, u32[]{:S(2)}, u32[]{:S(2)}) collective-permute-start(f32[2,32,2,132]{3,2,1,0:T(2,128)S(1)} %get-tuple-element.43), channel_id=1, source_target_pairs={{0,1},{1,2},{2,3},{4,5},{5,6},{6,7},{8,9},{9,10},{10,11},{12,13},{... | collective-permute-start | bytes 202760 | tf_op jit(solution)/shard_map/ppermute | solution.py:18
  79.4 2.6 %copy-start.9 = (f32[2,32,16,2]{3,2,1,0:T(8,128)S(1)}, f32[2,32,16,2]{3,2,1,0:T(8,128)}, u32[]{:S(2)}) copy-start(f32[2,32,16,2]{3,2,1,0:T(8,128)} %copy-done.8) | copy-start | bytes 24580
  79.4 2.6 %copy-start.11 = (f32[2,32,16,2]{3,2,1,0:T(8,128)S(1)}, f32[2,32,16,2]{3,2,1,0:T(8,128)}, u32[]{:S(2)}) copy-start(f32[2,32,16,2]{3,2,1,0:T(8,128)} %copy-done.10) | copy-start | bytes 24580
  79.8 13.3 %collective-permute-start.15 = (f32[2,32,2,132]{3,2,1,0:T(2,128)S(1)}, f32[2,32,2,132]{3,2,1,0:T(2,128)S(1)}, u32[]{:S(2)}, u32[]{:S(2)}) collective-permute-start(f32[2,32,2,132]{3,2,1,0:T(2,128)S(1)} %get-tuple-element.44), channel_id=1, source_target_pairs={{1,0},{2,1},{3,2},{5,4},{6,5},{7,6},{9,8},{10,9},{11,10},{13,12},{... | collective-permute-start | bytes 202760 | tf_op jit(solution)/shard_map/ppermute | solution.py:20
  88.9 21.4 %collective-permute-start.8 = (f32[2,32,16,2]{3,2,1,0:T(8,128)S(1)}, f32[2,32,16,2]{3,2,1,0:T(8,128)S(1)}, u32[]{:S(2)}, u32[]{:S(2)}) collective-permute-start(f32[2,32,16,2]{3,2,1,0:T(8,128)S(1)} %get-tuple-element.55), channel_id=1, source_target_pairs={{0,4},{4,8},{8,12},{12,16},{16,20},{20,24},{24,28},{28,0},{1,5},{5... | collective-permute-start | bytes 24584 | tf_op jit(solution)/shard_map/ppermute | solution.py:18
  89.0 23.5 %collective-permute-start.9 = (f32[2,32,16,2]{3,2,1,0:T(8,128)S(1)}, f32[2,32,16,2]{3,2,1,0:T(8,128)S(1)}, u32[]{:S(2)}, u32[]{:S(2)}) collective-permute-start(f32[2,32,16,2]{3,2,1,0:T(8,128)S(1)} %get-tuple-element.56), channel_id=1, source_target_pairs={{4,0},{8,4},{12,8},{16,12},{20,16},{24,20},{28,24},{0,28},{5,1},{9... | collective-permute-start | bytes 24584 | tf_op jit(solution)/shard_map/ppermute | solution.py:20
  113.0 7.1 %collective-permute-start.10 = (f32[2,32,2,132]{3,2,1,0:T(2,128)S(1)}, f32[2,32,2,132]{3,2,1,0:T(2,128)S(1)}, u32[]{:S(2)}, u32[]{:S(2)}) collective-permute-start(f32[2,32,2,132]{3,2,1,0:T(2,128)S(1)} %get-tuple-element.32), channel_id=1, source_target_pairs={{0,1},{1,2},{2,3},{4,5},{5,6},{6,7},{8,9},{9,10},{10,11},{12,13},{... | collective-permute-start | bytes 202760 | tf_op jit(solution)/shard_map/ppermute | solution.py:18
  117.0 6.3 %collective-permute-start.11 = (f32[2,32,2,132]{3,2,1,0:T(2,128)S(1)}, f32[2,32,2,132]{3,2,1,0:T(2,128)S(1)}, u32[]{:S(2)}, u32[]{:S(2)}) collective-permute-start(f32[2,32,2,132]{3,2,1,0:T(2,128)S(1)} %get-tuple-element.33), channel_id=1, source_target_pairs={{1,0},{2,1},{3,2},{5,4},{6,5},{7,6},{9,8},{10,9},{11,10},{13,12},{... | collective-permute-start | bytes 202760 | tf_op jit(solution)/shard_map/ppermute | solution.py:20
  126.5 20.4 %collective-permute-start.16 = (f32[2,32,16,2]{3,2,1,0:T(8,128)S(1)}, f32[2,32,16,2]{3,2,1,0:T(8,128)S(1)}, u32[]{:S(2)}, u32[]{:S(2)}) collective-permute-start(f32[2,32,16,2]{3,2,1,0:T(8,128)S(1)} %get-tuple-element.49), channel_id=1, source_target_pairs={{0,4},{4,8},{8,12},{12,16},{16,20},{20,24},{24,28},{28,0},{1,5},{5... | collective-permute-start | bytes 24584 | tf_op jit(solution)/shard_map/ppermute | solution.py:18
  126.6 22.5 %collective-permute-start.17 = (f32[2,32,16,2]{3,2,1,0:T(8,128)S(1)}, f32[2,32,16,2]{3,2,1,0:T(8,128)S(1)}, u32[]{:S(2)}, u32[]{:S(2)}) collective-permute-start(f32[2,32,16,2]{3,2,1,0:T(8,128)S(1)} %get-tuple-element.50), channel_id=1, source_target_pairs={{4,0},{8,4},{12,8},{16,12},{20,16},{24,20},{28,24},{0,28},{5,1},{9... | collective-permute-start | bytes 24584 | tf_op jit(solution)/shard_map/ppermute | solution.py:20
  149.7 4.7 %collective-permute-start.18 = (f32[2,32,2,132]{3,2,1,0:T(2,128)S(1)}, f32[2,32,2,132]{3,2,1,0:T(2,128)S(1)}, u32[]{:S(2)}, u32[]{:S(2)}) collective-permute-start(f32[2,32,2,132]{3,2,1,0:T(2,128)S(1)} %get-tuple-element.41), channel_id=1, source_target_pairs={{0,1},{1,2},{2,3},{4,5},{5,6},{6,7},{8,9},{9,10},{10,11},{12,13},{... | collective-permute-start | bytes 202760 | tf_op jit(solution)/shard_map/ppermute | solution.py:18
  151.6 6.3 %collective-permute-start.19 = (f32[2,32,2,132]{3,2,1,0:T(2,128)S(1)}, f32[2,32,2,132]{3,2,1,0:T(2,128)S(1)}, u32[]{:S(2)}, u32[]{:S(2)}) collective-permute-start(f32[2,32,2,132]{3,2,1,0:T(2,128)S(1)} %get-tuple-element.42), channel_id=1, source_target_pairs={{1,0},{2,1},{3,2},{5,4},{6,5},{7,6},{9,8},{10,9},{11,10},{13,12},{... | collective-permute-start | bytes 202760 | tf_op jit(solution)/shard_map/ppermute | solution.py:20
  (4 other events, 4.1 us)
where the time goes:
time: 161 us; the launch traced here: 160 us
  waiting for transfers between devices  69 us (43%)
  starting transfers between devices  50.8 us (32%)
  other arithmetic  25.1 us (16%)
  local copies, waits for them, and re-layouts  13.9 us (9%)
    ppermute x10, waiting for transfers between devices, padded_2(): lax.ppermute(tail, axis, [(i, (i + 1) % count) for i in range(ends)])  57.9 us
    ppermute x10, starting transfers between devices, padded_2(): lax.ppermute(head, axis, [((i + 1) % count, i) for i in range(ends)])  30.2 us
    ppermute x10, starting transfers between devices, padded_2(): lax.ppermute(tail, axis, [(i, (i + 1) % count) for i in range(ends)])  20.6 us
    ppermute x10, waiting for transfers between devices, padded_2(): lax.ppermute(head, axis, [((i + 1) % count, i) for i in range(ends)])  11.1 us
    unnamed x40, local copies, waits for them, and re-layouts  5.81 us
    concatenate x4, other arithmetic, padded_2(): jnp.concatenate([lax.ppermute(tail, axis, [(i, (i + 1) % count) for i in...  5.74 us
    mul x5, other arithmetic, face_change(): open_face * (weights[0] * far_left + weights[1] * left + weights[2] * rig...  4.12 us
    mul x4, other arithmetic, face_adjoint(): weighted = wetness * field  4.1 us
  transfers between devices with their start and end apart: 20, of which 7 were waited for; matrix products, arithmetic and copies ran while one was open for 16% of the time, Pallas kernels for 0%

commit v1 on v0

v1 whole, which is shorter than its diff:
```python
import jax
import jax.numpy as jnp
from jax import lax
from jax.experimental import pallas as pl
from jax.experimental.pallas import tpu as pltpu
from jax.sharding import PartitionSpec as P

horizontal_mix = 0.05
vertical_mix = 0.2

F32 = jnp.float32
K = 32
R = 16
W = 128
HALO = 4
E = R + 2 * HALO
FIELDS = 7
U, V, M = 4, 5, 6
EDGE_BLOCKS = 4
SIDE_BLOCKS = 28
ROWS_AT = (0, 4, 8, 12, 24, 16, 20)
CORNERS_AT = 26
MIB = 1 << 20


def lanes():
    return lax.broadcasted_iota(jnp.int32, (K, W), 1)


def turn(x, amount):
    return pltpu.roll(x, amount % W, 1)


def row_of(ref, j):
    return ref[pl.ds(j, K, stride=R), :].astype(F32)


def pack_edges(*refs):
    fields, (east, west) = refs[:FIELDS], refs[FIELDS:]
    lane = lanes()
    for block in range(EDGE_BLOCKS):
        to_east = to_west = jnp.zeros((K, W), F32)
        for f in range(2 * block, min(2 * block + 2, FIELDS)):
            for r in range(R):
                start = 64 * (f % 2) + 4 * r
                turned = turn(row_of(fields[f], r), start + 4)
                group = lane // 4
                to_east = jnp.where(group == start // 4, turned, to_east)
                to_west = jnp.where(group == (start // 4 + 1) % (W // 4), turned, to_west)
        east[block] = to_east
        west[block] = to_west


def pack_sides(*refs):
    fields, (from_west, from_east, first, second) = refs[:FIELDS], refs[FIELDS:]
    odd = lax.axis_index("ns") % 2
    lane = lanes()
    for out, north in ((first, 1 - odd), (second, odd)):
        start = (R - HALO) * north
        for f in range(FIELDS):
            for r in range(2 if f == U else HALO):
                shift = 2 * north if f == U else 0
                out[ROWS_AT[f] + r] = row_of(fields[f], start + shift + r)
        left = right = jnp.zeros((K, W), F32)
        for f in range(FIELDS):
            amount = lax.rem(16 * f + 2 * W - 64 * (f % 2) - 4 * start, W)
            a = pltpu.roll(from_west[f // 2], amount, 1)
            b = pltpu.roll(from_east[f // 2], amount, 1)
            left = jnp.where((lane >= 16 * f) & (lane < 16 * f + 16), a, left)
            right = jnp.where((lane >= 16 * f + 4) & (lane < 16 * f + 20), b, right)
        out[CORNERS_AT] = left
        out[CORNERS_AT + 1] = right


def shifted(c, h, d, lane):
    if d > 0:
        return turn(jnp.where(lane < d, h, c), -d)
    return turn(jnp.where(lane >= W + d, h, c), -d)


def face_weights(speed, open_face):
    magnitude = jnp.abs(speed)
    forth = (-speed - magnitude) / 12.0
    back = (-speed + magnitude) / 12.0
    near = (7.0 * speed + 3.0 * magnitude) / 12.0 + horizontal_mix
    far = (7.0 * speed - 3.0 * magnitude) / 12.0 - horizontal_mix
    return forth * open_face, near * open_face, far * open_face, back * open_face


def compute(*refs):
    fields = refs[:FIELDS]
    from_west, from_east, first, second = refs[FIELDS : FIELDS + 4]
    outs = refs[FIELDS + 4 : FIELDS + 8]
    c_ref, h_ref, c1_ref, h1_ref, y_ref, yh_ref, x_ref, xh_ref = refs[FIELDS + 8 :]
    lane = lanes()
    place = lax.axis_index("ns")
    last = lax.axis_size("ns") - 1
    odd = place % 2

    def fill(r, carry):
        for f in range(FIELDS):
            c_ref[f, r + HALO] = row_of(fields[f], r)
            start = 64 * (f % 2) + 4 * r
            a = from_west[f // 2]
            b = from_east[f // 2]
            h = jnp.where((lane >= start) & (lane < start + 4), a, b)
            h_ref[f, r + HALO] = pltpu.roll(h, lax.rem(2 * W - 4 - start, W), 1)
        return carry

    lax.fori_loop(0, R, fill, 0)

    def halo(ref, base, keep, north):
        for f in range(FIELDS):
            rows = range(2) if f == U else range(HALO)
            for r in rows:
                at = base + r + (2 if f == U and not north else 0)
                c_ref[f, at] = jnp.where(keep, ref[ROWS_AT[f] + r], 0.0)
            for r in (range(0, 2) if north else range(2, 4)):
                start = 16 * f + 4 * r
                h = jnp.where(
                    (lane >= start) & (lane < start + 4), ref[CORNERS_AT], ref[CORNERS_AT + 1]
                )
                h_ref[f, base + r] = jnp.where(keep, turn(h, W - 4 - start), 0.0)

    @pl.when(odd == 0)
    def _():
        halo(first, HALO + R, place < last, True)
        halo(second, 0, place > 0, False)

    @pl.when(odd == 1)
    def _():
        halo(second, HALO + R, place < last, True)
        halo(first, 0, place > 0, False)

    def y_faces(source, target):
        def body(e, carry):
            speed = source[V, e]
            open_face = source[M, e] * source[M, e + 1]
            w = face_weights(speed, open_face)
            for k in range(4):
                target[k, e] = w[k]
            return carry

        return body

    lax.fori_loop(0, E - 1, y_faces(c_ref, y_ref), 0)
    lax.fori_loop(2, E - 3, y_faces(h_ref, yh_ref), 0)

    def x_coefficients(e, carry):
        m, mh = c_ref[M, e], h_ref[M, e]
        u, uh = c_ref[U, e], h_ref[U, e]
        w = face_weights(u, m * shifted(m, mh, 1, lane))
        wh = face_weights(uh, mh * shifted(mh, m, 1, lane))
        vertical = lax.broadcasted_iota(jnp.int32, (K, W), 0) < K - 1
        for own, other, mask, target, y in ((w, wh, m, x_ref, y_ref), (wh, w, mh, xh_ref, yh_ref)):
            back = [shifted(own[k], other[k], -1, lane) for k in range(4)]
            q0 = shifted(own[0], other[0], 1, lane)
            b2 = back[3] - own[2]
            up = jnp.where(vertical, vertical_mix * mask * pltpu.roll(mask, K - 1, 0), 0.0)
            down = pltpu.roll(up, 1, 0)
            w3back2 = shifted(own[3], other[3], -2, lane)
            target[0, e] = back[0]
            target[1, e] = back[1] - own[0]
            target[2, e] = b2
            target[3, e] = -own[3]
            target[4, e] = -w3back2
            target[5, e] = w3back2 - back[2]
            target[6, e] = own[1] - q0
            target[7, e] = q0
            target[8, e] = up
            target[9, e] = down
            target[10, e] = 1.0 + (back[2] - own[1]) - up - down + (y[2, e - 1] - y[1, e])
        return carry

    lax.fori_loop(2, E - 2, x_coefficients, 0)

    def stencil(source, h_source, x, y, e, forward, swap, fields_here):
        if forward:
            xs = [x[k, e] for k in (0, 1, 2, 3)]
            ys = [
                y[0, e - 1],
                y[1, e - 1] - y[0, e],
                y[3, e - 1] - y[2, e],
                -y[3, e],
            ]
        else:
            xs = [x[k, e] for k in (4, 5, 6, 7)]
            ys = [
                -y[3, e - 2],
                y[3, e - 2] - y[2, e - 1],
                y[1, e] - y[0, e + 1],
                y[0, e + 1],
            ]
        up, down, centre = x[8, e], x[9, e], x[10, e]
        results = []
        for f in fields_here:
            own, other = (h_source, source) if swap else (source, h_source)
            c, h = own[f, e], other[f, e]
            total = centre * c
            total += up * pltpu.roll(c, K - 1, 0) + down * pltpu.roll(c, 1, 0)
            for coefficient, d in zip(xs, (-2, -1, 1, 2)):
                total += coefficient * shifted(c, h, d, lane)
            for coefficient, d in zip(ys, (-2, -1, 1, 2)):
                total += coefficient * own[f, e + d]
            results.append(total)
        return results

    def first_step(e, carry):
        inside = ((place > 0) | (e >= HALO)) & ((place < last) | (e < HALO + R))
        for forward, here in ((True, (0, 1)), (False, (2, 3))):
            got = stencil(c_ref, h_ref, x_ref, y_ref, e, forward, False, here)
            for f, value in zip(here, got):
                c1_ref[f, e] = value if forward else jnp.where(inside, value, 0.0)
        return carry

    lax.fori_loop(2, E - 2, first_step, 0)

    def first_step_halo(e, carry):
        for forward, here in ((True, (0, 1)), (False, (2, 3))):
            got = stencil(c_ref, h_ref, xh_ref, yh_ref, e, forward, True, here)
            for f, value in zip(here, got):
                h1_ref[f, e] = value
        return carry

    lax.fori_loop(HALO, HALO + R, first_step_halo, 0)

    def second_step(e, carry):
        for forward, here in ((True, (0, 1)), (False, (2, 3))):
            got = stencil(c1_ref, h1_ref, x_ref, y_ref, e, forward, False, here)
            for f, value in zip(here, got):
                outs[f][pl.ds(e - HALO, K, stride=R), :] = value
        return carry

    lax.fori_loop(HALO, HALO + R, second_step, 0)


def vmem():
    return pl.BlockSpec(memory_space=pltpu.VMEM)


def call(kernel, n_in, out_shapes, scratch=(), limit=24 * MIB):
    return pl.pallas_call(
        kernel,
        out_shape=[jax.ShapeDtypeStruct(shape, F32) for shape in out_shapes],
        in_specs=[vmem()] * n_in,
        out_specs=[vmem()] * len(out_shapes),
        scratch_shapes=list(scratch),
        compiler_params=pltpu.CompilerParams(vmem_limit_bytes=limit),
    )


def local(temp, salt, u_east, v_north, wet, cot_temp, cot_salt):
    flat = [a.reshape(K * R, W) for a in (temp, salt, cot_temp, cot_salt, u_east, v_north, wet)]

    n = lax.axis_size("ew")
    edge = (EDGE_BLOCKS, K, W)
    to_east, to_west = call(pack_edges, FIELDS, [edge, edge])(*flat)
    from_west = lax.ppermute(to_east, "ew", [(i, (i + 1) % n) for i in range(n)])
    from_east = lax.ppermute(to_west, "ew", [((i + 1) % n, i) for i in range(n)])

    n = lax.axis_size("ns")
    side = (SIDE_BLOCKS, K, W)
    first, second = call(pack_sides, FIELDS + 2, [side, side])(*flat, from_west, from_east)

    def partners(odd):
        pairs = [(i, i + 1) for i in range(odd, n - 1, 2)]
        met = {i for pair in pairs for i in pair}
        return pairs + [(b, a) for a, b in pairs] + [(i, i) for i in range(n) if i not in met]

    second = lax.ppermute(second, "ns", partners(1))
    first = lax.ppermute(first, "ns", partners(0))

    outs = call(
        compute,
        FIELDS + 4,
        [(K * R, W)] * 4,
        [
            pltpu.VMEM((FIELDS, E, K, W), F32),
            pltpu.VMEM((FIELDS, E, K, W), F32),
            pltpu.VMEM((4, E, K, W), F32),
            pltpu.VMEM((4, E, K, W), F32),
            pltpu.VMEM((4, E, K, W), F32),
            pltpu.VMEM((4, E, K, W), F32),
            pltpu.VMEM((11, E, K, W), F32),
            pltpu.VMEM((11, E, K, W), F32),
        ],
        limit=40 * MIB,
    )(*flat, from_west, from_east, first, second)
    return tuple(a.reshape(K, R, W) for a in outs)


def solution(mesh):
    spec = P(None, "ns", "ew")
    return jax.shard_map(
        local, mesh=mesh, in_specs=(spec,) * 7, out_specs=(spec,) * 4, check_vma=False
    )
```

time: 161 us -> 43.3 us (0.27)
  waiting for transfers between devices: 69 us -> 8.34 us
  starting transfers between devices: 50.8 us -> 10.3 us
  other arithmetic: 25.1 us -> 0 us
  Pallas kernels: 0 us -> 16.9 us
  local copies, waits for them, and re-layouts: 13.9 us -> 6.68 us
    ppermute x20 -> x4, waiting for transfers between devices: 69 us -> 8.34 us  [the longest x1 6.72 us: local(): second = lax.ppermute(second, 'ns', partners(1))]
    ppermute x20 -> x4, starting transfers between devices: 50.8 us -> 10.3 us  [the longest x1 3.14 us: local(): lax.ppermute(to_west, 'ew', [((i + 1) % n, i) for i in range(n)])]
    pallas_call x0 -> x3, Pallas kernels: none -> 16.9 us  [the longest x1 15.8 us: local(): call(compute, FIELDS + 4, [(K * R, W)] * 4, [pltpu.VMEM((FIELDS, E, K, W)...]
    mul x24 -> x0, other arithmetic: 12.7 us -> none  [the longest x5 4.12 us: face_change(): open_face * (weights[0] * far_left + weights[1] * left + weights[2] * rig...]
    concatenate x4 -> x0, other arithmetic: 5.74 us -> none  [padded_2(): jnp.concatenate([lax.ppermute(tail, axis, [(i, (i + 1) % count) for i in...]
    ppermute x2 -> x0, local copies, waits for them, and re-layouts: 4.14 us -> none  [the longest x1 2.09 us: padded_2(): lax.ppermute(tail, axis, [(i, (i + 1) % count) for i in range(ends)])]
    another operation x3 -> x0, other arithmetic: 2.4 us -> none  [the longest x1 1.12 us: local(): sensitivity = evolve(jnp.stack([cot_temp, cot_salt]), flow_wide, retreat)]
    convert_element_type x1 -> x0, other arithmetic: 1.69 us -> none  [local(): wet.astype(jnp.float32)]
  transfers between devices with their start and end apart: 20 -> 4, of which waited for: 7 -> 2; matrix products, arithmetic and copies ran while one was open for 16% -> 0% of each run, Pallas kernels for 0% -> 0%
where the time goes in v1:
time: 43.3 us; the launch traced here: 42.9 us
  Pallas kernels  16.9 us (39%)
  starting transfers between devices  10.3 us (24%)
  waiting for transfers between devices  8.34 us (19%)
  local copies, waits for them, and re-layouts  6.68 us (15%)
  between operations  0.74 us (2%)
    pallas_call x1, Pallas kernels, local(): call(compute, FIELDS + 4, [(K * R, W)] * 4, [pltpu.VMEM((FIELDS, E, K, W)...  15.8 us
    ppermute x1, waiting for transfers between devices, local(): second = lax.ppermute(second, 'ns', partners(1))  6.72 us
    unnamed x28, local copies, waits for them, and re-layouts  6.68 us
    ppermute x1, starting transfers between devices, local(): lax.ppermute(to_west, 'ew', [((i + 1) % n, i) for i in range(n)])  3.14 us
    ppermute x1, starting transfers between devices, local(): second = lax.ppermute(second, 'ns', partners(1))  3.05 us
    ppermute x1, starting transfers between devices, local(): lax.ppermute(to_east, 'ew', [(i, (i + 1) % n) for i in range(n)])  2.09 us
    ppermute x1, starting transfers between devices, local(): first = lax.ppermute(first, 'ns', partners(0))  1.98 us
    ppermute x1, waiting for transfers between devices, local(): lax.ppermute(to_east, 'ew', [(i, (i + 1) % n) for i in range(n)])  1.61 us
  transfers between devices with their start and end apart: 4, of which 2 were waited for; matrix products, arithmetic and copies ran while one was open for 0% of the time, Pallas kernels for 0%

profile of v1, /device:TPU:1, one launch (start us, length us, event | category | flops | bytes accessed | tf_op | source)
XLA Modules:
  0.0 42.9 jit_solution(14631571588954270022)
XLA Ops:
  0.6 0.0 copy-start
  0.6 0.9 %copy-done = f32[32,16,128]{2,1,0:T(8,128)S(1)} copy-done((f32[32,16,128]{2,1,0:T(8,128)S(1)}, f32[32,16,128]{2,1,0:T(8,128)}, u32[]{:S(2)}) %copy-start) | copy-done | bytes 262168
  1.6 0.0 copy-start.2
  1.6 0.9 %copy-done.2 = f32[32,16,128]{2,1,0:T(8,128)S(1)} copy-done((f32[32,16,128]{2,1,0:T(8,128)S(1)}, f32[32,16,128]{2,1,0:T(8,128)}, u32[]{:S(2)}) %copy-start.2) | copy-done | bytes 262168
  2.5 0.0 copy-start.4
  2.5 0.9 %copy-done.4 = f32[32,16,128]{2,1,0:T(8,128)S(1)} copy-done((f32[32,16,128]{2,1,0:T(8,128)S(1)}, f32[32,16,128]{2,1,0:T(8,128)}, u32[]{:S(2)}) %copy-start.4) | copy-done | bytes 262168
  3.5 0.0 copy-start.6
  3.5 0.9 %copy-done.6 = f32[32,16,128]{2,1,0:T(8,128)S(1)} copy-done((f32[32,16,128]{2,1,0:T(8,128)S(1)}, f32[32,16,128]{2,1,0:T(8,128)}, u32[]{:S(2)}) %copy-start.6) | copy-done | bytes 262168
  4.4 0.9 %copy-done.8 = f32[32,16,128]{2,1,0:T(8,128)S(1)} copy-done((f32[32,16,128]{2,1,0:T(8,128)S(1)}, f32[32,16,128]{2,1,0:T(8,128)}, u32[]{:S(2)}) %copy-start.8) | copy-done | bytes 262168
  5.4 0.9 %copy-done.10 = f32[32,16,128]{2,1,0:T(8,128)S(1)} copy-done((f32[32,16,128]{2,1,0:T(8,128)S(1)}, f32[32,16,128]{2,1,0:T(8,128)}, u32[]{:S(2)}) %copy-start.10) | copy-done | bytes 262168
  6.3 0.9 %copy-done.12 = s32[32,16,128]{2,1,0:T(8,128)S(1)} copy-done((s32[32,16,128]{2,1,0:T(8,128)S(1)}, s32[32,16,128]{2,1,0:T(8,128)}, u32[]{:S(2)}) %copy-start.12) | copy-done | bytes 262168
  7.3 0.6 %shard_map.102 = (f32[4,32,128]{2,1,0:T(8,128)S(1)}, f32[4,32,128]{2,1,0:T(8,128)S(1)}) custom-call(f32[512,128]{1,0:T(8,128)S(1)} %bitcast.11, f32[512,128]{1,0:T(8,128)S(1)} %bitcast.14, f32[512,128]{1,0:T(8,128)S(1)} %bitcast.17, f32[512,128]{1,0:T(8,128)S(1)} %bitcast.20, f32[512,128]{1,0:T(8,128)S(1)} %bitcast.23, f32[512,128]{1,0:T(8,128)S(1)} %bitcast.26, ...), custom_call_target="tpu_custom_call" | custom-call | tf_op jit(solution)/shard_map/pallas_call | solution.py:257
  7.9 2.1 %collective-permute-start = (f32[4,32,128]{2,1,0:T(8,128)S(1)}, f32[4,32,128]{2,1,0:T(8,128)S(1)}, u32[]{:S(2)}, u32[]{:S(2)}) collective-permute-start(f32[4,32,128]{2,1,0:T(8,128)S(1)} %get-tuple-element.12), channel_id=1, source_target_pairs={{0,4},{4,8},{8,12},{12,16},{16,20},{20,24},{24,28},{28,0},{1,5},{5... | collective-permute-start | bytes 196616 | tf_op jit(solution)/shard_map/ppermute | solution.py:258
  10.0 0.0 copy-start.9
  10.1 0.0 copy-start.11
  10.1 0.0 copy-start.13
  10.1 3.1 %collective-permute-start.1 = (f32[4,32,128]{2,1,0:T(8,128)S(1)}, f32[4,32,128]{2,1,0:T(8,128)S(1)}, u32[]{:S(2)}, u32[]{:S(2)}) collective-permute-start(f32[4,32,128]{2,1,0:T(8,128)S(1)} %get-tuple-element.13), channel_id=1, source_target_pairs={{4,0},{8,4},{12,8},{16,12},{20,16},{24,20},{28,24},{0,28},{5,1},{9... | collective-permute-start | bytes 196616 | tf_op jit(solution)/shard_map/ppermute | solution.py:259
  13.2 1.6 %collective-permute-done.refs_7_ = f32[4,32,128]{2,1,0:T(8,128)S(1)} collective-permute-done((f32[4,32,128]{2,1,0:T(8,128)S(1)}, f32[4,32,128]{2,1,0:T(8,128)S(1)}, u32[]{:S(2)}, u32[]{:S(2)}) %collective-permute-start) | collective-permute-done | bytes 65568 | tf_op jit(solution)/shard_map/ppermute | solution.py:258
  14.8 0.0 collective-permute-done.1.refs_8_
  14.8 0.4 %shard_map.103 = (f32[28,32,128]{2,1,0:T(8,128)S(1)}, f32[28,32,128]{2,1,0:T(8,128)S(1)}) custom-call(f32[512,128]{1,0:T(8,128)S(1)} %bitcast.12, f32[512,128]{1,0:T(8,128)S(1)} %bitcast.15, f32[512,128]{1,0:T(8,128)S(1)} %bitcast.18, f32[512,128]{1,0:T(8,128)S(1)} %bitcast.21, f32[512,128]{1,0:T(8,128)S(1)} %bitcast.24, f32[512,128]{1,0:T(8,128)S(1)} %bitcast.27, ...), custom_call_target="tpu_custom_call" | custom-call | tf_op jit(solution)/shard_map/pallas_call | solution.py:263
  15.3 2.0 %collective-permute-start.2 = (f32[28,32,128]{2,1,0:T(8,128)S(1)}, f32[28,32,128]{2,1,0:T(8,128)S(1)}, u32[]{:S(2)}, u32[]{:S(2)}) collective-permute-start(f32[28,32,128]{2,1,0:T(8,128)S(1)} %get-tuple-element.14), channel_id=1, source_target_pairs={{0,1},{2,3},{1,0},{3,2},{4,5},{6,7},{5,4},{7,6},{8,9},{10,11},{9,8... | collective-permute-start | bytes 1376264 | tf_op jit(solution)/shard_map/ppermute | solution.py:271
  17.3 3.0 %collective-permute-start.3 = (f32[28,32,128]{2,1,0:T(8,128)S(1)}, f32[28,32,128]{2,1,0:T(8,128)S(1)}, u32[]{:S(2)}, u32[]{:S(2)}) collective-permute-start(f32[28,32,128]{2,1,0:T(8,128)S(1)} %get-tuple-element.15), channel_id=1, source_target_pairs={{1,2},{2,1},{0,0},{3,3},{5,6},{6,5},{4,4},{7,7},{9,10},{10,9},{8,8... | collective-permute-start | bytes 1376264 | tf_op jit(solution)/shard_map/ppermute | solution.py:270
  20.3 0.0 collective-permute-done.2.refs_9_
  20.3 6.7 %collective-permute-done.3.refs_10_ = f32[28,32,128]{2,1,0:T(8,128)S(1)} collective-permute-done((f32[28,32,128]{2,1,0:T(8,128)S(1)}, f32[28,32,128]{2,1,0:T(8,128)S(1)}, u32[]{:S(2)}, u32[]{:S(2)}) %collective-permute-start.3) | collective-permute-done | bytes 458784 | tf_op jit(solution)/shard_map/ppermute | solution.py:270
  27.1 0.0 copy-done.1
  27.1 0.0 copy-done.3
  27.1 0.0 copy-done.5
  27.1 0.0 copy-done.7
  27.1 0.0 copy-done.9
  27.1 0.0 copy-done.11
  27.1 0.0 copy-done.13
  27.1 15.8 %shard_map.104 = (f32[512,128]{1,0:T(8,128)}, f32[512,128]{1,0:T(8,128)}, f32[512,128]{1,0:T(8,128)}, f32[512,128]{1,0:T(8,128)}) custom-call(f32[512,128]{1,0:T(8,128)S(1)} %bitcast.13, f32[512,128]{1,0:T(8,128)S(1)} %bitcast.16, f32[512,128]{1,0:T(8,128)S(1)} %bitcast.19, f32[512,128]{1,0:T(8,128)S(1)} %bitcast.22, f32[512,128]{1,0:T(8,128)S(1)} %bitcast.25, ...), custom_call_target="tpu_custom_call" | custom-call | tf_op jit(solution)/shard_map/pallas_call | solution.py:273
  (7 shorter events, 0.0 us)
Async XLA Ops:
  0.6 1.0 %copy-start = (f32[32,16,128]{2,1,0:T(8,128)S(1)}, f32[32,16,128]{2,1,0:T(8,128)}, u32[]{:S(2)}) copy-start(f32[32,16,128]{2,1,0:T(8,128)} %param.7) | copy-start | bytes 786436
  1.6 0.9 %copy-start.2 = (f32[32,16,128]{2,1,0:T(8,128)S(1)}, f32[32,16,128]{2,1,0:T(8,128)}, u32[]{:S(2)}) copy-start(f32[32,16,128]{2,1,0:T(8,128)} %param.8) | copy-start | bytes 786436
  2.5 0.9 %copy-start.4 = (f32[32,16,128]{2,1,0:T(8,128)S(1)}, f32[32,16,128]{2,1,0:T(8,128)}, u32[]{:S(2)}) copy-start(f32[32,16,128]{2,1,0:T(8,128)} %param.12) | copy-start | bytes 786436
  3.5 0.9 %copy-start.6 = (f32[32,16,128]{2,1,0:T(8,128)S(1)}, f32[32,16,128]{2,1,0:T(8,128)}, u32[]{:S(2)}) copy-start(f32[32,16,128]{2,1,0:T(8,128)} %param.13) | copy-start | bytes 786436
  4.4 0.9 %copy-start.8 = (f32[32,16,128]{2,1,0:T(8,128)S(1)}, f32[32,16,128]{2,1,0:T(8,128)}, u32[]{:S(2)}) copy-start(f32[32,16,128]{2,1,0:T(8,128)} %param.9) | copy-start | bytes 786436
  5.4 0.9 %copy-start.10 = (f32[32,16,128]{2,1,0:T(8,128)S(1)}, f32[32,16,128]{2,1,0:T(8,128)}, u32[]{:S(2)}) copy-start(f32[32,16,128]{2,1,0:T(8,128)} %param.10) | copy-start | bytes 786436
  6.3 0.9 %copy-start.12 = (s32[32,16,128]{2,1,0:T(8,128)S(1)}, s32[32,16,128]{2,1,0:T(8,128)}, u32[]{:S(2)}) copy-start(s32[32,16,128]{2,1,0:T(8,128)} %param.11) | copy-start | bytes 786436
  7.9 6.9 %collective-permute-start = (f32[4,32,128]{2,1,0:T(8,128)S(1)}, f32[4,32,128]{2,1,0:T(8,128)S(1)}, u32[]{:S(2)}, u32[]{:S(2)}) collective-permute-start(f32[4,32,128]{2,1,0:T(8,128)S(1)} %get-tuple-element.12), channel_id=1, source_target_pairs={{0,4},{4,8},{8,12},{12,16},{16,20},{20,24},{24,28},{28,0},{1,5},{5... | collective-permute-start | bytes 196616 | tf_op jit(solution)/shard_map/ppermute | solution.py:258
  10.0 17.0 %copy-start.1 = (f32[32,16,128]{2,1,0:T(8,128)S(1)}, f32[32,16,128]{2,1,0:T(8,128)}, u32[]{:S(2)}) copy-start(f32[32,16,128]{2,1,0:T(8,128)} %param.7) | copy-start | bytes 786436
  10.0 17.0 %copy-start.3 = (f32[32,16,128]{2,1,0:T(8,128)S(1)}, f32[32,16,128]{2,1,0:T(8,128)}, u32[]{:S(2)}) copy-start(f32[32,16,128]{2,1,0:T(8,128)} %param.8) | copy-start | bytes 786436
  10.0 17.0 %copy-start.5 = (f32[32,16,128]{2,1,0:T(8,128)S(1)}, f32[32,16,128]{2,1,0:T(8,128)}, u32[]{:S(2)}) copy-start(f32[32,16,128]{2,1,0:T(8,128)} %param.12) | copy-start | bytes 786436
  10.0 17.0 %copy-start.7 = (f32[32,16,128]{2,1,0:T(8,128)S(1)}, f32[32,16,128]{2,1,0:T(8,128)}, u32[]{:S(2)}) copy-start(f32[32,16,128]{2,1,0:T(8,128)} %param.13) | copy-start | bytes 786436
  10.0 17.0 %copy-start.9 = (f32[32,16,128]{2,1,0:T(8,128)S(1)}, f32[32,16,128]{2,1,0:T(8,128)}, u32[]{:S(2)}) copy-start(f32[32,16,128]{2,1,0:T(8,128)} %param.9) | copy-start | bytes 786436
  10.1 17.0 %copy-start.11 = (f32[32,16,128]{2,1,0:T(8,128)S(1)}, f32[32,16,128]{2,1,0:T(8,128)}, u32[]{:S(2)}) copy-start(f32[32,16,128]{2,1,0:T(8,128)} %param.10) | copy-start | bytes 786436
  10.1 17.0 %copy-start.13 = (s32[32,16,128]{2,1,0:T(8,128)S(1)}, s32[32,16,128]{2,1,0:T(8,128)}, u32[]{:S(2)}) copy-start(s32[32,16,128]{2,1,0:T(8,128)} %param.11) | copy-start | bytes 786436
  10.1 4.8 %collective-permute-start.1 = (f32[4,32,128]{2,1,0:T(8,128)S(1)}, f32[4,32,128]{2,1,0:T(8,128)S(1)}, u32[]{:S(2)}, u32[]{:S(2)}) collective-permute-start(f32[4,32,128]{2,1,0:T(8,128)S(1)} %get-tuple-element.13), channel_id=1, source_target_pairs={{4,0},{8,4},{12,8},{16,12},{20,16},{24,20},{28,24},{0,28},{5,1},{9... | collective-permute-start | bytes 196616 | tf_op jit(solution)/shard_map/ppermute | solution.py:259
  15.3 5.0 %collective-permute-start.2 = (f32[28,32,128]{2,1,0:T(8,128)S(1)}, f32[28,32,128]{2,1,0:T(8,128)S(1)}, u32[]{:S(2)}, u32[]{:S(2)}) collective-permute-start(f32[28,32,128]{2,1,0:T(8,128)S(1)} %get-tuple-element.14), channel_id=1, source_target_pairs={{0,1},{2,3},{1,0},{3,2},{4,5},{6,7},{5,4},{7,6},{8,9},{10,11},{9,8... | collective-permute-start | bytes 1376264 | tf_op jit(solution)/shard_map/ppermute | solution.py:271
  17.3 9.8 %collective-permute-start.3 = (f32[28,32,128]{2,1,0:T(8,128)S(1)}, f32[28,32,128]{2,1,0:T(8,128)S(1)}, u32[]{:S(2)}, u32[]{:S(2)}) collective-permute-start(f32[28,32,128]{2,1,0:T(8,128)S(1)} %get-tuple-element.15), channel_id=1, source_target_pairs={{1,2},{2,1},{0,0},{3,3},{5,6},{6,5},{4,4},{7,7},{9,10},{10,9},{8,8... | collective-permute-start | bytes 1376264 | tf_op jit(solution)/shard_map/ppermute | solution.py:270

commit v2 on v0

v2 whole, which is shorter than its diff:
```python
import jax
import jax.numpy as jnp
from jax import lax
from jax.experimental import pallas as pl
from jax.experimental.pallas import tpu as pltpu
from jax.sharding import PartitionSpec as P

horizontal_mix = 0.05
vertical_mix = 0.2

F32 = jnp.float32
K = 32
R = 16
W = 128
G = W // R
HALO = 4
FIELDS = 7
U, V, M = 4, 5, 6
PAIRS = 4
SIDE_BLOCKS = 28
ROWS_AT = (0, 4, 8, 12, 24, 16, 20)
CORNERS_AT = 26
SOUTH, NORTH = 0, 1
MIB = 1 << 20


def lanes():
    return lax.broadcasted_iota(jnp.int32, (K, W), 1)


def turn(x, amount):
    return pltpu.roll(x, amount % W, 1)


def pack_edges(*refs):
    sources = refs[:FIELDS]
    rows, own, to_east, to_west, raw, raw_wet, arrived = refs[FIELDS:]
    copies = []
    for f in range(FIELDS):
        target = raw_wet if f == M else raw.at[f]
        copies.append(pltpu.make_async_copy(sources[f], target, arrived.at[f]))
        copies[-1].start()
    lane = lanes()
    group = lane // G
    packed = []
    for f in range(FIELDS):
        copies[f].wait()
        source = raw_wet if f == M else raw.at[f]
        edges = jnp.zeros((K, W), F32)
        for r in range(R):
            x = source[pl.ds(r, K, stride=R), :].astype(F32)
            rows[f, r] = x
            edges = jnp.where(group == r, turn(x, G * r + HALO), edges)
        own[f] = edges
        packed.append(edges)
    west_half = lane % G < HALO
    packed.append(jnp.zeros((K, W), F32))
    for p in range(PAIRS):
        a, b = packed[2 * p], packed[2 * p + 1]
        to_east[p] = jnp.where(west_half, a, turn(b, HALO))
        to_west[p] = jnp.where(west_half, turn(b, -HALO), a)


def pack_sides(rows, own, from_west, from_east, _, left, right, merged, first, second):
    odd = lax.axis_index("ns") % 2
    lane = lanes()
    column = lane % G
    west_half = column < HALO
    for f in range(FIELDS):
        a, b = from_west[f // 2], from_east[f // 2]
        if f % 2:
            a, b = turn(a, -HALO), turn(b, HALO)
        left_f = jnp.where(west_half, a, own[f])
        right_f = jnp.where(west_half, own[f], b)
        left[f] = left_f
        right[f] = right_f
        merged[f] = jnp.where(west_half, left_f, right_f)
    for out, north in ((first, 1 - odd), (second, odd)):
        for f in range(FIELDS):
            count = 2 if f == U else HALO
            start = (R - count) * north
            for r in range(count):
                out[ROWS_AT[f] + r] = rows[f, start + r]
        for side, edges in enumerate((left, right)):
            block = jnp.zeros((K, W), F32)
            for f in range(FIELDS):
                amount = lax.rem(2 * G * f + W - (W - 2 * G) * north, W)
                moved = pltpu.roll(edges[f], amount, 1)
                block = jnp.where(lane // (2 * G) == f, moved, block)
            out[CORNERS_AT + side] = block


def coefficients(speed, mask):
    opened = {d: mask[d] * mask[d + 1] for d in (-2, -1, 0, 1)}
    s = {d: speed[d] * opened[d] * (1.0 / 12.0) for d in opened}
    a = {d: jnp.abs(s[d]) for d in s}
    w0 = {d: -(s[d] + a[d]) for d in (-1, 0, 1)}
    w3 = {d: a[d] - s[d] for d in (-2, -1, 0)}
    w1, w2 = {}, {}
    for d in (-1, 0):
        even, odd = 7.0 * s[d], 3.0 * a[d] + horizontal_mix * opened[d]
        w1[d], w2[d] = even + odd, even - odd
    forward = [w0[-1], w1[-1] - w0[0], w3[-1] - w2[0], -w3[0]]
    transposed = [-w3[-2], w3[-2] - w2[-1], w1[0] - w0[1], w0[1]]
    return forward + transposed + [w2[-1] - w1[0]]


def shifted(c, h, d, lane, step=1):
    if d == 0:
        return c
    if d > 0:
        return turn(jnp.where(lane < step * d, h, c), -step * d)
    return turn(jnp.where(lane >= W + step * d, h, c), -step * d)


def x_coefficients(u, uh, m, mh, lane):
    return coefficients(
        {d: shifted(u, uh, d, lane) for d in (-2, -1, 0, 1)},
        {d: shifted(m, mh, d, lane) for d in (-2, -1, 0, 1, 2)},
    )


def vertical_coefficient(m):
    inner = lax.broadcasted_iota(jnp.int32, (K, W), 0) < K - 1
    return jnp.where(inner, vertical_mix * m * pltpu.roll(m, K - 1, 0), 0.0)


def step_row(cell, halo, x_of, y_of, vertical, store, lane):
    for direction in (0, 1):
        here = (2 * direction, 2 * direction + 1)
        halos, verticals = [], []
        for f in here:
            c = cell(f, 0)[...]
            flux = vertical * (c - pltpu.roll(c, K - 1, 0))
            verticals.append(pltpu.roll(flux, 1, 0) - flux)
            halos.append(halo(f))
        for q in range(0, K, 8):
            part = pl.ds(q, 8)
            lane_q = lane[:8]
            xs = [x_of.at[4 * direction + k][part] for k in range(4)]
            ys = [y_of.at[4 * direction + k][part] for k in range(4)]
            centre = 1.0 + x_of.at[8][part] + y_of.at[8][part]
            for f, h, z in zip(here, halos, verticals):
                c = cell(f, 0)[part]
                total = centre * c + z[q : q + 8]
                for coefficient, d in zip(xs, (-2, -1, 1, 2)):
                    total += coefficient * shifted(c, h[q : q + 8], d, lane_q)
                for coefficient, d in zip(ys, (-2, -1, 1, 2)):
                    total += coefficient * cell(f, d)[part]
                store(f, part, total)


def halo_columns(merged, j):
    return pltpu.roll(merged, lax.rem(2 * W - HALO - G * j, W), 1)


def edge_step(left, right, left_rows, right_rows, store):
    lane = lanes()
    column = lane % G
    west_half = column < HALO
    sides = []
    for side, rows in ((left, left_rows), (right, right_rows)):
        u, v, m = side[U], side[V], side[M]
        xs = coefficients(
            {d: turn(u, -d) for d in (-2, -1, 0, 1)},
            {d: turn(m, -d) for d in (-2, -1, 0, 1, 2)},
        )
        vh, mh = rows(V), rows(M)
        ys = coefficients(
            {d: shifted(v, vh, d, lane, G) for d in (-2, -1, 0, 1)},
            {d: shifted(m, mh, d, lane, G) for d in (-2, -1, 0, 1, 2)},
        )
        centre = 1.0 + xs[8] + ys[8]
        vertical = vertical_coefficient(m)
        results = []
        for f in range(4):
            c, ch = side[f], rows(f)
            at = 4 * (f // 2)
            flux = vertical * (c - pltpu.roll(c, K - 1, 0))
            total = centre * c + (pltpu.roll(flux, 1, 0) - flux)
            for coefficient, d in zip(xs[at : at + 4], (-2, -1, 1, 2)):
                total += coefficient * turn(c, -d)
            for coefficient, d in zip(ys[at : at + 4], (-2, -1, 1, 2)):
                total += coefficient * shifted(c, ch, d, lane, G)
            results.append(total)
        sides.append(results)
    for f in range(4):
        store(f, jnp.where(west_half, sides[0][f], sides[1][f]))


def y_coefficients_at(row, j):
    return coefficients(
        {d: row(V, j + d)[...] for d in (-2, -1, 0, 1)},
        {d: row(M, j + d)[...] for d in (-2, -1, 0, 1, 2)},
    )


def prepare(rows, y_out, vertical_out):
    def body(j, carry):
        got = y_coefficients_at(lambda f, r: rows.at[f, r], j)
        for k in range(9):
            y_out[j - 2, k] = got[k]
        return carry

    lax.fori_loop(2, R - 2, body, 0)

    def levels(j, carry):
        vertical_out[j] = vertical_coefficient(rows[M, j])
        return carry

    lax.fori_loop(0, R, levels, 0)


def interior(rows, left, right, merged, y_in, vertical_in, x_out, c1_out, c2_out, merged1):
    lane = lanes()

    def x_body(j, carry):
        got = x_coefficients(
            rows[U, j], halo_columns(merged[U], j), rows[M, j], halo_columns(merged[M], j), lane
        )
        for k in range(9):
            x_out[j, k] = got[k]
        return carry

    lax.fori_loop(0, R, x_body, 0)

    def keep(f, value):
        merged1[f] = value

    edge_step(left, right, lambda f: left[f], lambda f: right[f], keep)

    def first(j, carry):
        def store(f, part, value):
            c1_out.at[f, j - 2][part] = value

        step_row(
            lambda f, d: rows.at[f, j + d],
            lambda f: halo_columns(merged[f], j),
            x_out.at[j],
            y_in.at[j - 2],
            vertical_in[j],
            store,
            lane,
        )
        return carry

    lax.fori_loop(2, R - 2, first, 0)

    def second(j, carry):
        def store(f, part, value):
            c2_out.at[f, j - 4][part] = value

        step_row(
            lambda f, d: c1_out.at[f, j - 2 + d],
            lambda f: halo_columns(merged1[f], j),
            x_out.at[j],
            y_in.at[j - 2],
            vertical_in[j],
            store,
            lane,
        )
        return carry

    lax.fori_loop(4, R - 4, second, 0)


def boundary(*refs):
    rows, left, right, merged, y_in, vertical_in, x_in, c1_in, c2_in, first, second = refs[:11]
    outs = refs[11:15]
    sides, x_new, y_new, vertical_new, c1_new, merged1, rows_halo = refs[15:]
    lane = lanes()
    place = lax.axis_index("ns")
    last = lax.axis_size("ns") - 1
    odd = place % 2
    there = (place > 0, place < last)

    def unpack(b, carry):
        for source, side in ((first, 1 - odd), (second, odd)):
            here = jnp.where(side == NORTH, place < last, place > 0)
            sides[side, b] = jnp.where(here, source[b], 0.0)
        return carry

    lax.fori_loop(0, SIDE_BLOCKS, unpack, 0)

    def row(f, j):
        if j < 0:
            return sides.at[SOUTH, ROWS_AT[f] + j + (2 if f == U else HALO)]
        if j >= R:
            return sides.at[NORTH, ROWS_AT[f] + j - R]
        return rows.at[f, j]

    for s in range(2):
        for f in range(FIELDS):
            south = turn(sides[SOUTH, CORNERS_AT + s], W - 2 * G - 2 * G * f)
            north = turn(sides[NORTH, CORNERS_AT + s], -2 * G * f)
            rows_halo[s, f] = jnp.where(lane >= W // 2, south, north)

    def keep(f, value):
        merged1[f] = value

    edge_step(
        left, right, lambda f: rows_halo[0, f], lambda f: rows_halo[1, f], keep
    )

    west_half = lane % G < HALO

    def halo(f, j):
        if 0 <= j < R:
            return halo_columns(merged[f], j)
        corner = jnp.where(west_half, rows_halo[0, f], rows_halo[1, f])
        return halo_columns(corner, j % R)

    edge_rows = (-2, -1, 0, 1, R - 2, R - 1, R, R + 1)
    new_at = {j: i for i, j in enumerate(edge_rows)}
    for j in edge_rows:
        got = y_coefficients_at(row, j)
        for k in range(9):
            y_new[new_at[j], k] = got[k]
        if not 0 <= j < R:
            got = x_coefficients(row(U, j)[...], halo(U, j), row(M, j)[...], halo(M, j), lane)
            for k in range(9):
                x_new[new_at[j], k] = got[k]
            vertical_new[new_at[j]] = vertical_coefficient(row(M, j)[...])

    def x_of(j):
        return x_in.at[j] if 0 <= j < R else x_new.at[new_at[j]]

    def y_of(j):
        return y_new.at[new_at[j]] if j in new_at else y_in.at[j - 2]

    def vertical_of(j):
        return vertical_in[j] if 0 <= j < R else vertical_new[new_at[j]]

    for j in edge_rows:
        def store(f, part, value, j=j):
            if f >= 2 and not 0 <= j < R:
                value = jnp.where(there[0 if j < 0 else 1], value, 0.0)
            c1_new.at[f, new_at[j]][part] = value

        step_row(
            lambda f, d: row(f, j + d),
            lambda f: halo(f, j),
            x_of(j),
            y_of(j),
            vertical_of(j),
            store,
            lane,
        )

    def row1(f, j):
        return c1_new.at[f, new_at[j]] if j in new_at else c1_in.at[f, j - 2]

    for j in (0, 1, 2, 3, R - 4, R - 3, R - 2, R - 1):
        def store(f, part, value, j=j):
            outs[f][pl.ds(part.start * R + j, 8, stride=R), :] = value

        step_row(
            lambda f, d: row1(f, j + d),
            lambda f: halo_columns(merged1[f], j),
            x_of(j),
            y_of(j),
            vertical_of(j),
            store,
            lane,
        )

    def copy(j, carry):
        for f in range(4):
            outs[f][pl.ds(j, K, stride=R), :] = c2_in[f, j - 4]
        return carry

    lax.fori_loop(4, R - 4, copy, 0)


def vmem():
    return pl.BlockSpec(memory_space=pltpu.VMEM)


def call(kernel, in_specs, out_shapes, scratch=(), limit=16 * MIB, cost=0):
    return pl.pallas_call(
        kernel,
        out_shape=[jax.ShapeDtypeStruct(shape, F32) for shape in out_shapes],
        in_specs=in_specs,
        out_specs=[vmem()] * len(out_shapes),
        scratch_shapes=list(scratch),
        compiler_params=pltpu.CompilerParams(vmem_limit_bytes=limit),
        cost_estimate=pl.CostEstimate(flops=cost, bytes_accessed=MIB, transcendentals=0),
    )


def local(temp, salt, u_east, v_north, wet, cot_temp, cot_salt):
    flat = [a.reshape(K * R, W) for a in (temp, salt, cot_temp, cot_salt, u_east, v_north, wet)]

    rows, own, to_east, to_west = call(
        pack_edges,
        [pl.BlockSpec(memory_space=pltpu.HBM)] * FIELDS,
        [(FIELDS, R, K, W), (FIELDS, K, W), (PAIRS, K, W), (PAIRS, K, W)],
        [
            pltpu.VMEM((FIELDS - 1, K * R, W), F32),
            pltpu.VMEM((K * R, W), jnp.int32),
            pltpu.SemaphoreType.DMA((FIELDS,)),
        ],
    )(*[pltpu.with_memory_space_constraint(a, pltpu.HBM) for a in flat])

    n = lax.axis_size("ew")
    from_west = lax.ppermute(to_east, "ew", [(i, (i + 1) % n) for i in range(n)])
    from_east = lax.ppermute(to_west, "ew", [((i + 1) % n, i) for i in range(n)])

    y_in, vertical = call(
        prepare, [vmem()], [(R - 4, 9, K, W), (R, K, W)], cost=10_000_000
    )(rows)

    left, right, merged, first, second = call(
        pack_sides,
        [vmem()] * 4 + [pl.BlockSpec(memory_space=pl.ANY)],
        [(FIELDS, K, W)] * 3 + [(SIDE_BLOCKS, K, W)] * 2,
    )(rows, own, from_west, from_east, vertical)

    n = lax.axis_size("ns")

    def partners(odd):
        pairs = [(i, i + 1) for i in range(odd, n - 1, 2)]
        met = {i for pair in pairs for i in pair}
        return pairs + [(b, a) for a, b in pairs] + [(i, i) for i in range(n) if i not in met]

    second = lax.ppermute(second, "ns", partners(1))
    first = lax.ppermute(first, "ns", partners(0))

    x_in, c1, c2 = call(
        interior,
        [vmem()] * 6,
        [(R, 9, K, W), (4, R - 4, K, W), (4, R - 8, K, W)],
        [pltpu.VMEM((4, K, W), F32)],
        cost=10_000_000,
    )(rows, left, right, merged, y_in, vertical)

    outs = call(
        boundary,
        [vmem()] * 11,
        [(K * R, W)] * 4,
        [
            pltpu.VMEM((2, SIDE_BLOCKS, K, W), F32),
            pltpu.VMEM((8, 9, K, W), F32),
            pltpu.VMEM((8, 9, K, W), F32),
            pltpu.VMEM((8, K, W), F32),
            pltpu.VMEM((4, 8, K, W), F32),
            pltpu.VMEM((4, K, W), F32),
            pltpu.VMEM((2, FIELDS, K, W), F32),
        ],
        cost=10_000_000,
    )(rows, left, right, merged, y_in, vertical, x_in, c1, c2, first, second)
    return tuple(a.reshape(K, R, W) for a in outs)


def solution(mesh):
    spec = P(None, "ns", "ew")
    return jax.shard_map(
        local, mesh=mesh, in_specs=(spec,) * 7, out_specs=(spec,) * 4, check_vma=False
    )
```

time: 161 us -> 28.3 us (0.18)
  waiting for transfers between devices: 69 us -> 1.21 us
  starting transfers between devices: 50.8 us -> 10.1 us
  other arithmetic: 25.1 us -> 0 us
  Pallas kernels: 0 us -> 16.1 us
  local copies, waits for them, and re-layouts: 13.9 us -> 0 us
    ppermute x20 -> x4, waiting for transfers between devices: 69 us -> 1.21 us  [the longest x1 1.2 us: local(): lax.ppermute(to_east, 'ew', [(i, (i + 1) % n) for i in range(n)])]
    ppermute x20 -> x4, starting transfers between devices: 50.8 us -> 10.1 us  [the longest x1 3.1 us: local(): lax.ppermute(to_west, 'ew', [((i + 1) % n, i) for i in range(n)])]
    pallas_call x0 -> x5, Pallas kernels: none -> 16.1 us  [the longest x1 7.45 us: local(): call(interior, [vmem()] * 6, [(R, 9, K, W), (4, R - 4, K, W), (4, R - 8,...]
    mul x24 -> x0, other arithmetic: 12.7 us -> none  [the longest x5 4.12 us: face_change(): open_face * (weights[0] * far_left + weights[1] * left + weights[2] * rig...]
    unnamed x40 -> x0, local copies, waits for them, and re-layouts: 5.81 us -> none
    concatenate x4 -> x0, other arithmetic: 5.74 us -> none  [padded_2(): jnp.concatenate([lax.ppermute(tail, axis, [(i, (i + 1) % count) for i in...]
    ppermute x2 -> x0, local copies, waits for them, and re-layouts: 4.14 us -> none  [the longest x1 2.09 us: padded_2(): lax.ppermute(tail, axis, [(i, (i + 1) % count) for i in range(ends)])]
    another operation x3 -> x0, other arithmetic: 2.4 us -> none  [the longest x1 1.12 us: local(): sensitivity = evolve(jnp.stack([cot_temp, cot_salt]), flow_wide, retreat)]
  transfers between devices with their start and end apart: 20 -> 4, of which waited for: 7 -> 1; matrix products, arithmetic and copies ran while one was open for 16% -> 0% of each run, Pallas kernels for 0% -> 28%
where the time goes in v2:
time: 28.3 us; the launch traced here: 28.1 us
  Pallas kernels  16.1 us (57%)
  starting transfers between devices  10.1 us (36%)
  waiting for transfers between devices  1.21 us (4%)
  between operations  0.69 us (2%)
    pallas_call x1, Pallas kernels, local(): call(interior, [vmem()] * 6, [(R, 9, K, W), (4, R - 4, K, W), (4, R - 8,...  7.45 us
    pallas_call x1, Pallas kernels, local(): call(boundary, [vmem()] * 11, [(K * R, W)] * 4, [pltpu.VMEM((2, SIDE_BLOC...  5.82 us
    ppermute x1, starting transfers between devices, local(): lax.ppermute(to_west, 'ew', [((i + 1) % n, i) for i in range(n)])  3.1 us
    ppermute x1, starting transfers between devices, local(): second = lax.ppermute(second, 'ns', partners(1))  3.05 us
    pallas_call x1, Pallas kernels, local(): call(pack_edges, [pl.BlockSpec(memory_space=pltpu.HBM)] * FIELDS, [(FIELD...  2.13 us
    ppermute x1, starting transfers between devices, local(): lax.ppermute(to_east, 'ew', [(i, (i + 1) % n) for i in range(n)])  2.09 us
    ppermute x1, starting transfers between devices, local(): first = lax.ppermute(first, 'ns', partners(0))  1.89 us
    ppermute x1, waiting for transfers between devices, local(): lax.ppermute(to_east, 'ew', [(i, (i + 1) % n) for i in range(n)])  1.2 us
  transfers between devices with their start and end apart: 4, of which 1 were waited for; matrix products, arithmetic and copies ran while one was open for 0% of the time, Pallas kernels for 28%

profile of v2, /device:TPU:1, one launch (start us, length us, event | category | flops | bytes accessed | tf_op | source)
XLA Modules:
  0.0 28.1 jit_solution(14367525482334660320)
XLA Ops:
  0.6 2.1 %shard_map.102 = (f32[7,16,32,128]{3,2,1,0:T(8,128)S(1)}, f32[7,32,128]{2,1,0:T(8,128)S(1)}, f32[4,32,128]{2,1,0:T(8,128)S(1)}, f32[4,32,128]{2,1,0:T(8,128)S(1)}) custom-call(f32[512,128]{1,0:T(8,128)} %bitcast.11, f32[512,128]{1,0:T(8,128)} %bitcast.12, f32[512,128]{1,0:T(8,128)} %bitcast.13, f32[512,128]{1,0:T(8,128)} %bitcast.14, f32[512,128]{1,0:T(8,128)} %bitcast.15, ...), custom_call_target="tpu_custom_call" | custom-call | bytes 1048576 | tf_op jit(solution)/shard_map/pallas_call | solution.py:394
  2.8 2.1 %collective-permute-start = (f32[4,32,128]{2,1,0:T(8,128)S(1)}, f32[4,32,128]{2,1,0:T(8,128)S(1)}, u32[]{:S(2)}, u32[]{:S(2)}) collective-permute-start(f32[4,32,128]{2,1,0:T(8,128)S(1)} %get-tuple-element.24), channel_id=1, source_target_pairs={{0,4},{4,8},{8,12},{12,16},{16,20},{20,24},{24,28},{28,0},{1,5},{5... | collective-permute-start | bytes 196616 | tf_op jit(solution)/shard_map/ppermute | solution.py:406
  4.9 3.1 %collective-permute-start.1 = (f32[4,32,128]{2,1,0:T(8,128)S(1)}, f32[4,32,128]{2,1,0:T(8,128)S(1)}, u32[]{:S(2)}, u32[]{:S(2)}) collective-permute-start(f32[4,32,128]{2,1,0:T(8,128)S(1)} %get-tuple-element.25), channel_id=1, source_target_pairs={{4,0},{8,4},{12,8},{16,12},{20,16},{24,20},{28,24},{0,28},{5,1},{9... | collective-permute-start | bytes 196616 | tf_op jit(solution)/shard_map/ppermute | solution.py:407
  8.0 0.5 %shard_map.103 = (f32[12,9,32,128]{3,2,1,0:T(8,128)S(1)}, f32[16,32,128]{2,1,0:T(8,128)S(1)}) custom-call(f32[7,16,32,128]{3,2,1,0:T(8,128)S(1)} %get-tuple-element.22.rows.refs_0_), custom_call_target="tpu_custom_call" | custom-call | flops 10000000 | bytes 1048576 | tf_op jit(solution)/shard_map/pallas_call | solution.py:409
  8.5 1.2 %collective-permute-done.from_west = f32[4,32,128]{2,1,0:T(8,128)S(1)} collective-permute-done((f32[4,32,128]{2,1,0:T(8,128)S(1)}, f32[4,32,128]{2,1,0:T(8,128)S(1)}, u32[]{:S(2)}, u32[]{:S(2)}) %collective-permute-start) | collective-permute-done | bytes 65568 | tf_op jit(solution)/shard_map/ppermute | solution.py:406
  9.7 0.0 collective-permute-done.1.from_east
  9.7 0.2 shard_map.104
  9.9 1.9 %collective-permute-start.2 = (f32[28,32,128]{2,1,0:T(8,128)S(1)}, f32[28,32,128]{2,1,0:T(8,128)S(1)}, u32[]{:S(2)}, u32[]{:S(2)}) collective-permute-start(f32[28,32,128]{2,1,0:T(8,128)S(1)} %get-tuple-element.34), channel_id=1, source_target_pairs={{0,1},{2,3},{1,0},{3,2},{4,5},{6,7},{5,4},{7,6},{8,9},{10,11},{9,8... | collective-permute-start | bytes 1376264 | tf_op jit(solution)/shard_map/ppermute | solution.py:427
  11.8 3.0 %collective-permute-start.3 = (f32[28,32,128]{2,1,0:T(8,128)S(1)}, f32[28,32,128]{2,1,0:T(8,128)S(1)}, u32[]{:S(2)}, u32[]{:S(2)}) collective-permute-start(f32[28,32,128]{2,1,0:T(8,128)S(1)} %get-tuple-element.35), channel_id=1, source_target_pairs={{1,2},{2,1},{0,0},{3,3},{5,6},{6,5},{4,4},{7,7},{9,10},{10,9},{8,8... | collective-permute-start | bytes 1376264 | tf_op jit(solution)/shard_map/ppermute | solution.py:426
  14.8 7.5 %shard_map.105 = (f32[16,9,32,128]{3,2,1,0:T(8,128)S(1)}, f32[4,12,32,128]{3,2,1,0:T(8,128)S(1)}, f32[4,8,32,128]{3,2,1,0:T(8,128)S(1)}) custom-call(f32[7,16,32,128]{3,2,1,0:T(8,128)S(1)} %get-tuple-element.22.rows.refs_0_, f32[7,32,128]{2,1,0:T(8,128)S(1)} %get-tuple-element.27.left.refs_1_, f32[7,32,128]{2,1,0:T(8,128)S(1)} %get-tuple-element.28.right.refs_2_, ...), custom_call_target="tpu_custom_call" | custom-call | flops 10000000 | bytes 1048576 | tf_op jit(solution)/shard_map/pallas_call | solution.py:429
  22.3 0.0 collective-permute-done.2.refs_9_
  22.3 0.0 collective-permute-done.3.refs_10_
  22.3 5.8 %shard_map.106 = (f32[512,128]{1,0:T(8,128)}, f32[512,128]{1,0:T(8,128)}, f32[512,128]{1,0:T(8,128)}, f32[512,128]{1,0:T(8,128)}) custom-call(f32[7,16,32,128]{3,2,1,0:T(8,128)S(1)} %get-tuple-element.22.rows.refs_0_, f32[7,32,128]{2,1,0:T(8,128)S(1)} %get-tuple-element.27.left.refs_1_, f32[7,32,128]{2,1,0:T(8,128)S(1)} %get-tuple-element.28.right.refs_2_, ...), custom_call_target="tpu_custom_call" | custom-call | flops 10000000 | bytes 1048576 | tf_op jit(solution)/shard_map/pallas_call | solution.py:437
Async XLA Ops:
  2.8 6.9 %collective-permute-start = (f32[4,32,128]{2,1,0:T(8,128)S(1)}, f32[4,32,128]{2,1,0:T(8,128)S(1)}, u32[]{:S(2)}, u32[]{:S(2)}) collective-permute-start(f32[4,32,128]{2,1,0:T(8,128)S(1)} %get-tuple-element.24), channel_id=1, source_target_pairs={{0,4},{4,8},{8,12},{12,16},{16,20},{20,24},{24,28},{28,0},{1,5},{5... | collective-permute-start | bytes 196616 | tf_op jit(solution)/shard_map/ppermute | solution.py:406
  4.9 4.8 %collective-permute-start.1 = (f32[4,32,128]{2,1,0:T(8,128)S(1)}, f32[4,32,128]{2,1,0:T(8,128)S(1)}, u32[]{:S(2)}, u32[]{:S(2)}) collective-permute-start(f32[4,32,128]{2,1,0:T(8,128)S(1)} %get-tuple-element.25), channel_id=1, source_target_pairs={{4,0},{8,4},{12,8},{16,12},{20,16},{24,20},{28,24},{0,28},{5,1},{9... | collective-permute-start | bytes 196616 | tf_op jit(solution)/shard_map/ppermute | solution.py:407
  9.9 12.4 %collective-permute-start.2 = (f32[28,32,128]{2,1,0:T(8,128)S(1)}, f32[28,32,128]{2,1,0:T(8,128)S(1)}, u32[]{:S(2)}, u32[]{:S(2)}) collective-permute-start(f32[28,32,128]{2,1,0:T(8,128)S(1)} %get-tuple-element.34), channel_id=1, source_target_pairs={{0,1},{2,3},{1,0},{3,2},{4,5},{6,7},{5,4},{7,6},{8,9},{10,11},{9,8... | collective-permute-start | bytes 1376264 | tf_op jit(solution)/shard_map/ppermute | solution.py:427
  11.8 10.5 %collective-permute-start.3 = (f32[28,32,128]{2,1,0:T(8,128)S(1)}, f32[28,32,128]{2,1,0:T(8,128)S(1)}, u32[]{:S(2)}, u32[]{:S(2)}) collective-permute-start(f32[28,32,128]{2,1,0:T(8,128)S(1)} %get-tuple-element.35), channel_id=1, source_target_pairs={{1,2},{2,1},{0,0},{3,3},{5,6},{6,5},{4,4},{7,7},{9,10},{10,9},{8,8... | collective-permute-start | bytes 1376264 | tf_op jit(solution)/shard_map/ppermute | solution.py:426

commit v3 on v2

--- a/solution.py
+++ b/solution.py
@@ -126,6 +126,7 @@
 
 
 def step_row(cell, halo, x_of, y_of, vertical, store, lane):
+    results = []
     for direction in (0, 1):
         here = (2 * direction, 2 * direction + 1)
         halos, verticals = [], []
@@ -147,7 +148,9 @@
                     total += coefficient * shifted(c, h[q : q + 8], d, lane_q)
                 for coefficient, d in zip(ys, (-2, -1, 1, 2)):
                     total += coefficient * cell(f, d)[part]
-                store(f, part, total)
+                results.append((f, part, total))
+    for result in results:
+        store(*result)
 
 
 def halo_columns(merged, j):
@@ -265,7 +268,7 @@
 
 
 def boundary(*refs):
-    rows, left, right, merged, y_in, vertical_in, x_in, c1_in, c2_in, first, second = refs[:11]
+    rows, left, right, merged, y_in, vertical_in, x_in, c1_in, c2_in, second, first = refs[:11]
     outs = refs[11:15]
     sides, x_new, y_new, vertical_new, c1_new, merged1, rows_halo = refs[15:]
     lane = lanes()
@@ -448,7 +451,7 @@
             pltpu.VMEM((2, FIELDS, K, W), F32),
         ],
         cost=10_000_000,
-    )(rows, left, right, merged, y_in, vertical, x_in, c1, c2, first, second)
+    )(rows, left, right, merged, y_in, vertical, x_in, c1, c2, second, first)
     return tuple(a.reshape(K, R, W) for a in outs)
 
 

time: 28.3 us -> 28.8 us (1.018)
  the two profiles are of different devices: /device:TPU:1 before, /device:TPU:0 now
where the time goes in v3:
time: 28.8 us; the launch traced here: 28.6 us
  Pallas kernels  16.1 us (56%)
  starting transfers between devices  9.7 us (34%)
  waiting for transfers between devices  2.08 us (7%)
  between operations  0.69 us (2%)
    pallas_call x1, Pallas kernels, local(): call(interior, [vmem()] * 6, [(R, 9, K, W), (4, R - 4, K, W), (4, R - 8,...  7.46 us
    pallas_call x1, Pallas kernels, local(): call(boundary, [vmem()] * 11, [(K * R, W)] * 4, [pltpu.VMEM((2, SIDE_BLOC...  5.82 us
    ppermute x1, starting transfers between devices, local(): lax.ppermute(to_west, 'ew', [((i + 1) % n, i) for i in range(n)])  3.1 us
    ppermute x1, starting transfers between devices, local(): lax.ppermute(to_east, 'ew', [(i, (i + 1) % n) for i in range(n)])  2.99 us
    ppermute x1, starting transfers between devices, local(): first = lax.ppermute(first, 'ns', partners(0))  2.92 us
    pallas_call x1, Pallas kernels, local(): call(pack_edges, [pl.BlockSpec(memory_space=pltpu.HBM)] * FIELDS, [(FIELD...  2.13 us
    ppermute x1, waiting for transfers between devices, local(): lax.ppermute(to_east, 'ew', [(i, (i + 1) % n) for i in range(n)])  1.74 us
    ppermute x1, starting transfers between devices, local(): second = lax.ppermute(second, 'ns', partners(1))  0.69 us
  transfers between devices with their start and end apart: 4, of which 2 were waited for; matrix products, arithmetic and copies ran while one was open for 0% of the time, Pallas kernels for 28%

profile of v3, /device:TPU:0, one launch (start us, length us, event | category | flops | bytes accessed | tf_op | source)
XLA Modules:
  0.0 28.6 jit_solution(11690676947610083493)
XLA Ops:
  0.6 2.1 %shard_map.102 = (f32[7,16,32,128]{3,2,1,0:T(8,128)S(1)}, f32[7,32,128]{2,1,0:T(8,128)S(1)}, f32[4,32,128]{2,1,0:T(8,128)S(1)}, f32[4,32,128]{2,1,0:T(8,128)S(1)}) custom-call(f32[512,128]{1,0:T(8,128)} %bitcast.11, f32[512,128]{1,0:T(8,128)} %bitcast.12, f32[512,128]{1,0:T(8,128)} %bitcast.13, f32[512,128]{1,0:T(8,128)} %bitcast.14, f32[512,128]{1,0:T(8,128)} %bitcast.15, ...), custom_call_target="tpu_custom_call" | custom-call | bytes 1048576 | tf_op jit(solution)/shard_map/pallas_call | solution.py:397
  2.8 3.0 %collective-permute-start = (f32[4,32,128]{2,1,0:T(8,128)S(1)}, f32[4,32,128]{2,1,0:T(8,128)S(1)}, u32[]{:S(2)}, u32[]{:S(2)}) collective-permute-start(f32[4,32,128]{2,1,0:T(8,128)S(1)} %get-tuple-element.24), channel_id=1, source_target_pairs={{0,4},{4,8},{8,12},{12,16},{16,20},{20,24},{24,28},{28,0},{1,5},{5... | collective-permute-start | bytes 196616 | tf_op jit(solution)/shard_map/ppermute | solution.py:409
  5.8 3.1 %collective-permute-start.1 = (f32[4,32,128]{2,1,0:T(8,128)S(1)}, f32[4,32,128]{2,1,0:T(8,128)S(1)}, u32[]{:S(2)}, u32[]{:S(2)}) collective-permute-start(f32[4,32,128]{2,1,0:T(8,128)S(1)} %get-tuple-element.25), channel_id=1, source_target_pairs={{4,0},{8,4},{12,8},{16,12},{20,16},{24,20},{28,24},{0,28},{5,1},{9... | collective-permute-start | bytes 196616 | tf_op jit(solution)/shard_map/ppermute | solution.py:410
  8.9 0.5 %shard_map.103 = (f32[12,9,32,128]{3,2,1,0:T(8,128)S(1)}, f32[16,32,128]{2,1,0:T(8,128)S(1)}) custom-call(f32[7,16,32,128]{3,2,1,0:T(8,128)S(1)} %get-tuple-element.22.rows.refs_0_), custom_call_target="tpu_custom_call" | custom-call | flops 10000000 | bytes 1048576 | tf_op jit(solution)/shard_map/pallas_call | solution.py:412
  9.4 1.7 %collective-permute-done.from_west = f32[4,32,128]{2,1,0:T(8,128)S(1)} collective-permute-done((f32[4,32,128]{2,1,0:T(8,128)S(1)}, f32[4,32,128]{2,1,0:T(8,128)S(1)}, u32[]{:S(2)}, u32[]{:S(2)}) %collective-permute-start) | collective-permute-done | bytes 65568 | tf_op jit(solution)/shard_map/ppermute | solution.py:409
  11.1 0.3 %collective-permute-done.1.from_east = f32[4,32,128]{2,1,0:T(8,128)S(1)} collective-permute-done((f32[4,32,128]{2,1,0:T(8,128)S(1)}, f32[4,32,128]{2,1,0:T(8,128)S(1)}, u32[]{:S(2)}, u32[]{:S(2)}) %collective-permute-start.1) | collective-permute-done | bytes 65568 | tf_op jit(solution)/shard_map/ppermute | solution.py:410
  11.4 0.2 shard_map.104
  11.7 0.7 %collective-permute-start.2 = (f32[28,32,128]{2,1,0:T(8,128)S(1)}, f32[28,32,128]{2,1,0:T(8,128)S(1)}, u32[]{:S(2)}, u32[]{:S(2)}) collective-permute-start(f32[28,32,128]{2,1,0:T(8,128)S(1)} %get-tuple-element.34), channel_id=1, source_target_pairs={{1,2},{2,1},{0,0},{3,3},{5,6},{6,5},{4,4},{7,7},{9,10},{10,9},{8,8... | collective-permute-start | bytes 1376264 | tf_op jit(solution)/shard_map/ppermute | solution.py:429
  12.4 2.9 %collective-permute-start.3 = (f32[28,32,128]{2,1,0:T(8,128)S(1)}, f32[28,32,128]{2,1,0:T(8,128)S(1)}, u32[]{:S(2)}, u32[]{:S(2)}) collective-permute-start(f32[28,32,128]{2,1,0:T(8,128)S(1)} %get-tuple-element.35), channel_id=1, source_target_pairs={{0,1},{2,3},{1,0},{3,2},{4,5},{6,7},{5,4},{7,6},{8,9},{10,11},{9,8... | collective-permute-start | bytes 1376264 | tf_op jit(solution)/shard_map/ppermute | solution.py:430
  15.3 7.5 %shard_map.105 = (f32[16,9,32,128]{3,2,1,0:T(8,128)S(1)}, f32[4,12,32,128]{3,2,1,0:T(8,128)S(1)}, f32[4,8,32,128]{3,2,1,0:T(8,128)S(1)}) custom-call(f32[7,16,32,128]{3,2,1,0:T(8,128)S(1)} %get-tuple-element.22.rows.refs_0_, f32[7,32,128]{2,1,0:T(8,128)S(1)} %get-tuple-element.27.left.refs_1_, f32[7,32,128]{2,1,0:T(8,128)S(1)} %get-tuple-element.28.right.refs_2_, ...), custom_call_target="tpu_custom_call" | custom-call | flops 10000000 | bytes 1048576 | tf_op jit(solution)/shard_map/pallas_call | solution.py:432
  22.7 0.0 collective-permute-done.2.refs_9_
  22.8 0.0 collective-permute-done.3.refs_10_
  22.8 5.8 %shard_map.106 = (f32[512,128]{1,0:T(8,128)}, f32[512,128]{1,0:T(8,128)}, f32[512,128]{1,0:T(8,128)}, f32[512,128]{1,0:T(8,128)}) custom-call(f32[7,16,32,128]{3,2,1,0:T(8,128)S(1)} %get-tuple-element.22.rows.refs_0_, f32[7,32,128]{2,1,0:T(8,128)S(1)} %get-tuple-element.27.left.refs_1_, f32[7,32,128]{2,1,0:T(8,128)S(1)} %get-tuple-element.28.right.refs_2_, ...), custom_call_target="tpu_custom_call" | custom-call | flops 10000000 | bytes 1048576 | tf_op jit(solution)/shard_map/pallas_call | solution.py:440
Async XLA Ops:
  2.8 8.3 %collective-permute-start = (f32[4,32,128]{2,1,0:T(8,128)S(1)}, f32[4,32,128]{2,1,0:T(8,128)S(1)}, u32[]{:S(2)}, u32[]{:S(2)}) collective-permute-start(f32[4,32,128]{2,1,0:T(8,128)S(1)} %get-tuple-element.24), channel_id=1, source_target_pairs={{0,4},{4,8},{8,12},{12,16},{16,20},{20,24},{24,28},{28,0},{1,5},{5... | collective-permute-start | bytes 196616 | tf_op jit(solution)/shard_map/ppermute | solution.py:409
  5.8 5.7 %collective-permute-start.1 = (f32[4,32,128]{2,1,0:T(8,128)S(1)}, f32[4,32,128]{2,1,0:T(8,128)S(1)}, u32[]{:S(2)}, u32[]{:S(2)}) collective-permute-start(f32[4,32,128]{2,1,0:T(8,128)S(1)} %get-tuple-element.25), channel_id=1, source_target_pairs={{4,0},{8,4},{12,8},{16,12},{20,16},{24,20},{28,24},{0,28},{5,1},{9... | collective-permute-start | bytes 196616 | tf_op jit(solution)/shard_map/ppermute | solution.py:410
  11.7 11.1 %collective-permute-start.2 = (f32[28,32,128]{2,1,0:T(8,128)S(1)}, f32[28,32,128]{2,1,0:T(8,128)S(1)}, u32[]{:S(2)}, u32[]{:S(2)}) collective-permute-start(f32[28,32,128]{2,1,0:T(8,128)S(1)} %get-tuple-element.34), channel_id=1, source_target_pairs={{1,2},{2,1},{0,0},{3,3},{5,6},{6,5},{4,4},{7,7},{9,10},{10,9},{8,8... | collective-permute-start | bytes 1376264 | tf_op jit(solution)/shard_map/ppermute | solution.py:429
  12.4 10.4 %collective-permute-start.3 = (f32[28,32,128]{2,1,0:T(8,128)S(1)}, f32[28,32,128]{2,1,0:T(8,128)S(1)}, u32[]{:S(2)}, u32[]{:S(2)}) collective-permute-start(f32[28,32,128]{2,1,0:T(8,128)S(1)} %get-tuple-element.35), channel_id=1, source_target_pairs={{0,1},{2,3},{1,0},{3,2},{4,5},{6,7},{5,4},{7,6},{8,9},{10,11},{9,8... | collective-permute-start | bytes 1376264 | tf_op jit(solution)/shard_map/ppermute | solution.py:430

commit v4 on v3

--- a/solution.py
+++ b/solution.py
@@ -214,6 +214,15 @@
     lax.fori_loop(0, R, levels, 0)
 
 
+def by_fours(start, stop, body):
+    def four(i, carry):
+        for k in range(4):
+            body(start + 4 * i + k, carry)
+        return carry
+
+    lax.fori_loop(0, (stop - start) // 4, four, 0)
+
+
 def interior(rows, left, right, merged, y_in, vertical_in, x_out, c1_out, c2_out, merged1):
     lane = lanes()
 
@@ -225,7 +234,7 @@
             x_out[j, k] = got[k]
         return carry
 
-    lax.fori_loop(0, R, x_body, 0)
+    by_fours(0, R, x_body)
 
     def keep(f, value):
         merged1[f] = value
@@ -247,7 +256,7 @@
         )
         return carry
 
-    lax.fori_loop(2, R - 2, first, 0)
+    by_fours(2, R - 2, first)
 
     def second(j, carry):
         def store(f, part, value):
@@ -264,7 +273,7 @@
         )
         return carry
 
-    lax.fori_loop(4, R - 4, second, 0)
+    by_fours(4, R - 4, second)
 
 
 def boundary(*refs):
@@ -391,6 +400,19 @@
     )
 
 
+def partners(odd, n_ew, n_ns):
+    pairs = []
+    for e in range(n_ew):
+        for s in range(n_ns):
+            step = 1 if (s - odd) % 2 == 0 else -1
+            if 0 <= s + step < n_ns:
+                to = (e, s + step)
+            else:
+                to = (e ^ 1 if e ^ 1 < n_ew else e, s)
+            pairs.append((e * n_ns + s, to[0] * n_ns + to[1]))
+    return pairs
+
+
 def local(temp, salt, u_east, v_north, wet, cot_temp, cot_salt):
     flat = [a.reshape(K * R, W) for a in (temp, salt, cot_temp, cot_salt, u_east, v_north, wet)]
 
@@ -421,13 +443,8 @@
 
     n = lax.axis_size("ns")
 
-    def partners(odd):
-        pairs = [(i, i + 1) for i in range(odd, n - 1, 2)]
-        met = {i for pair in pairs for i in pair}
-        return pairs + [(b, a) for a, b in pairs] + [(i, i) for i in range(n) if i not in met]
-
-    second = lax.ppermute(second, "ns", partners(1))
-    first = lax.ppermute(first, "ns", partners(0))
+    second = lax.ppermute(second, ("ew", "ns"), partners(1, lax.axis_size("ew"), n))
+    first = lax.ppermute(first, ("ew", "ns"), partners(0, lax.axis_size("ew"), n))
 
     x_in, c1, c2 = call(
         interior,

time: 28.8 us -> 26.2 us (0.910)
  starting transfers between devices: 9.7 us -> 7.79 us
  Pallas kernels: 16.1 us -> 14.2 us
  waiting for transfers between devices: 2.08 us -> 3.31 us
    ppermute x2, starting transfers between devices: 3.61 us -> 1.7 us  [the longest x1 1.11 us: local(): lax.ppermute(second, ('ew', 'ns'), partners(1, lax.axis_size('ew'), n))]
    pallas_call x1, Pallas kernels: 7.46 us -> 5.6 us  [local(): call(interior, [vmem()] * 6, [(R, 9, K, W), (4, R - 4, K, W), (4, R - 8,...]
    ppermute x2, waiting for transfers between devices: 0.01 us -> 1.24 us  [the longest x1 1.24 us: local(): lax.ppermute(second, ('ew', 'ns'), partners(1, lax.axis_size('ew'), n))]
  transfers between devices with their start and end apart: 4 -> 4, of which waited for: 2 -> 3; matrix products, arithmetic and copies ran while one was open for 0% -> 0% of each run, Pallas kernels for 28% -> 23%
where the time goes in v4:
time: 26.2 us; the launch traced here: 26 us
  Pallas kernels  14.2 us (54%)
  starting transfers between devices  7.79 us (30%)
  waiting for transfers between devices  3.31 us (13%)
  between operations  0.67 us (3%)
    pallas_call x1, Pallas kernels, local(): call(boundary, [vmem()] * 11, [(K * R, W)] * 4, [pltpu.VMEM((2, SIDE_BLOC...  5.8 us
    pallas_call x1, Pallas kernels, local(): call(interior, [vmem()] * 6, [(R, 9, K, W), (4, R - 4, K, W), (4, R - 8,...  5.6 us
    ppermute x1, starting transfers between devices, local(): lax.ppermute(to_west, 'ew', [((i + 1) % n, i) for i in range(n)])  3.1 us
    ppermute x1, starting transfers between devices, local(): lax.ppermute(to_east, 'ew', [(i, (i + 1) % n) for i in range(n)])  2.99 us
    pallas_call x1, Pallas kernels, local(): call(pack_edges, [pl.BlockSpec(memory_space=pltpu.HBM)] * FIELDS, [(FIELD...  2.13 us
    ppermute x1, waiting for transfers between devices, local(): lax.ppermute(to_east, 'ew', [(i, (i + 1) % n) for i in range(n)])  1.74 us
    ppermute x1, waiting for transfers between devices, local(): lax.ppermute(second, ('ew', 'ns'), partners(1, lax.axis_size('ew'), n))  1.24 us
    ppermute x1, starting transfers between devices, local(): lax.ppermute(second, ('ew', 'ns'), partners(1, lax.axis_size('ew'), n))  1.11 us
  transfers between devices with their start and end apart: 4, of which 3 were waited for; matrix products, arithmetic and copies ran while one was open for 0% of the time, Pallas kernels for 23%

profile of v4, /device:TPU:0, one launch (start us, length us, event | category | flops | bytes accessed | tf_op | source)
XLA Modules:
  0.0 26.0 jit_solution(1522979891786272732)
XLA Ops:
  0.6 2.1 %shard_map.102 = (f32[7,16,32,128]{3,2,1,0:T(8,128)S(1)}, f32[7,32,128]{2,1,0:T(8,128)S(1)}, f32[4,32,128]{2,1,0:T(8,128)S(1)}, f32[4,32,128]{2,1,0:T(8,128)S(1)}) custom-call(f32[512,128]{1,0:T(8,128)} %bitcast.11, f32[512,128]{1,0:T(8,128)} %bitcast.12, f32[512,128]{1,0:T(8,128)} %bitcast.13, f32[512,128]{1,0:T(8,128)} %bitcast.14, f32[512,128]{1,0:T(8,128)} %bitcast.15, ...), custom_call_target="tpu_custom_call" | custom-call | bytes 1048576 | tf_op jit(solution)/shard_map/pallas_call | solution.py:419
  2.8 3.0 %collective-permute-start = (f32[4,32,128]{2,1,0:T(8,128)S(1)}, f32[4,32,128]{2,1,0:T(8,128)S(1)}, u32[]{:S(2)}, u32[]{:S(2)}) collective-permute-start(f32[4,32,128]{2,1,0:T(8,128)S(1)} %get-tuple-element.24), channel_id=1, source_target_pairs={{0,4},{4,8},{8,12},{12,16},{16,20},{20,24},{24,28},{28,0},{1,5},{5... | collective-permute-start | bytes 196616 | tf_op jit(solution)/shard_map/ppermute | solution.py:431
  5.8 3.1 %collective-permute-start.1 = (f32[4,32,128]{2,1,0:T(8,128)S(1)}, f32[4,32,128]{2,1,0:T(8,128)S(1)}, u32[]{:S(2)}, u32[]{:S(2)}) collective-permute-start(f32[4,32,128]{2,1,0:T(8,128)S(1)} %get-tuple-element.25), channel_id=1, source_target_pairs={{4,0},{8,4},{12,8},{16,12},{20,16},{24,20},{28,24},{0,28},{5,1},{9... | collective-permute-start | bytes 196616 | tf_op jit(solution)/shard_map/ppermute | solution.py:432
  8.9 0.5 %shard_map.103 = (f32[12,9,32,128]{3,2,1,0:T(8,128)S(1)}, f32[16,32,128]{2,1,0:T(8,128)S(1)}) custom-call(f32[7,16,32,128]{3,2,1,0:T(8,128)S(1)} %get-tuple-element.22.rows.refs_0_), custom_call_target="tpu_custom_call" | custom-call | flops 10000000 | bytes 1048576 | tf_op jit(solution)/shard_map/pallas_call | solution.py:434
  9.4 1.7 %collective-permute-done.from_west = f32[4,32,128]{2,1,0:T(8,128)S(1)} collective-permute-done((f32[4,32,128]{2,1,0:T(8,128)S(1)}, f32[4,32,128]{2,1,0:T(8,128)S(1)}, u32[]{:S(2)}, u32[]{:S(2)}) %collective-permute-start) | collective-permute-done | bytes 65568 | tf_op jit(solution)/shard_map/ppermute | solution.py:431
  11.1 0.3 %collective-permute-done.1.from_east = f32[4,32,128]{2,1,0:T(8,128)S(1)} collective-permute-done((f32[4,32,128]{2,1,0:T(8,128)S(1)}, f32[4,32,128]{2,1,0:T(8,128)S(1)}, u32[]{:S(2)}, u32[]{:S(2)}) %collective-permute-start.1) | collective-permute-done | bytes 65568 | tf_op jit(solution)/shard_map/ppermute | solution.py:432
  11.4 0.2 shard_map.104
  11.7 1.1 %collective-permute-start.2 = (f32[28,32,128]{2,1,0:T(8,128)S(1)}, f32[28,32,128]{2,1,0:T(8,128)S(1)}, u32[]{:S(2)}, u32[]{:S(2)}) collective-permute-start(f32[28,32,128]{2,1,0:T(8,128)S(1)} %get-tuple-element.34), channel_id=1, source_target_pairs={{0,4},{1,2},{2,1},{3,7},{4,0},{5,6},{6,5},{7,3},{8,12},{9,10},{10,... | collective-permute-start | bytes 1376264 | tf_op jit(solution)/shard_map/ppermute | solution.py:446
  12.8 0.6 %collective-permute-start.3 = (f32[28,32,128]{2,1,0:T(8,128)S(1)}, f32[28,32,128]{2,1,0:T(8,128)S(1)}, u32[]{:S(2)}, u32[]{:S(2)}) collective-permute-start(f32[28,32,128]{2,1,0:T(8,128)S(1)} %get-tuple-element.35), channel_id=1, source_target_pairs={{0,1},{1,0},{2,3},{3,2},{4,5},{5,4},{6,7},{7,6},{8,9},{9,8},{10,11... | collective-permute-start | bytes 1376264 | tf_op jit(solution)/shard_map/ppermute | solution.py:447
  13.4 5.6 %shard_map.105 = (f32[16,9,32,128]{3,2,1,0:T(8,128)S(1)}, f32[4,12,32,128]{3,2,1,0:T(8,128)S(1)}, f32[4,8,32,128]{3,2,1,0:T(8,128)S(1)}) custom-call(f32[7,16,32,128]{3,2,1,0:T(8,128)S(1)} %get-tuple-element.22.rows.refs_0_, f32[7,32,128]{2,1,0:T(8,128)S(1)} %get-tuple-element.27.left.refs_1_, f32[7,32,128]{2,1,0:T(8,128)S(1)} %get-tuple-element.28.right.refs_2_, ...), custom_call_target="tpu_custom_call" | custom-call | flops 10000000 | bytes 1048576 | tf_op jit(solution)/shard_map/pallas_call | solution.py:449
  19.0 1.2 %collective-permute-done.2.refs_9_ = f32[28,32,128]{2,1,0:T(8,128)S(1)} collective-permute-done((f32[28,32,128]{2,1,0:T(8,128)S(1)}, f32[28,32,128]{2,1,0:T(8,128)S(1)}, u32[]{:S(2)}, u32[]{:S(2)}) %collective-permute-start.2) | collective-permute-done | bytes 458784 | tf_op jit(solution)/shard_map/ppermute | solution.py:446
  20.2 0.0 collective-permute-done.3.refs_10_
  20.2 5.8 %shard_map.106 = (f32[512,128]{1,0:T(8,128)}, f32[512,128]{1,0:T(8,128)}, f32[512,128]{1,0:T(8,128)}, f32[512,128]{1,0:T(8,128)}) custom-call(f32[7,16,32,128]{3,2,1,0:T(8,128)S(1)} %get-tuple-element.22.rows.refs_0_, f32[7,32,128]{2,1,0:T(8,128)S(1)} %get-tuple-element.27.left.refs_1_, f32[7,32,128]{2,1,0:T(8,128)S(1)} %get-tuple-element.28.right.refs_2_, ...), custom_call_target="tpu_custom_call" | custom-call | flops 10000000 | bytes 1048576 | tf_op jit(solution)/shard_map/pallas_call | solution.py:457
Async XLA Ops:
  2.8 8.3 %collective-permute-start = (f32[4,32,128]{2,1,0:T(8,128)S(1)}, f32[4,32,128]{2,1,0:T(8,128)S(1)}, u32[]{:S(2)}, u32[]{:S(2)}) collective-permute-start(f32[4,32,128]{2,1,0:T(8,128)S(1)} %get-tuple-element.24), channel_id=1, source_target_pairs={{0,4},{4,8},{8,12},{12,16},{16,20},{20,24},{24,28},{28,0},{1,5},{5... | collective-permute-start | bytes 196616 | tf_op jit(solution)/shard_map/ppermute | solution.py:431
  5.8 5.7 %collective-permute-start.1 = (f32[4,32,128]{2,1,0:T(8,128)S(1)}, f32[4,32,128]{2,1,0:T(8,128)S(1)}, u32[]{:S(2)}, u32[]{:S(2)}) collective-permute-start(f32[4,32,128]{2,1,0:T(8,128)S(1)} %get-tuple-element.25), channel_id=1, source_target_pairs={{4,0},{8,4},{12,8},{16,12},{20,16},{24,20},{28,24},{0,28},{5,1},{9... | collective-permute-start | bytes 196616 | tf_op jit(solution)/shard_map/ppermute | solution.py:432
  11.7 8.5 %collective-permute-start.2 = (f32[28,32,128]{2,1,0:T(8,128)S(1)}, f32[28,32,128]{2,1,0:T(8,128)S(1)}, u32[]{:S(2)}, u32[]{:S(2)}) collective-permute-start(f32[28,32,128]{2,1,0:T(8,128)S(1)} %get-tuple-element.34), channel_id=1, source_target_pairs={{0,4},{1,2},{2,1},{3,7},{4,0},{5,6},{6,5},{7,3},{8,12},{9,10},{10,... | collective-permute-start | bytes 1376264 | tf_op jit(solution)/shard_map/ppermute | solution.py:446
  12.8 7.4 %collective-permute-start.3 = (f32[28,32,128]{2,1,0:T(8,128)S(1)}, f32[28,32,128]{2,1,0:T(8,128)S(1)}, u32[]{:S(2)}, u32[]{:S(2)}) collective-permute-start(f32[28,32,128]{2,1,0:T(8,128)S(1)} %get-tuple-element.35), channel_id=1, source_target_pairs={{0,1},{1,0},{2,3},{3,2},{4,5},{5,4},{6,7},{7,6},{8,9},{9,8},{10,11... | collective-permute-start | bytes 1376264 | tf_op jit(solution)/shard_map/ppermute | solution.py:447

commit v5 on v4

v5 whole, which is shorter than its diff:
```python
import jax
import jax.numpy as jnp
from jax import lax
from jax.experimental import pallas as pl
from jax.experimental.pallas import tpu as pltpu
from jax.sharding import PartitionSpec as P

horizontal_mix = 0.05
vertical_mix = 0.2

F32 = jnp.float32
K = 32
R = 16
W = 128
G = W // R
HALO = 4
FIELDS = 7
U, V, M = 4, 5, 6
PAIRS = 4
SIDE_BLOCKS = 26
ROWS_AT = (0, 4, 8, 12, 24, 16, 20)
SOUTH, NORTH = 0, 1
MIB = 1 << 20


def lanes():
    return lax.broadcasted_iota(jnp.int32, (K, W), 1)


def turn(x, amount):
    return pltpu.roll(x, amount % W, 1)


def pack_edges(*refs):
    sources = refs[:FIELDS]
    rows, raw, own, to_east, to_west, raw_flow, raw_wet, arrived = refs[FIELDS:]
    copies = []
    for f in range(FIELDS):
        target = raw.at[f, pl.ds(R, K * R)] if f < 4 else raw_wet if f == M else raw_flow.at[f - U]
        copies.append(pltpu.make_async_copy(sources[f], target, arrived.at[f]))
        copies[-1].start()
    for f in range(4):
        raw[f, pl.ds(0, R)] = jnp.zeros((R, W), F32)
        raw[f, pl.ds((K + 1) * R, R)] = jnp.zeros((R, W), F32)
    lane = lanes()
    group = lane // G
    packed = []
    for f in range(FIELDS):
        copies[f].wait()
        source = raw.at[f] if f < 4 else raw_wet if f == M else raw_flow.at[f - U]
        edges = jnp.zeros((K, W), F32)
        for r in range(R):
            x = source[pl.ds(R + r if f < 4 else r, K, stride=R), :].astype(F32)
            rows[f, r] = x
            edges = jnp.where(group == r, turn(x, G * r + HALO), edges)
        own[f] = edges
        packed.append(edges)
    west_half = lane % G < HALO
    packed.append(jnp.zeros((K, W), F32))
    for p in range(PAIRS):
        a, b = packed[2 * p], packed[2 * p + 1]
        to_east[p] = jnp.where(west_half, a, turn(b, HALO))
        to_west[p] = jnp.where(west_half, turn(b, -HALO), a)


def pack_sides(rows, first, second):
    odd = lax.axis_index("ns") % 2
    for out, north in ((first, 1 - odd), (second, odd)):
        for f in range(FIELDS):
            count = 2 if f == U else HALO
            start = (R - count) * north
            for r in range(count):
                out[ROWS_AT[f] + r] = rows[f, start + r]


def pack_corners(own, from_west, from_east, _, left, right, merged, first, second):
    odd = lax.axis_index("ns") % 2
    lane = lanes()
    west_half = lane % G < HALO
    for f in range(FIELDS):
        a, b = from_west[f // 2], from_east[f // 2]
        if f % 2:
            a, b = turn(a, -HALO), turn(b, HALO)
        left_f = jnp.where(west_half, a, own[f])
        right_f = jnp.where(west_half, own[f], b)
        left[f] = left_f
        right[f] = right_f
        merged[f] = jnp.where(west_half, left_f, right_f)
    for out, north in ((first, 1 - odd), (second, odd)):
        for side, edges in enumerate((left, right)):
            block = jnp.zeros((K, W), F32)
            for f in range(FIELDS):
                amount = lax.rem(2 * G * f + W - (W - 2 * G) * north, W)
                moved = pltpu.roll(edges[f], amount, 1)
                block = jnp.where(lane // (2 * G) == f, moved, block)
            out[side] = block


def coefficients(speed, mask):
    opened = {d: mask[d] * mask[d + 1] for d in (-2, -1, 0, 1)}
    s = {d: speed[d] * opened[d] * (1.0 / 12.0) for d in opened}
    a = {d: jnp.abs(s[d]) for d in s}
    w0 = {d: -(s[d] + a[d]) for d in (-1, 0, 1)}
    w3 = {d: a[d] - s[d] for d in (-2, -1, 0)}
    w1, w2 = {}, {}
    for d in (-1, 0):
        even, odd = 7.0 * s[d], 3.0 * a[d] + horizontal_mix * opened[d]
        w1[d], w2[d] = even + odd, even - odd
    forward = [w0[-1], w1[-1] - w0[0], w3[-1] - w2[0], -w3[0]]
    transposed = [-w3[-2], w3[-2] - w2[-1], w1[0] - w0[1], w0[1]]
    return forward + transposed + [w2[-1] - w1[0]]


def shifted(c, h, d, lane, step=1):
    if d == 0:
        return c
    if d > 0:
        return turn(jnp.where(lane < step * d, h, c), -step * d)
    return turn(jnp.where(lane >= W + step * d, h, c), -step * d)


def x_coefficients(u, uh, m, mh, lane):
    return coefficients(
        {d: shifted(u, uh, d, lane) for d in (-2, -1, 0, 1)},
        {d: shifted(m, mh, d, lane) for d in (-2, -1, 0, 1, 2)},
    )


def level_coefficients(m):
    inner = lax.broadcasted_iota(jnp.int32, (K, W), 0) < K - 1
    after = jnp.where(inner, vertical_mix * m * pltpu.roll(m, K - 1, 0), 0.0)
    before = pltpu.roll(after, 1, 0)
    return after, before, 1.0 - after - before


def chunk(q):
    return pl.ds(8 * q, 8)


def strided(q, j, stride, shift=0):
    return pl.ds((8 * q + 1 + shift) * stride + j, 8, stride=stride)


def step_row(store, load, x=None, y=None, z=None, base=None):
    lane = lanes()[:8]
    results = []
    for q in range(K // 8):
        part = chunk(q)
        centre = None
        for term in (x and x[0].at[8], y and y.at[8], z and z[0].at[2]):
            if term is not None:
                centre = term[part] if centre is None else centre + term[part]
        if z:
            after, before = z[0].at[0][part], z[0].at[1][part]
        for direction in (0, 1):
            ks = range(4 * direction, 4 * direction + 4)
            xs = [x[0].at[k][part] for k in ks] if x else []
            ys = [y.at[k][part] for k in ks] if y else []
            for f in (2 * direction, 2 * direction + 1):
                c = load(f, 0, q)
                total = centre * c
                if base:
                    total += base(f, q)
                if x:
                    h = x[1](f, q)
                for coefficient, d in zip(xs, (-2, -1, 1, 2)):
                    total += coefficient * shifted(c, h, d, lane)
                for coefficient, d in zip(ys, (-2, -1, 1, 2)):
                    total += coefficient * load(f, d, q)
                if z:
                    c_after, c_before = z[1](f, q)
                    total += after * c_after + before * c_before
                results.append((f, q, total))
    for result in results:
        store(*result)


def halo_columns(merged, j):
    return pltpu.roll(merged, lax.rem(2 * W - HALO - G * j, W), 1)


def edge_columns_and_levels(edges):
    u, m = edges[U], edges[M]
    xs = coefficients(
        {d: turn(u, -d) for d in (-2, -1, 0, 1)},
        {d: turn(m, -d) for d in (-2, -1, 0, 1, 2)},
    )
    after, before, centre = level_coefficients(m)
    results = []
    for f in range(4):
        c = edges[f]
        total = (centre + xs[8]) * c
        total += after * pltpu.roll(c, K - 1, 0) + before * pltpu.roll(c, 1, 0)
        for coefficient, d in zip(xs[4 * (f // 2) :], (-2, -1, 1, 2)):
            total += coefficient * turn(c, -d)
        results.append(total)
    return results


def edge_rows(edges, beyond):
    lane = lanes()
    v, m = edges[V], edges[M]
    vh, mh = beyond(V), beyond(M)
    ys = coefficients(
        {d: shifted(v, vh, d, lane, G) for d in (-2, -1, 0, 1)},
        {d: shifted(m, mh, d, lane, G) for d in (-2, -1, 0, 1, 2)},
    )
    results = []
    for f in range(4):
        c, ch = edges[f], beyond(f)
        total = ys[8] * c
        for coefficient, d in zip(ys[4 * (f // 2) :], (-2, -1, 1, 2)):
            total += coefficient * shifted(c, ch, d, lane, G)
        results.append(total)
    return results


def y_coefficients_at(row, j):
    return coefficients(
        {d: row(V, j + d)[...] for d in (-2, -1, 0, 1)},
        {d: row(M, j + d)[...] for d in (-2, -1, 0, 1, 2)},
    )


def by_fours(start, stop, body):
    def four(i, carry):
        for k in range(4):
            body(start + 4 * i + k)
        return carry

    lax.fori_loop(0, (stop - start) // 4, four, 0)


def raw_levels(raw, j):
    return lambda f, q: (raw.at[f][strided(q, j, R, 1), :], raw.at[f][strided(q, j, R, -1), :])


def prepare(rows, raw, y_out, level_out, base_out):
    def levels(j):
        for k, value in enumerate(level_coefficients(rows[M, j])):
            level_out[j, k] = value

    by_fours(0, R, levels)

    def across(j):
        got = y_coefficients_at(lambda f, r: rows.at[f, r], j)
        for k in range(9):
            y_out[j - 2, k] = got[k]

    by_fours(2, R - 2, across)

    def first(j):
        def store(f, q, value):
            base_out.at[f, j - 2][chunk(q)] = value

        step_row(
            store,
            lambda f, d, q: rows.at[f, j + d][chunk(q)],
            y=y_out.at[j - 2],
            z=(level_out.at[j], raw_levels(raw, j)),
        )

    by_fours(2, R - 2, first)


def interior(*refs):
    rows, raw, left, right, merged, y_in, level_in, base_in = refs[:8]
    x_out, c1_out, part1_out, c2_out, part2_out, edge_out, merged1 = refs[8:]
    lane = lanes()
    west_half = lane % G < HALO
    for f in range(4):
        c1_out[f, pl.ds(0, R)] = jnp.zeros((R, W), F32)
        c1_out[f, pl.ds((K + 1) * R, R)] = jnp.zeros((R, W), F32)

    def x_body(j):
        got = x_coefficients(
            rows[U, j], halo_columns(merged[U], j), rows[M, j], halo_columns(merged[M], j), lane
        )
        for k in range(9):
            x_out[j, k] = got[k]

    by_fours(0, R, x_body)

    both = []
    for side, edges in enumerate((left, right)):
        partial = edge_columns_and_levels(edges)
        across = edge_rows(edges, lambda f: edges[f])
        for f in range(4):
            edge_out[side, f] = partial[f]
        both.append([p + a for p, a in zip(partial, across)])
    for f in range(4):
        merged1[f] = jnp.where(west_half, both[0][f], both[1][f])

    def halo(source, j):
        return lambda f, q: halo_columns(source.at[f][chunk(q)], j)

    def first(j):
        def store(f, q, value):
            c1_out.at[f][strided(q, j, R), :] = value

        step_row(
            store,
            lambda f, d, q: rows.at[f, j][chunk(q)],
            x=(x_out.at[j], halo(merged, j)),
            base=lambda f, q: base_in.at[f, j - 2][chunk(q)],
        )

    by_fours(2, R - 2, first)

    for i, j in enumerate((0, 1, R - 2, R - 1)):
        def store(f, q, value):
            part1_out.at[f, i][chunk(q)] = value

        step_row(
            store,
            lambda f, d, q: rows.at[f, j][chunk(q)],
            x=(x_out.at[j], halo(merged, j)),
            z=(level_in.at[j], raw_levels(raw, j)),
        )

    def second(j):
        def store(f, q, value):
            c2_out.at[f, j - 4][chunk(q)] = value

        step_row(
            store,
            lambda f, d, q: c1_out.at[f][strided(q, j + d, R), :],
            x=(x_out.at[j], halo(merged1, j)),
            y=y_in.at[j - 2],
            z=(level_in.at[j], raw_levels(c1_out, j)),
        )

    by_fours(4, R - 4, second)

    for i, j in enumerate((2, 3, R - 4, R - 3)):
        def store(f, q, value):
            part2_out.at[f, i][chunk(q)] = value

        step_row(
            store,
            lambda f, d, q: c1_out.at[f][strided(q, j, R), :],
            x=(x_out.at[j], halo(merged1, j)),
            z=(level_in.at[j], raw_levels(c1_out, j)),
        )


def boundary(*refs):
    rows, left, right, merged, y_in, level_in, x_in, c1_in, part1_in, c2_in, part2_in, edge_in = refs[:12]
    messages = refs[12:16]
    outs = refs[16:20]
    sides, corners, x_new, y_new, level_new, c1_new, merged1, beyond = refs[20:]
    lane = lanes()
    west_half = lane % G < HALO
    place = lax.axis_index("ns")
    last = lax.axis_size("ns") - 1
    odd = place % 2
    inside = {SOUTH: place > 0, NORTH: place < last}
    slots = 8
    near = (-2, -1, 0, 1, R - 2, R - 1, R, R + 1)
    new_at = {j: i for i, j in enumerate(near)}
    for f in range(4):
        c1_new[f, pl.ds(0, slots)] = jnp.zeros((slots, W), F32)
        c1_new[f, pl.ds((K + 1) * slots, slots)] = jnp.zeros((slots, W), F32)

    for source, target in ((0, sides), (1, corners)):
        def unpack(b, carry):
            for message, side in ((messages[source], odd), (messages[source + 2], 1 - odd)):
                here = jnp.where(side == NORTH, place < last, place > 0)
                target[side, b] = jnp.where(here, message[b], 0.0)
            return carry

        lax.fori_loop(0, target.shape[1], unpack, 0, unroll=2)

    def row(f, j):
        if j < 0:
            return sides.at[SOUTH, ROWS_AT[f] + j + (2 if f == U else HALO)]
        if j >= R:
            return sides.at[NORTH, ROWS_AT[f] + j - R]
        return rows.at[f, j]

    for s in range(2):
        for f in range(FIELDS):
            south = turn(corners[SOUTH, s], W - 2 * G - 2 * G * f)
            north = turn(corners[NORTH, s], -2 * G * f)
            beyond[s, f] = jnp.where(lane >= W // 2, south, north)

    both = []
    for s, edges in enumerate((left, right)):
        across = edge_rows(edges, lambda f: beyond[s, f])
        both.append([edge_in[s, f] + a for f, a in enumerate(across)])
    for f in range(4):
        merged1[f] = jnp.where(west_half, both[0][f], both[1][f])

    def halo_beyond(f, j):
        return halo_columns(jnp.where(west_half, beyond[0, f], beyond[1, f]), j % R)

    for j in near:
        got = y_coefficients_at(row, j)
        for k in range(9):
            y_new[new_at[j], k] = got[k]
        if not 0 <= j < R:
            got = x_coefficients(
                row(U, j)[...], halo_beyond(U, j), row(M, j)[...], halo_beyond(M, j), lane
            )
            for k in range(9):
                x_new[new_at[j], k] = got[k]
            for k, value in enumerate(level_coefficients(row(M, j)[...])):
                level_new[new_at[j], k] = value

    for j in near:
        side = SOUTH if j < R // 2 else NORTH

        def store(f, q, value):
            if f >= 2 and not 0 <= j < R:
                value = jnp.where(inside[side], value, 0.0)
            c1_new.at[f][strided(q, new_at[j], slots), :] = value

        def load(f, d, q):
            return row(f, j + d)[chunk(q)]

        if 0 <= j < R:
            i = (0, 1, R - 2, R - 1).index(j)
            step_row(
                store, load, y=y_new.at[new_at[j]], base=lambda f, q: part1_in.at[f, i][chunk(q)]
            )
        else:
            halos = [halo_beyond(f, j) for f in range(4)]
            after = [pltpu.roll(row(f, j)[...], K - 1, 0) for f in range(4)]
            before = [pltpu.roll(row(f, j)[...], 1, 0) for f in range(4)]
            at = lambda x, q: x[8 * q : 8 * q + 8]
            step_row(
                store,
                load,
                x=(x_new.at[new_at[j]], lambda f, q: at(halos[f], q)),
                y=y_new.at[new_at[j]],
                z=(level_new.at[new_at[j]], lambda f, q: (at(after[f], q), at(before[f], q))),
            )

    def load1(f, j, q):
        if j in new_at:
            return c1_new.at[f][strided(q, new_at[j], slots), :]
        return c1_in.at[f][strided(q, j, R), :]

    for j in (0, 1, 2, 3, R - 4, R - 3, R - 2, R - 1):
        def store(f, q, value):
            outs[f][pl.ds(8 * q * R + j, 8, stride=R), :] = value

        def load(f, d, q):
            return load1(f, j + d, q)

        if j in new_at:
            def neighbours(f, q):
                ref, at = c1_new.at[f], new_at[j]
                return ref[strided(q, at, slots, 1), :], ref[strided(q, at, slots, -1), :]

            step_row(
                store,
                load,
                x=(x_in.at[j], lambda f, q: halo_columns(merged1.at[f][chunk(q)], j)),
                y=y_new.at[new_at[j]],
                z=(level_in.at[j], neighbours),
            )
        else:
            i = (2, 3, R - 4, R - 3).index(j)
            step_row(
                store, load, y=y_in.at[j - 2], base=lambda f, q: part2_in.at[f, i][chunk(q)]
            )

    def copy(j, carry):
        for f in range(4):
            outs[f][pl.ds(j, K, stride=R), :] = c2_in[f, j - 4]
        return carry

    lax.fori_loop(4, R - 4, copy, 0, unroll=2)


def vmem():
    return pl.BlockSpec(memory_space=pltpu.VMEM)


def call(kernel, in_specs, out_shapes, scratch=(), limit=16 * MIB, cost=0):
    return pl.pallas_call(
        kernel,
        out_shape=[jax.ShapeDtypeStruct(shape, F32) for shape in out_shapes],
        in_specs=in_specs,
        out_specs=[vmem()] * len(out_shapes),
        scratch_shapes=list(scratch),
        compiler_params=pltpu.CompilerParams(vmem_limit_bytes=limit),
        cost_estimate=pl.CostEstimate(flops=cost, bytes_accessed=MIB, transcendentals=0),
    )


def partners(odd, n_ew, n_ns):
    pairs = []
    for e in range(n_ew):
        for s in range(n_ns):
            step = 1 if (s - odd) % 2 == 0 else -1
            if 0 <= s + step < n_ns:
                to = (e, s + step)
            else:
                to = (e ^ 1 if e ^ 1 < n_ew else e, s)
            pairs.append((e * n_ns + s, to[0] * n_ns + to[1]))
    return pairs


def local(temp, salt, u_east, v_north, wet, cot_temp, cot_salt):
    flat = [a.reshape(K * R, W) for a in (temp, salt, cot_temp, cot_salt, u_east, v_north, wet)]

    row = (K, W)
    padded = ((K + 2) * R, W)
    rows, raw, own, to_east, to_west = call(
        pack_edges,
        [pl.BlockSpec(memory_space=pltpu.HBM)] * FIELDS,
        [(FIELDS, R) + row, (4,) + padded, (FIELDS,) + row, (PAIRS,) + row, (PAIRS,) + row],
        [
            pltpu.VMEM((2, K * R, W), F32),
            pltpu.VMEM((K * R, W), jnp.int32),
            pltpu.SemaphoreType.DMA((FIELDS,)),
        ],
    )(*[pltpu.with_memory_space_constraint(a, pltpu.HBM) for a in flat])

    n_ew, n_ns = lax.axis_size("ew"), lax.axis_size("ns")
    from_west = lax.ppermute(to_east, "ew", [(i, (i + 1) % n_ew) for i in range(n_ew)])
    from_east = lax.ppermute(to_west, "ew", [((i + 1) % n_ew, i) for i in range(n_ew)])

    def swap(odd, message):
        return lax.ppermute(message, ("ew", "ns"), partners(odd, n_ew, n_ns))

    first, second = call(pack_sides, [vmem()], [(SIDE_BLOCKS,) + row] * 2)(rows)
    second = swap(1, second)
    first = swap(0, first)

    y_in, level, base = call(
        prepare,
        [vmem()] * 2,
        [(R - 4, 9) + row, (R, 3) + row, (4, R - 4) + row],
        cost=10_000_000,
    )(rows, raw)

    left, right, merged, first_corners, second_corners = call(
        pack_corners,
        [vmem()] * 3 + [pl.BlockSpec(memory_space=pl.ANY)],
        [(FIELDS,) + row] * 3 + [(2,) + row] * 2,
    )(own, from_west, from_east, level)
    second_corners = swap(1, second_corners)
    first_corners = swap(0, first_corners)

    x_in, c1, part1, c2, part2, edge = call(
        interior,
        [vmem()] * 8,
        [(R, 9) + row, (4,) + padded, (4, 4) + row, (4, R - 8) + row, (4, 4) + row, (2, 4) + row],
        [pltpu.VMEM((4,) + row, F32)],
        cost=10_000_000,
    )(rows, raw, left, right, merged, y_in, level, base)

    outs = call(
        boundary,
        [vmem()] * 16,
        [(K * R, W)] * 4,
        [
            pltpu.VMEM((2, SIDE_BLOCKS) + row, F32),
            pltpu.VMEM((2, 2) + row, F32),
            pltpu.VMEM((8, 9) + row, F32),
            pltpu.VMEM((8, 9) + row, F32),
            pltpu.VMEM((8, 3) + row, F32),
            pltpu.VMEM((4, (K + 2) * 8, W), F32),
            pltpu.VMEM((4,) + row, F32),
            pltpu.VMEM((2, FIELDS) + row, F32),
        ],
        cost=10_000_000,
    )(
        *(rows, left, right, merged, y_in, level, x_in, c1, part1, c2, part2, edge),
        *(second, second_corners, first, first_corners),
    )
    return tuple(a.reshape(K, R, W) for a in outs)


def solution(mesh):
    spec = P(None, "ns", "ew")
    return jax.shard_map(
        local, mesh=mesh, in_specs=(spec,) * 7, out_specs=(spec,) * 4, check_vma=False
    )
```

time: 26.2 us -> 45.9 us (1.75)
  Pallas kernels: 14.2 us -> 32.6 us
  starting transfers between devices: 7.79 us -> 9.98 us
  waiting for transfers between devices: 3.31 us -> 2.39 us
    pallas_call x4 -> x5, Pallas kernels: 12.1 us -> 30.5 us  [the longest x1 22 us: local(): call(interior, [vmem()] * 8, [(R, 9) + row, (4,) + padded, (4, 4) + row,...]
    ppermute x4 -> x6, starting transfers between devices: 7.79 us -> 9.98 us  [the longest x4 5.24 us: swap(): return lax.ppermute(message, ('ew', 'ns'), partners(odd, n_ew, n_ns))]
    ppermute x4 -> x6, waiting for transfers between devices: 3.31 us -> 2.39 us  [the longest x1 1.92 us: local(): lax.ppermute(to_east, 'ew', [(i, (i + 1) % n_ew) for i in range(n_ew)])]
  transfers between devices with their start and end apart: 4 -> 6, of which waited for: 3 -> 2; matrix products, arithmetic and copies ran while one was open for 0% -> 0% of each run, Pallas kernels for 23% -> 52%
where the time goes in v5:
time: 45.9 us; the launch traced here: 45.6 us
  Pallas kernels  32.6 us (71%)
  starting transfers between devices  9.98 us (22%)
  waiting for transfers between devices  2.39 us (5%)
  between operations  0.7 us (2%)
    pallas_call x1, Pallas kernels, local(): call(interior, [vmem()] * 8, [(R, 9) + row, (4,) + padded, (4, 4) + row,...  22 us
    pallas_call x1, Pallas kernels, local(): call(boundary, [vmem()] * 16, [(K * R, W)] * 4, [pltpu.VMEM((2, SIDE_BLOC...  6.49 us
    ppermute x4, starting transfers between devices, swap(): return lax.ppermute(message, ('ew', 'ns'), partners(odd, n_ew, n_ns))  5.24 us
    ppermute x1, starting transfers between devices, local(): lax.ppermute(to_west, 'ew', [((i + 1) % n_ew, i) for i in range(n_ew)])  3.25 us
    pallas_call x1, Pallas kernels, local(): call(pack_edges, [pl.BlockSpec(memory_space=pltpu.HBM)] * FIELDS, [(FIELD...  2.12 us
    ppermute x1, waiting for transfers between devices, local(): lax.ppermute(to_east, 'ew', [(i, (i + 1) % n_ew) for i in range(n_ew)])  1.92 us
    pallas_call x1, Pallas kernels, local(): call(prepare, [vmem()] * 2, [(R - 4, 9) + row, (R, 3) + row, (4, R - 4) +...  1.65 us
    ppermute x1, starting transfers between devices, local(): lax.ppermute(to_east, 'ew', [(i, (i + 1) % n_ew) for i in range(n_ew)])  1.49 us
  transfers between devices with their start and end apart: 6, of which 2 were waited for; matrix products, arithmetic and copies ran while one was open for 0% of the time, Pallas kernels for 52%

profile of v5, /device:TPU:0, one launch (start us, length us, event | category | flops | bytes accessed | tf_op | source)
XLA Modules:
  0.0 45.6 jit_solution(17831249305601424933)
XLA Ops:
  0.6 2.1 %shard_map.102 = (f32[7,16,32,128]{3,2,1,0:T(8,128)S(1)}, f32[4,544,128]{2,1,0:T(8,128)S(1)}, f32[7,32,128]{2,1,0:T(8,128)S(1)}, f32[4,32,128]{2,1,0:T(8,128)S(1)}, f32[4,32,128]{2,1,0:T(8,128)S(1)}) custom-call(f32[512,128]{1,0:T(8,128)} %bitcast.11, f32[512,128]{1,0:T(8,128)} %bitcast.12, f32[512,128]{1,0:T(8,128)} %bitcast.13, f32[512,128]{1,0:T(8,128)} %bitcast.14, ...), custom_call_target="tpu_custom_call" | custom-call | bytes 1048576 | tf_op jit(solution)/shard_map/pallas_call | solution.py:511
  2.8 0.1 shard_map.106
  2.8 3.0 %collective-permute-start.2 = (f32[26,32,128]{2,1,0:T(8,128)S(1)}, f32[26,32,128]{2,1,0:T(8,128)S(1)}, u32[]{:S(2)}, u32[]{:S(2)}) collective-permute-start(f32[26,32,128]{2,1,0:T(8,128)S(1)} %get-tuple-element.46), channel_id=1, source_target_pairs={{0,4},{1,2},{2,1},{3,7},{4,0},{5,6},{6,5},{7,3},{8,12},{9,10},{10,... | collective-permute-start | bytes 1277960 | tf_op jit(solution)/shard_map/ppermute | solution.py:527
  5.8 0.1 collective-permute-start.4
  6.0 1.5 %collective-permute-start = (f32[4,32,128]{2,1,0:T(8,128)S(1)}, f32[4,32,128]{2,1,0:T(8,128)S(1)}, u32[]{:S(2)}, u32[]{:S(2)}) collective-permute-start(f32[4,32,128]{2,1,0:T(8,128)S(1)} %get-tuple-element.31), channel_id=1, source_target_pairs={{0,4},{4,8},{8,12},{12,16},{16,20},{20,24},{24,28},{28,0},{1,5},{5... | collective-permute-start | bytes 196616 | tf_op jit(solution)/shard_map/ppermute | solution.py:523
  7.5 3.2 %collective-permute-start.1 = (f32[4,32,128]{2,1,0:T(8,128)S(1)}, f32[4,32,128]{2,1,0:T(8,128)S(1)}, u32[]{:S(2)}, u32[]{:S(2)}) collective-permute-start(f32[4,32,128]{2,1,0:T(8,128)S(1)} %get-tuple-element.32), channel_id=1, source_target_pairs={{4,0},{8,4},{12,8},{16,12},{20,16},{24,20},{28,24},{0,28},{5,1},{9... | collective-permute-start | bytes 196616 | tf_op jit(solution)/shard_map/ppermute | solution.py:524
  10.7 1.6 %shard_map.103 = (f32[12,9,32,128]{3,2,1,0:T(8,128)S(1)}, f32[16,3,32,128]{3,2,1,0:T(8,128)S(1)}, f32[4,12,32,128]{3,2,1,0:T(8,128)S(1)}) custom-call(f32[7,16,32,128]{3,2,1,0:T(8,128)S(1)} %get-tuple-element.29.rows.refs_0_, f32[4,544,128]{2,1,0:T(8,128)S(1)} %get-tuple-element.33.raw.refs_1_), custom_call_target="tpu_custom_call" | custom-call | flops 10000000 | bytes 1048576 | tf_op jit(solution)/shard_map/pallas_call | solution.py:533
  12.4 1.9 %collective-permute-done.from_west = f32[4,32,128]{2,1,0:T(8,128)S(1)} collective-permute-done((f32[4,32,128]{2,1,0:T(8,128)S(1)}, f32[4,32,128]{2,1,0:T(8,128)S(1)}, u32[]{:S(2)}, u32[]{:S(2)}) %collective-permute-start) | collective-permute-done | bytes 65568 | tf_op jit(solution)/shard_map/ppermute | solution.py:523
  14.3 0.5 %collective-permute-done.1.from_east = f32[4,32,128]{2,1,0:T(8,128)S(1)} collective-permute-done((f32[4,32,128]{2,1,0:T(8,128)S(1)}, f32[4,32,128]{2,1,0:T(8,128)S(1)}, u32[]{:S(2)}, u32[]{:S(2)}) %collective-permute-start.1) | collective-permute-done | bytes 65568 | tf_op jit(solution)/shard_map/ppermute | solution.py:524
  14.8 0.2 shard_map.104
  15.0 2.1 %collective-permute-start.3 = (f32[2,32,128]{2,1,0:T(8,128)S(1)}, f32[2,32,128]{2,1,0:T(8,128)S(1)}, u32[]{:S(2)}, u32[]{:S(2)}) collective-permute-start(f32[2,32,128]{2,1,0:T(8,128)S(1)} %get-tuple-element.47), channel_id=1, source_target_pairs={{0,4},{1,2},{2,1},{3,7},{4,0},{5,6},{6,5},{7,3},{8,12},{9,10},{10,... | collective-permute-start | bytes 98312 | tf_op jit(solution)/shard_map/ppermute | solution.py:527
  17.1 0.0 collective-permute-start.5
  17.1 22.0 %shard_map.105 = (f32[16,9,32,128]{3,2,1,0:T(8,128)S(1)}, f32[4,544,128]{2,1,0:T(8,128)S(1)}, f32[4,4,32,128]{3,2,1,0:T(8,128)S(1)}, f32[4,8,32,128]{3,2,1,0:T(8...) custom-call(f32[7,16,32,128]{3,2,1,0:T(8,128)S(1)} %get-tuple-element.29.rows.refs_0_, ...), custom_call_target="tpu_custom_call" | custom-call | flops 10000000 | bytes 1048576 | tf_op jit(solution)/shard_map/pallas_call | solution.py:548
  39.1 0.0 collective-permute-done.3.refs_13_
  39.1 0.0 collective-permute-done.5.refs_15_
  39.1 0.0 collective-permute-done.2.refs_12_
  39.2 0.0 collective-permute-done.4.refs_14_
  39.2 6.5 %shard_map.107 = (f32[512,128]{1,0:T(8,128)}, f32[512,128]{1,0:T(8,128)}, f32[512,128]{1,0:T(8,128)}, f32[512,128]{1,0:T(8,128)}) custom-call(f32[7,16,32,128]{3,2,1,0:T(8,128)S(1)} %get-tuple-element.29.rows.refs_0_, f32[7,32,128]{2,1,0:T(8,128)S(1)} %get-tuple-element.35.refs_2_.refs_1_, f32[7,32,128]{2,1,0:T(8,128)S(1)} %get-tuple-element.36.refs_3_.refs_2_, ...), custom_call_target="tpu_custom_call" | custom-call | flops 10000000 | bytes 1048576 | tf_op jit(solution)/shard_map/pallas_call | solution.py:556
Async XLA Ops:
  2.8 36.3 %collective-permute-start.2 = (f32[26,32,128]{2,1,0:T(8,128)S(1)}, f32[26,32,128]{2,1,0:T(8,128)S(1)}, u32[]{:S(2)}, u32[]{:S(2)}) collective-permute-start(f32[26,32,128]{2,1,0:T(8,128)S(1)} %get-tuple-element.46), channel_id=1, source_target_pairs={{0,4},{1,2},{2,1},{3,7},{4,0},{5,6},{6,5},{7,3},{8,12},{9,10},{10,... | collective-permute-start | bytes 1277960 | tf_op jit(solution)/shard_map/ppermute | solution.py:527
  5.8 33.3 %collective-permute-start.4 = (f32[26,32,128]{2,1,0:T(8,128)S(1)}, f32[26,32,128]{2,1,0:T(8,128)S(1)}, u32[]{:S(2)}, u32[]{:S(2)}) collective-permute-start(f32[26,32,128]{2,1,0:T(8,128)S(1)} %get-tuple-element.48), channel_id=1, source_target_pairs={{0,1},{1,0},{2,3},{3,2},{4,5},{5,4},{6,7},{7,6},{8,9},{9,8},{10,11... | collective-permute-start | bytes 1277960 | tf_op jit(solution)/shard_map/ppermute | solution.py:527
  6.0 8.3 %collective-permute-start = (f32[4,32,128]{2,1,0:T(8,128)S(1)}, f32[4,32,128]{2,1,0:T(8,128)S(1)}, u32[]{:S(2)}, u32[]{:S(2)}) collective-permute-start(f32[4,32,128]{2,1,0:T(8,128)S(1)} %get-tuple-element.31), channel_id=1, source_target_pairs={{0,4},{4,8},{8,12},{12,16},{16,20},{20,24},{24,28},{28,0},{1,5},{5... | collective-permute-start | bytes 196616 | tf_op jit(solution)/shard_map/ppermute | solution.py:523
  7.5 7.3 %collective-permute-start.1 = (f32[4,32,128]{2,1,0:T(8,128)S(1)}, f32[4,32,128]{2,1,0:T(8,128)S(1)}, u32[]{:S(2)}, u32[]{:S(2)}) collective-permute-start(f32[4,32,128]{2,1,0:T(8,128)S(1)} %get-tuple-element.32), channel_id=1, source_target_pairs={{4,0},{8,4},{12,8},{16,12},{20,16},{24,20},{28,24},{0,28},{5,1},{9... | collective-permute-start | bytes 196616 | tf_op jit(solution)/shard_map/ppermute | solution.py:524
  15.0 24.1 %collective-permute-start.3 = (f32[2,32,128]{2,1,0:T(8,128)S(1)}, f32[2,32,128]{2,1,0:T(8,128)S(1)}, u32[]{:S(2)}, u32[]{:S(2)}) collective-permute-start(f32[2,32,128]{2,1,0:T(8,128)S(1)} %get-tuple-element.47), channel_id=1, source_target_pairs={{0,4},{1,2},{2,1},{3,7},{4,0},{5,6},{6,5},{7,3},{8,12},{9,10},{10,... | collective-permute-start | bytes 98312 | tf_op jit(solution)/shard_map/ppermute | solution.py:527
  17.1 22.0 %collective-permute-start.5 = (f32[2,32,128]{2,1,0:T(8,128)S(1)}, f32[2,32,128]{2,1,0:T(8,128)S(1)}, u32[]{:S(2)}, u32[]{:S(2)}) collective-permute-start(f32[2,32,128]{2,1,0:T(8,128)S(1)} %get-tuple-element.49), channel_id=1, source_target_pairs={{0,1},{1,0},{2,3},{3,2},{4,5},{5,4},{6,7},{7,6},{8,9},{9,8},{10,11... | collective-permute-start | bytes 98312 | tf_op jit(solution)/shard_map/ppermute | solution.py:527

commit v6 on v5

--- a/solution.py
+++ b/solution.py
@@ -235,6 +235,12 @@
     return lambda f, q: (raw.at[f][strided(q, j, R, 1), :], raw.at[f][strided(q, j, R, -1), :])
 
 
+def rolled_levels(load):
+    after = [pltpu.roll(load(f), K - 1, 0) for f in range(4)]
+    before = [pltpu.roll(load(f), 1, 0) for f in range(4)]
+    return lambda f, q: (after[f][8 * q : 8 * q + 8], before[f][8 * q : 8 * q + 8])
+
+
 def prepare(rows, raw, y_out, level_out, base_out):
     def levels(j):
         for k, value in enumerate(level_coefficients(rows[M, j])):
@@ -268,10 +274,6 @@
     x_out, c1_out, part1_out, c2_out, part2_out, edge_out, merged1 = refs[8:]
     lane = lanes()
     west_half = lane % G < HALO
-    for f in range(4):
-        c1_out[f, pl.ds(0, R)] = jnp.zeros((R, W), F32)
-        c1_out[f, pl.ds((K + 1) * R, R)] = jnp.zeros((R, W), F32)
-
     def x_body(j):
         got = x_coefficients(
             rows[U, j], halo_columns(merged[U], j), rows[M, j], halo_columns(merged[M], j), lane
@@ -292,11 +294,12 @@
         merged1[f] = jnp.where(west_half, both[0][f], both[1][f])
 
     def halo(source, j):
-        return lambda f, q: halo_columns(source.at[f][chunk(q)], j)
+        halos = [halo_columns(source[f], j) for f in range(4)]
+        return lambda f, q: halos[f][8 * q : 8 * q + 8]
 
     def first(j):
         def store(f, q, value):
-            c1_out.at[f][strided(q, j, R), :] = value
+            c1_out.at[f, j - 2][chunk(q)] = value
 
         step_row(
             store,
@@ -324,10 +327,10 @@
 
         step_row(
             store,
-            lambda f, d, q: c1_out.at[f][strided(q, j + d, R), :],
+            lambda f, d, q: c1_out.at[f, j - 2 + d][chunk(q)],
             x=(x_out.at[j], halo(merged1, j)),
             y=y_in.at[j - 2],
-            z=(level_in.at[j], raw_levels(c1_out, j)),
+            z=(level_in.at[j], rolled_levels(lambda f: c1_out[f, j - 2])),
         )
 
     by_fours(4, R - 4, second)
@@ -338,9 +341,9 @@
 
         step_row(
             store,
-            lambda f, d, q: c1_out.at[f][strided(q, j, R), :],
+            lambda f, d, q: c1_out.at[f, j - 2][chunk(q)],
             x=(x_out.at[j], halo(merged1, j)),
-            z=(level_in.at[j], raw_levels(c1_out, j)),
+            z=(level_in.at[j], rolled_levels(lambda f: c1_out[f, j - 2])),
         )
 
 
@@ -355,13 +358,8 @@
     last = lax.axis_size("ns") - 1
     odd = place % 2
     inside = {SOUTH: place > 0, NORTH: place < last}
-    slots = 8
     near = (-2, -1, 0, 1, R - 2, R - 1, R, R + 1)
     new_at = {j: i for i, j in enumerate(near)}
-    for f in range(4):
-        c1_new[f, pl.ds(0, slots)] = jnp.zeros((slots, W), F32)
-        c1_new[f, pl.ds((K + 1) * slots, slots)] = jnp.zeros((slots, W), F32)
-
     for source, target in ((0, sides), (1, corners)):
         def unpack(b, carry):
             for message, side in ((messages[source], odd), (messages[source + 2], 1 - odd)):
@@ -413,7 +411,7 @@
         def store(f, q, value):
             if f >= 2 and not 0 <= j < R:
                 value = jnp.where(inside[side], value, 0.0)
-            c1_new.at[f][strided(q, new_at[j], slots), :] = value
+            c1_new.at[f, new_at[j]][chunk(q)] = value
 
         def load(f, d, q):
             return row(f, j + d)[chunk(q)]
@@ -425,21 +423,18 @@
             )
         else:
             halos = [halo_beyond(f, j) for f in range(4)]
-            after = [pltpu.roll(row(f, j)[...], K - 1, 0) for f in range(4)]
-            before = [pltpu.roll(row(f, j)[...], 1, 0) for f in range(4)]
-            at = lambda x, q: x[8 * q : 8 * q + 8]
             step_row(
                 store,
                 load,
-                x=(x_new.at[new_at[j]], lambda f, q: at(halos[f], q)),
+                x=(x_new.at[new_at[j]], lambda f, q: halos[f][8 * q : 8 * q + 8]),
                 y=y_new.at[new_at[j]],
-                z=(level_new.at[new_at[j]], lambda f, q: (at(after[f], q), at(before[f], q))),
+                z=(level_new.at[new_at[j]], rolled_levels(lambda f: row(f, j)[...])),
             )
 
     def load1(f, j, q):
         if j in new_at:
-            return c1_new.at[f][strided(q, new_at[j], slots), :]
-        return c1_in.at[f][strided(q, j, R), :]
+            return c1_new.at[f, new_at[j]][chunk(q)]
+        return c1_in.at[f, j - 2][chunk(q)]
 
     for j in (0, 1, 2, 3, R - 4, R - 3, R - 2, R - 1):
         def store(f, q, value):
@@ -449,16 +444,13 @@
             return load1(f, j + d, q)
 
         if j in new_at:
-            def neighbours(f, q):
-                ref, at = c1_new.at[f], new_at[j]
-                return ref[strided(q, at, slots, 1), :], ref[strided(q, at, slots, -1), :]
-
+            halos = [halo_columns(merged1[f], j) for f in range(4)]
             step_row(
                 store,
                 load,
-                x=(x_in.at[j], lambda f, q: halo_columns(merged1.at[f][chunk(q)], j)),
+                x=(x_in.at[j], lambda f, q: halos[f][8 * q : 8 * q + 8]),
                 y=y_new.at[new_at[j]],
-                z=(level_in.at[j], neighbours),
+                z=(level_in.at[j], rolled_levels(lambda f: c1_new[f, new_at[j]])),
             )
         else:
             i = (2, 3, R - 4, R - 3).index(j)
@@ -548,7 +540,7 @@
     x_in, c1, part1, c2, part2, edge = call(
         interior,
         [vmem()] * 8,
-        [(R, 9) + row, (4,) + padded, (4, 4) + row, (4, R - 8) + row, (4, 4) + row, (2, 4) + row],
+        [(R, 9) + row, (4, R - 4) + row, (4, 4) + row, (4, R - 8) + row, (4, 4) + row, (2, 4) + row],
         [pltpu.VMEM((4,) + row, F32)],
         cost=10_000_000,
     )(rows, raw, left, right, merged, y_in, level, base)
@@ -563,7 +555,7 @@
             pltpu.VMEM((8, 9) + row, F32),
             pltpu.VMEM((8, 9) + row, F32),
             pltpu.VMEM((8, 3) + row, F32),
-            pltpu.VMEM((4, (K + 2) * 8, W), F32),
+            pltpu.VMEM((4, 8) + row, F32),
             pltpu.VMEM((4,) + row, F32),
             pltpu.VMEM((2, FIELDS) + row, F32),
         ],

time: 45.9 us -> 27.1 us (0.59)
  Pallas kernels: 32.6 us -> 13.8 us
    pallas_call x1, Pallas kernels: 22 us -> 6.12 us  [local(): call(interior, [vmem()] * 8, [(R, 9) + row, (4, R - 4) + row, (4, 4) + ro...]
    pallas_call x1, Pallas kernels: 6.49 us -> 3.61 us  [local(): call(boundary, [vmem()] * 16, [(K * R, W)] * 4, [pltpu.VMEM((2, SIDE_BLOC...]
  transfers between devices with their start and end apart: 6 -> 6, of which waited for: 2 -> 2; matrix products, arithmetic and copies ran while one was open for 0% -> 0% of each run, Pallas kernels for 52% -> 30%
where the time goes in v6:
time: 27.1 us; the launch traced here: 26.9 us
  Pallas kernels  13.8 us (51%)
  starting transfers between devices  9.98 us (37%)
  waiting for transfers between devices  2.39 us (9%)
  between operations  0.7 us (3%)
    pallas_call x1, Pallas kernels, local(): call(interior, [vmem()] * 8, [(R, 9) + row, (4, R - 4) + row, (4, 4) + ro...  6.12 us
    ppermute x4, starting transfers between devices, swap(): return lax.ppermute(message, ('ew', 'ns'), partners(odd, n_ew, n_ns))  5.24 us
    pallas_call x1, Pallas kernels, local(): call(boundary, [vmem()] * 16, [(K * R, W)] * 4, [pltpu.VMEM((2, SIDE_BLOC...  3.61 us
    ppermute x1, starting transfers between devices, local(): lax.ppermute(to_west, 'ew', [((i + 1) % n_ew, i) for i in range(n_ew)])  3.25 us
    pallas_call x1, Pallas kernels, local(): call(pack_edges, [pl.BlockSpec(memory_space=pltpu.HBM)] * FIELDS, [(FIELD...  2.12 us
    ppermute x1, waiting for transfers between devices, local(): lax.ppermute(to_east, 'ew', [(i, (i + 1) % n_ew) for i in range(n_ew)])  1.92 us
    pallas_call x1, Pallas kernels, local(): call(prepare, [vmem()] * 2, [(R - 4, 9) + row, (R, 3) + row, (4, R - 4) +...  1.65 us
    ppermute x1, starting transfers between devices, local(): lax.ppermute(to_east, 'ew', [(i, (i + 1) % n_ew) for i in range(n_ew)])  1.49 us
  transfers between devices with their start and end apart: 6, of which 2 were waited for; matrix products, arithmetic and copies ran while one was open for 0% of the time, Pallas kernels for 30%

profile of v6, /device:TPU:0, one launch (start us, length us, event | category | flops | bytes accessed | tf_op | source)
XLA Modules:
  0.0 26.9 jit_solution(12295523973438631656)
XLA Ops:
  0.6 2.1 %shard_map.102 = (f32[7,16,32,128]{3,2,1,0:T(8,128)S(1)}, f32[4,544,128]{2,1,0:T(8,128)S(1)}, f32[7,32,128]{2,1,0:T(8,128)S(1)}, f32[4,32,128]{2,1,0:T(8,128)S(1)}, f32[4,32,128]{2,1,0:T(8,128)S(1)}) custom-call(f32[512,128]{1,0:T(8,128)} %bitcast.11, f32[512,128]{1,0:T(8,128)} %bitcast.12, f32[512,128]{1,0:T(8,128)} %bitcast.13, f32[512,128]{1,0:T(8,128)} %bitcast.14, ...), custom_call_target="tpu_custom_call" | custom-call | bytes 1048576 | tf_op jit(solution)/shard_map/pallas_call | solution.py:503
  2.8 0.1 shard_map.106
  2.8 3.0 %collective-permute-start.2 = (f32[26,32,128]{2,1,0:T(8,128)S(1)}, f32[26,32,128]{2,1,0:T(8,128)S(1)}, u32[]{:S(2)}, u32[]{:S(2)}) collective-permute-start(f32[26,32,128]{2,1,0:T(8,128)S(1)} %get-tuple-element.46), channel_id=1, source_target_pairs={{0,4},{1,2},{2,1},{3,7},{4,0},{5,6},{6,5},{7,3},{8,12},{9,10},{10,... | collective-permute-start | bytes 1277960 | tf_op jit(solution)/shard_map/ppermute | solution.py:519
  5.8 0.1 collective-permute-start.4
  6.0 1.5 %collective-permute-start = (f32[4,32,128]{2,1,0:T(8,128)S(1)}, f32[4,32,128]{2,1,0:T(8,128)S(1)}, u32[]{:S(2)}, u32[]{:S(2)}) collective-permute-start(f32[4,32,128]{2,1,0:T(8,128)S(1)} %get-tuple-element.31), channel_id=1, source_target_pairs={{0,4},{4,8},{8,12},{12,16},{16,20},{20,24},{24,28},{28,0},{1,5},{5... | collective-permute-start | bytes 196616 | tf_op jit(solution)/shard_map/ppermute | solution.py:515
  7.5 3.2 %collective-permute-start.1 = (f32[4,32,128]{2,1,0:T(8,128)S(1)}, f32[4,32,128]{2,1,0:T(8,128)S(1)}, u32[]{:S(2)}, u32[]{:S(2)}) collective-permute-start(f32[4,32,128]{2,1,0:T(8,128)S(1)} %get-tuple-element.32), channel_id=1, source_target_pairs={{4,0},{8,4},{12,8},{16,12},{20,16},{24,20},{28,24},{0,28},{5,1},{9... | collective-permute-start | bytes 196616 | tf_op jit(solution)/shard_map/ppermute | solution.py:516
  10.7 1.6 %shard_map.103 = (f32[12,9,32,128]{3,2,1,0:T(8,128)S(1)}, f32[16,3,32,128]{3,2,1,0:T(8,128)S(1)}, f32[4,12,32,128]{3,2,1,0:T(8,128)S(1)}) custom-call(f32[7,16,32,128]{3,2,1,0:T(8,128)S(1)} %get-tuple-element.29.rows.refs_0_, f32[4,544,128]{2,1,0:T(8,128)S(1)} %get-tuple-element.33.raw.refs_1_), custom_call_target="tpu_custom_call" | custom-call | flops 10000000 | bytes 1048576 | tf_op jit(solution)/shard_map/pallas_call | solution.py:525
  12.4 1.9 %collective-permute-done.from_west = f32[4,32,128]{2,1,0:T(8,128)S(1)} collective-permute-done((f32[4,32,128]{2,1,0:T(8,128)S(1)}, f32[4,32,128]{2,1,0:T(8,128)S(1)}, u32[]{:S(2)}, u32[]{:S(2)}) %collective-permute-start) | collective-permute-done | bytes 65568 | tf_op jit(solution)/shard_map/ppermute | solution.py:515
  14.3 0.5 %collective-permute-done.1.from_east = f32[4,32,128]{2,1,0:T(8,128)S(1)} collective-permute-done((f32[4,32,128]{2,1,0:T(8,128)S(1)}, f32[4,32,128]{2,1,0:T(8,128)S(1)}, u32[]{:S(2)}, u32[]{:S(2)}) %collective-permute-start.1) | collective-permute-done | bytes 65568 | tf_op jit(solution)/shard_map/ppermute | solution.py:516
  14.8 0.2 shard_map.104
  15.0 2.1 %collective-permute-start.3 = (f32[2,32,128]{2,1,0:T(8,128)S(1)}, f32[2,32,128]{2,1,0:T(8,128)S(1)}, u32[]{:S(2)}, u32[]{:S(2)}) collective-permute-start(f32[2,32,128]{2,1,0:T(8,128)S(1)} %get-tuple-element.47), channel_id=1, source_target_pairs={{0,4},{1,2},{2,1},{3,7},{4,0},{5,6},{6,5},{7,3},{8,12},{9,10},{10,... | collective-permute-start | bytes 98312 | tf_op jit(solution)/shard_map/ppermute | solution.py:519
  17.1 0.0 collective-permute-start.5
  17.1 6.1 %shard_map.105 = (f32[16,9,32,128]{3,2,1,0:T(8,128)S(1)}, f32[4,12,32,128]{3,2,1,0:T(8,128)S(1)}, f32[4,4,32,128]{3,2,1,0:T(8,128)S(1)}, f32[4,8,32,128]{3,2,1,0...) custom-call(f32[7,16,32,128]{3,2,1,0:T(8,128)S(1)} %get-tuple-element.29.rows.refs_0_, ...), custom_call_target="tpu_custom_call" | custom-call | flops 10000000 | bytes 1048576 | tf_op jit(solution)/shard_map/pallas_call | solution.py:540
  23.2 0.0 collective-permute-done.3.refs_13_
  23.2 0.0 collective-permute-done.5.refs_15_
  23.2 0.0 collective-permute-done.2.refs_12_
  23.2 0.0 collective-permute-done.4.refs_14_
  23.3 3.6 %shard_map.107 = (f32[512,128]{1,0:T(8,128)}, f32[512,128]{1,0:T(8,128)}, f32[512,128]{1,0:T(8,128)}, f32[512,128]{1,0:T(8,128)}) custom-call(f32[7,16,32,128]{3,2,1,0:T(8,128)S(1)} %get-tuple-element.29.rows.refs_0_, f32[7,32,128]{2,1,0:T(8,128)S(1)} %get-tuple-element.35.refs_2_.refs_1_, f32[7,32,128]{2,1,0:T(8,128)S(1)} %get-tuple-element.36.refs_3_.refs_2_, ...), custom_call_target="tpu_custom_call" | custom-call | flops 10000000 | bytes 1048576 | tf_op jit(solution)/shard_map/pallas_call | solution.py:548
Async XLA Ops:
  2.8 20.4 %collective-permute-start.2 = (f32[26,32,128]{2,1,0:T(8,128)S(1)}, f32[26,32,128]{2,1,0:T(8,128)S(1)}, u32[]{:S(2)}, u32[]{:S(2)}) collective-permute-start(f32[26,32,128]{2,1,0:T(8,128)S(1)} %get-tuple-element.46), channel_id=1, source_target_pairs={{0,4},{1,2},{2,1},{3,7},{4,0},{5,6},{6,5},{7,3},{8,12},{9,10},{10,... | collective-permute-start | bytes 1277960 | tf_op jit(solution)/shard_map/ppermute | solution.py:519
  5.8 17.4 %collective-permute-start.4 = (f32[26,32,128]{2,1,0:T(8,128)S(1)}, f32[26,32,128]{2,1,0:T(8,128)S(1)}, u32[]{:S(2)}, u32[]{:S(2)}) collective-permute-start(f32[26,32,128]{2,1,0:T(8,128)S(1)} %get-tuple-element.48), channel_id=1, source_target_pairs={{0,1},{1,0},{2,3},{3,2},{4,5},{5,4},{6,7},{7,6},{8,9},{9,8},{10,11... | collective-permute-start | bytes 1277960 | tf_op jit(solution)/shard_map/ppermute | solution.py:519
  6.0 8.3 %collective-permute-start = (f32[4,32,128]{2,1,0:T(8,128)S(1)}, f32[4,32,128]{2,1,0:T(8,128)S(1)}, u32[]{:S(2)}, u32[]{:S(2)}) collective-permute-start(f32[4,32,128]{2,1,0:T(8,128)S(1)} %get-tuple-element.31), channel_id=1, source_target_pairs={{0,4},{4,8},{8,12},{12,16},{16,20},{20,24},{24,28},{28,0},{1,5},{5... | collective-permute-start | bytes 196616 | tf_op jit(solution)/shard_map/ppermute | solution.py:515
  7.5 7.3 %collective-permute-start.1 = (f32[4,32,128]{2,1,0:T(8,128)S(1)}, f32[4,32,128]{2,1,0:T(8,128)S(1)}, u32[]{:S(2)}, u32[]{:S(2)}) collective-permute-start(f32[4,32,128]{2,1,0:T(8,128)S(1)} %get-tuple-element.32), channel_id=1, source_target_pairs={{4,0},{8,4},{12,8},{16,12},{20,16},{24,20},{28,24},{0,28},{5,1},{9... | collective-permute-start | bytes 196616 | tf_op jit(solution)/shard_map/ppermute | solution.py:516
  15.0 8.2 %collective-permute-start.3 = (f32[2,32,128]{2,1,0:T(8,128)S(1)}, f32[2,32,128]{2,1,0:T(8,128)S(1)}, u32[]{:S(2)}, u32[]{:S(2)}) collective-permute-start(f32[2,32,128]{2,1,0:T(8,128)S(1)} %get-tuple-element.47), channel_id=1, source_target_pairs={{0,4},{1,2},{2,1},{3,7},{4,0},{5,6},{6,5},{7,3},{8,12},{9,10},{10,... | collective-permute-start | bytes 98312 | tf_op jit(solution)/shard_map/ppermute | solution.py:519
  17.1 6.1 %collective-permute-start.5 = (f32[2,32,128]{2,1,0:T(8,128)S(1)}, f32[2,32,128]{2,1,0:T(8,128)S(1)}, u32[]{:S(2)}, u32[]{:S(2)}) collective-permute-start(f32[2,32,128]{2,1,0:T(8,128)S(1)} %get-tuple-element.49), channel_id=1, source_target_pairs={{0,1},{1,0},{2,3},{3,2},{4,5},{5,4},{6,7},{7,6},{8,9},{9,8},{10,11... | collective-permute-start | bytes 98312 | tf_op jit(solution)/shard_map/ppermute | solution.py:519

commit v7 on v6

--- a/solution.py
+++ b/solution.py
@@ -61,16 +61,6 @@
         a, b = packed[2 * p], packed[2 * p + 1]
         to_east[p] = jnp.where(west_half, a, turn(b, HALO))
         to_west[p] = jnp.where(west_half, turn(b, -HALO), a)
-
-
-def pack_sides(rows, first, second):
-    odd = lax.axis_index("ns") % 2
-    for out, north in ((first, 1 - odd), (second, odd)):
-        for f in range(FIELDS):
-            count = 2 if f == U else HALO
-            start = (R - count) * north
-            for r in range(count):
-                out[ROWS_AT[f] + r] = rows[f, start + r]
 
 
 def pack_corners(own, from_west, from_east, _, left, right, merged, first, second):
@@ -241,7 +231,19 @@
     return lambda f, q: (after[f][8 * q : 8 * q + 8], before[f][8 * q : 8 * q + 8])
 
 
-def prepare(rows, raw, y_out, level_out, base_out):
+def pack_sides(rows, first, second):
+    odd = lax.axis_index("ns") % 2
+    for out, north in ((first, 1 - odd), (second, odd)):
+        for f in range(FIELDS):
+            count = 2 if f == U else HALO
+            start = (R - count) * north
+            for r in range(count):
+                out[ROWS_AT[f] + r] = rows[f, start + r]
+
+
+def prepare(rows, raw, y_out, level_out, base_out, first_out, second_out):
+    pack_sides(rows, first_out, second_out)
+
     def levels(j):
         for k, value in enumerate(level_coefficients(rows[M, j])):
             level_out[j, k] = value
@@ -281,7 +283,8 @@
         for k in range(9):
             x_out[j, k] = got[k]
 
-    by_fours(0, R, x_body)
+    for j in range(R):
+        x_body(j)
 
     both = []
     for side, edges in enumerate((left, right)):
@@ -308,7 +311,8 @@
             base=lambda f, q: base_in.at[f, j - 2][chunk(q)],
         )
 
-    by_fours(2, R - 2, first)
+    for j in range(2, R - 2):
+        first(j)
 
     for i, j in enumerate((0, 1, R - 2, R - 1)):
         def store(f, q, value):
@@ -333,7 +337,8 @@
             z=(level_in.at[j], rolled_levels(lambda f: c1_out[f, j - 2])),
         )
 
-    by_fours(4, R - 4, second)
+    for j in range(4, R - 4):
+        second(j)
 
     for i, j in enumerate((2, 3, R - 4, R - 3)):
         def store(f, q, value):
@@ -518,16 +523,14 @@
     def swap(odd, message):
         return lax.ppermute(message, ("ew", "ns"), partners(odd, n_ew, n_ns))
 
-    first, second = call(pack_sides, [vmem()], [(SIDE_BLOCKS,) + row] * 2)(rows)
+    y_in, level, base, first, second = call(
+        prepare,
+        [vmem()] * 2,
+        [(R - 4, 9) + row, (R, 3) + row, (4, R - 4) + row] + [(SIDE_BLOCKS,) + row] * 2,
+        cost=10_000_000,
+    )(rows, raw)
     second = swap(1, second)
     first = swap(0, first)
-
-    y_in, level, base = call(
-        prepare,
-        [vmem()] * 2,
-        [(R - 4, 9) + row, (R, 3) + row, (4, R - 4) + row],
-        cost=10_000_000,
-    )(rows, raw)
 
     left, right, merged, first_corners, second_corners = call(
         pack_corners,

time: 27.1 us -> 28.5 us (1.052)
  waiting for transfers between devices: 2.39 us -> 4.04 us
    ppermute x1, waiting for transfers between devices: 1.92 us -> 3.57 us  [local(): lax.ppermute(to_east, 'ew', [(i, (i + 1) % n_ew) for i in range(n_ew)])]
  transfers between devices with their start and end apart: 6 -> 6, of which waited for: 2 -> 2; matrix products, arithmetic and copies ran while one was open for 0% -> 0% of each run, Pallas kernels for 30% -> 22%
where the time goes in v7:
time: 28.5 us; the launch traced here: 28.3 us
  Pallas kernels  13.6 us (48%)
  starting transfers between devices  9.98 us (35%)
  waiting for transfers between devices  4.04 us (14%)
  between operations  0.7 us (2%)
    pallas_call x1, Pallas kernels, local(): call(interior, [vmem()] * 8, [(R, 9) + row, (4, R - 4) + row, (4, 4) + ro...  5.92 us
    ppermute x4, starting transfers between devices, swap(): return lax.ppermute(message, ('ew', 'ns'), partners(odd, n_ew, n_ns))  5.24 us
    pallas_call x1, Pallas kernels, local(): call(boundary, [vmem()] * 16, [(K * R, W)] * 4, [pltpu.VMEM((2, SIDE_BLOC...  3.61 us
    ppermute x1, waiting for transfers between devices, local(): lax.ppermute(to_east, 'ew', [(i, (i + 1) % n_ew) for i in range(n_ew)])  3.57 us
    ppermute x1, starting transfers between devices, local(): lax.ppermute(to_west, 'ew', [((i + 1) % n_ew, i) for i in range(n_ew)])  3.25 us
    pallas_call x1, Pallas kernels, local(): call(pack_edges, [pl.BlockSpec(memory_space=pltpu.HBM)] * FIELDS, [(FIELD...  2.12 us
    pallas_call x1, Pallas kernels, local(): call(prepare, [vmem()] * 2, [(R - 4, 9) + row, (R, 3) + row, (4, R - 4) +...  1.72 us
    ppermute x1, starting transfers between devices, local(): lax.ppermute(to_east, 'ew', [(i, (i + 1) % n_ew) for i in range(n_ew)])  1.49 us
  transfers between devices with their start and end apart: 6, of which 2 were waited for; matrix products, arithmetic and copies ran while one was open for 0% of the time, Pallas kernels for 22%

profile of v7, /device:TPU:0, one launch (start us, length us, event | category | flops | bytes accessed | tf_op | source)
XLA Modules:
  0.0 28.3 jit_solution(16500364899828718160)
XLA Ops:
  0.6 2.1 %shard_map.102 = (f32[7,16,32,128]{3,2,1,0:T(8,128)S(1)}, f32[4,544,128]{2,1,0:T(8,128)S(1)}, f32[7,32,128]{2,1,0:T(8,128)S(1)}, f32[4,32,128]{2,1,0:T(8,128)S(1)}, f32[4,32,128]{2,1,0:T(8,128)S(1)}) custom-call(f32[512,128]{1,0:T(8,128)} %bitcast.11, f32[512,128]{1,0:T(8,128)} %bitcast.12, f32[512,128]{1,0:T(8,128)} %bitcast.13, f32[512,128]{1,0:T(8,128)} %bitcast.14, ...), custom_call_target="tpu_custom_call" | custom-call | bytes 1048576 | tf_op jit(solution)/shard_map/pallas_call | solution.py:508
  2.8 1.7 %shard_map.103 = (f32[12,9,32,128]{3,2,1,0:T(8,128)S(1)}, f32[16,3,32,128]{3,2,1,0:T(8,128)S(1)}, f32[4,12,32,128]{3,2,1,0:T(8,128)S(1)}, f32[26,32,128]{2,1,0:T(8,128)S(1)}, f32[26,32,128]{2,1,0:T(8,128)S(1)}) custom-call(f32[7,16,32,128]{3,2,1,0:T(8,128)S(1)} %get-tuple-element.29.rows.refs_0_, f32[4,544,128]{2,1,0:T(8,128)S(1)} %get-tuple-element.33.raw.refs_1_), custom_call_target="tpu_custom_call" | custom-call | flops 10000000 | bytes 1048576 | tf_op jit(solution)/shard_map/pallas_call | solution.py:526
  4.5 3.0 %collective-permute-start.2 = (f32[26,32,128]{2,1,0:T(8,128)S(1)}, f32[26,32,128]{2,1,0:T(8,128)S(1)}, u32[]{:S(2)}, u32[]{:S(2)}) collective-permute-start(f32[26,32,128]{2,1,0:T(8,128)S(1)} %get-tuple-element.46), channel_id=1, source_target_pairs={{0,4},{1,2},{2,1},{3,7},{4,0},{5,6},{6,5},{7,3},{8,12},{9,10},{10,... | collective-permute-start | bytes 1277960 | tf_op jit(solution)/shard_map/ppermute | solution.py:524
  7.5 0.1 collective-permute-start.4
  7.6 1.5 %collective-permute-start = (f32[4,32,128]{2,1,0:T(8,128)S(1)}, f32[4,32,128]{2,1,0:T(8,128)S(1)}, u32[]{:S(2)}, u32[]{:S(2)}) collective-permute-start(f32[4,32,128]{2,1,0:T(8,128)S(1)} %get-tuple-element.31), channel_id=1, source_target_pairs={{0,4},{4,8},{8,12},{12,16},{16,20},{20,24},{24,28},{28,0},{1,5},{5... | collective-permute-start | bytes 196616 | tf_op jit(solution)/shard_map/ppermute | solution.py:520
  9.1 3.2 %collective-permute-start.1 = (f32[4,32,128]{2,1,0:T(8,128)S(1)}, f32[4,32,128]{2,1,0:T(8,128)S(1)}, u32[]{:S(2)}, u32[]{:S(2)}) collective-permute-start(f32[4,32,128]{2,1,0:T(8,128)S(1)} %get-tuple-element.32), channel_id=1, source_target_pairs={{4,0},{8,4},{12,8},{16,12},{20,16},{24,20},{28,24},{0,28},{5,1},{9... | collective-permute-start | bytes 196616 | tf_op jit(solution)/shard_map/ppermute | solution.py:521
  12.4 3.6 %collective-permute-done.from_west = f32[4,32,128]{2,1,0:T(8,128)S(1)} collective-permute-done((f32[4,32,128]{2,1,0:T(8,128)S(1)}, f32[4,32,128]{2,1,0:T(8,128)S(1)}, u32[]{:S(2)}, u32[]{:S(2)}) %collective-permute-start) | collective-permute-done | bytes 65568 | tf_op jit(solution)/shard_map/ppermute | solution.py:520
  15.9 0.5 %collective-permute-done.1.from_east = f32[4,32,128]{2,1,0:T(8,128)S(1)} collective-permute-done((f32[4,32,128]{2,1,0:T(8,128)S(1)}, f32[4,32,128]{2,1,0:T(8,128)S(1)}, u32[]{:S(2)}, u32[]{:S(2)}) %collective-permute-start.1) | collective-permute-done | bytes 65568 | tf_op jit(solution)/shard_map/ppermute | solution.py:521
  16.4 0.2 shard_map.104
  16.6 2.1 %collective-permute-start.3 = (f32[2,32,128]{2,1,0:T(8,128)S(1)}, f32[2,32,128]{2,1,0:T(8,128)S(1)}, u32[]{:S(2)}, u32[]{:S(2)}) collective-permute-start(f32[2,32,128]{2,1,0:T(8,128)S(1)} %get-tuple-element.47), channel_id=1, source_target_pairs={{0,4},{1,2},{2,1},{3,7},{4,0},{5,6},{6,5},{7,3},{8,12},{9,10},{10,... | collective-permute-start | bytes 98312 | tf_op jit(solution)/shard_map/ppermute | solution.py:524
  18.7 0.0 collective-permute-start.5
  18.7 5.9 %shard_map.105 = (f32[16,9,32,128]{3,2,1,0:T(8,128)S(1)}, f32[4,12,32,128]{3,2,1,0:T(8,128)S(1)}, f32[4,4,32,128]{3,2,1,0:T(8,128)S(1)}, f32[4,8,32,128]{3,2,1,0...) custom-call(f32[7,16,32,128]{3,2,1,0:T(8,128)S(1)} %get-tuple-element.29.rows.refs_0_, ...), custom_call_target="tpu_custom_call" | custom-call | flops 10000000 | bytes 1048576 | tf_op jit(solution)/shard_map/pallas_call | solution.py:543
  24.7 0.0 collective-permute-done.3.refs_13_
  24.7 0.0 collective-permute-done.5.refs_15_
  24.7 0.0 collective-permute-done.2.refs_12_
  24.7 0.0 collective-permute-done.4.refs_14_
  24.7 3.6 %shard_map.106 = (f32[512,128]{1,0:T(8,128)}, f32[512,128]{1,0:T(8,128)}, f32[512,128]{1,0:T(8,128)}, f32[512,128]{1,0:T(8,128)}) custom-call(f32[7,16,32,128]{3,2,1,0:T(8,128)S(1)} %get-tuple-element.29.rows.refs_0_, f32[7,32,128]{2,1,0:T(8,128)S(1)} %get-tuple-element.35.refs_2_.refs_1_, f32[7,32,128]{2,1,0:T(8,128)S(1)} %get-tuple-element.36.refs_3_.refs_2_, ...), custom_call_target="tpu_custom_call" | custom-call | flops 10000000 | bytes 1048576 | tf_op jit(solution)/shard_map/pallas_call | solution.py:551
Async XLA Ops:
  4.5 20.2 %collective-permute-start.2 = (f32[26,32,128]{2,1,0:T(8,128)S(1)}, f32[26,32,128]{2,1,0:T(8,128)S(1)}, u32[]{:S(2)}, u32[]{:S(2)}) collective-permute-start(f32[26,32,128]{2,1,0:T(8,128)S(1)} %get-tuple-element.46), channel_id=1, source_target_pairs={{0,4},{1,2},{2,1},{3,7},{4,0},{5,6},{6,5},{7,3},{8,12},{9,10},{10,... | collective-permute-start | bytes 1277960 | tf_op jit(solution)/shard_map/ppermute | solution.py:524
  7.5 17.2 %collective-permute-start.4 = (f32[26,32,128]{2,1,0:T(8,128)S(1)}, f32[26,32,128]{2,1,0:T(8,128)S(1)}, u32[]{:S(2)}, u32[]{:S(2)}) collective-permute-start(f32[26,32,128]{2,1,0:T(8,128)S(1)} %get-tuple-element.48), channel_id=1, source_target_pairs={{0,1},{1,0},{2,3},{3,2},{4,5},{5,4},{6,7},{7,6},{8,9},{9,8},{10,11... | collective-permute-start | bytes 1277960 | tf_op jit(solution)/shard_map/ppermute | solution.py:524
  7.6 8.3 %collective-permute-start = (f32[4,32,128]{2,1,0:T(8,128)S(1)}, f32[4,32,128]{2,1,0:T(8,128)S(1)}, u32[]{:S(2)}, u32[]{:S(2)}) collective-permute-start(f32[4,32,128]{2,1,0:T(8,128)S(1)} %get-tuple-element.31), channel_id=1, source_target_pairs={{0,4},{4,8},{8,12},{12,16},{16,20},{20,24},{24,28},{28,0},{1,5},{5... | collective-permute-start | bytes 196616 | tf_op jit(solution)/shard_map/ppermute | solution.py:520
  9.1 7.3 %collective-permute-start.1 = (f32[4,32,128]{2,1,0:T(8,128)S(1)}, f32[4,32,128]{2,1,0:T(8,128)S(1)}, u32[]{:S(2)}, u32[]{:S(2)}) collective-permute-start(f32[4,32,128]{2,1,0:T(8,128)S(1)} %get-tuple-element.32), channel_id=1, source_target_pairs={{4,0},{8,4},{12,8},{16,12},{20,16},{24,20},{28,24},{0,28},{5,1},{9... | collective-permute-start | bytes 196616 | tf_op jit(solution)/shard_map/ppermute | solution.py:521
  16.6 8.0 %collective-permute-start.3 = (f32[2,32,128]{2,1,0:T(8,128)S(1)}, f32[2,32,128]{2,1,0:T(8,128)S(1)}, u32[]{:S(2)}, u32[]{:S(2)}) collective-permute-start(f32[2,32,128]{2,1,0:T(8,128)S(1)} %get-tuple-element.47), channel_id=1, source_target_pairs={{0,4},{1,2},{2,1},{3,7},{4,0},{5,6},{6,5},{7,3},{8,12},{9,10},{10,... | collective-permute-start | bytes 98312 | tf_op jit(solution)/shard_map/ppermute | solution.py:524
  18.7 5.9 %collective-permute-start.5 = (f32[2,32,128]{2,1,0:T(8,128)S(1)}, f32[2,32,128]{2,1,0:T(8,128)S(1)}, u32[]{:S(2)}, u32[]{:S(2)}) collective-permute-start(f32[2,32,128]{2,1,0:T(8,128)S(1)} %get-tuple-element.49), channel_id=1, source_target_pairs={{0,1},{1,0},{2,3},{3,2},{4,5},{5,4},{6,7},{7,6},{8,9},{9,8},{10,11... | collective-permute-start | bytes 98312 | tf_op jit(solution)/shard_map/ppermute | solution.py:524

commit v8 on v6

--- a/solution.py
+++ b/solution.py
@@ -17,8 +17,9 @@
 FIELDS = 7
 U, V, M = 4, 5, 6
 PAIRS = 4
-SIDE_BLOCKS = 26
+SIDE_BLOCKS = 28
 ROWS_AT = (0, 4, 8, 12, 24, 16, 20)
+CORNERS_AT = 26
 SOUTH, NORTH = 0, 1
 MIB = 1 << 20
 
@@ -63,17 +64,7 @@
         to_west[p] = jnp.where(west_half, turn(b, -HALO), a)
 
 
-def pack_sides(rows, first, second):
-    odd = lax.axis_index("ns") % 2
-    for out, north in ((first, 1 - odd), (second, odd)):
-        for f in range(FIELDS):
-            count = 2 if f == U else HALO
-            start = (R - count) * north
-            for r in range(count):
-                out[ROWS_AT[f] + r] = rows[f, start + r]
-
-
-def pack_corners(own, from_west, from_east, _, left, right, merged, first, second):
+def pack_sides(rows, own, from_west, from_east, _, left, right, merged, second, first):
     odd = lax.axis_index("ns") % 2
     lane = lanes()
     west_half = lane % G < HALO
@@ -86,14 +77,19 @@
         left[f] = left_f
         right[f] = right_f
         merged[f] = jnp.where(west_half, left_f, right_f)
-    for out, north in ((first, 1 - odd), (second, odd)):
+    for out, north in ((second, odd), (first, 1 - odd)):
+        for f in range(FIELDS):
+            count = 2 if f == U else HALO
+            start = (R - count) * north
+            for r in range(count):
+                out[ROWS_AT[f] + r] = rows[f, start + r]
         for side, edges in enumerate((left, right)):
             block = jnp.zeros((K, W), F32)
             for f in range(FIELDS):
                 amount = lax.rem(2 * G * f + W - (W - 2 * G) * north, W)
                 moved = pltpu.roll(edges[f], amount, 1)
                 block = jnp.where(lane // (2 * G) == f, moved, block)
-            out[side] = block
+            out[CORNERS_AT + side] = block
 
 
 def coefficients(speed, mask):
@@ -349,9 +345,9 @@
 
 def boundary(*refs):
     rows, left, right, merged, y_in, level_in, x_in, c1_in, part1_in, c2_in, part2_in, edge_in = refs[:12]
-    messages = refs[12:16]
-    outs = refs[16:20]
-    sides, corners, x_new, y_new, level_new, c1_new, merged1, beyond = refs[20:]
+    second, first = refs[12:14]
+    outs = refs[14:18]
+    sides, x_new, y_new, level_new, c1_new, merged1, beyond = refs[18:]
     lane = lanes()
     west_half = lane % G < HALO
     place = lax.axis_index("ns")
@@ -360,14 +356,13 @@
     inside = {SOUTH: place > 0, NORTH: place < last}
     near = (-2, -1, 0, 1, R - 2, R - 1, R, R + 1)
     new_at = {j: i for i, j in enumerate(near)}
-    for source, target in ((0, sides), (1, corners)):
-        def unpack(b, carry):
-            for message, side in ((messages[source], odd), (messages[source + 2], 1 - odd)):
-                here = jnp.where(side == NORTH, place < last, place > 0)
-                target[side, b] = jnp.where(here, message[b], 0.0)
-            return carry
-
-        lax.fori_loop(0, target.shape[1], unpack, 0, unroll=2)
+    def unpack(b, carry):
+        for message, side in ((second, odd), (first, 1 - odd)):
+            here = jnp.where(side == NORTH, place < last, place > 0)
+            sides[side, b] = jnp.where(here, message[b], 0.0)
+        return carry
+
+    lax.fori_loop(0, SIDE_BLOCKS, unpack, 0, unroll=2)
 
     def row(f, j):
         if j < 0:
@@ -378,8 +373,8 @@
 
     for s in range(2):
         for f in range(FIELDS):
-            south = turn(corners[SOUTH, s], W - 2 * G - 2 * G * f)
-            north = turn(corners[NORTH, s], -2 * G * f)
+            south = turn(sides[SOUTH, CORNERS_AT + s], W - 2 * G - 2 * G * f)
+            north = turn(sides[NORTH, CORNERS_AT + s], -2 * G * f)
             beyond[s, f] = jnp.where(lane >= W // 2, south, north)
 
     both = []
@@ -470,7 +465,7 @@
     return pl.BlockSpec(memory_space=pltpu.VMEM)
 
 
-def call(kernel, in_specs, out_shapes, scratch=(), limit=16 * MIB, cost=0):
+def call(kernel, in_specs, out_shapes, scratch=(), limit=16 * MIB, cost=0.0):
     return pl.pallas_call(
         kernel,
         out_shape=[jax.ShapeDtypeStruct(shape, F32) for shape in out_shapes],
@@ -478,7 +473,7 @@
         out_specs=[vmem()] * len(out_shapes),
         scratch_shapes=list(scratch),
         compiler_params=pltpu.CompilerParams(vmem_limit_bytes=limit),
-        cost_estimate=pl.CostEstimate(flops=cost, bytes_accessed=MIB, transcendentals=0),
+        cost_estimate=pl.CostEstimate(flops=0, bytes_accessed=int(cost * MIB), transcendentals=0),
     )
 
 
@@ -518,40 +513,36 @@
     def swap(odd, message):
         return lax.ppermute(message, ("ew", "ns"), partners(odd, n_ew, n_ns))
 
-    first, second = call(pack_sides, [vmem()], [(SIDE_BLOCKS,) + row] * 2)(rows)
-    second = swap(1, second)
-    first = swap(0, first)
-
     y_in, level, base = call(
         prepare,
         [vmem()] * 2,
         [(R - 4, 9) + row, (R, 3) + row, (4, R - 4) + row],
-        cost=10_000_000,
+        cost=6,
     )(rows, raw)
 
-    left, right, merged, first_corners, second_corners = call(
-        pack_corners,
-        [vmem()] * 3 + [pl.BlockSpec(memory_space=pl.ANY)],
-        [(FIELDS,) + row] * 3 + [(2,) + row] * 2,
-    )(own, from_west, from_east, level)
-    second_corners = swap(1, second_corners)
-    first_corners = swap(0, first_corners)
+    left, right, merged, second, first = call(
+        pack_sides,
+        [vmem()] * 4 + [pl.BlockSpec(memory_space=pl.ANY)],
+        [(FIELDS,) + row] * 3 + [(SIDE_BLOCKS,) + row] * 2,
+        cost=1,
+    )(rows, own, from_west, from_east, level)
+    second = swap(1, second)
+    first = swap(0, first)
 
     x_in, c1, part1, c2, part2, edge = call(
         interior,
         [vmem()] * 8,
         [(R, 9) + row, (4, R - 4) + row, (4, 4) + row, (4, R - 8) + row, (4, 4) + row, (2, 4) + row],
         [pltpu.VMEM((4,) + row, F32)],
-        cost=10_000_000,
+        cost=20,
     )(rows, raw, left, right, merged, y_in, level, base)
 
     outs = call(
         boundary,
-        [vmem()] * 16,
+        [vmem()] * 14,
         [(K * R, W)] * 4,
         [
             pltpu.VMEM((2, SIDE_BLOCKS) + row, F32),
-            pltpu.VMEM((2, 2) + row, F32),
             pltpu.VMEM((8, 9) + row, F32),
             pltpu.VMEM((8, 9) + row, F32),
             pltpu.VMEM((8, 3) + row, F32),
@@ -559,10 +550,10 @@
             pltpu.VMEM((4,) + row, F32),
             pltpu.VMEM((2, FIELDS) + row, F32),
         ],
-        cost=10_000_000,
+        cost=20,
     )(
         *(rows, left, right, merged, y_in, level, x_in, c1, part1, c2, part2, edge),
-        *(second, second_corners, first, first_corners),
+        *(second, first),
     )
     return tuple(a.reshape(K, R, W) for a in outs)
 

time: 27.1 us -> 24 us (0.89)
  starting transfers between devices: 9.98 us -> 7.79 us
  waiting for transfers between devices: 2.39 us -> 1.63 us
    ppermute x4 -> x2, starting transfers between devices: 5.24 us -> 1.7 us  [swap(): return lax.ppermute(message, ('ew', 'ns'), partners(odd, n_ew, n_ns))]
    ppermute x1, starting transfers between devices: 1.49 us -> 2.99 us  [local(): lax.ppermute(to_east, 'ew', [(i, (i + 1) % n_ew) for i in range(n_ew)])]
    ppermute x1, waiting for transfers between devices: 1.92 us -> 0.58 us  [local(): lax.ppermute(to_east, 'ew', [(i, (i + 1) % n_ew) for i in range(n_ew)])]
    ppermute x4 -> x2, waiting for transfers between devices: 0.01 us -> 0.72 us  [swap(): return lax.ppermute(message, ('ew', 'ns'), partners(odd, n_ew, n_ns))]
    pallas_call x3 -> x2, Pallas kernels: 3.91 us -> 3.84 us  [the longest x1 3.61 us: local(): call(boundary, [vmem()] * 14, [(K * R, W)] * 4, [pltpu.VMEM((2, SIDE_BLOC...]
  transfers between devices with their start and end apart: 6 -> 4, of which waited for: 2 -> 3; matrix products, arithmetic and copies ran while one was open for 0% -> 0% of each run, Pallas kernels for 30% -> 33%
where the time goes in v8:
time: 24 us; the launch traced here: 23.8 us
  Pallas kernels  13.7 us (57%)
  starting transfers between devices  7.79 us (32%)
  waiting for transfers between devices  1.63 us (7%)
  between operations  0.66 us (3%)
    pallas_call x1, Pallas kernels, local(): call(interior, [vmem()] * 8, [(R, 9) + row, (4, R - 4) + row, (4, 4) + ro...  6.12 us
    pallas_call x1, Pallas kernels, local(): call(boundary, [vmem()] * 14, [(K * R, W)] * 4, [pltpu.VMEM((2, SIDE_BLOC...  3.61 us
    ppermute x1, starting transfers between devices, local(): lax.ppermute(to_west, 'ew', [((i + 1) % n_ew, i) for i in range(n_ew)])  3.1 us
    ppermute x1, starting transfers between devices, local(): lax.ppermute(to_east, 'ew', [(i, (i + 1) % n_ew) for i in range(n_ew)])  2.99 us
    pallas_call x1, Pallas kernels, local(): call(pack_edges, [pl.BlockSpec(memory_space=pltpu.HBM)] * FIELDS, [(FIELD...  2.12 us
    ppermute x2, starting transfers between devices, swap(): return lax.ppermute(message, ('ew', 'ns'), partners(odd, n_ew, n_ns))  1.7 us
    pallas_call x1, Pallas kernels, local(): call(prepare, [vmem()] * 2, [(R - 4, 9) + row, (R, 3) + row, (4, R - 4) +...  1.65 us
    ppermute x2, waiting for transfers between devices, swap(): return lax.ppermute(message, ('ew', 'ns'), partners(odd, n_ew, n_ns))  0.72 us
  transfers between devices with their start and end apart: 4, of which 3 were waited for; matrix products, arithmetic and copies ran while one was open for 0% of the time, Pallas kernels for 33%

profile of v8, /device:TPU:0, one launch (start us, length us, event | category | flops | bytes accessed | tf_op | source)
XLA Modules:
  0.0 23.8 jit_solution(10042265491733037969)
XLA Ops:
  0.6 2.1 %shard_map.102 = (f32[7,16,32,128]{3,2,1,0:T(8,128)S(1)}, f32[4,544,128]{2,1,0:T(8,128)S(1)}, f32[7,32,128]{2,1,0:T(8,128)S(1)}, f32[4,32,128]{2,1,0:T(8,128)S(1)}, f32[4,32,128]{2,1,0:T(8,128)S(1)}) custom-call(f32[512,128]{1,0:T(8,128)} %bitcast.11, f32[512,128]{1,0:T(8,128)} %bitcast.12, f32[512,128]{1,0:T(8,128)} %bitcast.13, f32[512,128]{1,0:T(8,128)} %bitcast.14, ...), custom_call_target="tpu_custom_call" | custom-call | tf_op jit(solution)/shard_map/pallas_call | solution.py:498
  2.8 3.0 %collective-permute-start = (f32[4,32,128]{2,1,0:T(8,128)S(1)}, f32[4,32,128]{2,1,0:T(8,128)S(1)}, u32[]{:S(2)}, u32[]{:S(2)}) collective-permute-start(f32[4,32,128]{2,1,0:T(8,128)S(1)} %get-tuple-element.29), channel_id=1, source_target_pairs={{0,4},{4,8},{8,12},{12,16},{16,20},{20,24},{24,28},{28,0},{1,5},{5... | collective-permute-start | bytes 196616 | tf_op jit(solution)/shard_map/ppermute | solution.py:510
  5.8 3.1 %collective-permute-start.1 = (f32[4,32,128]{2,1,0:T(8,128)S(1)}, f32[4,32,128]{2,1,0:T(8,128)S(1)}, u32[]{:S(2)}, u32[]{:S(2)}) collective-permute-start(f32[4,32,128]{2,1,0:T(8,128)S(1)} %get-tuple-element.30), channel_id=1, source_target_pairs={{4,0},{8,4},{12,8},{16,12},{20,16},{24,20},{28,24},{0,28},{5,1},{9... | collective-permute-start | bytes 196616 | tf_op jit(solution)/shard_map/ppermute | solution.py:511
  8.9 1.6 %shard_map.103 = (f32[12,9,32,128]{3,2,1,0:T(8,128)S(1)}, f32[16,3,32,128]{3,2,1,0:T(8,128)S(1)}, f32[4,12,32,128]{3,2,1,0:T(8,128)S(1)}) custom-call(f32[7,16,32,128]{3,2,1,0:T(8,128)S(1)} %get-tuple-element.27.rows.refs_0_, f32[4,544,128]{2,1,0:T(8,128)S(1)} %get-tuple-element.31.raw.refs_1_), custom_call_target="tpu_custom_call" | custom-call | bytes 6291456 | tf_op jit(solution)/shard_map/pallas_call | solution.py:516
  10.5 0.6 %collective-permute-done.from_west = f32[4,32,128]{2,1,0:T(8,128)S(1)} collective-permute-done((f32[4,32,128]{2,1,0:T(8,128)S(1)}, f32[4,32,128]{2,1,0:T(8,128)S(1)}, u32[]{:S(2)}, u32[]{:S(2)}) %collective-permute-start) | collective-permute-done | bytes 65568 | tf_op jit(solution)/shard_map/ppermute | solution.py:510
  11.1 0.3 %collective-permute-done.1.from_east = f32[4,32,128]{2,1,0:T(8,128)S(1)} collective-permute-done((f32[4,32,128]{2,1,0:T(8,128)S(1)}, f32[4,32,128]{2,1,0:T(8,128)S(1)}, u32[]{:S(2)}, u32[]{:S(2)}) %collective-permute-start.1) | collective-permute-done | bytes 65568 | tf_op jit(solution)/shard_map/ppermute | solution.py:511
  11.4 0.2 shard_map.104
  11.7 1.1 %collective-permute-start.2 = (f32[28,32,128]{2,1,0:T(8,128)S(1)}, f32[28,32,128]{2,1,0:T(8,128)S(1)}, u32[]{:S(2)}, u32[]{:S(2)}) collective-permute-start(f32[28,32,128]{2,1,0:T(8,128)S(1)} %get-tuple-element.44), channel_id=1, source_target_pairs={{0,4},{1,2},{2,1},{3,7},{4,0},{5,6},{6,5},{7,3},{8,12},{9,10},{10,... | collective-permute-start | bytes 1376264 | tf_op jit(solution)/shard_map/ppermute | solution.py:514
  12.8 0.6 %collective-permute-start.3 = (f32[28,32,128]{2,1,0:T(8,128)S(1)}, f32[28,32,128]{2,1,0:T(8,128)S(1)}, u32[]{:S(2)}, u32[]{:S(2)}) collective-permute-start(f32[28,32,128]{2,1,0:T(8,128)S(1)} %get-tuple-element.45), channel_id=1, source_target_pairs={{0,1},{1,0},{2,3},{3,2},{4,5},{5,4},{6,7},{7,6},{8,9},{9,8},{10,11... | collective-permute-start | bytes 1376264 | tf_op jit(solution)/shard_map/ppermute | solution.py:514
  13.4 6.1 %shard_map.105 = (f32[16,9,32,128]{3,2,1,0:T(8,128)S(1)}, f32[4,12,32,128]{3,2,1,0:T(8,128)S(1)}, f32[4,4,32,128]{3,2,1,0:T(8,128)S(1)}, f32[4,8,32,128]{3,2,1,0...) custom-call(f32[7,16,32,128]{3,2,1,0:T(8,128)S(1)} %get-tuple-element.27.rows.refs_0_, ...), custom_call_target="tpu_custom_call" | custom-call | bytes 20971520 | tf_op jit(solution)/shard_map/pallas_call | solution.py:532
  19.5 0.7 %collective-permute-done.2.refs_12_ = f32[28,32,128]{2,1,0:T(8,128)S(1)} collective-permute-done((f32[28,32,128]{2,1,0:T(8,128)S(1)}, f32[28,32,128]{2,1,0:T(8,128)S(1)}, u32[]{:S(2)}, u32[]{:S(2)}) %collective-permute-start.2) | collective-permute-done | bytes 458784 | tf_op jit(solution)/shard_map/ppermute | solution.py:514
  20.2 0.0 collective-permute-done.3.refs_13_
  20.2 3.6 %shard_map.106 = (f32[512,128]{1,0:T(8,128)}, f32[512,128]{1,0:T(8,128)}, f32[512,128]{1,0:T(8,128)}, f32[512,128]{1,0:T(8,128)}) custom-call(f32[7,16,32,128]{3,2,1,0:T(8,128)S(1)} %get-tuple-element.27.rows.refs_0_, f32[7,32,128]{2,1,0:T(8,128)S(1)} %get-tuple-element.33.refs_2_.refs_1_, f32[7,32,128]{2,1,0:T(8,128)S(1)} %get-tuple-element.34.refs_3_.refs_2_, ...), custom_call_target="tpu_custom_call" | custom-call | bytes 20971520 | tf_op jit(solution)/shard_map/pallas_call | solution.py:540
Async XLA Ops:
  2.8 8.3 %collective-permute-start = (f32[4,32,128]{2,1,0:T(8,128)S(1)}, f32[4,32,128]{2,1,0:T(8,128)S(1)}, u32[]{:S(2)}, u32[]{:S(2)}) collective-permute-start(f32[4,32,128]{2,1,0:T(8,128)S(1)} %get-tuple-element.29), channel_id=1, source_target_pairs={{0,4},{4,8},{8,12},{12,16},{16,20},{20,24},{24,28},{28,0},{1,5},{5... | collective-permute-start | bytes 196616 | tf_op jit(solution)/shard_map/ppermute | solution.py:510
  5.8 5.7 %collective-permute-start.1 = (f32[4,32,128]{2,1,0:T(8,128)S(1)}, f32[4,32,128]{2,1,0:T(8,128)S(1)}, u32[]{:S(2)}, u32[]{:S(2)}) collective-permute-start(f32[4,32,128]{2,1,0:T(8,128)S(1)} %get-tuple-element.30), channel_id=1, source_target_pairs={{4,0},{8,4},{12,8},{16,12},{20,16},{24,20},{28,24},{0,28},{5,1},{9... | collective-permute-start | bytes 196616 | tf_op jit(solution)/shard_map/ppermute | solution.py:511
  11.7 8.5 %collective-permute-start.2 = (f32[28,32,128]{2,1,0:T(8,128)S(1)}, f32[28,32,128]{2,1,0:T(8,128)S(1)}, u32[]{:S(2)}, u32[]{:S(2)}) collective-permute-start(f32[28,32,128]{2,1,0:T(8,128)S(1)} %get-tuple-element.44), channel_id=1, source_target_pairs={{0,4},{1,2},{2,1},{3,7},{4,0},{5,6},{6,5},{7,3},{8,12},{9,10},{10,... | collective-permute-start | bytes 1376264 | tf_op jit(solution)/shard_map/ppermute | solution.py:514
  12.8 7.4 %collective-permute-start.3 = (f32[28,32,128]{2,1,0:T(8,128)S(1)}, f32[28,32,128]{2,1,0:T(8,128)S(1)}, u32[]{:S(2)}, u32[]{:S(2)}) collective-permute-start(f32[28,32,128]{2,1,0:T(8,128)S(1)} %get-tuple-element.45), channel_id=1, source_target_pairs={{0,1},{1,0},{2,3},{3,2},{4,5},{5,4},{6,7},{7,6},{8,9},{9,8},{10,11... | collective-permute-start | bytes 1376264 | tf_op jit(solution)/shard_map/ppermute | solution.py:514

commit v9 on v8

--- a/solution.py
+++ b/solution.py
@@ -16,8 +16,9 @@
 HALO = 4
 FIELDS = 7
 U, V, M = 4, 5, 6
-PAIRS = 4
-SIDE_BLOCKS = 28
+PAIRS = ((0, 1), (2, 3), (U, M))
+EDGE_ROWS = len(PAIRS) * K + 8
+SIDE_BLOCKS = 27
 ROWS_AT = (0, 4, 8, 12, 24, 16, 20)
 CORNERS_AT = 26
 SOUTH, NORTH = 0, 1
@@ -57,44 +58,61 @@
         own[f] = edges
         packed.append(edges)
     west_half = lane % G < HALO
-    packed.append(jnp.zeros((K, W), F32))
-    for p in range(PAIRS):
-        a, b = packed[2 * p], packed[2 * p + 1]
-        to_east[p] = jnp.where(west_half, a, turn(b, HALO))
-        to_west[p] = jnp.where(west_half, turn(b, -HALO), a)
+    for p, (f, g) in enumerate(PAIRS):
+        a, b = packed[f], packed[g]
+        to_east[pl.ds(p * K, K)] = jnp.where(west_half, a, turn(b, HALO))
+        to_west[pl.ds(p * K, K)] = jnp.where(west_half, turn(b, -HALO), a)
+    part = lane[:8] % G // 2
+    for target, column in ((to_east, HALO - 2), (to_west, HALO)):
+        block = jnp.zeros((8, W), F32)
+        for q in range(K // 8):
+            moved = turn(packed[V][8 * q : 8 * q + 8], 2 * q - column)
+            block = jnp.where(part == q, moved, block)
+        target[pl.ds(len(PAIRS) * K, 8)] = block
 
 
 def pack_sides(rows, own, from_west, from_east, _, left, right, merged, second, first):
     odd = lax.axis_index("ns") % 2
     lane = lanes()
     west_half = lane % G < HALO
+    halos = {}
+    for p, (f, g) in enumerate(PAIRS):
+        a, b = from_west[pl.ds(p * K, K)], from_east[pl.ds(p * K, K)]
+        halos[f], halos[g] = (a, b), (turn(a, -HALO), turn(b, HALO))
+    a, b = from_west[pl.ds(len(PAIRS) * K, 8)], from_east[pl.ds(len(PAIRS) * K, 8)]
+    halos[V] = [
+        jnp.concatenate([turn(x, column - 2 * q) for q in range(K // 8)], axis=0)
+        for x, column in ((a, HALO - 2), (b, HALO))
+    ]
     for f in range(FIELDS):
-        a, b = from_west[f // 2], from_east[f // 2]
-        if f % 2:
-            a, b = turn(a, -HALO), turn(b, HALO)
-        left_f = jnp.where(west_half, a, own[f])
-        right_f = jnp.where(west_half, own[f], b)
-        left[f] = left_f
-        right[f] = right_f
-        merged[f] = jnp.where(west_half, left_f, right_f)
+        a, b = halos[f]
+        left[f] = jnp.where(west_half, a, own[f])
+        right[f] = jnp.where(west_half, own[f], b)
+        merged[f] = jnp.where(west_half, a, b)
     for out, north in ((second, odd), (first, 1 - odd)):
         for f in range(FIELDS):
             count = 2 if f == U else HALO
             start = (R - count) * north
             for r in range(count):
                 out[ROWS_AT[f] + r] = rows[f, start + r]
-        for side, edges in enumerate((left, right)):
-            block = jnp.zeros((K, W), F32)
-            for f in range(FIELDS):
-                amount = lax.rem(2 * G * f + W - (W - 2 * G) * north, W)
-                moved = pltpu.roll(edges[f], amount, 1)
-                block = jnp.where(lane // (2 * G) == f, moved, block)
-            out[CORNERS_AT + side] = block
+        block = jnp.zeros((K, W), F32)
+        for f in range(FIELDS):
+            amount = lax.rem(2 * G * f + W - (W - 2 * G) * north, W)
+            moved = pltpu.roll(merged[f], amount, 1)
+            block = jnp.where(lane // (2 * G) == f, moved, block)
+        out[CORNERS_AT] = block
 
 
 def coefficients(speed, mask):
     opened = {d: mask[d] * mask[d + 1] for d in (-2, -1, 0, 1)}
-    s = {d: speed[d] * opened[d] * (1.0 / 12.0) for d in opened}
+    return face_coefficients({d: scaled(speed[d], opened[d]) for d in opened}, opened)
+
+
+def scaled(speed, opened):
+    return speed * opened * (1.0 / 12.0)
+
+
+def face_coefficients(s, opened):
     a = {d: jnp.abs(s[d]) for d in s}
     w0 = {d: -(s[d] + a[d]) for d in (-1, 0, 1)}
     w3 = {d: a[d] - s[d] for d in (-2, -1, 0)}
@@ -175,11 +193,15 @@
     return pltpu.roll(merged, lax.rem(2 * W - HALO - G * j, W), 1)
 
 
-def edge_columns_and_levels(edges):
-    u, m = edges[U], edges[M]
-    xs = coefficients(
-        {d: turn(u, -d) for d in (-2, -1, 0, 1)},
-        {d: turn(m, -d) for d in (-2, -1, 0, 1, 2)},
+def edge_faces(edges):
+    opened = edges[M] * turn(edges[M], -1)
+    return scaled(edges[U], opened), opened
+
+
+def edge_columns_and_levels(edges, s, opened):
+    m = edges[M]
+    xs = face_coefficients(
+        {d: turn(s, -d) if d else s for d in (-2, -1, 0, 1)}, {-1: turn(opened, 1), 0: opened}
     )
     after, before, centre = level_coefficients(m)
     results = []
@@ -231,6 +253,22 @@
     return lambda f, q: (raw.at[f][strided(q, j, R, 1), :], raw.at[f][strided(q, j, R, -1), :])
 
 
+TALL = K + 16
+
+
+def moved_chunk(q, shift=0):
+    return pl.ds(8 + 8 * q + shift, 8)
+
+
+def clear_ends(ref):
+    ref[pl.ds(0, 8)] = jnp.zeros((8, W), F32)
+    ref[pl.ds(8 + K, 8)] = jnp.zeros((8, W), F32)
+
+
+def moved_levels(row):
+    return lambda f, q: (row(f)[moved_chunk(q, 1)], row(f)[moved_chunk(q, -1)])
+
+
 def rolled_levels(load):
     after = [pltpu.roll(load(f), K - 1, 0) for f in range(4)]
     before = [pltpu.roll(load(f), 1, 0) for f in range(4)]
@@ -267,12 +305,24 @@
 
 def interior(*refs):
     rows, raw, left, right, merged, y_in, level_in, base_in = refs[:8]
-    x_out, c1_out, part1_out, c2_out, part2_out, edge_out, merged1 = refs[8:]
+    x_out, c1_out, part1_out, c2_out, part2_out, edge_out, merged1, halo_s, halo_mixed = refs[8:]
     lane = lanes()
     west_half = lane % G < HALO
+    for f in range(4):
+        for r in range(R - 4):
+            clear_ends(c1_out.at[f, r])
+    faces = [edge_faces(edges) for edges in (left, right)]
+    halo_s[...] = jnp.where(west_half, faces[0][0], faces[1][0])
+    halo_mixed[...] = jnp.where(west_half, faces[0][1], right[M])
+
     def x_body(j):
-        got = x_coefficients(
-            rows[U, j], halo_columns(merged[U], j), rows[M, j], halo_columns(merged[M], j), lane
+        hs, hm = halo_columns(halo_s[...], j), halo_columns(halo_mixed[...], j)
+        m = rows[M, j]
+        opened = m * shifted(m, hm, 1, lane)
+        s = scaled(rows[U, j], opened)
+        got = face_coefficients(
+            {d: shifted(s, hs, d, lane) for d in (-2, -1, 0, 1)},
+            {-1: shifted(opened, hm, -1, lane), 0: opened},
         )
         for k in range(9):
             x_out[j, k] = got[k]
@@ -281,7 +331,7 @@
 
     both = []
     for side, edges in enumerate((left, right)):
-        partial = edge_columns_and_levels(edges)
+        partial = edge_columns_and_levels(edges, *faces[side])
         across = edge_rows(edges, lambda f: edges[f])
         for f in range(4):
             edge_out[side, f] = partial[f]
@@ -295,7 +345,7 @@
 
     def first(j):
         def store(f, q, value):
-            c1_out.at[f, j - 2][chunk(q)] = value
+            c1_out.at[f, j - 2][moved_chunk(q)] = value
 
         step_row(
             store,
@@ -323,10 +373,10 @@
 
         step_row(
             store,
-            lambda f, d, q: c1_out.at[f, j - 2 + d][chunk(q)],
+            lambda f, d, q: c1_out.at[f, j - 2 + d][moved_chunk(q)],
             x=(x_out.at[j], halo(merged1, j)),
             y=y_in.at[j - 2],
-            z=(level_in.at[j], rolled_levels(lambda f: c1_out[f, j - 2])),
+            z=(level_in.at[j], moved_levels(lambda f: c1_out.at[f, j - 2])),
         )
 
     by_fours(4, R - 4, second)
@@ -337,9 +387,9 @@
 
         step_row(
             store,
-            lambda f, d, q: c1_out.at[f, j - 2][chunk(q)],
+            lambda f, d, q: c1_out.at[f, j - 2][moved_chunk(q)],
             x=(x_out.at[j], halo(merged1, j)),
-            z=(level_in.at[j], rolled_levels(lambda f: c1_out[f, j - 2])),
+            z=(level_in.at[j], moved_levels(lambda f: c1_out.at[f, j - 2])),
         )
 
 
@@ -371,21 +421,23 @@
             return sides.at[NORTH, ROWS_AT[f] + j - R]
         return rows.at[f, j]
 
-    for s in range(2):
-        for f in range(FIELDS):
-            south = turn(sides[SOUTH, CORNERS_AT + s], W - 2 * G - 2 * G * f)
-            north = turn(sides[NORTH, CORNERS_AT + s], -2 * G * f)
-            beyond[s, f] = jnp.where(lane >= W // 2, south, north)
+    for f in range(FIELDS):
+        south = turn(sides[SOUTH, CORNERS_AT], W - 2 * G - 2 * G * f)
+        north = turn(sides[NORTH, CORNERS_AT], -2 * G * f)
+        beyond[f] = jnp.where(lane >= W // 2, south, north)
+    for f in range(4):
+        for i in range(2, 6):
+            clear_ends(c1_new.at[f, i])
 
     both = []
     for s, edges in enumerate((left, right)):
-        across = edge_rows(edges, lambda f: beyond[s, f])
+        across = edge_rows(edges, lambda f: beyond[f])
         both.append([edge_in[s, f] + a for f, a in enumerate(across)])
     for f in range(4):
         merged1[f] = jnp.where(west_half, both[0][f], both[1][f])
 
     def halo_beyond(f, j):
-        return halo_columns(jnp.where(west_half, beyond[0, f], beyond[1, f]), j % R)
+        return halo_columns(beyond[f], j % R)
 
     for j in near:
         got = y_coefficients_at(row, j)
@@ -406,7 +458,7 @@
         def store(f, q, value):
             if f >= 2 and not 0 <= j < R:
                 value = jnp.where(inside[side], value, 0.0)
-            c1_new.at[f, new_at[j]][chunk(q)] = value
+            c1_new.at[f, new_at[j]][moved_chunk(q)] = value
 
         def load(f, d, q):
             return row(f, j + d)[chunk(q)]
@@ -428,8 +480,8 @@
 
     def load1(f, j, q):
         if j in new_at:
-            return c1_new.at[f, new_at[j]][chunk(q)]
-        return c1_in.at[f, j - 2][chunk(q)]
+            return c1_new.at[f, new_at[j]][moved_chunk(q)]
+        return c1_in.at[f, j - 2][moved_chunk(q)]
 
     for j in (0, 1, 2, 3, R - 4, R - 3, R - 2, R - 1):
         def store(f, q, value):
@@ -445,7 +497,7 @@
                 load,
                 x=(x_in.at[j], lambda f, q: halos[f][8 * q : 8 * q + 8]),
                 y=y_new.at[new_at[j]],
-                z=(level_in.at[j], rolled_levels(lambda f: c1_new[f, new_at[j]])),
+                z=(level_in.at[j], moved_levels(lambda f: c1_new.at[f, new_at[j]])),
             )
         else:
             i = (2, 3, R - 4, R - 3).index(j)
@@ -498,7 +550,7 @@
     rows, raw, own, to_east, to_west = call(
         pack_edges,
         [pl.BlockSpec(memory_space=pltpu.HBM)] * FIELDS,
-        [(FIELDS, R) + row, (4,) + padded, (FIELDS,) + row, (PAIRS,) + row, (PAIRS,) + row],
+        [(FIELDS, R) + row, (4,) + padded, (FIELDS,) + row, (EDGE_ROWS, W), (EDGE_ROWS, W)],
         [
             pltpu.VMEM((2, K * R, W), F32),
             pltpu.VMEM((K * R, W), jnp.int32),
@@ -532,8 +584,8 @@
     x_in, c1, part1, c2, part2, edge = call(
         interior,
         [vmem()] * 8,
-        [(R, 9) + row, (4, R - 4) + row, (4, 4) + row, (4, R - 8) + row, (4, 4) + row, (2, 4) + row],
-        [pltpu.VMEM((4,) + row, F32)],
+        [(R, 9) + row, (4, R - 4, TALL, W), (4, 4) + row, (4, R - 8) + row, (4, 4) + row, (2, 4) + row],
+        [pltpu.VMEM((4,) + row, F32), pltpu.VMEM(row, F32), pltpu.VMEM(row, F32)],
         cost=20,
     )(rows, raw, left, right, merged, y_in, level, base)
 
@@ -546,9 +598,9 @@
             pltpu.VMEM((8, 9) + row, F32),
             pltpu.VMEM((8, 9) + row, F32),
             pltpu.VMEM((8, 3) + row, F32),
-            pltpu.VMEM((4, 8) + row, F32),
+            pltpu.VMEM((4, 8, TALL, W), F32),
             pltpu.VMEM((4,) + row, F32),
-            pltpu.VMEM((2, FIELDS) + row, F32),
+            pltpu.VMEM((FIELDS,) + row, F32),
         ],
         cost=20,
     )(

time: 24 us -> 23.3 us (0.971)
  waiting for transfers between devices: 1.63 us -> 1.12 us
    ppermute x1, waiting for transfers between devices: 0.33 us -> 0.07 us  [local(): lax.ppermute(to_west, 'ew', [((i + 1) % n_ew, i) for i in range(n_ew)])]
where the time goes in v9:
time: 23.3 us; the launch traced here: 23.1 us
  Pallas kernels  13.5 us (58%)
  starting transfers between devices  7.86 us (34%)
  waiting for transfers between devices  1.12 us (5%)
  between operations  0.67 us (3%)
    pallas_call x1, Pallas kernels, local(): call(interior, [vmem()] * 8, [(R, 9) + row, (4, R - 4, TALL, W), (4, 4) +...  6 us
    pallas_call x1, Pallas kernels, local(): call(boundary, [vmem()] * 14, [(K * R, W)] * 4, [pltpu.VMEM((2, SIDE_BLOC...  3.48 us
    ppermute x1, starting transfers between devices, local(): lax.ppermute(to_west, 'ew', [((i + 1) % n_ew, i) for i in range(n_ew)])  3.1 us
    ppermute x1, starting transfers between devices, local(): lax.ppermute(to_east, 'ew', [(i, (i + 1) % n_ew) for i in range(n_ew)])  2.99 us
    pallas_call x1, Pallas kernels, local(): call(pack_edges, [pl.BlockSpec(memory_space=pltpu.HBM)] * FIELDS, [(FIELD...  2.17 us
    ppermute x2, starting transfers between devices, swap(): return lax.ppermute(message, ('ew', 'ns'), partners(odd, n_ew, n_ns))  1.77 us
    pallas_call x1, Pallas kernels, local(): call(prepare, [vmem()] * 2, [(R - 4, 9) + row, (R, 3) + row, (4, R - 4) +...  1.65 us
    ppermute x2, waiting for transfers between devices, swap(): return lax.ppermute(message, ('ew', 'ns'), partners(odd, n_ew, n_ns))  0.6 us
  transfers between devices with their start and end apart: 4, of which 3 were waited for; matrix products, arithmetic and copies ran while one was open for 0% of the time, Pallas kernels for 33%

profile of v9, /device:TPU:0, one launch (start us, length us, event | category | flops | bytes accessed | tf_op | source)
XLA Modules:
  0.0 23.1 jit_solution(5791872283567636047)
XLA Ops:
  0.6 2.2 %shard_map.102 = (f32[7,16,32,128]{3,2,1,0:T(8,128)S(1)}, f32[4,544,128]{2,1,0:T(8,128)S(1)}, f32[7,32,128]{2,1,0:T(8,128)S(1)}, f32[104,128]{1,0:T(8,128)S(1)}, f32[104,128]{1,0:T(8,128)S(1)}) custom-call(f32[512,128]{1,0:T(8,128)} %bitcast.11, f32[512,128]{1,0:T(8,128)} %bitcast.12, f32[512,128]{1,0:T(8,128)} %bitcast.13, f32[512,128]{1,0:T(8,128)} %bitcast.14, ...), custom_call_target="tpu_custom_call" | custom-call | tf_op jit(solution)/shard_map/pallas_call | solution.py:550
  2.8 3.0 %collective-permute-start = (f32[104,128]{1,0:T(8,128)S(1)}, f32[104,128]{1,0:T(8,128)S(1)}, u32[]{:S(2)}, u32[]{:S(2)}) collective-permute-start(f32[104,128]{1,0:T(8,128)S(1)} %get-tuple-element.29), channel_id=1, source_target_pairs={{0,4},{4,8},{8,12},{12,16},{16,20},{20,24},{24,28},{28,0},{1,5},{5... | collective-permute-start | bytes 159752 | tf_op jit(solution)/shard_map/ppermute | solution.py:562
  5.8 3.1 %collective-permute-start.1 = (f32[104,128]{1,0:T(8,128)S(1)}, f32[104,128]{1,0:T(8,128)S(1)}, u32[]{:S(2)}, u32[]{:S(2)}) collective-permute-start(f32[104,128]{1,0:T(8,128)S(1)} %get-tuple-element.30), channel_id=1, source_target_pairs={{4,0},{8,4},{12,8},{16,12},{20,16},{24,20},{28,24},{0,28},{5,1},{9... | collective-permute-start | bytes 159752 | tf_op jit(solution)/shard_map/ppermute | solution.py:563
  8.9 1.6 %shard_map.103 = (f32[12,9,32,128]{3,2,1,0:T(8,128)S(1)}, f32[16,3,32,128]{3,2,1,0:T(8,128)S(1)}, f32[4,12,32,128]{3,2,1,0:T(8,128)S(1)}) custom-call(f32[7,16,32,128]{3,2,1,0:T(8,128)S(1)} %get-tuple-element.27.rows.refs_0_, f32[4,544,128]{2,1,0:T(8,128)S(1)} %get-tuple-element.31.raw.refs_1_), custom_call_target="tpu_custom_call" | custom-call | bytes 6291456 | tf_op jit(solution)/shard_map/pallas_call | solution.py:568
  10.6 0.5 %collective-permute-done.from_west = f32[104,128]{1,0:T(8,128)S(1)} collective-permute-done((f32[104,128]{1,0:T(8,128)S(1)}, f32[104,128]{1,0:T(8,128)S(1)}, u32[]{:S(2)}, u32[]{:S(2)}) %collective-permute-start) | collective-permute-done | bytes 53280 | tf_op jit(solution)/shard_map/ppermute | solution.py:562
  11.0 0.1 collective-permute-done.1.from_east
  11.1 0.2 shard_map.104
  11.3 1.4 %collective-permute-start.2 = (f32[27,32,128]{2,1,0:T(8,128)S(1)}, f32[27,32,128]{2,1,0:T(8,128)S(1)}, u32[]{:S(2)}, u32[]{:S(2)}) collective-permute-start(f32[27,32,128]{2,1,0:T(8,128)S(1)} %get-tuple-element.44), channel_id=1, source_target_pairs={{0,4},{1,2},{2,1},{3,7},{4,0},{5,6},{6,5},{7,3},{8,12},{9,10},{10,... | collective-permute-start | bytes 1327112 | tf_op jit(solution)/shard_map/ppermute | solution.py:566
  12.6 0.4 %collective-permute-start.3 = (f32[27,32,128]{2,1,0:T(8,128)S(1)}, f32[27,32,128]{2,1,0:T(8,128)S(1)}, u32[]{:S(2)}, u32[]{:S(2)}) collective-permute-start(f32[27,32,128]{2,1,0:T(8,128)S(1)} %get-tuple-element.45), channel_id=1, source_target_pairs={{0,1},{1,0},{2,3},{3,2},{4,5},{5,4},{6,7},{7,6},{8,9},{9,8},{10,11... | collective-permute-start | bytes 1327112 | tf_op jit(solution)/shard_map/ppermute | solution.py:566
  13.0 6.0 %shard_map.105 = (f32[16,9,32,128]{3,2,1,0:T(8,128)S(1)}, f32[4,12,48,128]{3,2,1,0:T(8,128)S(1)}, f32[4,4,32,128]{3,2,1,0:T(8,128)S(1)}, f32[4,8,32,128]{3,2,1,0...) custom-call(f32[7,16,32,128]{3,2,1,0:T(8,128)S(1)} %get-tuple-element.27.rows.refs_0_, ...), custom_call_target="tpu_custom_call" | custom-call | bytes 20971520 | tf_op jit(solution)/shard_map/pallas_call | solution.py:584
  19.0 0.6 %collective-permute-done.2.refs_12_ = f32[27,32,128]{2,1,0:T(8,128)S(1)} collective-permute-done((f32[27,32,128]{2,1,0:T(8,128)S(1)}, f32[27,32,128]{2,1,0:T(8,128)S(1)}, u32[]{:S(2)}, u32[]{:S(2)}) %collective-permute-start.2) | collective-permute-done | bytes 442400 | tf_op jit(solution)/shard_map/ppermute | solution.py:566
  19.6 0.0 collective-permute-done.3.refs_13_
  19.6 3.5 %shard_map.106 = (f32[512,128]{1,0:T(8,128)}, f32[512,128]{1,0:T(8,128)}, f32[512,128]{1,0:T(8,128)}, f32[512,128]{1,0:T(8,128)}) custom-call(f32[7,16,32,128]{3,2,1,0:T(8,128)S(1)} %get-tuple-element.27.rows.refs_0_, f32[7,32,128]{2,1,0:T(8,128)S(1)} %get-tuple-element.33.refs_2_.refs_1_, f32[7,32,128]{2,1,0:T(8,128)S(1)} %get-tuple-element.34.refs_3_.refs_2_, ...), custom_call_target="tpu_custom_call" | custom-call | bytes 20971520 | tf_op jit(solution)/shard_map/pallas_call | solution.py:592
Async XLA Ops:
  2.8 8.2 %collective-permute-start = (f32[104,128]{1,0:T(8,128)S(1)}, f32[104,128]{1,0:T(8,128)S(1)}, u32[]{:S(2)}, u32[]{:S(2)}) collective-permute-start(f32[104,128]{1,0:T(8,128)S(1)} %get-tuple-element.29), channel_id=1, source_target_pairs={{0,4},{4,8},{8,12},{12,16},{16,20},{20,24},{24,28},{28,0},{1,5},{5... | collective-permute-start | bytes 159752 | tf_op jit(solution)/shard_map/ppermute | solution.py:562
  5.8 5.3 %collective-permute-start.1 = (f32[104,128]{1,0:T(8,128)S(1)}, f32[104,128]{1,0:T(8,128)S(1)}, u32[]{:S(2)}, u32[]{:S(2)}) collective-permute-start(f32[104,128]{1,0:T(8,128)S(1)} %get-tuple-element.30), channel_id=1, source_target_pairs={{4,0},{8,4},{12,8},{16,12},{20,16},{24,20},{28,24},{0,28},{5,1},{9... | collective-permute-start | bytes 159752 | tf_op jit(solution)/shard_map/ppermute | solution.py:563
  11.3 8.4 %collective-permute-start.2 = (f32[27,32,128]{2,1,0:T(8,128)S(1)}, f32[27,32,128]{2,1,0:T(8,128)S(1)}, u32[]{:S(2)}, u32[]{:S(2)}) collective-permute-start(f32[27,32,128]{2,1,0:T(8,128)S(1)} %get-tuple-element.44), channel_id=1, source_target_pairs={{0,4},{1,2},{2,1},{3,7},{4,0},{5,6},{6,5},{7,3},{8,12},{9,10},{10,... | collective-permute-start | bytes 1327112 | tf_op jit(solution)/shard_map/ppermute | solution.py:566
  12.6 7.0 %collective-permute-start.3 = (f32[27,32,128]{2,1,0:T(8,128)S(1)}, f32[27,32,128]{2,1,0:T(8,128)S(1)}, u32[]{:S(2)}, u32[]{:S(2)}) collective-permute-start(f32[27,32,128]{2,1,0:T(8,128)S(1)} %get-tuple-element.45), channel_id=1, source_target_pairs={{0,1},{1,0},{2,3},{3,2},{4,5},{5,4},{6,7},{7,6},{8,9},{9,8},{10,11... | collective-permute-start | bytes 1327112 | tf_op jit(solution)/shard_map/ppermute | solution.py:566

commit v10 on v9

--- a/solution.py
+++ b/solution.py
@@ -155,7 +155,7 @@
     return pl.ds((8 * q + 1 + shift) * stride + j, 8, stride=stride)
 
 
-def step_row(store, load, x=None, y=None, z=None, base=None):
+def step_row(store, load, x=None, y=None, z=None, base=None, directions=(0, 1)):
     lane = lanes()[:8]
     results = []
     for q in range(K // 8):
@@ -166,7 +166,7 @@
                 centre = term[part] if centre is None else centre + term[part]
         if z:
             after, before = z[0].at[0][part], z[0].at[1][part]
-        for direction in (0, 1):
+        for direction in directions:
             ks = range(4 * direction, 4 * direction + 4)
             xs = [x[0].at[k][part] for k in ks] if x else []
             ys = [y.at[k][part] for k in ks] if y else []
@@ -215,9 +215,9 @@
     return results
 
 
-def edge_rows(edges, beyond):
+def edge_rows(merged, beyond):
     lane = lanes()
-    v, m = edges[V], edges[M]
+    v, m = merged[V], merged[M]
     vh, mh = beyond(V), beyond(M)
     ys = coefficients(
         {d: shifted(v, vh, d, lane, G) for d in (-2, -1, 0, 1)},
@@ -225,7 +225,7 @@
     )
     results = []
     for f in range(4):
-        c, ch = edges[f], beyond(f)
+        c, ch = merged[f], beyond(f)
         total = ys[8] * c
         for coefficient, d in zip(ys[4 * (f // 2) :], (-2, -1, 1, 2)):
             total += coefficient * shifted(c, ch, d, lane, G)
@@ -269,9 +269,9 @@
     return lambda f, q: (row(f)[moved_chunk(q, 1)], row(f)[moved_chunk(q, -1)])
 
 
-def rolled_levels(load):
-    after = [pltpu.roll(load(f), K - 1, 0) for f in range(4)]
-    before = [pltpu.roll(load(f), 1, 0) for f in range(4)]
+def rolled_levels(load, fields):
+    after = {f: pltpu.roll(load(f), K - 1, 0) for f in fields}
+    before = {f: pltpu.roll(load(f), 1, 0) for f in fields}
     return lambda f, q: (after[f][8 * q : 8 * q + 8], before[f][8 * q : 8 * q + 8])
 
 
@@ -329,15 +329,12 @@
 
     by_fours(0, R, x_body)
 
-    both = []
-    for side, edges in enumerate((left, right)):
-        partial = edge_columns_and_levels(edges, *faces[side])
-        across = edge_rows(edges, lambda f: edges[f])
-        for f in range(4):
-            edge_out[side, f] = partial[f]
-        both.append([p + a for p, a in zip(partial, across)])
+    partial = [edge_columns_and_levels(e, *f) for e, f in zip((left, right), faces)]
+    across = edge_rows(merged, lambda f: merged[f])
     for f in range(4):
-        merged1[f] = jnp.where(west_half, both[0][f], both[1][f])
+        edge = jnp.where(west_half, partial[0][f], partial[1][f])
+        edge_out[f] = edge
+        merged1[f] = edge + across[f]
 
     def halo(source, j):
         halos = [halo_columns(source[f], j) for f in range(4)]
@@ -394,12 +391,11 @@
 
 
 def boundary(*refs):
-    rows, left, right, merged, y_in, level_in, x_in, c1_in, part1_in, c2_in, part2_in, edge_in = refs[:12]
-    second, first = refs[12:14]
-    outs = refs[14:18]
-    sides, x_new, y_new, level_new, c1_new, merged1, beyond = refs[18:]
+    rows, merged, y_in, level_in, x_in, c1_in, part1_in, c2_in, part2_in, edge_in = refs[:10]
+    second, first = refs[10:12]
+    outs = refs[12:16]
+    sides, x_new, y_new, level_new, c1_new, merged1, beyond, final, left_by = refs[16:]
     lane = lanes()
-    west_half = lane % G < HALO
     place = lax.axis_index("ns")
     last = lax.axis_size("ns") - 1
     odd = place % 2
@@ -429,12 +425,8 @@
         for i in range(2, 6):
             clear_ends(c1_new.at[f, i])
 
-    both = []
-    for s, edges in enumerate((left, right)):
-        across = edge_rows(edges, lambda f: beyond[f])
-        both.append([edge_in[s, f] + a for f, a in enumerate(across)])
-    for f in range(4):
-        merged1[f] = jnp.where(west_half, both[0][f], both[1][f])
+    for f, across in enumerate(edge_rows(merged, lambda f: beyond[f])):
+        merged1[f] = edge_in[f] + across
 
     def halo_beyond(f, j):
         return halo_columns(beyond[f], j % R)
@@ -452,77 +444,91 @@
             for k, value in enumerate(level_coefficients(row(M, j)[...])):
                 level_new[new_at[j], k] = value
 
-    for j in near:
-        side = SOUTH if j < R // 2 else NORTH
-
-        def store(f, q, value):
-            if f >= 2 and not 0 <= j < R:
-                value = jnp.where(inside[side], value, 0.0)
-            c1_new.at[f, new_at[j]][moved_chunk(q)] = value
-
-        def load(f, d, q):
-            return row(f, j + d)[chunk(q)]
-
-        if 0 <= j < R:
-            i = (0, 1, R - 2, R - 1).index(j)
-            step_row(
-                store, load, y=y_new.at[new_at[j]], base=lambda f, q: part1_in.at[f, i][chunk(q)]
-            )
-        else:
-            halos = [halo_beyond(f, j) for f in range(4)]
-            step_row(
-                store,
-                load,
-                x=(x_new.at[new_at[j]], lambda f, q: halos[f][8 * q : 8 * q + 8]),
-                y=y_new.at[new_at[j]],
-                z=(level_new.at[new_at[j]], rolled_levels(lambda f: row(f, j)[...])),
-            )
-
     def load1(f, j, q):
         if j in new_at:
             return c1_new.at[f, new_at[j]][moved_chunk(q)]
         return c1_in.at[f, j - 2][moved_chunk(q)]
 
-    for j in (0, 1, 2, 3, R - 4, R - 3, R - 2, R - 1):
-        def store(f, q, value):
-            outs[f][pl.ds(8 * q * R + j, 8, stride=R), :] = value
-
-        def load(f, d, q):
-            return load1(f, j + d, q)
-
-        if j in new_at:
-            halos = [halo_columns(merged1[f], j) for f in range(4)]
-            step_row(
-                store,
-                load,
-                x=(x_in.at[j], lambda f, q: halos[f][8 * q : 8 * q + 8]),
-                y=y_new.at[new_at[j]],
-                z=(level_in.at[j], moved_levels(lambda f: c1_new.at[f, new_at[j]])),
-            )
-        else:
-            i = (2, 3, R - 4, R - 3).index(j)
-            step_row(
-                store, load, y=y_in.at[j - 2], base=lambda f, q: part2_in.at[f, i][chunk(q)]
-            )
-
     def copy(j, carry):
         for f in range(4):
-            outs[f][pl.ds(j, K, stride=R), :] = c2_in[f, j - 4]
+            final[f, pl.ds(j, K, stride=R), :] = c2_in[f, j - 4]
         return carry
 
     lax.fori_loop(4, R - 4, copy, 0, unroll=2)
+
+    copies = []
+    for direction in (0, 1):
+        directions = (direction,)
+        here = (2 * direction, 2 * direction + 1)
+        for j in near:
+            side = SOUTH if j < R // 2 else NORTH
+
+            def store(f, q, value):
+                if f >= 2 and not 0 <= j < R:
+                    value = jnp.where(inside[side], value, 0.0)
+                c1_new.at[f, new_at[j]][moved_chunk(q)] = value
+
+            def load(f, d, q):
+                return row(f, j + d)[chunk(q)]
+
+            if 0 <= j < R:
+                i = (0, 1, R - 2, R - 1).index(j)
+                step_row(
+                    store, load, y=y_new.at[new_at[j]], base=lambda f, q: part1_in.at[f, i][chunk(q)],
+                    directions=directions,
+                )
+            else:
+                halos = {f: halo_beyond(f, j) for f in here}
+                step_row(
+                    store,
+                    load,
+                    x=(x_new.at[new_at[j]], lambda f, q: halos[f][8 * q : 8 * q + 8]),
+                    y=y_new.at[new_at[j]],
+                    z=(level_new.at[new_at[j]], rolled_levels(lambda f: row(f, j)[...], here)),
+                    directions=directions,
+                )
+
+        for j in (0, 1, 2, 3, R - 4, R - 3, R - 2, R - 1):
+            def store(f, q, value):
+                final[f, pl.ds(8 * q * R + j, 8, stride=R), :] = value
+
+            def load(f, d, q):
+                return load1(f, j + d, q)
+
+            if j in new_at:
+                halos = {f: halo_columns(merged1[f], j) for f in here}
+                step_row(
+                    store,
+                    load,
+                    x=(x_in.at[j], lambda f, q: halos[f][8 * q : 8 * q + 8]),
+                    y=y_new.at[new_at[j]],
+                    z=(level_in.at[j], moved_levels(lambda f: c1_new.at[f, new_at[j]])),
+                    directions=directions,
+                )
+            else:
+                i = (2, 3, R - 4, R - 3).index(j)
+                step_row(
+                    store, load, y=y_in.at[j - 2], base=lambda f, q: part2_in.at[f, i][chunk(q)],
+                    directions=directions,
+                )
+
+        for f in here:
+            copies.append(pltpu.make_async_copy(final.at[f], outs[f], left_by.at[f]))
+            copies[-1].start()
+    for copy_out in copies:
+        copy_out.wait()
 
 
 def vmem():
     return pl.BlockSpec(memory_space=pltpu.VMEM)
 
 
-def call(kernel, in_specs, out_shapes, scratch=(), limit=16 * MIB, cost=0.0):
+def call(kernel, in_specs, out_shapes, scratch=(), out_space=pltpu.VMEM, limit=16 * MIB, cost=0.0):
     return pl.pallas_call(
         kernel,
         out_shape=[jax.ShapeDtypeStruct(shape, F32) for shape in out_shapes],
         in_specs=in_specs,
-        out_specs=[vmem()] * len(out_shapes),
+        out_specs=[pl.BlockSpec(memory_space=out_space)] * len(out_shapes),
         scratch_shapes=list(scratch),
         compiler_params=pltpu.CompilerParams(vmem_limit_bytes=limit),
         cost_estimate=pl.CostEstimate(flops=0, bytes_accessed=int(cost * MIB), transcendentals=0),
@@ -584,14 +590,14 @@
     x_in, c1, part1, c2, part2, edge = call(
         interior,
         [vmem()] * 8,
-        [(R, 9) + row, (4, R - 4, TALL, W), (4, 4) + row, (4, R - 8) + row, (4, 4) + row, (2, 4) + row],
+        [(R, 9) + row, (4, R - 4, TALL, W), (4, 4) + row, (4, R - 8) + row, (4, 4) + row, (4,) + row],
         [pltpu.VMEM((4,) + row, F32), pltpu.VMEM(row, F32), pltpu.VMEM(row, F32)],
         cost=20,
     )(rows, raw, left, right, merged, y_in, level, base)
 
     outs = call(
         boundary,
-        [vmem()] * 14,
+        [vmem()] * 12,
         [(K * R, W)] * 4,
         [
             pltpu.VMEM((2, SIDE_BLOCKS) + row, F32),
@@ -601,10 +607,13 @@
             pltpu.VMEM((4, 8, TALL, W), F32),
             pltpu.VMEM((4,) + row, F32),
             pltpu.VMEM((FIELDS,) + row, F32),
+            pltpu.VMEM((4, K * R, W), F32),
+            pltpu.SemaphoreType.DMA((4,)),
         ],
+        out_space=pltpu.HBM,
         cost=20,
     )(
-        *(rows, left, right, merged, y_in, level, x_in, c1, part1, c2, part2, edge),
+        *(rows, merged, y_in, level, x_in, c1, part1, c2, part2, edge),
         *(second, first),
     )
     return tuple(a.reshape(K, R, W) for a in outs)

time: 23.3 us -> 23.4 us (level)
  transfers between devices with their start and end apart: 4 -> 4, of which waited for: 3 -> 3; matrix products, arithmetic and copies ran while one was open for 0% -> 0% of each run, Pallas kernels for 33% -> 32%
where the time goes in v10:
time: 23.4 us; the launch traced here: 23.3 us
  Pallas kernels  13.5 us (58%)
  starting transfers between devices  7.86 us (34%)
  waiting for transfers between devices  1.22 us (5%)
  between operations  0.67 us (3%)
    pallas_call x1, Pallas kernels, local(): call(interior, [vmem()] * 8, [(R, 9) + row, (4, R - 4, TALL, W), (4, 4) +...  5.89 us
    pallas_call x1, Pallas kernels, local(): call(boundary, [vmem()] * 12, [(K * R, W)] * 4, [pltpu.VMEM((2, SIDE_BLOC...  3.66 us
    ppermute x1, starting transfers between devices, local(): lax.ppermute(to_west, 'ew', [((i + 1) % n_ew, i) for i in range(n_ew)])  3.1 us
    ppermute x1, starting transfers between devices, local(): lax.ppermute(to_east, 'ew', [(i, (i + 1) % n_ew) for i in range(n_ew)])  2.99 us
    pallas_call x1, Pallas kernels, local(): call(pack_edges, [pl.BlockSpec(memory_space=pltpu.HBM)] * FIELDS, [(FIELD...  2.17 us
    ppermute x2, starting transfers between devices, swap(): return lax.ppermute(message, ('ew', 'ns'), partners(odd, n_ew, n_ns))  1.77 us
    pallas_call x1, Pallas kernels, local(): call(prepare, [vmem()] * 2, [(R - 4, 9) + row, (R, 3) + row, (4, R - 4) +...  1.65 us
    ppermute x2, waiting for transfers between devices, swap(): return lax.ppermute(message, ('ew', 'ns'), partners(odd, n_ew, n_ns))  0.7 us
  transfers between devices with their start and end apart: 4, of which 3 were waited for; matrix products, arithmetic and copies ran while one was open for 0% of the time, Pallas kernels for 32%

profile of v10, /device:TPU:0, one launch (start us, length us, event | category | flops | bytes accessed | tf_op | source)
XLA Modules:
  0.0 23.3 jit_solution(4521821682983040497)
XLA Ops:
  0.6 2.2 %shard_map.102 = (f32[7,16,32,128]{3,2,1,0:T(8,128)S(1)}, f32[4,544,128]{2,1,0:T(8,128)S(1)}, f32[7,32,128]{2,1,0:T(8,128)S(1)}, f32[104,128]{1,0:T(8,128)S(1)}, f32[104,128]{1,0:T(8,128)S(1)}) custom-call(f32[512,128]{1,0:T(8,128)} %bitcast.11, f32[512,128]{1,0:T(8,128)} %bitcast.12, f32[512,128]{1,0:T(8,128)} %bitcast.13, f32[512,128]{1,0:T(8,128)} %bitcast.14, ...), custom_call_target="tpu_custom_call" | custom-call | tf_op jit(solution)/shard_map/pallas_call | solution.py:556
  2.8 3.0 %collective-permute-start = (f32[104,128]{1,0:T(8,128)S(1)}, f32[104,128]{1,0:T(8,128)S(1)}, u32[]{:S(2)}, u32[]{:S(2)}) collective-permute-start(f32[104,128]{1,0:T(8,128)S(1)} %get-tuple-element.29), channel_id=1, source_target_pairs={{0,4},{4,8},{8,12},{12,16},{16,20},{20,24},{24,28},{28,0},{1,5},{5... | collective-permute-start | bytes 159752 | tf_op jit(solution)/shard_map/ppermute | solution.py:568
  5.8 3.1 %collective-permute-start.1 = (f32[104,128]{1,0:T(8,128)S(1)}, f32[104,128]{1,0:T(8,128)S(1)}, u32[]{:S(2)}, u32[]{:S(2)}) collective-permute-start(f32[104,128]{1,0:T(8,128)S(1)} %get-tuple-element.30), channel_id=1, source_target_pairs={{4,0},{8,4},{12,8},{16,12},{20,16},{24,20},{28,24},{0,28},{5,1},{9... | collective-permute-start | bytes 159752 | tf_op jit(solution)/shard_map/ppermute | solution.py:569
  8.9 1.6 %shard_map.103 = (f32[12,9,32,128]{3,2,1,0:T(8,128)S(1)}, f32[16,3,32,128]{3,2,1,0:T(8,128)S(1)}, f32[4,12,32,128]{3,2,1,0:T(8,128)S(1)}) custom-call(f32[7,16,32,128]{3,2,1,0:T(8,128)S(1)} %get-tuple-element.27.rows.refs_0_, f32[4,544,128]{2,1,0:T(8,128)S(1)} %get-tuple-element.31.raw.refs_1_), custom_call_target="tpu_custom_call" | custom-call | bytes 6291456 | tf_op jit(solution)/shard_map/pallas_call | solution.py:574
  10.6 0.5 %collective-permute-done.from_west = f32[104,128]{1,0:T(8,128)S(1)} collective-permute-done((f32[104,128]{1,0:T(8,128)S(1)}, f32[104,128]{1,0:T(8,128)S(1)}, u32[]{:S(2)}, u32[]{:S(2)}) %collective-permute-start) | collective-permute-done | bytes 53280 | tf_op jit(solution)/shard_map/ppermute | solution.py:568
  11.0 0.1 collective-permute-done.1.from_east
  11.1 0.2 shard_map.104
  11.3 1.4 %collective-permute-start.2 = (f32[27,32,128]{2,1,0:T(8,128)S(1)}, f32[27,32,128]{2,1,0:T(8,128)S(1)}, u32[]{:S(2)}, u32[]{:S(2)}) collective-permute-start(f32[27,32,128]{2,1,0:T(8,128)S(1)} %get-tuple-element.44), channel_id=1, source_target_pairs={{0,4},{1,2},{2,1},{3,7},{4,0},{5,6},{6,5},{7,3},{8,12},{9,10},{10,... | collective-permute-start | bytes 1327112 | tf_op jit(solution)/shard_map/ppermute | solution.py:572
  12.6 0.4 %collective-permute-start.3 = (f32[27,32,128]{2,1,0:T(8,128)S(1)}, f32[27,32,128]{2,1,0:T(8,128)S(1)}, u32[]{:S(2)}, u32[]{:S(2)}) collective-permute-start(f32[27,32,128]{2,1,0:T(8,128)S(1)} %get-tuple-element.45), channel_id=1, source_target_pairs={{0,1},{1,0},{2,3},{3,2},{4,5},{5,4},{6,7},{7,6},{8,9},{9,8},{10,11... | collective-permute-start | bytes 1327112 | tf_op jit(solution)/shard_map/ppermute | solution.py:572
  13.0 5.9 %shard_map.105 = (f32[16,9,32,128]{3,2,1,0:T(8,128)S(1)}, f32[4,12,48,128]{3,2,1,0:T(8,128)S(1)}, f32[4,4,32,128]{3,2,1,0:T(8,128)S(1)}, f32[4,8,32,128]{3,2,1,0...) custom-call(f32[7,16,32,128]{3,2,1,0:T(8,128)S(1)} %get-tuple-element.27.rows.refs_0_, ...), custom_call_target="tpu_custom_call" | custom-call | bytes 20971520 | tf_op jit(solution)/shard_map/pallas_call | solution.py:590
  18.9 0.7 %collective-permute-done.2.refs_10_ = f32[27,32,128]{2,1,0:T(8,128)S(1)} collective-permute-done((f32[27,32,128]{2,1,0:T(8,128)S(1)}, f32[27,32,128]{2,1,0:T(8,128)S(1)}, u32[]{:S(2)}, u32[]{:S(2)}) %collective-permute-start.2) | collective-permute-done | bytes 442400 | tf_op jit(solution)/shard_map/ppermute | solution.py:572
  19.6 0.0 collective-permute-done.3.refs_11_
  19.6 3.7 %shard_map.106 = (f32[512,128]{1,0:T(8,128)}, f32[512,128]{1,0:T(8,128)}, f32[512,128]{1,0:T(8,128)}, f32[512,128]{1,0:T(8,128)}) custom-call(f32[7,16,32,128]{3,2,1,0:T(8,128)S(1)} %get-tuple-element.27.rows.refs_0_, f32[7,32,128]{2,1,0:T(8,128)S(1)} %get-tuple-element.33.refs_4_.refs_1_, f32[12,9,32,128]{3,2,1,0:T(8,128)S(1)} %get-tuple-element.34.refs_5_.refs_2_, ...), custom_call_target="tpu_custom_call" | custom-call | bytes 20971520 | tf_op jit(solution)/shard_map/pallas_call | solution.py:598
Async XLA Ops:
  2.8 8.2 %collective-permute-start = (f32[104,128]{1,0:T(8,128)S(1)}, f32[104,128]{1,0:T(8,128)S(1)}, u32[]{:S(2)}, u32[]{:S(2)}) collective-permute-start(f32[104,128]{1,0:T(8,128)S(1)} %get-tuple-element.29), channel_id=1, source_target_pairs={{0,4},{4,8},{8,12},{12,16},{16,20},{20,24},{24,28},{28,0},{1,5},{5... | collective-permute-start | bytes 159752 | tf_op jit(solution)/shard_map/ppermute | solution.py:568
  5.8 5.3 %collective-permute-start.1 = (f32[104,128]{1,0:T(8,128)S(1)}, f32[104,128]{1,0:T(8,128)S(1)}, u32[]{:S(2)}, u32[]{:S(2)}) collective-permute-start(f32[104,128]{1,0:T(8,128)S(1)} %get-tuple-element.30), channel_id=1, source_target_pairs={{4,0},{8,4},{12,8},{16,12},{20,16},{24,20},{28,24},{0,28},{5,1},{9... | collective-permute-start | bytes 159752 | tf_op jit(solution)/shard_map/ppermute | solution.py:569
  11.3 8.4 %collective-permute-start.2 = (f32[27,32,128]{2,1,0:T(8,128)S(1)}, f32[27,32,128]{2,1,0:T(8,128)S(1)}, u32[]{:S(2)}, u32[]{:S(2)}) collective-permute-start(f32[27,32,128]{2,1,0:T(8,128)S(1)} %get-tuple-element.44), channel_id=1, source_target_pairs={{0,4},{1,2},{2,1},{3,7},{4,0},{5,6},{6,5},{7,3},{8,12},{9,10},{10,... | collective-permute-start | bytes 1327112 | tf_op jit(solution)/shard_map/ppermute | solution.py:572
  12.6 7.0 %collective-permute-start.3 = (f32[27,32,128]{2,1,0:T(8,128)S(1)}, f32[27,32,128]{2,1,0:T(8,128)S(1)}, u32[]{:S(2)}, u32[]{:S(2)}) collective-permute-start(f32[27,32,128]{2,1,0:T(8,128)S(1)} %get-tuple-element.45), channel_id=1, source_target_pairs={{0,1},{1,0},{2,3},{3,2},{4,5},{5,4},{6,7},{7,6},{8,9},{9,8},{10,11... | collective-permute-start | bytes 1327112 | tf_op jit(solution)/shard_map/ppermute | solution.py:572

commit v11 on v9

--- a/solution.py
+++ b/solution.py
@@ -35,7 +35,8 @@
 
 def pack_edges(*refs):
     sources = refs[:FIELDS]
-    rows, raw, own, to_east, to_west, raw_flow, raw_wet, arrived = refs[FIELDS:]
+    rows, raw, own, first, second, raw_flow, raw_wet, arrived = refs[FIELDS:]
+    odd = lax.axis_index("ew") % 2 == 1
     copies = []
     for f in range(FIELDS):
         target = raw.at[f, pl.ds(R, K * R)] if f < 4 else raw_wet if f == M else raw_flow.at[f - U]
@@ -60,26 +61,35 @@
     west_half = lane % G < HALO
     for p, (f, g) in enumerate(PAIRS):
         a, b = packed[f], packed[g]
-        to_east[pl.ds(p * K, K)] = jnp.where(west_half, a, turn(b, HALO))
-        to_west[pl.ds(p * K, K)] = jnp.where(west_half, turn(b, -HALO), a)
+        to_east = jnp.where(west_half, a, turn(b, HALO))
+        to_west = jnp.where(west_half, turn(b, -HALO), a)
+        first[pl.ds(p * K, K)] = jnp.where(odd, to_west, to_east)
+        second[pl.ds(p * K, K)] = jnp.where(odd, to_east, to_west)
     part = lane[:8] % G // 2
-    for target, column in ((to_east, HALO - 2), (to_west, HALO)):
-        block = jnp.zeros((8, W), F32)
-        for q in range(K // 8):
-            moved = turn(packed[V][8 * q : 8 * q + 8], 2 * q - column)
-            block = jnp.where(part == q, moved, block)
-        target[pl.ds(len(PAIRS) * K, 8)] = block
-
-
-def pack_sides(rows, own, from_west, from_east, _, left, right, merged, second, first):
+    to_east = to_west = jnp.zeros((8, W), F32)
+    for q in range(K // 8):
+        v = packed[V][8 * q : 8 * q + 8]
+        to_east = jnp.where(part == q, turn(v, 2 * q - HALO + 2), to_east)
+        to_west = jnp.where(part == q, turn(v, 2 * q - HALO), to_west)
+    first[pl.ds(len(PAIRS) * K, 8)] = jnp.where(odd, to_west, to_east)
+    second[pl.ds(len(PAIRS) * K, 8)] = jnp.where(odd, to_east, to_west)
+
+
+def pack_sides(rows, own, from_first, from_second, _, left, right, merged, second, first):
     odd = lax.axis_index("ns") % 2
     lane = lanes()
     west_half = lane % G < HALO
+    odd_ew = lax.axis_index("ew") % 2 == 1
+
+    def from_sides(part):
+        x, y = from_first[part], from_second[part]
+        return jnp.where(odd_ew, x, y), jnp.where(odd_ew, y, x)
+
     halos = {}
     for p, (f, g) in enumerate(PAIRS):
-        a, b = from_west[pl.ds(p * K, K)], from_east[pl.ds(p * K, K)]
+        a, b = from_sides(pl.ds(p * K, K))
         halos[f], halos[g] = (a, b), (turn(a, -HALO), turn(b, HALO))
-    a, b = from_west[pl.ds(len(PAIRS) * K, 8)], from_east[pl.ds(len(PAIRS) * K, 8)]
+    a, b = from_sides(pl.ds(len(PAIRS) * K, 8))
     halos[V] = [
         jnp.concatenate([turn(x, column - 2 * q) for q in range(K // 8)], axis=0)
         for x, column in ((a, HALO - 2), (b, HALO))
@@ -157,7 +167,6 @@
 
 def step_row(store, load, x=None, y=None, z=None, base=None):
     lane = lanes()[:8]
-    results = []
     for q in range(K // 8):
         part = chunk(q)
         centre = None
@@ -184,9 +193,7 @@
                 if z:
                     c_after, c_before = z[1](f, q)
                     total += after * c_after + before * c_before
-                results.append((f, q, total))
-    for result in results:
-        store(*result)
+                store(f, q, total)
 
 
 def halo_columns(merged, j):
@@ -215,9 +222,9 @@
     return results
 
 
-def edge_rows(edges, beyond):
+def edge_rows(merged, beyond):
     lane = lanes()
-    v, m = edges[V], edges[M]
+    v, m = merged[V], merged[M]
     vh, mh = beyond(V), beyond(M)
     ys = coefficients(
         {d: shifted(v, vh, d, lane, G) for d in (-2, -1, 0, 1)},
@@ -225,7 +232,7 @@
     )
     results = []
     for f in range(4):
-        c, ch = edges[f], beyond(f)
+        c, ch = merged[f], beyond(f)
         total = ys[8] * c
         for coefficient, d in zip(ys[4 * (f // 2) :], (-2, -1, 1, 2)):
             total += coefficient * shifted(c, ch, d, lane, G)
@@ -269,9 +276,9 @@
     return lambda f, q: (row(f)[moved_chunk(q, 1)], row(f)[moved_chunk(q, -1)])
 
 
-def rolled_levels(load):
-    after = [pltpu.roll(load(f), K - 1, 0) for f in range(4)]
-    before = [pltpu.roll(load(f), 1, 0) for f in range(4)]
+def rolled_levels(load, fields):
+    after = {f: pltpu.roll(load(f), K - 1, 0) for f in fields}
+    before = {f: pltpu.roll(load(f), 1, 0) for f in fields}
     return lambda f, q: (after[f][8 * q : 8 * q + 8], before[f][8 * q : 8 * q + 8])
 
 
@@ -329,19 +336,15 @@
 
     by_fours(0, R, x_body)
 
-    both = []
-    for side, edges in enumerate((left, right)):
-        partial = edge_columns_and_levels(edges, *faces[side])
-        across = edge_rows(edges, lambda f: edges[f])
-        for f in range(4):
-            edge_out[side, f] = partial[f]
-        both.append([p + a for p, a in zip(partial, across)])
+    partial = [edge_columns_and_levels(e, *f) for e, f in zip((left, right), faces)]
+    across = edge_rows(merged, lambda f: merged[f])
     for f in range(4):
-        merged1[f] = jnp.where(west_half, both[0][f], both[1][f])
+        edge = jnp.where(west_half, partial[0][f], partial[1][f])
+        edge_out[f] = edge
+        merged1[f] = edge + across[f]
 
     def halo(source, j):
-        halos = [halo_columns(source[f], j) for f in range(4)]
-        return lambda f, q: halos[f][8 * q : 8 * q + 8]
+        return lambda f, q: halo_columns(source.at[f][chunk(q)], j)
 
     def first(j):
         def store(f, q, value):
@@ -394,12 +397,11 @@
 
 
 def boundary(*refs):
-    rows, left, right, merged, y_in, level_in, x_in, c1_in, part1_in, c2_in, part2_in, edge_in = refs[:12]
-    second, first = refs[12:14]
-    outs = refs[14:18]
-    sides, x_new, y_new, level_new, c1_new, merged1, beyond = refs[18:]
+    rows, merged, y_in, level_in, x_in, c1_in, part1_in, c2_in, part2_in, edge_in = refs[:10]
+    second, first = refs[10:12]
+    outs = refs[12:16]
+    sides, x_new, y_new, level_new, c1_new, merged1, beyond = refs[16:]
     lane = lanes()
-    west_half = lane % G < HALO
     place = lax.axis_index("ns")
     last = lax.axis_size("ns") - 1
     odd = place % 2
@@ -429,12 +431,8 @@
         for i in range(2, 6):
             clear_ends(c1_new.at[f, i])
 
-    both = []
-    for s, edges in enumerate((left, right)):
-        across = edge_rows(edges, lambda f: beyond[f])
-        both.append([edge_in[s, f] + a for f, a in enumerate(across)])
-    for f in range(4):
-        merged1[f] = jnp.where(west_half, both[0][f], both[1][f])
+    for f, across in enumerate(edge_rows(merged, lambda f: beyond[f])):
+        merged1[f] = edge_in[f] + across
 
     def halo_beyond(f, j):
         return halo_columns(beyond[f], j % R)
@@ -475,7 +473,7 @@
                 load,
                 x=(x_new.at[new_at[j]], lambda f, q: halos[f][8 * q : 8 * q + 8]),
                 y=y_new.at[new_at[j]],
-                z=(level_new.at[new_at[j]], rolled_levels(lambda f: row(f, j)[...])),
+                z=(level_new.at[new_at[j]], rolled_levels(lambda f: row(f, j)[...], range(4))),
             )
 
     def load1(f, j, q):
@@ -547,7 +545,7 @@
 
     row = (K, W)
     padded = ((K + 2) * R, W)
-    rows, raw, own, to_east, to_west = call(
+    rows, raw, own, ew_first, ew_second = call(
         pack_edges,
         [pl.BlockSpec(memory_space=pltpu.HBM)] * FIELDS,
         [(FIELDS, R) + row, (4,) + padded, (FIELDS,) + row, (EDGE_ROWS, W), (EDGE_ROWS, W)],
@@ -559,8 +557,11 @@
     )(*[pltpu.with_memory_space_constraint(a, pltpu.HBM) for a in flat])
 
     n_ew, n_ns = lax.axis_size("ew"), lax.axis_size("ns")
-    from_west = lax.ppermute(to_east, "ew", [(i, (i + 1) % n_ew) for i in range(n_ew)])
-    from_east = lax.ppermute(to_west, "ew", [((i + 1) % n_ew, i) for i in range(n_ew)])
+    assert n_ew % 2 == 0
+    ew_first = lax.ppermute(ew_first, "ew", [(i, i ^ 1) for i in range(n_ew)])
+    ew_second = lax.ppermute(
+        ew_second, "ew", [(i, (((i + 1) ^ 1) - 1) % n_ew) for i in range(n_ew)]
+    )
 
     def swap(odd, message):
         return lax.ppermute(message, ("ew", "ns"), partners(odd, n_ew, n_ns))
@@ -577,21 +578,21 @@
         [vmem()] * 4 + [pl.BlockSpec(memory_space=pl.ANY)],
         [(FIELDS,) + row] * 3 + [(SIDE_BLOCKS,) + row] * 2,
         cost=1,
-    )(rows, own, from_west, from_east, level)
+    )(rows, own, ew_first, ew_second, level)
     second = swap(1, second)
     first = swap(0, first)
 
     x_in, c1, part1, c2, part2, edge = call(
         interior,
         [vmem()] * 8,
-        [(R, 9) + row, (4, R - 4, TALL, W), (4, 4) + row, (4, R - 8) + row, (4, 4) + row, (2, 4) + row],
+        [(R, 9) + row, (4, R - 4, TALL, W), (4, 4) + row, (4, R - 8) + row, (4, 4) + row, (4,) + row],
         [pltpu.VMEM((4,) + row, F32), pltpu.VMEM(row, F32), pltpu.VMEM(row, F32)],
         cost=20,
     )(rows, raw, left, right, merged, y_in, level, base)
 
     outs = call(
         boundary,
-        [vmem()] * 14,
+        [vmem()] * 12,
         [(K * R, W)] * 4,
         [
             pltpu.VMEM((2, SIDE_BLOCKS) + row, F32),
@@ -604,7 +605,7 @@
         ],
         cost=20,
     )(
-        *(rows, left, right, merged, y_in, level, x_in, c1, part1, c2, part2, edge),
+        *(rows, merged, y_in, level, x_in, c1, part1, c2, part2, edge),
         *(second, first),
     )
     return tuple(a.reshape(K, R, W) for a in outs)

time: 23.3 us -> 39.7 us (1.70)
  Pallas kernels: 13.5 us -> 29 us
  waiting for transfers between devices: 1.12 us -> 1.6 us
  starting transfers between devices: 7.86 us -> 8.27 us
    pallas_call x1, Pallas kernels: 6 us -> 21.6 us  [local(): call(interior, [vmem()] * 8, [(R, 9) + row, (4, R - 4, TALL, W), (4, 4) +...]
    ppermute x2, waiting for transfers between devices: 0.52 us -> 1.6 us  [the longest x1 1.59 us: local(): lax.ppermute(ew_second, 'ew', [(i, ((i + 1 ^ 1) - 1) % n_ew) for i in ran...]
    ppermute x2, waiting for transfers between devices: 0.6 us -> 0.01 us  [swap(): return lax.ppermute(message, ('ew', 'ns'), partners(odd, n_ew, n_ns))]
    ppermute x2, starting transfers between devices: 6.09 us -> 6.58 us  [the longest x1 3.57 us: local(): lax.ppermute(ew_second, 'ew', [(i, ((i + 1 ^ 1) - 1) % n_ew) for i in ran...]
  transfers between devices with their start and end apart: 4 -> 4, of which waited for: 3 -> 1; matrix products, arithmetic and copies ran while one was open for 0% -> 0% of each run, Pallas kernels for 33% -> 59%
where the time goes in v11:
time: 39.7 us; the launch traced here: 39.5 us
  Pallas kernels  29 us (73%)
  starting transfers between devices  8.27 us (21%)
  waiting for transfers between devices  1.6 us (4%)
  between operations  0.69 us (2%)
    pallas_call x1, Pallas kernels, local(): call(interior, [vmem()] * 8, [(R, 9) + row, (4, R - 4, TALL, W), (4, 4) +...  21.6 us
    ppermute x1, starting transfers between devices, local(): lax.ppermute(ew_second, 'ew', [(i, ((i + 1 ^ 1) - 1) % n_ew) for i in ran...  3.57 us
    pallas_call x1, Pallas kernels, local(): call(boundary, [vmem()] * 12, [(K * R, W)] * 4, [pltpu.VMEM((2, SIDE_BLOC...  3.4 us
    ppermute x1, starting transfers between devices, local(): ew_first = lax.ppermute(ew_first, 'ew', [(i, i ^ 1) for i in range(n_ew)])  3 us
    pallas_call x1, Pallas kernels, local(): call(pack_edges, [pl.BlockSpec(memory_space=pltpu.HBM)] * FIELDS, [(FIELD...  2.17 us
    ppermute x2, starting transfers between devices, swap(): return lax.ppermute(message, ('ew', 'ns'), partners(odd, n_ew, n_ns))  1.69 us
    pallas_call x1, Pallas kernels, local(): call(prepare, [vmem()] * 2, [(R - 4, 9) + row, (R, 3) + row, (4, R - 4) +...  1.65 us
    ppermute x1, waiting for transfers between devices, local(): lax.ppermute(ew_second, 'ew', [(i, ((i + 1 ^ 1) - 1) % n_ew) for i in ran...  1.59 us
  transfers between devices with their start and end apart: 4, of which 1 were waited for; matrix products, arithmetic and copies ran while one was open for 0% of the time, Pallas kernels for 59%

profile of v11, /device:TPU:0, one launch (start us, length us, event | category | flops | bytes accessed | tf_op | source)
XLA Modules:
  0.0 39.5 jit_solution(2850096649219230090)
XLA Ops:
  0.6 2.2 %shard_map.102 = (f32[7,16,32,128]{3,2,1,0:T(8,128)S(1)}, f32[4,544,128]{2,1,0:T(8,128)S(1)}, f32[7,32,128]{2,1,0:T(8,128)S(1)}, f32[104,128]{1,0:T(8,128)S(1)}, f32[104,128]{1,0:T(8,128)S(1)}) custom-call(f32[512,128]{1,0:T(8,128)} %bitcast.11, f32[512,128]{1,0:T(8,128)} %bitcast.12, f32[512,128]{1,0:T(8,128)} %bitcast.13, f32[512,128]{1,0:T(8,128)} %bitcast.14, ...), custom_call_target="tpu_custom_call" | custom-call | tf_op jit(solution)/shard_map/pallas_call | solution.py:548
  2.8 3.0 %collective-permute-start = (f32[104,128]{1,0:T(8,128)S(1)}, f32[104,128]{1,0:T(8,128)S(1)}, u32[]{:S(2)}, u32[]{:S(2)}) collective-permute-start(f32[104,128]{1,0:T(8,128)S(1)} %get-tuple-element.29), channel_id=1, source_target_pairs={{0,4},{4,0},{8,12},{12,8},{16,20},{20,16},{24,28},{28,24},{1,5},{5... | collective-permute-start | bytes 159752 | tf_op jit(solution)/shard_map/ppermute | solution.py:561
  5.8 3.6 %collective-permute-start.1 = (f32[104,128]{1,0:T(8,128)S(1)}, f32[104,128]{1,0:T(8,128)S(1)}, u32[]{:S(2)}, u32[]{:S(2)}) collective-permute-start(f32[104,128]{1,0:T(8,128)S(1)} %get-tuple-element.30), channel_id=1, source_target_pairs={{0,28},{4,8},{8,4},{12,16},{16,12},{20,24},{24,20},{28,0},{1,29},{... | collective-permute-start | bytes 159752 | tf_op jit(solution)/shard_map/ppermute | solution.py:562
  9.4 1.6 %shard_map.103 = (f32[12,9,32,128]{3,2,1,0:T(8,128)S(1)}, f32[16,3,32,128]{3,2,1,0:T(8,128)S(1)}, f32[4,12,32,128]{3,2,1,0:T(8,128)S(1)}) custom-call(f32[7,16,32,128]{3,2,1,0:T(8,128)S(1)} %get-tuple-element.27.rows.refs_0_, f32[4,544,128]{2,1,0:T(8,128)S(1)} %get-tuple-element.31.raw.refs_1_), custom_call_target="tpu_custom_call" | custom-call | bytes 6291456 | tf_op jit(solution)/shard_map/pallas_call | solution.py:569
  11.0 0.0 collective-permute-done.from_first
  11.0 1.6 %collective-permute-done.1.from_second = f32[104,128]{1,0:T(8,128)S(1)} collective-permute-done((f32[104,128]{1,0:T(8,128)S(1)}, f32[104,128]{1,0:T(8,128)S(1)}, u32[]{:S(2)}, u32[]{:S(2)}) %collective-permute-start.1) | collective-permute-done | bytes 53280 | tf_op jit(solution)/shard_map/ppermute | solution.py:562
  12.6 0.2 shard_map.104
  12.8 0.1 collective-permute-start.2
  12.9 1.6 %collective-permute-start.3 = (f32[27,32,128]{2,1,0:T(8,128)S(1)}, f32[27,32,128]{2,1,0:T(8,128)S(1)}, u32[]{:S(2)}, u32[]{:S(2)}) collective-permute-start(f32[27,32,128]{2,1,0:T(8,128)S(1)} %get-tuple-element.45), channel_id=1, source_target_pairs={{0,1},{1,0},{2,3},{3,2},{4,5},{5,4},{6,7},{7,6},{8,9},{9,8},{10,11... | collective-permute-start | bytes 1327112 | tf_op jit(solution)/shard_map/ppermute | solution.py:567
  14.5 21.6 %shard_map.105 = (f32[16,9,32,128]{3,2,1,0:T(8,128)S(1)}, f32[4,12,48,128]{3,2,1,0:T(8,128)S(1)}, f32[4,4,32,128]{3,2,1,0:T(8,128)S(1)}, f32[4,8,32,128]{3,2,1,0...) custom-call(f32[7,16,32,128]{3,2,1,0:T(8,128)S(1)} %get-tuple-element.27.rows.refs_0_, ...), custom_call_target="tpu_custom_call" | custom-call | bytes 20971520 | tf_op jit(solution)/shard_map/pallas_call | solution.py:585
  36.1 0.0 collective-permute-done.2.refs_10_
  36.1 0.0 collective-permute-done.3.refs_11_
  36.1 3.4 %shard_map.106 = (f32[512,128]{1,0:T(8,128)}, f32[512,128]{1,0:T(8,128)}, f32[512,128]{1,0:T(8,128)}, f32[512,128]{1,0:T(8,128)}) custom-call(f32[7,16,32,128]{3,2,1,0:T(8,128)S(1)} %get-tuple-element.27.rows.refs_0_, f32[7,32,128]{2,1,0:T(8,128)S(1)} %get-tuple-element.33.refs_4_.refs_1_, f32[12,9,32,128]{3,2,1,0:T(8,128)S(1)} %get-tuple-element.34.refs_5_.refs_2_, ...), custom_call_target="tpu_custom_call" | custom-call | bytes 20971520 | tf_op jit(solution)/shard_map/pallas_call | solution.py:593
Async XLA Ops:
  2.8 8.2 %collective-permute-start = (f32[104,128]{1,0:T(8,128)S(1)}, f32[104,128]{1,0:T(8,128)S(1)}, u32[]{:S(2)}, u32[]{:S(2)}) collective-permute-start(f32[104,128]{1,0:T(8,128)S(1)} %get-tuple-element.29), channel_id=1, source_target_pairs={{0,4},{4,0},{8,12},{12,8},{16,20},{20,16},{24,28},{28,24},{1,5},{5... | collective-permute-start | bytes 159752 | tf_op jit(solution)/shard_map/ppermute | solution.py:561
  5.8 6.8 %collective-permute-start.1 = (f32[104,128]{1,0:T(8,128)S(1)}, f32[104,128]{1,0:T(8,128)S(1)}, u32[]{:S(2)}, u32[]{:S(2)}) collective-permute-start(f32[104,128]{1,0:T(8,128)S(1)} %get-tuple-element.30), channel_id=1, source_target_pairs={{0,28},{4,8},{8,4},{12,16},{16,12},{20,24},{24,20},{28,0},{1,29},{... | collective-permute-start | bytes 159752 | tf_op jit(solution)/shard_map/ppermute | solution.py:562
  12.8 23.3 %collective-permute-start.2 = (f32[27,32,128]{2,1,0:T(8,128)S(1)}, f32[27,32,128]{2,1,0:T(8,128)S(1)}, u32[]{:S(2)}, u32[]{:S(2)}) collective-permute-start(f32[27,32,128]{2,1,0:T(8,128)S(1)} %get-tuple-element.44), channel_id=1, source_target_pairs={{0,4},{1,2},{2,1},{3,7},{4,0},{5,6},{6,5},{7,3},{8,12},{9,10},{10,... | collective-permute-start | bytes 1327112 | tf_op jit(solution)/shard_map/ppermute | solution.py:567
  12.9 23.2 %collective-permute-start.3 = (f32[27,32,128]{2,1,0:T(8,128)S(1)}, f32[27,32,128]{2,1,0:T(8,128)S(1)}, u32[]{:S(2)}, u32[]{:S(2)}) collective-permute-start(f32[27,32,128]{2,1,0:T(8,128)S(1)} %get-tuple-element.45), channel_id=1, source_target_pairs={{0,1},{1,0},{2,3},{3,2},{4,5},{5,4},{6,7},{7,6},{8,9},{9,8},{10,11... | collective-permute-start | bytes 1327112 | tf_op jit(solution)/shard_map/ppermute | solution.py:567

commit v12 on v11

--- a/solution.py
+++ b/solution.py
@@ -35,8 +35,7 @@
 
 def pack_edges(*refs):
     sources = refs[:FIELDS]
-    rows, raw, own, first, second, raw_flow, raw_wet, arrived = refs[FIELDS:]
-    odd = lax.axis_index("ew") % 2 == 1
+    rows, raw, own, to_east, to_west, raw_flow, raw_wet, arrived = refs[FIELDS:]
     copies = []
     for f in range(FIELDS):
         target = raw.at[f, pl.ds(R, K * R)] if f < 4 else raw_wet if f == M else raw_flow.at[f - U]
@@ -61,35 +60,26 @@
     west_half = lane % G < HALO
     for p, (f, g) in enumerate(PAIRS):
         a, b = packed[f], packed[g]
-        to_east = jnp.where(west_half, a, turn(b, HALO))
-        to_west = jnp.where(west_half, turn(b, -HALO), a)
-        first[pl.ds(p * K, K)] = jnp.where(odd, to_west, to_east)
-        second[pl.ds(p * K, K)] = jnp.where(odd, to_east, to_west)
+        to_east[pl.ds(p * K, K)] = jnp.where(west_half, a, turn(b, HALO))
+        to_west[pl.ds(p * K, K)] = jnp.where(west_half, turn(b, -HALO), a)
     part = lane[:8] % G // 2
-    to_east = to_west = jnp.zeros((8, W), F32)
-    for q in range(K // 8):
-        v = packed[V][8 * q : 8 * q + 8]
-        to_east = jnp.where(part == q, turn(v, 2 * q - HALO + 2), to_east)
-        to_west = jnp.where(part == q, turn(v, 2 * q - HALO), to_west)
-    first[pl.ds(len(PAIRS) * K, 8)] = jnp.where(odd, to_west, to_east)
-    second[pl.ds(len(PAIRS) * K, 8)] = jnp.where(odd, to_east, to_west)
-
-
-def pack_sides(rows, own, from_first, from_second, _, left, right, merged, second, first):
+    for target, column in ((to_east, HALO - 2), (to_west, HALO)):
+        block = jnp.zeros((8, W), F32)
+        for q in range(K // 8):
+            moved = turn(packed[V][8 * q : 8 * q + 8], 2 * q - column)
+            block = jnp.where(part == q, moved, block)
+        target[pl.ds(len(PAIRS) * K, 8)] = block
+
+
+def pack_sides(rows, own, from_west, from_east, _, left, right, merged, second, first):
     odd = lax.axis_index("ns") % 2
     lane = lanes()
     west_half = lane % G < HALO
-    odd_ew = lax.axis_index("ew") % 2 == 1
-
-    def from_sides(part):
-        x, y = from_first[part], from_second[part]
-        return jnp.where(odd_ew, x, y), jnp.where(odd_ew, y, x)
-
     halos = {}
     for p, (f, g) in enumerate(PAIRS):
-        a, b = from_sides(pl.ds(p * K, K))
+        a, b = from_west[pl.ds(p * K, K)], from_east[pl.ds(p * K, K)]
         halos[f], halos[g] = (a, b), (turn(a, -HALO), turn(b, HALO))
-    a, b = from_sides(pl.ds(len(PAIRS) * K, 8))
+    a, b = from_west[pl.ds(len(PAIRS) * K, 8)], from_east[pl.ds(len(PAIRS) * K, 8)]
     halos[V] = [
         jnp.concatenate([turn(x, column - 2 * q) for q in range(K // 8)], axis=0)
         for x, column in ((a, HALO - 2), (b, HALO))
@@ -197,7 +187,7 @@
 
 
 def halo_columns(merged, j):
-    return pltpu.roll(merged, lax.rem(2 * W - HALO - G * j, W), 1)
+    return turn(merged, -HALO - G * j)
 
 
 def edge_faces(edges):
@@ -256,6 +246,23 @@
     lax.fori_loop(0, (stop - start) // 4, four, 0)
 
 
+def by_fours_packed(start, stop, body, packed, turned):
+    for f, source in enumerate(packed):
+        turned[f] = turn(source, -G * start)
+
+    def four(i, carry):
+        for k in range(4):
+            body(
+                start + 4 * i + k,
+                lambda f, part: turn(turned.at[f][part], W - HALO - G * k),
+            )
+        for f in range(len(packed)):
+            turned[f] = turn(turned[f], -4 * G)
+        return carry
+
+    lax.fori_loop(0, (stop - start) // 4, four, 0)
+
+
 def raw_levels(raw, j):
     return lambda f, q: (raw.at[f][strided(q, j, R, 1), :], raw.at[f][strided(q, j, R, -1), :])
 
@@ -312,18 +319,18 @@
 
 def interior(*refs):
     rows, raw, left, right, merged, y_in, level_in, base_in = refs[:8]
-    x_out, c1_out, part1_out, c2_out, part2_out, edge_out, merged1, halo_s, halo_mixed = refs[8:]
+    x_out, c1_out, part1_out, c2_out, part2_out, edge_out, merged1, turned = refs[8:]
     lane = lanes()
     west_half = lane % G < HALO
     for f in range(4):
         for r in range(R - 4):
             clear_ends(c1_out.at[f, r])
     faces = [edge_faces(edges) for edges in (left, right)]
-    halo_s[...] = jnp.where(west_half, faces[0][0], faces[1][0])
-    halo_mixed[...] = jnp.where(west_half, faces[0][1], right[M])
-
-    def x_body(j):
-        hs, hm = halo_columns(halo_s[...], j), halo_columns(halo_mixed[...], j)
+    halo_s = jnp.where(west_half, faces[0][0], faces[1][0])
+    halo_mixed = jnp.where(west_half, faces[0][1], right[M])
+
+    def x_body(j, halo):
+        hs, hm = halo(0, pl.ds(0, K)), halo(1, pl.ds(0, K))
         m = rows[M, j]
         opened = m * shifted(m, hm, 1, lane)
         s = scaled(rows[U, j], opened)
@@ -334,7 +341,7 @@
         for k in range(9):
             x_out[j, k] = got[k]
 
-    by_fours(0, R, x_body)
+    by_fours_packed(0, R, x_body, (halo_s, halo_mixed), turned)
 
     partial = [edge_columns_and_levels(e, *f) for e, f in zip((left, right), faces)]
     across = edge_rows(merged, lambda f: merged[f])
@@ -343,21 +350,21 @@
         edge_out[f] = edge
         merged1[f] = edge + across[f]
 
-    def halo(source, j):
+    def halo_at(source, j):
         return lambda f, q: halo_columns(source.at[f][chunk(q)], j)
 
-    def first(j):
+    def first(j, halo):
         def store(f, q, value):
             c1_out.at[f, j - 2][moved_chunk(q)] = value
 
         step_row(
             store,
             lambda f, d, q: rows.at[f, j][chunk(q)],
-            x=(x_out.at[j], halo(merged, j)),
+            x=(x_out.at[j], lambda f, q: halo(f, chunk(q))),
             base=lambda f, q: base_in.at[f, j - 2][chunk(q)],
         )
 
-    by_fours(2, R - 2, first)
+    by_fours_packed(2, R - 2, first, [merged[f] for f in range(4)], turned)
 
     for i, j in enumerate((0, 1, R - 2, R - 1)):
         def store(f, q, value):
@@ -366,23 +373,23 @@
         step_row(
             store,
             lambda f, d, q: rows.at[f, j][chunk(q)],
-            x=(x_out.at[j], halo(merged, j)),
+            x=(x_out.at[j], halo_at(merged, j)),
             z=(level_in.at[j], raw_levels(raw, j)),
         )
 
-    def second(j):
+    def second(j, halo):
         def store(f, q, value):
             c2_out.at[f, j - 4][chunk(q)] = value
 
         step_row(
             store,
             lambda f, d, q: c1_out.at[f, j - 2 + d][moved_chunk(q)],
-            x=(x_out.at[j], halo(merged1, j)),
+            x=(x_out.at[j], lambda f, q: halo(f, chunk(q))),
             y=y_in.at[j - 2],
             z=(level_in.at[j], moved_levels(lambda f: c1_out.at[f, j - 2])),
         )
 
-    by_fours(4, R - 4, second)
+    by_fours_packed(4, R - 4, second, [merged1[f] for f in range(4)], turned)
 
     for i, j in enumerate((2, 3, R - 4, R - 3)):
         def store(f, q, value):
@@ -391,7 +398,7 @@
         step_row(
             store,
             lambda f, d, q: c1_out.at[f, j - 2][moved_chunk(q)],
-            x=(x_out.at[j], halo(merged1, j)),
+            x=(x_out.at[j], halo_at(merged1, j)),
             z=(level_in.at[j], moved_levels(lambda f: c1_out.at[f, j - 2])),
         )
 
@@ -545,7 +552,7 @@
 
     row = (K, W)
     padded = ((K + 2) * R, W)
-    rows, raw, own, ew_first, ew_second = call(
+    rows, raw, own, to_east, to_west = call(
         pack_edges,
         [pl.BlockSpec(memory_space=pltpu.HBM)] * FIELDS,
         [(FIELDS, R) + row, (4,) + padded, (FIELDS,) + row, (EDGE_ROWS, W), (EDGE_ROWS, W)],
@@ -557,11 +564,8 @@
     )(*[pltpu.with_memory_space_constraint(a, pltpu.HBM) for a in flat])
 
     n_ew, n_ns = lax.axis_size("ew"), lax.axis_size("ns")
-    assert n_ew % 2 == 0
-    ew_first = lax.ppermute(ew_first, "ew", [(i, i ^ 1) for i in range(n_ew)])
-    ew_second = lax.ppermute(
-        ew_second, "ew", [(i, (((i + 1) ^ 1) - 1) % n_ew) for i in range(n_ew)]
-    )
+    from_west = lax.ppermute(to_east, "ew", [(i, (i + 1) % n_ew) for i in range(n_ew)])
+    from_east = lax.ppermute(to_west, "ew", [((i + 1) % n_ew, i) for i in range(n_ew)])
 
     def swap(odd, message):
         return lax.ppermute(message, ("ew", "ns"), partners(odd, n_ew, n_ns))
@@ -578,7 +582,7 @@
         [vmem()] * 4 + [pl.BlockSpec(memory_space=pl.ANY)],
         [(FIELDS,) + row] * 3 + [(SIDE_BLOCKS,) + row] * 2,
         cost=1,
-    )(rows, own, ew_first, ew_second, level)
+    )(rows, own, from_west, from_east, level)
     second = swap(1, second)
     first = swap(0, first)
 
@@ -586,7 +590,7 @@
         interior,
         [vmem()] * 8,
         [(R, 9) + row, (4, R - 4, TALL, W), (4, 4) + row, (4, R - 8) + row, (4, 4) + row, (4,) + row],
-        [pltpu.VMEM((4,) + row, F32), pltpu.VMEM(row, F32), pltpu.VMEM(row, F32)],
+        [pltpu.VMEM((4,) + row, F32), pltpu.VMEM((4,) + row, F32)],
         cost=20,
     )(rows, raw, left, right, merged, y_in, level, base)
 

time: 39.7 us -> 39.8 us (level)
  Pallas kernels: 29 us -> 30.6 us
  waiting for transfers between devices: 1.6 us -> 0.52 us
  starting transfers between devices: 8.27 us -> 7.86 us
    pallas_call x1, Pallas kernels: 21.6 us -> 23.2 us  [local(): call(interior, [vmem()] * 8, [(R, 9) + row, (4, R - 4, TALL, W), (4, 4) +...]
    ppermute x2, waiting for transfers between devices: 1.6 us -> 0.52 us  [the longest x1 0.45 us: local(): lax.ppermute(to_east, 'ew', [(i, (i + 1) % n_ew) for i in range(n_ew)])]
    ppermute x2, starting transfers between devices: 6.58 us -> 6.09 us  [the longest x1 3.1 us: local(): lax.ppermute(to_west, 'ew', [((i + 1) % n_ew, i) for i in range(n_ew)])]
  transfers between devices with their start and end apart: 4 -> 4, of which waited for: 1 -> 2; matrix products, arithmetic and copies ran while one was open for 0% -> 0% of each run, Pallas kernels for 59% -> 63%
where the time goes in v12:
time: 39.8 us; the launch traced here: 39.6 us
  Pallas kernels  30.6 us (77%)
  starting transfers between devices  7.86 us (20%)
  between operations  0.68 us (2%)
  waiting for transfers between devices  0.52 us (1%)
    pallas_call x1, Pallas kernels, local(): call(interior, [vmem()] * 8, [(R, 9) + row, (4, R - 4, TALL, W), (4, 4) +...  23.2 us
    pallas_call x1, Pallas kernels, local(): call(boundary, [vmem()] * 12, [(K * R, W)] * 4, [pltpu.VMEM((2, SIDE_BLOC...  3.4 us
    ppermute x1, starting transfers between devices, local(): lax.ppermute(to_west, 'ew', [((i + 1) % n_ew, i) for i in range(n_ew)])  3.1 us
    ppermute x1, starting transfers between devices, local(): lax.ppermute(to_east, 'ew', [(i, (i + 1) % n_ew) for i in range(n_ew)])  2.99 us
    pallas_call x1, Pallas kernels, local(): call(pack_edges, [pl.BlockSpec(memory_space=pltpu.HBM)] * FIELDS, [(FIELD...  2.17 us
    ppermute x2, starting transfers between devices, swap(): return lax.ppermute(message, ('ew', 'ns'), partners(odd, n_ew, n_ns))  1.77 us
    pallas_call x1, Pallas kernels, local(): call(prepare, [vmem()] * 2, [(R - 4, 9) + row, (R, 3) + row, (4, R - 4) +...  1.65 us
  transfers between devices with their start and end apart: 4, of which 2 were waited for; matrix products, arithmetic and copies ran while one was open for 0% of the time, Pallas kernels for 63%

profile of v12, /device:TPU:0, one launch (start us, length us, event | category | flops | bytes accessed | tf_op | source)
XLA Modules:
  0.0 39.6 jit_solution(14029245159975098560)
XLA Ops:
  0.6 2.2 %shard_map.102 = (f32[7,16,32,128]{3,2,1,0:T(8,128)S(1)}, f32[4,544,128]{2,1,0:T(8,128)S(1)}, f32[7,32,128]{2,1,0:T(8,128)S(1)}, f32[104,128]{1,0:T(8,128)S(1)}, f32[104,128]{1,0:T(8,128)S(1)}) custom-call(f32[512,128]{1,0:T(8,128)} %bitcast.11, f32[512,128]{1,0:T(8,128)} %bitcast.12, f32[512,128]{1,0:T(8,128)} %bitcast.13, f32[512,128]{1,0:T(8,128)} %bitcast.14, ...), custom_call_target="tpu_custom_call" | custom-call | tf_op jit(solution)/shard_map/pallas_call | solution.py:555
  2.8 3.0 %collective-permute-start = (f32[104,128]{1,0:T(8,128)S(1)}, f32[104,128]{1,0:T(8,128)S(1)}, u32[]{:S(2)}, u32[]{:S(2)}) collective-permute-start(f32[104,128]{1,0:T(8,128)S(1)} %get-tuple-element.29), channel_id=1, source_target_pairs={{0,4},{4,8},{8,12},{12,16},{16,20},{20,24},{24,28},{28,0},{1,5},{5... | collective-permute-start | bytes 159752 | tf_op jit(solution)/shard_map/ppermute | solution.py:567
  5.8 3.1 %collective-permute-start.1 = (f32[104,128]{1,0:T(8,128)S(1)}, f32[104,128]{1,0:T(8,128)S(1)}, u32[]{:S(2)}, u32[]{:S(2)}) collective-permute-start(f32[104,128]{1,0:T(8,128)S(1)} %get-tuple-element.30), channel_id=1, source_target_pairs={{4,0},{8,4},{12,8},{16,12},{20,16},{24,20},{28,24},{0,28},{5,1},{9... | collective-permute-start | bytes 159752 | tf_op jit(solution)/shard_map/ppermute | solution.py:568
  8.9 1.6 %shard_map.103 = (f32[12,9,32,128]{3,2,1,0:T(8,128)S(1)}, f32[16,3,32,128]{3,2,1,0:T(8,128)S(1)}, f32[4,12,32,128]{3,2,1,0:T(8,128)S(1)}) custom-call(f32[7,16,32,128]{3,2,1,0:T(8,128)S(1)} %get-tuple-element.27.rows.refs_0_, f32[4,544,128]{2,1,0:T(8,128)S(1)} %get-tuple-element.31.raw.refs_1_), custom_call_target="tpu_custom_call" | custom-call | bytes 6291456 | tf_op jit(solution)/shard_map/pallas_call | solution.py:573
  10.6 0.5 %collective-permute-done.from_west = f32[104,128]{1,0:T(8,128)S(1)} collective-permute-done((f32[104,128]{1,0:T(8,128)S(1)}, f32[104,128]{1,0:T(8,128)S(1)}, u32[]{:S(2)}, u32[]{:S(2)}) %collective-permute-start) | collective-permute-done | bytes 53280 | tf_op jit(solution)/shard_map/ppermute | solution.py:567
  11.0 0.1 collective-permute-done.1.from_east
  11.1 0.2 shard_map.104
  11.3 1.4 %collective-permute-start.2 = (f32[27,32,128]{2,1,0:T(8,128)S(1)}, f32[27,32,128]{2,1,0:T(8,128)S(1)}, u32[]{:S(2)}, u32[]{:S(2)}) collective-permute-start(f32[27,32,128]{2,1,0:T(8,128)S(1)} %get-tuple-element.44), channel_id=1, source_target_pairs={{0,4},{1,2},{2,1},{3,7},{4,0},{5,6},{6,5},{7,3},{8,12},{9,10},{10,... | collective-permute-start | bytes 1327112 | tf_op jit(solution)/shard_map/ppermute | solution.py:571
  12.6 0.4 %collective-permute-start.3 = (f32[27,32,128]{2,1,0:T(8,128)S(1)}, f32[27,32,128]{2,1,0:T(8,128)S(1)}, u32[]{:S(2)}, u32[]{:S(2)}) collective-permute-start(f32[27,32,128]{2,1,0:T(8,128)S(1)} %get-tuple-element.45), channel_id=1, source_target_pairs={{0,1},{1,0},{2,3},{3,2},{4,5},{5,4},{6,7},{7,6},{8,9},{9,8},{10,11... | collective-permute-start | bytes 1327112 | tf_op jit(solution)/shard_map/ppermute | solution.py:571
  13.0 23.2 %shard_map.105 = (f32[16,9,32,128]{3,2,1,0:T(8,128)S(1)}, f32[4,12,48,128]{3,2,1,0:T(8,128)S(1)}, f32[4,4,32,128]{3,2,1,0:T(8,128)S(1)}, f32[4,8,32,128]{3,2,1,0...) custom-call(f32[7,16,32,128]{3,2,1,0:T(8,128)S(1)} %get-tuple-element.27.rows.refs_0_, ...), custom_call_target="tpu_custom_call" | custom-call | bytes 20971520 | tf_op jit(solution)/shard_map/pallas_call | solution.py:589
  36.2 0.0 collective-permute-done.2.refs_10_
  36.2 0.0 collective-permute-done.3.refs_11_
  36.2 3.4 %shard_map.106 = (f32[512,128]{1,0:T(8,128)}, f32[512,128]{1,0:T(8,128)}, f32[512,128]{1,0:T(8,128)}, f32[512,128]{1,0:T(8,128)}) custom-call(f32[7,16,32,128]{3,2,1,0:T(8,128)S(1)} %get-tuple-element.27.rows.refs_0_, f32[7,32,128]{2,1,0:T(8,128)S(1)} %get-tuple-element.33.refs_4_.refs_1_, f32[12,9,32,128]{3,2,1,0:T(8,128)S(1)} %get-tuple-element.34.refs_5_.refs_2_, ...), custom_call_target="tpu_custom_call" | custom-call | bytes 20971520 | tf_op jit(solution)/shard_map/pallas_call | solution.py:597
Async XLA Ops:
  2.8 8.2 %collective-permute-start = (f32[104,128]{1,0:T(8,128)S(1)}, f32[104,128]{1,0:T(8,128)S(1)}, u32[]{:S(2)}, u32[]{:S(2)}) collective-permute-start(f32[104,128]{1,0:T(8,128)S(1)} %get-tuple-element.29), channel_id=1, source_target_pairs={{0,4},{4,8},{8,12},{12,16},{16,20},{20,24},{24,28},{28,0},{1,5},{5... | collective-permute-start | bytes 159752 | tf_op jit(solution)/shard_map/ppermute | solution.py:567
  5.8 5.3 %collective-permute-start.1 = (f32[104,128]{1,0:T(8,128)S(1)}, f32[104,128]{1,0:T(8,128)S(1)}, u32[]{:S(2)}, u32[]{:S(2)}) collective-permute-start(f32[104,128]{1,0:T(8,128)S(1)} %get-tuple-element.30), channel_id=1, source_target_pairs={{4,0},{8,4},{12,8},{16,12},{20,16},{24,20},{28,24},{0,28},{5,1},{9... | collective-permute-start | bytes 159752 | tf_op jit(solution)/shard_map/ppermute | solution.py:568
  11.3 25.0 %collective-permute-start.2 = (f32[27,32,128]{2,1,0:T(8,128)S(1)}, f32[27,32,128]{2,1,0:T(8,128)S(1)}, u32[]{:S(2)}, u32[]{:S(2)}) collective-permute-start(f32[27,32,128]{2,1,0:T(8,128)S(1)} %get-tuple-element.44), channel_id=1, source_target_pairs={{0,4},{1,2},{2,1},{3,7},{4,0},{5,6},{6,5},{7,3},{8,12},{9,10},{10,... | collective-permute-start | bytes 1327112 | tf_op jit(solution)/shard_map/ppermute | solution.py:571
  12.6 23.6 %collective-permute-start.3 = (f32[27,32,128]{2,1,0:T(8,128)S(1)}, f32[27,32,128]{2,1,0:T(8,128)S(1)}, u32[]{:S(2)}, u32[]{:S(2)}) collective-permute-start(f32[27,32,128]{2,1,0:T(8,128)S(1)} %get-tuple-element.45), channel_id=1, source_target_pairs={{0,1},{1,0},{2,3},{3,2},{4,5},{5,4},{6,7},{7,6},{8,9},{9,8},{10,11... | collective-permute-start | bytes 1327112 | tf_op jit(solution)/shard_map/ppermute | solution.py:571

commit v13 on v12

--- a/solution.py
+++ b/solution.py
@@ -155,35 +155,64 @@
     return pl.ds((8 * q + 1 + shift) * stride + j, 8, stride=stride)
 
 
-def step_row(store, load, x=None, y=None, z=None, base=None):
+def pipeline(items, issue, finish, depth=1):
+    pending = []
+    for item in items:
+        pending.append((item, issue(item)))
+        if len(pending) > depth:
+            finish(*pending.pop(0))
+    for late in pending:
+        finish(*late)
+
+
+def step_rows(jobs):
     lane = lanes()[:8]
-    for q in range(K // 8):
-        part = chunk(q)
+
+    def issue(item):
+        job, q = item
+        if "x" not in job:
+            return None
+        halo = job["x"][1]
+        rolled = []
+        for f in range(4):
+            c, h = job["load"](f, 0, q), halo(f, q)
+            rolled.append([shifted(c, h, d, lane) for d in (-2, -1, 1, 2)])
+        return rolled
+
+    def finish(item, rolled):
+        job, q = item
+        x, y, z = job.get("x"), job.get("y"), job.get("z")
+        load, part = job["load"], chunk(q)
         centre = None
         for term in (x and x[0].at[8], y and y.at[8], z and z[0].at[2]):
             if term is not None:
                 centre = term[part] if centre is None else centre + term[part]
         if z:
             after, before = z[0].at[0][part], z[0].at[1][part]
-        for direction in (0, 1):
-            ks = range(4 * direction, 4 * direction + 4)
-            xs = [x[0].at[k][part] for k in ks] if x else []
-            ys = [y.at[k][part] for k in ks] if y else []
-            for f in (2 * direction, 2 * direction + 1):
-                c = load(f, 0, q)
-                total = centre * c
-                if base:
-                    total += base(f, q)
-                if x:
-                    h = x[1](f, q)
-                for coefficient, d in zip(xs, (-2, -1, 1, 2)):
-                    total += coefficient * shifted(c, h, d, lane)
-                for coefficient, d in zip(ys, (-2, -1, 1, 2)):
-                    total += coefficient * load(f, d, q)
-                if z:
-                    c_after, c_before = z[1](f, q)
-                    total += after * c_after + before * c_before
-                store(f, q, total)
+        totals = []
+        for f in range(4):
+            total = centre * load(f, 0, q)
+            if "base" in job:
+                total += job["base"](f, q)
+            if z:
+                c_after, c_before = z[1](f, q)
+                total += after * c_after + before * c_before
+            totals.append(total)
+        for coefficients_at, values in (
+            (y, lambda f, i: load(f, (-2, -1, 1, 2)[i], q)),
+            (x and x[0], lambda f, i: rolled[f][i]),
+        ):
+            if coefficients_at is None:
+                continue
+            for i in range(4):
+                for direction in (0, 1):
+                    coefficient = coefficients_at.at[4 * direction + i][part]
+                    for f in (2 * direction, 2 * direction + 1):
+                        totals[f] += coefficient * values(f, i)
+        for f in range(4):
+            job["store"](f, q, totals[f])
+
+    pipeline([(job, q) for job in jobs for q in range(K // 8)], issue, finish)
 
 
 def halo_columns(merged, j):
@@ -239,25 +268,23 @@
 
 def by_fours(start, stop, body):
     def four(i, carry):
-        for k in range(4):
-            body(start + 4 * i + k)
+        body([start + 4 * i + k for k in range(4)])
         return carry
 
     lax.fori_loop(0, (stop - start) // 4, four, 0)
 
 
-def by_fours_packed(start, stop, body, packed, turned):
+def by_fours_packed(start, stop, body, packed, turned, halos):
     for f, source in enumerate(packed):
         turned[f] = turn(source, -G * start)
 
     def four(i, carry):
-        for k in range(4):
-            body(
-                start + 4 * i + k,
-                lambda f, part: turn(turned.at[f][part], W - HALO - G * k),
-            )
+        for f in range(len(packed)):
+            for k in range(4):
+                halos[k, f] = turn(turned[f], -HALO - G * k)
         for f in range(len(packed)):
             turned[f] = turn(turned[f], -4 * G)
+        body([start + 4 * i + k for k in range(4)])
         return carry
 
     lax.fori_loop(0, (stop - start) // 4, four, 0)
@@ -290,36 +317,41 @@
 
 
 def prepare(rows, raw, y_out, level_out, base_out):
-    def levels(j):
-        for k, value in enumerate(level_coefficients(rows[M, j])):
-            level_out[j, k] = value
+    def levels(js):
+        for j in js:
+            for k, value in enumerate(level_coefficients(rows[M, j])):
+                level_out[j, k] = value
 
     by_fours(0, R, levels)
 
-    def across(j):
-        got = y_coefficients_at(lambda f, r: rows.at[f, r], j)
-        for k in range(9):
-            y_out[j - 2, k] = got[k]
+    def across(js):
+        for j in js:
+            got = y_coefficients_at(lambda f, r: rows.at[f, r], j)
+            for k in range(9):
+                y_out[j - 2, k] = got[k]
 
     by_fours(2, R - 2, across)
 
-    def first(j):
-        def store(f, q, value):
-            base_out.at[f, j - 2][chunk(q)] = value
-
-        step_row(
-            store,
-            lambda f, d, q: rows.at[f, j + d][chunk(q)],
-            y=y_out.at[j - 2],
-            z=(level_out.at[j], raw_levels(raw, j)),
-        )
+    def first(js):
+        def job(j):
+            def store(f, q, value):
+                base_out.at[f, j - 2][chunk(q)] = value
+
+            return dict(
+                store=store,
+                load=lambda f, d, q: rows.at[f, j + d][chunk(q)],
+                y=y_out.at[j - 2],
+                z=(level_out.at[j], raw_levels(raw, j)),
+            )
+
+        step_rows([job(j) for j in js])
 
     by_fours(2, R - 2, first)
 
 
 def interior(*refs):
     rows, raw, left, right, merged, y_in, level_in, base_in = refs[:8]
-    x_out, c1_out, part1_out, c2_out, part2_out, edge_out, merged1, turned = refs[8:]
+    x_out, c1_out, part1_out, c2_out, part2_out, edge_out, merged1, turned, halos, faces_now = refs[8:]
     lane = lanes()
     west_half = lane % G < HALO
     for f in range(4):
@@ -329,19 +361,30 @@
     halo_s = jnp.where(west_half, faces[0][0], faces[1][0])
     halo_mixed = jnp.where(west_half, faces[0][1], right[M])
 
-    def x_body(j, halo):
-        hs, hm = halo(0, pl.ds(0, K)), halo(1, pl.ds(0, K))
-        m = rows[M, j]
-        opened = m * shifted(m, hm, 1, lane)
-        s = scaled(rows[U, j], opened)
-        got = face_coefficients(
-            {d: shifted(s, hs, d, lane) for d in (-2, -1, 0, 1)},
-            {-1: shifted(opened, hm, -1, lane), 0: opened},
-        )
-        for k in range(9):
-            x_out[j, k] = got[k]
-
-    by_fours_packed(0, R, x_body, (halo_s, halo_mixed), turned)
+    def x_body(js):
+        for k, j in enumerate(js):
+            m = rows[M, j]
+            opened = m * shifted(m, halos[k, 1], 1, lane)
+            faces_now[k, 0] = scaled(rows[U, j], opened)
+            faces_now[k, 1] = opened
+
+        def issue(item):
+            k, q = item
+            s, opened = faces_now.at[k, 0][chunk(q)], faces_now.at[k, 1][chunk(q)]
+            hs, hm = halos.at[k, 0][chunk(q)], halos.at[k, 1][chunk(q)]
+            return (
+                {d: shifted(s, hs, d, lane[:8]) for d in (-2, -1, 0, 1)},
+                {-1: shifted(opened, hm, -1, lane[:8]), 0: opened},
+            )
+
+        def finish(item, faces_here):
+            k, q = item
+            for i, value in enumerate(face_coefficients(*faces_here)):
+                x_out.at[js[k], i][chunk(q)] = value
+
+        pipeline([(k, q) for k in range(4) for q in range(K // 8)], issue, finish, 2)
+
+    by_fours_packed(0, R, x_body, (halo_s, halo_mixed), turned, halos)
 
     partial = [edge_columns_and_levels(e, *f) for e, f in zip((left, right), faces)]
     across = edge_rows(merged, lambda f: merged[f])
@@ -350,64 +393,83 @@
         edge_out[f] = edge
         merged1[f] = edge + across[f]
 
-    def halo_at(source, j):
-        return lambda f, q: halo_columns(source.at[f][chunk(q)], j)
-
-    def first(j, halo):
-        def store(f, q, value):
-            c1_out.at[f, j - 2][moved_chunk(q)] = value
-
-        step_row(
-            store,
-            lambda f, d, q: rows.at[f, j][chunk(q)],
-            x=(x_out.at[j], lambda f, q: halo(f, chunk(q))),
-            base=lambda f, q: base_in.at[f, j - 2][chunk(q)],
-        )
-
-    by_fours_packed(2, R - 2, first, [merged[f] for f in range(4)], turned)
-
-    for i, j in enumerate((0, 1, R - 2, R - 1)):
+    def kept(k):
+        return lambda f, q: halos.at[k, f][chunk(q)]
+
+    def keep(rows_now, source):
+        for f in range(4):
+            for k, j in enumerate(rows_now):
+                halos[k, f] = halo_columns(source[f], j)
+
+    def first(js):
+        def job(k, j):
+            def store(f, q, value):
+                c1_out.at[f, j - 2][moved_chunk(q)] = value
+
+            return dict(
+                store=store,
+                load=lambda f, d, q: rows.at[f, j][chunk(q)],
+                x=(x_out.at[j], kept(k)),
+                base=lambda f, q: base_in.at[f, j - 2][chunk(q)],
+            )
+
+        step_rows([job(k, j) for k, j in enumerate(js)])
+
+    by_fours_packed(2, R - 2, first, [merged[f] for f in range(4)], turned, halos)
+
+    def first_part(i, j):
         def store(f, q, value):
             part1_out.at[f, i][chunk(q)] = value
 
-        step_row(
-            store,
-            lambda f, d, q: rows.at[f, j][chunk(q)],
-            x=(x_out.at[j], halo_at(merged, j)),
+        return dict(
+            store=store,
+            load=lambda f, d, q: rows.at[f, j][chunk(q)],
+            x=(x_out.at[j], kept(i)),
             z=(level_in.at[j], raw_levels(raw, j)),
         )
 
-    def second(j, halo):
+    ends = (0, 1, R - 2, R - 1)
+    keep(ends, merged)
+    step_rows([first_part(i, j) for i, j in enumerate(ends)])
+
+    def second(js):
+        def job(k, j):
+            def store(f, q, value):
+                c2_out.at[f, j - 4][chunk(q)] = value
+
+            return dict(
+                store=store,
+                load=lambda f, d, q: c1_out.at[f, j - 2 + d][moved_chunk(q)],
+                x=(x_out.at[j], kept(k)),
+                y=y_in.at[j - 2],
+                z=(level_in.at[j], moved_levels(lambda f: c1_out.at[f, j - 2])),
+            )
+
+        step_rows([job(k, j) for k, j in enumerate(js)])
+
+    by_fours_packed(4, R - 4, second, [merged1[f] for f in range(4)], turned, halos)
+
+    def second_part(i, j):
         def store(f, q, value):
-            c2_out.at[f, j - 4][chunk(q)] = value
-
-        step_row(
-            store,
-            lambda f, d, q: c1_out.at[f, j - 2 + d][moved_chunk(q)],
-            x=(x_out.at[j], lambda f, q: halo(f, chunk(q))),
-            y=y_in.at[j - 2],
+            part2_out.at[f, i][chunk(q)] = value
+
+        return dict(
+            store=store,
+            load=lambda f, d, q: c1_out.at[f, j - 2][moved_chunk(q)],
+            x=(x_out.at[j], kept(i)),
             z=(level_in.at[j], moved_levels(lambda f: c1_out.at[f, j - 2])),
         )
 
-    by_fours_packed(4, R - 4, second, [merged1[f] for f in range(4)], turned)
-
-    for i, j in enumerate((2, 3, R - 4, R - 3)):
-        def store(f, q, value):
-            part2_out.at[f, i][chunk(q)] = value
-
-        step_row(
-            store,
-            lambda f, d, q: c1_out.at[f, j - 2][moved_chunk(q)],
-            x=(x_out.at[j], halo_at(merged1, j)),
-            z=(level_in.at[j], moved_levels(lambda f: c1_out.at[f, j - 2])),
-        )
+    ends = (2, 3, R - 4, R - 3)
+    keep(ends, merged1)
+    step_rows([second_part(i, j) for i, j in enumerate(ends)])
 
 
 def boundary(*refs):
     rows, merged, y_in, level_in, x_in, c1_in, part1_in, c2_in, part2_in, edge_in = refs[:10]
     second, first = refs[10:12]
     outs = refs[12:16]
-    sides, x_new, y_new, level_new, c1_new, merged1, beyond = refs[16:]
+    sides, x_new, y_new, level_new, c1_new, merged1, beyond, halos = refs[16:]
     lane = lanes()
     place = lax.axis_index("ns")
     last = lax.axis_size("ns") - 1
@@ -457,7 +519,15 @@
             for k, value in enumerate(level_coefficients(row(M, j)[...])):
                 level_new[new_at[j], k] = value
 
-    for j in near:
+    out_rows = [j for j in near if not 0 <= j < R]
+    for f in range(4):
+        for i, j in enumerate(out_rows):
+            halos[i, f] = halo_beyond(f, j)
+
+    def kept(k):
+        return lambda f, q: halos.at[k, f][chunk(q)]
+
+    def first_job(j):
         side = SOUTH if j < R // 2 else NORTH
 
         def store(f, q, value):
@@ -465,50 +535,44 @@
                 value = jnp.where(inside[side], value, 0.0)
             c1_new.at[f, new_at[j]][moved_chunk(q)] = value
 
-        def load(f, d, q):
-            return row(f, j + d)[chunk(q)]
-
+        job = dict(
+            store=store, load=lambda f, d, q: row(f, j + d)[chunk(q)], y=y_new.at[new_at[j]]
+        )
         if 0 <= j < R:
             i = (0, 1, R - 2, R - 1).index(j)
-            step_row(
-                store, load, y=y_new.at[new_at[j]], base=lambda f, q: part1_in.at[f, i][chunk(q)]
-            )
-        else:
-            halos = [halo_beyond(f, j) for f in range(4)]
-            step_row(
-                store,
-                load,
-                x=(x_new.at[new_at[j]], lambda f, q: halos[f][8 * q : 8 * q + 8]),
-                y=y_new.at[new_at[j]],
-                z=(level_new.at[new_at[j]], rolled_levels(lambda f: row(f, j)[...], range(4))),
-            )
+            return job | dict(base=lambda f, q: part1_in.at[f, i][chunk(q)])
+        return job | dict(
+            x=(x_new.at[new_at[j]], kept(out_rows.index(j))),
+            z=(level_new.at[new_at[j]], rolled_levels(lambda f: row(f, j)[...], range(4))),
+        )
+
+    step_rows([first_job(j) for j in (-2, 0, -1, 1, R, R - 2, R + 1, R - 1)])
 
     def load1(f, j, q):
         if j in new_at:
             return c1_new.at[f, new_at[j]][moved_chunk(q)]
         return c1_in.at[f, j - 2][moved_chunk(q)]
 
-    for j in (0, 1, 2, 3, R - 4, R - 3, R - 2, R - 1):
+    ends = (0, 1, R - 2, R - 1)
+    for f in range(4):
+        for i, j in enumerate(ends):
+            halos[i, f] = halo_columns(merged1[f], j)
+
+    def second_job(j):
         def store(f, q, value):
             outs[f][pl.ds(8 * q * R + j, 8, stride=R), :] = value
 
-        def load(f, d, q):
-            return load1(f, j + d, q)
-
-        if j in new_at:
-            halos = [halo_columns(merged1[f], j) for f in range(4)]
-            step_row(
-                store,
-                load,
-                x=(x_in.at[j], lambda f, q: halos[f][8 * q : 8 * q + 8]),
+        job = dict(store=store, load=lambda f, d, q: load1(f, j + d, q))
+        if j in ends:
+            return job | dict(
+                x=(x_in.at[j], kept(ends.index(j))),
                 y=y_new.at[new_at[j]],
                 z=(level_in.at[j], moved_levels(lambda f: c1_new.at[f, new_at[j]])),
             )
-        else:
-            i = (2, 3, R - 4, R - 3).index(j)
-            step_row(
-                store, load, y=y_in.at[j - 2], base=lambda f, q: part2_in.at[f, i][chunk(q)]
-            )
+        i = (2, 3, R - 4, R - 3).index(j)
+        return job | dict(y=y_in.at[j - 2], base=lambda f, q: part2_in.at[f, i][chunk(q)])
+
+    step_rows([second_job(j) for j in (0, 2, 1, 3, R - 2, R - 4, R - 1, R - 3)])
 
     def copy(j, carry):
         for f in range(4):
@@ -590,7 +654,12 @@
         interior,
         [vmem()] * 8,
         [(R, 9) + row, (4, R - 4, TALL, W), (4, 4) + row, (4, R - 8) + row, (4, 4) + row, (4,) + row],
-        [pltpu.VMEM((4,) + row, F32), pltpu.VMEM((4,) + row, F32)],
+        [
+            pltpu.VMEM((4,) + row, F32),
+            pltpu.VMEM((4,) + row, F32),
+            pltpu.VMEM((4, 4) + row, F32),
+            pltpu.VMEM((4, 2) + row, F32),
+        ],
         cost=20,
     )(rows, raw, left, right, merged, y_in, level, base)
 
@@ -606,6 +675,7 @@
             pltpu.VMEM((4, 8, TALL, W), F32),
             pltpu.VMEM((4,) + row, F32),
             pltpu.VMEM((FIELDS,) + row, F32),
+            pltpu.VMEM((4, 4) + row, F32),
         ],
         cost=20,
     )(

time: 39.8 us -> 22.8 us (0.57)
  Pallas kernels: 30.6 us -> 11.8 us
  waiting for transfers between devices: 0.52 us -> 2.3 us
    pallas_call x1, Pallas kernels: 23.2 us -> 4.8 us  [local(): call(interior, [vmem()] * 8, [(R, 9) + row, (4, R - 4, TALL, W), (4, 4) +...]
    ppermute x2, waiting for transfers between devices: 0.01 us -> 1.8 us  [swap(): return lax.ppermute(message, ('ew', 'ns'), partners(odd, n_ew, n_ns))]
    pallas_call x1, Pallas kernels: 3.4 us -> 3 us  [local(): call(boundary, [vmem()] * 12, [(K * R, W)] * 4, [pltpu.VMEM((2, SIDE_BLOC...]
  transfers between devices with their start and end apart: 4 -> 4, of which waited for: 2 -> 3; matrix products, arithmetic and copies ran while one was open for 0% -> 0% of each run, Pallas kernels for 63% -> 29%
where the time goes in v13:
time: 22.8 us; the launch traced here: 22.6 us
  Pallas kernels  11.8 us (52%)
  starting transfers between devices  7.86 us (34%)
  waiting for transfers between devices  2.3 us (10%)
  between operations  0.66 us (3%)
    pallas_call x1, Pallas kernels, local(): call(interior, [vmem()] * 8, [(R, 9) + row, (4, R - 4, TALL, W), (4, 4) +...  4.8 us
    ppermute x1, starting transfers between devices, local(): lax.ppermute(to_west, 'ew', [((i + 1) % n_ew, i) for i in range(n_ew)])  3.1 us
    pallas_call x1, Pallas kernels, local(): call(boundary, [vmem()] * 12, [(K * R, W)] * 4, [pltpu.VMEM((2, SIDE_BLOC...  3 us
    ppermute x1, starting transfers between devices, local(): lax.ppermute(to_east, 'ew', [(i, (i + 1) % n_ew) for i in range(n_ew)])  2.99 us
    pallas_call x1, Pallas kernels, local(): call(pack_edges, [pl.BlockSpec(memory_space=pltpu.HBM)] * FIELDS, [(FIELD...  2.17 us
    ppermute x2, waiting for transfers between devices, swap(): return lax.ppermute(message, ('ew', 'ns'), partners(odd, n_ew, n_ns))  1.8 us
    ppermute x2, starting transfers between devices, swap(): return lax.ppermute(message, ('ew', 'ns'), partners(odd, n_ew, n_ns))  1.77 us
    pallas_call x1, Pallas kernels, local(): call(prepare, [vmem()] * 2, [(R - 4, 9) + row, (R, 3) + row, (4, R - 4) +...  1.67 us
  transfers between devices with their start and end apart: 4, of which 3 were waited for; matrix products, arithmetic and copies ran while one was open for 0% of the time, Pallas kernels for 29%

profile of v13, /device:TPU:0, one launch (start us, length us, event | category | flops | bytes accessed | tf_op | source)
XLA Modules:
  0.0 22.6 jit_solution(3336387226152688214)
XLA Ops:
  0.6 2.2 %shard_map.102 = (f32[7,16,32,128]{3,2,1,0:T(8,128)S(1)}, f32[4,544,128]{2,1,0:T(8,128)S(1)}, f32[7,32,128]{2,1,0:T(8,128)S(1)}, f32[104,128]{1,0:T(8,128)S(1)}, f32[104,128]{1,0:T(8,128)S(1)}) custom-call(f32[512,128]{1,0:T(8,128)} %bitcast.11, f32[512,128]{1,0:T(8,128)} %bitcast.12, f32[512,128]{1,0:T(8,128)} %bitcast.13, f32[512,128]{1,0:T(8,128)} %bitcast.14, ...), custom_call_target="tpu_custom_call" | custom-call | tf_op jit(solution)/shard_map/pallas_call | solution.py:619
  2.8 3.0 %collective-permute-start = (f32[104,128]{1,0:T(8,128)S(1)}, f32[104,128]{1,0:T(8,128)S(1)}, u32[]{:S(2)}, u32[]{:S(2)}) collective-permute-start(f32[104,128]{1,0:T(8,128)S(1)} %get-tuple-element.29), channel_id=1, source_target_pairs={{0,4},{4,8},{8,12},{12,16},{16,20},{20,24},{24,28},{28,0},{1,5},{5... | collective-permute-start | bytes 159752 | tf_op jit(solution)/shard_map/ppermute | solution.py:631
  5.8 3.1 %collective-permute-start.1 = (f32[104,128]{1,0:T(8,128)S(1)}, f32[104,128]{1,0:T(8,128)S(1)}, u32[]{:S(2)}, u32[]{:S(2)}) collective-permute-start(f32[104,128]{1,0:T(8,128)S(1)} %get-tuple-element.30), channel_id=1, source_target_pairs={{4,0},{8,4},{12,8},{16,12},{20,16},{24,20},{28,24},{0,28},{5,1},{9... | collective-permute-start | bytes 159752 | tf_op jit(solution)/shard_map/ppermute | solution.py:632
  8.9 1.7 %shard_map.103 = (f32[12,9,32,128]{3,2,1,0:T(8,128)S(1)}, f32[16,3,32,128]{3,2,1,0:T(8,128)S(1)}, f32[4,12,32,128]{3,2,1,0:T(8,128)S(1)}) custom-call(f32[7,16,32,128]{3,2,1,0:T(8,128)S(1)} %get-tuple-element.27.rows.refs_0_, f32[4,544,128]{2,1,0:T(8,128)S(1)} %get-tuple-element.31.raw.refs_1_), custom_call_target="tpu_custom_call" | custom-call | bytes 6291456 | tf_op jit(solution)/shard_map/pallas_call | solution.py:637
  10.6 0.4 %collective-permute-done.from_west = f32[104,128]{1,0:T(8,128)S(1)} collective-permute-done((f32[104,128]{1,0:T(8,128)S(1)}, f32[104,128]{1,0:T(8,128)S(1)}, u32[]{:S(2)}, u32[]{:S(2)}) %collective-permute-start) | collective-permute-done | bytes 53280 | tf_op jit(solution)/shard_map/ppermute | solution.py:631
  11.0 0.1 collective-permute-done.1.from_east
  11.1 0.2 shard_map.104
  11.3 1.4 %collective-permute-start.2 = (f32[27,32,128]{2,1,0:T(8,128)S(1)}, f32[27,32,128]{2,1,0:T(8,128)S(1)}, u32[]{:S(2)}, u32[]{:S(2)}) collective-permute-start(f32[27,32,128]{2,1,0:T(8,128)S(1)} %get-tuple-element.44), channel_id=1, source_target_pairs={{0,4},{1,2},{2,1},{3,7},{4,0},{5,6},{6,5},{7,3},{8,12},{9,10},{10,... | collective-permute-start | bytes 1327112 | tf_op jit(solution)/shard_map/ppermute | solution.py:635
  12.6 0.4 %collective-permute-start.3 = (f32[27,32,128]{2,1,0:T(8,128)S(1)}, f32[27,32,128]{2,1,0:T(8,128)S(1)}, u32[]{:S(2)}, u32[]{:S(2)}) collective-permute-start(f32[27,32,128]{2,1,0:T(8,128)S(1)} %get-tuple-element.45), channel_id=1, source_target_pairs={{0,1},{1,0},{2,3},{3,2},{4,5},{5,4},{6,7},{7,6},{8,9},{9,8},{10,11... | collective-permute-start | bytes 1327112 | tf_op jit(solution)/shard_map/ppermute | solution.py:635
  13.0 4.8 %shard_map.105 = (f32[16,9,32,128]{3,2,1,0:T(8,128)S(1)}, f32[4,12,48,128]{3,2,1,0:T(8,128)S(1)}, f32[4,4,32,128]{3,2,1,0:T(8,128)S(1)}, f32[4,8,32,128]{3,2,1,0...) custom-call(f32[7,16,32,128]{3,2,1,0:T(8,128)S(1)} %get-tuple-element.27.rows.refs_0_, ...), custom_call_target="tpu_custom_call" | custom-call | bytes 20971520 | tf_op jit(solution)/shard_map/pallas_call | solution.py:653
  17.8 1.8 %collective-permute-done.2.refs_10_ = f32[27,32,128]{2,1,0:T(8,128)S(1)} collective-permute-done((f32[27,32,128]{2,1,0:T(8,128)S(1)}, f32[27,32,128]{2,1,0:T(8,128)S(1)}, u32[]{:S(2)}, u32[]{:S(2)}) %collective-permute-start.2) | collective-permute-done | bytes 442400 | tf_op jit(solution)/shard_map/ppermute | solution.py:635
  19.6 0.0 collective-permute-done.3.refs_11_
  19.6 3.0 %shard_map.106 = (f32[512,128]{1,0:T(8,128)}, f32[512,128]{1,0:T(8,128)}, f32[512,128]{1,0:T(8,128)}, f32[512,128]{1,0:T(8,128)}) custom-call(f32[7,16,32,128]{3,2,1,0:T(8,128)S(1)} %get-tuple-element.27.rows.refs_0_, f32[7,32,128]{2,1,0:T(8,128)S(1)} %get-tuple-element.33.refs_4_.refs_1_, f32[12,9,32,128]{3,2,1,0:T(8,128)S(1)} %get-tuple-element.34.refs_5_.refs_2_, ...), custom_call_target="tpu_custom_call" | custom-call | bytes 20971520 | tf_op jit(solution)/shard_map/pallas_call | solution.py:666
Async XLA Ops:
  2.8 8.2 %collective-permute-start = (f32[104,128]{1,0:T(8,128)S(1)}, f32[104,128]{1,0:T(8,128)S(1)}, u32[]{:S(2)}, u32[]{:S(2)}) collective-permute-start(f32[104,128]{1,0:T(8,128)S(1)} %get-tuple-element.29), channel_id=1, source_target_pairs={{0,4},{4,8},{8,12},{12,16},{16,20},{20,24},{24,28},{28,0},{1,5},{5... | collective-permute-start | bytes 159752 | tf_op jit(solution)/shard_map/ppermute | solution.py:631
  5.8 5.3 %collective-permute-start.1 = (f32[104,128]{1,0:T(8,128)S(1)}, f32[104,128]{1,0:T(8,128)S(1)}, u32[]{:S(2)}, u32[]{:S(2)}) collective-permute-start(f32[104,128]{1,0:T(8,128)S(1)} %get-tuple-element.30), channel_id=1, source_target_pairs={{4,0},{8,4},{12,8},{16,12},{20,16},{24,20},{28,24},{0,28},{5,1},{9... | collective-permute-start | bytes 159752 | tf_op jit(solution)/shard_map/ppermute | solution.py:632
  11.3 8.4 %collective-permute-start.2 = (f32[27,32,128]{2,1,0:T(8,128)S(1)}, f32[27,32,128]{2,1,0:T(8,128)S(1)}, u32[]{:S(2)}, u32[]{:S(2)}) collective-permute-start(f32[27,32,128]{2,1,0:T(8,128)S(1)} %get-tuple-element.44), channel_id=1, source_target_pairs={{0,4},{1,2},{2,1},{3,7},{4,0},{5,6},{6,5},{7,3},{8,12},{9,10},{10,... | collective-permute-start | bytes 1327112 | tf_op jit(solution)/shard_map/ppermute | solution.py:635
  12.6 7.0 %collective-permute-start.3 = (f32[27,32,128]{2,1,0:T(8,128)S(1)}, f32[27,32,128]{2,1,0:T(8,128)S(1)}, u32[]{:S(2)}, u32[]{:S(2)}) collective-permute-start(f32[27,32,128]{2,1,0:T(8,128)S(1)} %get-tuple-element.45), channel_id=1, source_target_pairs={{0,1},{1,0},{2,3},{3,2},{4,5},{5,4},{6,7},{7,6},{8,9},{9,8},{10,11... | collective-permute-start | bytes 1327112 | tf_op jit(solution)/shard_map/ppermute | solution.py:635

commit v14 on v13

--- a/solution.py
+++ b/solution.py
@@ -18,11 +18,11 @@
 U, V, M = 4, 5, 6
 PAIRS = ((0, 1), (2, 3), (U, M))
 EDGE_ROWS = len(PAIRS) * K + 8
-SIDE_BLOCKS = 27
+SIDE_BLOCKS = 26
 ROWS_AT = (0, 4, 8, 12, 24, 16, 20)
-CORNERS_AT = 26
 SOUTH, NORTH = 0, 1
 MIB = 1 << 20
+FLOPS_PER_US = 1.15e9
 
 
 def lanes():
@@ -71,7 +71,17 @@
         target[pl.ds(len(PAIRS) * K, 8)] = block
 
 
-def pack_sides(rows, own, from_west, from_east, _, left, right, merged, second, first):
+def pack_sides(rows, second, first):
+    odd = lax.axis_index("ns") % 2
+    for out, north in ((second, odd), (first, 1 - odd)):
+        for f in range(FIELDS):
+            count = 2 if f == U else HALO
+            start = (R - count) * north
+            for r in range(count):
+                out[ROWS_AT[f] + r] = rows[f, start + r]
+
+
+def pack_corners(own, from_west, from_east, _, left, right, merged, second, first):
     odd = lax.axis_index("ns") % 2
     lane = lanes()
     west_half = lane % G < HALO
@@ -90,17 +100,12 @@
         right[f] = jnp.where(west_half, own[f], b)
         merged[f] = jnp.where(west_half, a, b)
     for out, north in ((second, odd), (first, 1 - odd)):
-        for f in range(FIELDS):
-            count = 2 if f == U else HALO
-            start = (R - count) * north
-            for r in range(count):
-                out[ROWS_AT[f] + r] = rows[f, start + r]
         block = jnp.zeros((K, W), F32)
         for f in range(FIELDS):
             amount = lax.rem(2 * G * f + W - (W - 2 * G) * north, W)
             moved = pltpu.roll(merged[f], amount, 1)
             block = jnp.where(lane // (2 * G) == f, moved, block)
-        out[CORNERS_AT] = block
+        out[...] = block
 
 
 def coefficients(speed, mask):
@@ -467,9 +472,9 @@
 
 def boundary(*refs):
     rows, merged, y_in, level_in, x_in, c1_in, part1_in, c2_in, part2_in, edge_in = refs[:10]
-    second, first = refs[10:12]
-    outs = refs[12:16]
-    sides, x_new, y_new, level_new, c1_new, merged1, beyond, halos = refs[16:]
+    second, first, second_corners, first_corners = refs[10:14]
+    outs = refs[14:18]
+    sides, corners, x_new, y_new, level_new, c1_new, merged1, beyond, halos = refs[18:]
     lane = lanes()
     place = lax.axis_index("ns")
     last = lax.axis_size("ns") - 1
@@ -485,6 +490,10 @@
 
     lax.fori_loop(0, SIDE_BLOCKS, unpack, 0, unroll=2)
 
+    for message, side in ((second_corners, odd), (first_corners, 1 - odd)):
+        here = jnp.where(side == NORTH, place < last, place > 0)
+        corners[side] = jnp.where(here, message[...], 0.0)
+
     def row(f, j):
         if j < 0:
             return sides.at[SOUTH, ROWS_AT[f] + j + (2 if f == U else HALO)]
@@ -493,8 +502,8 @@
         return rows.at[f, j]
 
     for f in range(FIELDS):
-        south = turn(sides[SOUTH, CORNERS_AT], W - 2 * G - 2 * G * f)
-        north = turn(sides[NORTH, CORNERS_AT], -2 * G * f)
+        south = turn(corners[SOUTH], W - 2 * G - 2 * G * f)
+        north = turn(corners[NORTH], -2 * G * f)
         beyond[f] = jnp.where(lane >= W // 2, south, north)
     for f in range(4):
         for i in range(2, 6):
@@ -586,7 +595,7 @@
     return pl.BlockSpec(memory_space=pltpu.VMEM)
 
 
-def call(kernel, in_specs, out_shapes, scratch=(), limit=16 * MIB, cost=0.0):
+def call(kernel, in_specs, out_shapes, scratch=(), limit=16 * MIB, cost=0.1):
     return pl.pallas_call(
         kernel,
         out_shape=[jax.ShapeDtypeStruct(shape, F32) for shape in out_shapes],
@@ -594,7 +603,7 @@
         out_specs=[vmem()] * len(out_shapes),
         scratch_shapes=list(scratch),
         compiler_params=pltpu.CompilerParams(vmem_limit_bytes=limit),
-        cost_estimate=pl.CostEstimate(flops=0, bytes_accessed=int(cost * MIB), transcendentals=0),
+        cost_estimate=pl.CostEstimate(flops=int(cost * FLOPS_PER_US), bytes_accessed=MIB, transcendentals=0),
     )
 
 
@@ -625,6 +634,7 @@
             pltpu.VMEM((K * R, W), jnp.int32),
             pltpu.SemaphoreType.DMA((FIELDS,)),
         ],
+        cost=2.2,
     )(*[pltpu.with_memory_space_constraint(a, pltpu.HBM) for a in flat])
 
     n_ew, n_ns = lax.axis_size("ew"), lax.axis_size("ns")
@@ -633,22 +643,26 @@
 
     def swap(odd, message):
         return lax.ppermute(message, ("ew", "ns"), partners(odd, n_ew, n_ns))
+
+    second, first = call(pack_sides, [vmem()], [(SIDE_BLOCKS,) + row] * 2, cost=0.1)(rows)
+    second = swap(1, second)
+    first = swap(0, first)
 
     y_in, level, base = call(
         prepare,
         [vmem()] * 2,
         [(R - 4, 9) + row, (R, 3) + row, (4, R - 4) + row],
-        cost=6,
+        cost=1.7,
     )(rows, raw)
 
-    left, right, merged, second, first = call(
-        pack_sides,
-        [vmem()] * 4 + [pl.BlockSpec(memory_space=pl.ANY)],
-        [(FIELDS,) + row] * 3 + [(SIDE_BLOCKS,) + row] * 2,
-        cost=1,
-    )(rows, own, from_west, from_east, level)
-    second = swap(1, second)
-    first = swap(0, first)
+    left, right, merged, second_corners, first_corners = call(
+        pack_corners,
+        [vmem()] * 3 + [pl.BlockSpec(memory_space=pl.ANY)],
+        [(FIELDS,) + row] * 3 + [row] * 2,
+        cost=0.2,
+    )(own, from_west, from_east, level)
+    second_corners = swap(1, second_corners)
+    first_corners = swap(0, first_corners)
 
     x_in, c1, part1, c2, part2, edge = call(
         interior,
@@ -660,15 +674,16 @@
             pltpu.VMEM((4, 4) + row, F32),
             pltpu.VMEM((4, 2) + row, F32),
         ],
-        cost=20,
+        cost=4.7,
     )(rows, raw, left, right, merged, y_in, level, base)
 
     outs = call(
         boundary,
-        [vmem()] * 12,
+        [vmem()] * 14,
         [(K * R, W)] * 4,
         [
             pltpu.VMEM((2, SIDE_BLOCKS) + row, F32),
+            pltpu.VMEM((2,) + row, F32),
             pltpu.VMEM((8, 9) + row, F32),
             pltpu.VMEM((8, 9) + row, F32),
             pltpu.VMEM((8, 3) + row, F32),
@@ -677,10 +692,10 @@
             pltpu.VMEM((FIELDS,) + row, F32),
             pltpu.VMEM((4, 4) + row, F32),
         ],
-        cost=20,
+        cost=2.9,
     )(
         *(rows, merged, y_in, level, x_in, c1, part1, c2, part2, edge),
-        *(second, first),
+        *(second, first, second_corners, first_corners),
     )
     return tuple(a.reshape(K, R, W) for a in outs)
 

time: 22.8 us -> 21.1 us (0.925)
  waiting for transfers between devices: 2.3 us -> 0.02 us
  starting transfers between devices: 7.86 us -> 8.27 us
    ppermute x2 -> x4, waiting for transfers between devices: 1.8 us -> 0.01 us  [swap(): return lax.ppermute(message, ('ew', 'ns'), partners(odd, n_ew, n_ns))]
    ppermute x1, waiting for transfers between devices: 0.44 us -> 0.01 us  [local(): lax.ppermute(to_east, 'ew', [(i, (i + 1) % n_ew) for i in range(n_ew)])]
    ppermute x2 -> x4, starting transfers between devices: 1.77 us -> 2.18 us  [swap(): return lax.ppermute(message, ('ew', 'ns'), partners(odd, n_ew, n_ns))]
    pallas_call x2 -> x3, Pallas kernels: 3.18 us -> 3.25 us  [the longest x1 3.02 us: local(): call(boundary, [vmem()] * 14, [(K * R, W)] * 4, [pltpu.VMEM((2, SIDE_BLOC...]
  transfers between devices with their start and end apart: 4 -> 6, of which waited for: 3 -> 0; matrix products, arithmetic and copies ran while one was open for 0% -> 0% of each run, Pallas kernels for 29% -> 32%
where the time goes in v14:
time: 21.1 us; the launch traced here: 20.9 us
  Pallas kernels  11.9 us (56%)
  starting transfers between devices  8.27 us (39%)
  between operations  0.72 us (3%)
    pallas_call x1, Pallas kernels, local(): call(interior, [vmem()] * 8, [(R, 9) + row, (4, R - 4, TALL, W), (4, 4) +...  4.8 us
    ppermute x1, starting transfers between devices, local(): lax.ppermute(to_west, 'ew', [((i + 1) % n_ew, i) for i in range(n_ew)])  3.1 us
    pallas_call x1, Pallas kernels, local(): call(boundary, [vmem()] * 14, [(K * R, W)] * 4, [pltpu.VMEM((2, SIDE_BLOC...  3.02 us
    ppermute x1, starting transfers between devices, local(): lax.ppermute(to_east, 'ew', [(i, (i + 1) % n_ew) for i in range(n_ew)])  2.99 us
    ppermute x4, starting transfers between devices, swap(): return lax.ppermute(message, ('ew', 'ns'), partners(odd, n_ew, n_ns))  2.18 us
    pallas_call x1, Pallas kernels, local(): call(pack_edges, [pl.BlockSpec(memory_space=pltpu.HBM)] * FIELDS, [(FIELD...  2.17 us
    pallas_call x1, Pallas kernels, local(): call(prepare, [vmem()] * 2, [(R - 4, 9) + row, (R, 3) + row, (4, R - 4) +...  1.67 us
  transfers between devices with their start and end apart: 6, of which 0 were waited for; matrix products, arithmetic and copies ran while one was open for 0% of the time, Pallas kernels for 32%

profile of v14, /device:TPU:0, one launch (start us, length us, event | category | flops | bytes accessed | tf_op | source)
XLA Modules:
  0.0 20.9 jit_solution(15598781300129048197)
XLA Ops:
  0.6 2.2 %shard_map.102 = (f32[7,16,32,128]{3,2,1,0:T(8,128)S(1)}, f32[4,544,128]{2,1,0:T(8,128)S(1)}, f32[7,32,128]{2,1,0:T(8,128)S(1)}, f32[104,128]{1,0:T(8,128)S(1)}, f32[104,128]{1,0:T(8,128)S(1)}) custom-call(f32[512,128]{1,0:T(8,128)} %bitcast.11, f32[512,128]{1,0:T(8,128)} %bitcast.12, f32[512,128]{1,0:T(8,128)} %bitcast.13, f32[512,128]{1,0:T(8,128)} %bitcast.14, ...), custom_call_target="tpu_custom_call" | custom-call | flops 2529999872 | bytes 1048576 | tf_op jit(solution)/shard_map/pallas_call | solution.py:628
  2.8 3.0 %collective-permute-start = (f32[104,128]{1,0:T(8,128)S(1)}, f32[104,128]{1,0:T(8,128)S(1)}, u32[]{:S(2)}, u32[]{:S(2)}) collective-permute-start(f32[104,128]{1,0:T(8,128)S(1)} %get-tuple-element.31), channel_id=1, source_target_pairs={{0,4},{4,8},{8,12},{12,16},{16,20},{20,24},{24,28},{28,0},{1,5},{5... | collective-permute-start | bytes 159752 | tf_op jit(solution)/shard_map/ppermute | solution.py:641
  5.8 3.1 %collective-permute-start.1 = (f32[104,128]{1,0:T(8,128)S(1)}, f32[104,128]{1,0:T(8,128)S(1)}, u32[]{:S(2)}, u32[]{:S(2)}) collective-permute-start(f32[104,128]{1,0:T(8,128)S(1)} %get-tuple-element.32), channel_id=1, source_target_pairs={{4,0},{8,4},{12,8},{16,12},{20,16},{24,20},{28,24},{0,28},{5,1},{9... | collective-permute-start | bytes 159752 | tf_op jit(solution)/shard_map/ppermute | solution.py:642
  8.9 0.1 shard_map.106
  9.0 0.1 collective-permute-start.2
  9.0 1.7 %collective-permute-start.3 = (f32[26,32,128]{2,1,0:T(8,128)S(1)}, f32[26,32,128]{2,1,0:T(8,128)S(1)}, u32[]{:S(2)}, u32[]{:S(2)}) collective-permute-start(f32[26,32,128]{2,1,0:T(8,128)S(1)} %get-tuple-element.47), channel_id=1, source_target_pairs={{0,1},{1,0},{2,3},{3,2},{4,5},{5,4},{6,7},{7,6},{8,9},{9,8},{10,11... | collective-permute-start | bytes 1277960 | tf_op jit(solution)/shard_map/ppermute | solution.py:645
  10.8 1.7 %shard_map.103 = (f32[12,9,32,128]{3,2,1,0:T(8,128)S(1)}, f32[16,3,32,128]{3,2,1,0:T(8,128)S(1)}, f32[4,12,32,128]{3,2,1,0:T(8,128)S(1)}) custom-call(f32[7,16,32,128]{3,2,1,0:T(8,128)S(1)} %get-tuple-element.29.rows.refs_0_, f32[4,544,128]{2,1,0:T(8,128)S(1)} %get-tuple-element.33.raw.refs_1_), custom_call_target="tpu_custom_call" | custom-call | flops 1955000064 | bytes 1048576 | tf_op jit(solution)/shard_map/pallas_call | solution.py:651
  12.5 0.0 collective-permute-done.from_west
  12.5 0.0 collective-permute-done.1.from_east
  12.5 0.2 shard_map.104
  12.7 0.3 %collective-permute-start.4 = (f32[32,128]{1,0:T(8,128)S(1)}, f32[32,128]{1,0:T(8,128)S(1)}, u32[]{:S(2)}, u32[]{:S(2)}) collective-permute-start(f32[32,128]{1,0:T(8,128)S(1)} %get-tuple-element.48), channel_id=1, source_target_pairs={{0,4},{1,2},{2,1},{3,7},{4,0},{5,6},{6,5},{7,3},{8,12},{9,10},{10,... | collective-permute-start | bytes 49160 | tf_op jit(solution)/shard_map/ppermute | solution.py:645
  13.0 0.0 collective-permute-start.5
  13.0 4.8 %shard_map.105 = (f32[16,9,32,128]{3,2,1,0:T(8,128)S(1)}, f32[4,12,48,128]{3,2,1,0:T(8,128)S(1)}, f32[4,4,32,128]{3,2,1,0:T(8,128)S(1)}, f32[4,8,32,128]{3,2,1,0...) custom-call(f32[7,16,32,128]{3,2,1,0:T(8,128)S(1)} %get-tuple-element.29.rows.refs_0_, ...), custom_call_target="tpu_custom_call" | custom-call | flops 5405000192 | bytes 1048576 | tf_op jit(solution)/shard_map/pallas_call | solution.py:667
  17.8 0.0 collective-permute-done.4.refs_12_
  17.8 0.0 collective-permute-done.5.refs_13_
  17.9 0.0 collective-permute-done.2.refs_10_
  17.9 0.0 collective-permute-done.3.refs_11_
  17.9 3.0 %shard_map.107 = (f32[512,128]{1,0:T(8,128)}, f32[512,128]{1,0:T(8,128)}, f32[512,128]{1,0:T(8,128)}, f32[512,128]{1,0:T(8,128)}) custom-call(f32[7,16,32,128]{3,2,1,0:T(8,128)S(1)} %get-tuple-element.29.rows.refs_0_, f32[7,32,128]{2,1,0:T(8,128)S(1)} %get-tuple-element.35.refs_4_.refs_1_, f32[12,9,32,128]{3,2,1,0:T(8,128)S(1)} %get-tuple-element.36.refs_5_.refs_2_, ...), custom_call_target="tpu_custom_call" | custom-call | flops 3335000064 | bytes 1048576 | tf_op jit(solution)/shard_map/pallas_call | solution.py:680
Async XLA Ops:
  2.8 9.7 %collective-permute-start = (f32[104,128]{1,0:T(8,128)S(1)}, f32[104,128]{1,0:T(8,128)S(1)}, u32[]{:S(2)}, u32[]{:S(2)}) collective-permute-start(f32[104,128]{1,0:T(8,128)S(1)} %get-tuple-element.31), channel_id=1, source_target_pairs={{0,4},{4,8},{8,12},{12,16},{16,20},{20,24},{24,28},{28,0},{1,5},{5... | collective-permute-start | bytes 159752 | tf_op jit(solution)/shard_map/ppermute | solution.py:641
  5.8 6.7 %collective-permute-start.1 = (f32[104,128]{1,0:T(8,128)S(1)}, f32[104,128]{1,0:T(8,128)S(1)}, u32[]{:S(2)}, u32[]{:S(2)}) collective-permute-start(f32[104,128]{1,0:T(8,128)S(1)} %get-tuple-element.32), channel_id=1, source_target_pairs={{4,0},{8,4},{12,8},{16,12},{20,16},{24,20},{28,24},{0,28},{5,1},{9... | collective-permute-start | bytes 159752 | tf_op jit(solution)/shard_map/ppermute | solution.py:642
  9.0 8.9 %collective-permute-start.2 = (f32[26,32,128]{2,1,0:T(8,128)S(1)}, f32[26,32,128]{2,1,0:T(8,128)S(1)}, u32[]{:S(2)}, u32[]{:S(2)}) collective-permute-start(f32[26,32,128]{2,1,0:T(8,128)S(1)} %get-tuple-element.46), channel_id=1, source_target_pairs={{0,4},{1,2},{2,1},{3,7},{4,0},{5,6},{6,5},{7,3},{8,12},{9,10},{10,... | collective-permute-start | bytes 1277960 | tf_op jit(solution)/shard_map/ppermute | solution.py:645
  9.0 8.8 %collective-permute-start.3 = (f32[26,32,128]{2,1,0:T(8,128)S(1)}, f32[26,32,128]{2,1,0:T(8,128)S(1)}, u32[]{:S(2)}, u32[]{:S(2)}) collective-permute-start(f32[26,32,128]{2,1,0:T(8,128)S(1)} %get-tuple-element.47), channel_id=1, source_target_pairs={{0,1},{1,0},{2,3},{3,2},{4,5},{5,4},{6,7},{7,6},{8,9},{9,8},{10,11... | collective-permute-start | bytes 1277960 | tf_op jit(solution)/shard_map/ppermute | solution.py:645
  12.7 5.2 %collective-permute-start.4 = (f32[32,128]{1,0:T(8,128)S(1)}, f32[32,128]{1,0:T(8,128)S(1)}, u32[]{:S(2)}, u32[]{:S(2)}) collective-permute-start(f32[32,128]{1,0:T(8,128)S(1)} %get-tuple-element.48), channel_id=1, source_target_pairs={{0,4},{1,2},{2,1},{3,7},{4,0},{5,6},{6,5},{7,3},{8,12},{9,10},{10,... | collective-permute-start | bytes 49160 | tf_op jit(solution)/shard_map/ppermute | solution.py:645
  13.0 4.8 %collective-permute-start.5 = (f32[32,128]{1,0:T(8,128)S(1)}, f32[32,128]{1,0:T(8,128)S(1)}, u32[]{:S(2)}, u32[]{:S(2)}) collective-permute-start(f32[32,128]{1,0:T(8,128)S(1)} %get-tuple-element.49), channel_id=1, source_target_pairs={{0,1},{1,0},{2,3},{3,2},{4,5},{5,4},{6,7},{7,6},{8,9},{9,8},{10,11... | collective-permute-start | bytes 49160 | tf_op jit(solution)/shard_map/ppermute | solution.py:645

commit v15 on v14

--- a/solution.py
+++ b/solution.py
@@ -175,6 +175,8 @@
 
     def issue(item):
         job, q = item
+        if q == 0 and "ahead" in job:
+            job["ahead"]()
         if "x" not in job:
             return None
         halo = job["x"][1]
@@ -264,31 +266,24 @@
     return results
 
 
-def y_coefficients_at(row, j):
-    return coefficients(
-        {d: row(V, j + d)[...] for d in (-2, -1, 0, 1)},
-        {d: row(M, j + d)[...] for d in (-2, -1, 0, 1, 2)},
-    )
+def y_coefficients(low, high, load, emit):
+    for q in range(K // 8):
+        w = {}
+        for j in range(low - 2, high + 2):
+            opened = load(M, j, q) * load(M, j + 1, q)
+            s = scaled(load(V, j, q), opened)
+            a = jnp.abs(s)
+            even, odd = 7.0 * s, 3.0 * a + horizontal_mix * opened
+            w[j] = (-(s + a), even + odd, even - odd, a - s)
+            if j > low:
+                at = [w[j - 3], w[j - 2], w[j - 1], w[j]]
+                forward = [at[1][0], at[1][1] - at[2][0], at[1][3] - at[2][2], -at[2][3]]
+                transposed = [-at[0][3], at[0][3] - at[1][2], at[2][1] - at[3][0], at[3][0]]
+                emit(j - 1, q, forward + transposed + [at[1][2] - at[2][1]])
 
 
 def by_fours(start, stop, body):
     def four(i, carry):
-        body([start + 4 * i + k for k in range(4)])
-        return carry
-
-    lax.fori_loop(0, (stop - start) // 4, four, 0)
-
-
-def by_fours_packed(start, stop, body, packed, turned, halos):
-    for f, source in enumerate(packed):
-        turned[f] = turn(source, -G * start)
-
-    def four(i, carry):
-        for f in range(len(packed)):
-            for k in range(4):
-                halos[k, f] = turn(turned[f], -HALO - G * k)
-        for f in range(len(packed)):
-            turned[f] = turn(turned[f], -4 * G)
         body([start + 4 * i + k for k in range(4)])
         return carry
 
@@ -329,13 +324,11 @@
 
     by_fours(0, R, levels)
 
-    def across(js):
-        for j in js:
-            got = y_coefficients_at(lambda f, r: rows.at[f, r], j)
-            for k in range(9):
-                y_out[j - 2, k] = got[k]
-
-    by_fours(2, R - 2, across)
+    def emit(j, q, values):
+        for k in range(9):
+            y_out.at[j - 2, k][chunk(q)] = values[k]
+
+    y_coefficients(2, R - 3, lambda f, j, q: rows.at[f, j][chunk(q)], emit)
 
     def first(js):
         def job(j):
@@ -356,7 +349,7 @@
 
 def interior(*refs):
     rows, raw, left, right, merged, y_in, level_in, base_in = refs[:8]
-    x_out, c1_out, part1_out, c2_out, part2_out, edge_out, merged1, turned, halos, faces_now = refs[8:]
+    x_out, c1_out, part1_out, c2_out, part2_out, edge_out, merged1, halos, faces_now = refs[8:]
     lane = lanes()
     west_half = lane % G < HALO
     for f in range(4):
@@ -366,30 +359,41 @@
     halo_s = jnp.where(west_half, faces[0][0], faces[1][0])
     halo_mixed = jnp.where(west_half, faces[0][1], right[M])
 
-    def x_body(js):
-        for k, j in enumerate(js):
+    def x_halos(j):
+        if j < R:
+            halos[j, 0] = halo_columns(halo_s, j)
+            halos[j, 1] = halo_columns(halo_mixed, j)
+
+    def x_faces(j):
+        if j < R:
             m = rows[M, j]
-            opened = m * shifted(m, halos[k, 1], 1, lane)
-            faces_now[k, 0] = scaled(rows[U, j], opened)
-            faces_now[k, 1] = opened
-
-        def issue(item):
-            k, q = item
-            s, opened = faces_now.at[k, 0][chunk(q)], faces_now.at[k, 1][chunk(q)]
-            hs, hm = halos.at[k, 0][chunk(q)], halos.at[k, 1][chunk(q)]
-            return (
-                {d: shifted(s, hs, d, lane[:8]) for d in (-2, -1, 0, 1)},
-                {-1: shifted(opened, hm, -1, lane[:8]), 0: opened},
-            )
-
-        def finish(item, faces_here):
-            k, q = item
-            for i, value in enumerate(face_coefficients(*faces_here)):
-                x_out.at[js[k], i][chunk(q)] = value
-
-        pipeline([(k, q) for k in range(4) for q in range(K // 8)], issue, finish, 2)
-
-    by_fours_packed(0, R, x_body, (halo_s, halo_mixed), turned, halos)
+            opened = m * shifted(m, halos[j, 1], 1, lane)
+            faces_now[j, 0] = scaled(rows[U, j], opened)
+            faces_now[j, 1] = opened
+
+    for j in range(4):
+        x_halos(j)
+    for j in range(2):
+        x_faces(j)
+
+    def issue(item):
+        j, q = item
+        if q == 0:
+            x_halos(j + 4)
+            x_faces(j + 2)
+        s, opened = faces_now.at[j, 0][chunk(q)], faces_now.at[j, 1][chunk(q)]
+        hs, hm = halos.at[j, 0][chunk(q)], halos.at[j, 1][chunk(q)]
+        return (
+            {d: shifted(s, hs, d, lane[:8]) for d in (-2, -1, 0, 1)},
+            {-1: shifted(opened, hm, -1, lane[:8]), 0: opened},
+        )
+
+    def finish(item, faces_here):
+        j, q = item
+        for i, value in enumerate(face_coefficients(*faces_here)):
+            x_out.at[j, i][chunk(q)] = value
+
+    pipeline([(j, q) for j in range(R) for q in range(K // 8)], issue, finish, 2)
 
     partial = [edge_columns_and_levels(e, *f) for e, f in zip((left, right), faces)]
     across = edge_rows(merged, lambda f: merged[f])
@@ -398,76 +402,57 @@
         edge_out[f] = edge
         merged1[f] = edge + across[f]
 
-    def kept(k):
-        return lambda f, q: halos.at[k, f][chunk(q)]
-
-    def keep(rows_now, source):
-        for f in range(4):
-            for k, j in enumerate(rows_now):
-                halos[k, f] = halo_columns(source[f], j)
-
-    def first(js):
-        def job(k, j):
-            def store(f, q, value):
+    def kept(j):
+        return lambda f, q: halos.at[j, f][chunk(q)]
+
+    def run(jobs, source):
+        js = list(jobs)
+
+        def keep(k):
+            if k < len(js):
+                for f in range(4):
+                    halos[js[k], f] = halo_columns(source[f], js[k])
+
+        keep(0)
+        keep(1)
+        step_rows([job | dict(ahead=lambda k=k: keep(k + 2)) for k, job in enumerate(jobs.values())])
+
+    def first(j):
+        def store(f, q, value):
+            if j in ends1:
+                part1_out.at[f, ends1.index(j)][chunk(q)] = value
+            else:
                 c1_out.at[f, j - 2][moved_chunk(q)] = value
 
-            return dict(
-                store=store,
-                load=lambda f, d, q: rows.at[f, j][chunk(q)],
-                x=(x_out.at[j], kept(k)),
-                base=lambda f, q: base_in.at[f, j - 2][chunk(q)],
-            )
-
-        step_rows([job(k, j) for k, j in enumerate(js)])
-
-    by_fours_packed(2, R - 2, first, [merged[f] for f in range(4)], turned, halos)
-
-    def first_part(i, j):
-        def store(f, q, value):
-            part1_out.at[f, i][chunk(q)] = value
-
-        return dict(
+        job = dict(
             store=store,
             load=lambda f, d, q: rows.at[f, j][chunk(q)],
-            x=(x_out.at[j], kept(i)),
-            z=(level_in.at[j], raw_levels(raw, j)),
+            x=(x_out.at[j], kept(j)),
         )
-
-    ends = (0, 1, R - 2, R - 1)
-    keep(ends, merged)
-    step_rows([first_part(i, j) for i, j in enumerate(ends)])
-
-    def second(js):
-        def job(k, j):
-            def store(f, q, value):
+        if j in ends1:
+            return job | dict(z=(level_in.at[j], raw_levels(raw, j)))
+        return job | dict(base=lambda f, q: base_in.at[f, j - 2][chunk(q)])
+
+    ends1 = (0, 1, R - 2, R - 1)
+    run({j: first(j) for j in range(R)}, merged)
+
+    def second(j):
+        def store(f, q, value):
+            if j in ends2:
+                part2_out.at[f, ends2.index(j)][chunk(q)] = value
+            else:
                 c2_out.at[f, j - 4][chunk(q)] = value
 
-            return dict(
-                store=store,
-                load=lambda f, d, q: c1_out.at[f, j - 2 + d][moved_chunk(q)],
-                x=(x_out.at[j], kept(k)),
-                y=y_in.at[j - 2],
-                z=(level_in.at[j], moved_levels(lambda f: c1_out.at[f, j - 2])),
-            )
-
-        step_rows([job(k, j) for k, j in enumerate(js)])
-
-    by_fours_packed(4, R - 4, second, [merged1[f] for f in range(4)], turned, halos)
-
-    def second_part(i, j):
-        def store(f, q, value):
-            part2_out.at[f, i][chunk(q)] = value
-
-        return dict(
+        job = dict(
             store=store,
-            load=lambda f, d, q: c1_out.at[f, j - 2][moved_chunk(q)],
-            x=(x_out.at[j], kept(i)),
+            load=lambda f, d, q: c1_out.at[f, j - 2 + d][moved_chunk(q)],
+            x=(x_out.at[j], kept(j)),
             z=(level_in.at[j], moved_levels(lambda f: c1_out.at[f, j - 2])),
         )
-
-    ends = (2, 3, R - 4, R - 3)
-    keep(ends, merged1)
-    step_rows([second_part(i, j) for i, j in enumerate(ends)])
+        return job if j in ends2 else job | dict(y=y_in.at[j - 2])
+
+    ends2 = (2, 3, R - 4, R - 3)
+    run({j: second(j) for j in range(2, R - 2)}, merged1)
 
 
 def boundary(*refs):
@@ -515,10 +500,14 @@
     def halo_beyond(f, j):
         return halo_columns(beyond[f], j % R)
 
+    def emit(j, q, values):
+        for k in range(9):
+            y_new.at[new_at[j], k][chunk(q)] = values[k]
+
+    for low in (-2, R - 2):
+        y_coefficients(low, low + 3, lambda f, j, q: row(f, j)[chunk(q)], emit)
+
     for j in near:
-        got = y_coefficients_at(row, j)
-        for k in range(9):
-            y_new[new_at[j], k] = got[k]
         if not 0 <= j < R:
             got = x_coefficients(
                 row(U, j)[...], halo_beyond(U, j), row(M, j)[...], halo_beyond(M, j), lane
@@ -670,9 +659,8 @@
         [(R, 9) + row, (4, R - 4, TALL, W), (4, 4) + row, (4, R - 8) + row, (4, 4) + row, (4,) + row],
         [
             pltpu.VMEM((4,) + row, F32),
-            pltpu.VMEM((4,) + row, F32),
-            pltpu.VMEM((4, 4) + row, F32),
-            pltpu.VMEM((4, 2) + row, F32),
+            pltpu.VMEM((R, 4) + row, F32),
+            pltpu.VMEM((R, 2) + row, F32),
         ],
         cost=4.7,
     )(rows, raw, left, right, merged, y_in, level, base)

time: 21.1 us -> 20.5 us (0.972)
  Pallas kernels: 11.9 us -> 10.6 us
  waiting for transfers between devices: 0.02 us -> 0.81 us
    pallas_call x1, Pallas kernels: 4.8 us -> 3.51 us  [local(): call(interior, [vmem()] * 8, [(R, 9) + row, (4, R - 4, TALL, W), (4, 4) +...]
    ppermute x4, waiting for transfers between devices: 0.01 us -> 0.8 us  [swap(): return lax.ppermute(message, ('ew', 'ns'), partners(odd, n_ew, n_ns))]
  transfers between devices with their start and end apart: 6 -> 6, of which waited for: 0 -> 1; matrix products, arithmetic and copies ran while one was open for 0% -> 0% of each run, Pallas kernels for 32% -> 27%
where the time goes in v15:
time: 20.5 us; the launch traced here: 20.3 us
  Pallas kernels  10.6 us (52%)
  starting transfers between devices  8.26 us (40%)
  waiting for transfers between devices  0.81 us (4%)
  between operations  0.69 us (3%)
    pallas_call x1, Pallas kernels, local(): call(interior, [vmem()] * 8, [(R, 9) + row, (4, R - 4, TALL, W), (4, 4) +...  3.51 us
    ppermute x1, starting transfers between devices, local(): lax.ppermute(to_west, 'ew', [((i + 1) % n_ew, i) for i in range(n_ew)])  3.1 us
    ppermute x1, starting transfers between devices, local(): lax.ppermute(to_east, 'ew', [(i, (i + 1) % n_ew) for i in range(n_ew)])  2.99 us
    pallas_call x1, Pallas kernels, local(): call(boundary, [vmem()] * 14, [(K * R, W)] * 4, [pltpu.VMEM((2, SIDE_BLOC...  2.99 us
    pallas_call x1, Pallas kernels, local(): call(pack_edges, [pl.BlockSpec(memory_space=pltpu.HBM)] * FIELDS, [(FIELD...  2.17 us
    ppermute x4, starting transfers between devices, swap(): return lax.ppermute(message, ('ew', 'ns'), partners(odd, n_ew, n_ns))  2.16 us
    pallas_call x1, Pallas kernels, local(): call(prepare, [vmem()] * 2, [(R - 4, 9) + row, (R, 3) + row, (4, R - 4) +...  1.68 us
    ppermute x4, waiting for transfers between devices, swap(): return lax.ppermute(message, ('ew', 'ns'), partners(odd, n_ew, n_ns))  0.8 us
  transfers between devices with their start and end apart: 6, of which 1 were waited for; matrix products, arithmetic and copies ran while one was open for 0% of the time, Pallas kernels for 27%

profile of v15, /device:TPU:0, one launch (start us, length us, event | category | flops | bytes accessed | tf_op | source)
XLA Modules:
  0.0 20.3 jit_solution(1042636779374483535)
XLA Ops:
  0.6 2.2 %shard_map.102 = (f32[7,16,32,128]{3,2,1,0:T(8,128)S(1)}, f32[4,544,128]{2,1,0:T(8,128)S(1)}, f32[7,32,128]{2,1,0:T(8,128)S(1)}, f32[104,128]{1,0:T(8,128)S(1)}, f32[104,128]{1,0:T(8,128)S(1)}) custom-call(f32[512,128]{1,0:T(8,128)} %bitcast.11, f32[512,128]{1,0:T(8,128)} %bitcast.12, f32[512,128]{1,0:T(8,128)} %bitcast.13, f32[512,128]{1,0:T(8,128)} %bitcast.14, ...), custom_call_target="tpu_custom_call" | custom-call | flops 2529999872 | bytes 1048576 | tf_op jit(solution)/shard_map/pallas_call | solution.py:617
  2.8 3.0 %collective-permute-start = (f32[104,128]{1,0:T(8,128)S(1)}, f32[104,128]{1,0:T(8,128)S(1)}, u32[]{:S(2)}, u32[]{:S(2)}) collective-permute-start(f32[104,128]{1,0:T(8,128)S(1)} %get-tuple-element.31), channel_id=1, source_target_pairs={{0,4},{4,8},{8,12},{12,16},{16,20},{20,24},{24,28},{28,0},{1,5},{5... | collective-permute-start | bytes 159752 | tf_op jit(solution)/shard_map/ppermute | solution.py:630
  5.8 3.1 %collective-permute-start.1 = (f32[104,128]{1,0:T(8,128)S(1)}, f32[104,128]{1,0:T(8,128)S(1)}, u32[]{:S(2)}, u32[]{:S(2)}) collective-permute-start(f32[104,128]{1,0:T(8,128)S(1)} %get-tuple-element.32), channel_id=1, source_target_pairs={{4,0},{8,4},{12,8},{16,12},{20,16},{24,20},{28,24},{0,28},{5,1},{9... | collective-permute-start | bytes 159752 | tf_op jit(solution)/shard_map/ppermute | solution.py:631
  8.9 0.1 shard_map.106
  9.0 0.1 collective-permute-start.2
  9.0 1.7 %collective-permute-start.3 = (f32[26,32,128]{2,1,0:T(8,128)S(1)}, f32[26,32,128]{2,1,0:T(8,128)S(1)}, u32[]{:S(2)}, u32[]{:S(2)}) collective-permute-start(f32[26,32,128]{2,1,0:T(8,128)S(1)} %get-tuple-element.47), channel_id=1, source_target_pairs={{0,1},{1,0},{2,3},{3,2},{4,5},{5,4},{6,7},{7,6},{8,9},{9,8},{10,11... | collective-permute-start | bytes 1277960 | tf_op jit(solution)/shard_map/ppermute | solution.py:634
  10.8 1.7 %shard_map.103 = (f32[12,9,32,128]{3,2,1,0:T(8,128)S(1)}, f32[16,3,32,128]{3,2,1,0:T(8,128)S(1)}, f32[4,12,32,128]{3,2,1,0:T(8,128)S(1)}) custom-call(f32[7,16,32,128]{3,2,1,0:T(8,128)S(1)} %get-tuple-element.29.rows.refs_0_, f32[4,544,128]{2,1,0:T(8,128)S(1)} %get-tuple-element.33.raw.refs_1_), custom_call_target="tpu_custom_call" | custom-call | flops 1955000064 | bytes 1048576 | tf_op jit(solution)/shard_map/pallas_call | solution.py:640
  12.5 0.0 collective-permute-done.from_west
  12.5 0.0 collective-permute-done.1.from_east
  12.5 0.2 shard_map.104
  12.7 0.3 %collective-permute-start.4 = (f32[32,128]{1,0:T(8,128)S(1)}, f32[32,128]{1,0:T(8,128)S(1)}, u32[]{:S(2)}, u32[]{:S(2)}) collective-permute-start(f32[32,128]{1,0:T(8,128)S(1)} %get-tuple-element.48), channel_id=1, source_target_pairs={{0,4},{1,2},{2,1},{3,7},{4,0},{5,6},{6,5},{7,3},{8,12},{9,10},{10,... | collective-permute-start | bytes 49160 | tf_op jit(solution)/shard_map/ppermute | solution.py:634
  13.0 0.0 collective-permute-start.5
  13.0 3.5 %shard_map.105 = (f32[16,9,32,128]{3,2,1,0:T(8,128)S(1)}, f32[4,12,48,128]{3,2,1,0:T(8,128)S(1)}, f32[4,4,32,128]{3,2,1,0:T(8,128)S(1)}, f32[4,8,32,128]{3,2,1,0...) custom-call(f32[7,16,32,128]{3,2,1,0:T(8,128)S(1)} %get-tuple-element.29.rows.refs_0_, ...), custom_call_target="tpu_custom_call" | custom-call | flops 5405000192 | bytes 1048576 | tf_op jit(solution)/shard_map/pallas_call | solution.py:656
  16.5 0.8 %collective-permute-done.4.refs_12_ = f32[32,128]{1,0:T(8,128)S(1)} collective-permute-done((f32[32,128]{1,0:T(8,128)S(1)}, f32[32,128]{1,0:T(8,128)S(1)}, u32[]{:S(2)}, u32[]{:S(2)}) %collective-permute-start.4) | collective-permute-done | bytes 16416 | tf_op jit(solution)/shard_map/ppermute | solution.py:634
  17.3 0.0 collective-permute-done.5.refs_13_
  17.3 0.0 collective-permute-done.2.refs_10_
  17.3 0.0 collective-permute-done.3.refs_11_
  17.3 3.0 %shard_map.107 = (f32[512,128]{1,0:T(8,128)}, f32[512,128]{1,0:T(8,128)}, f32[512,128]{1,0:T(8,128)}, f32[512,128]{1,0:T(8,128)}) custom-call(f32[7,16,32,128]{3,2,1,0:T(8,128)S(1)} %get-tuple-element.29.rows.refs_0_, f32[7,32,128]{2,1,0:T(8,128)S(1)} %get-tuple-element.35.refs_4_.refs_1_, f32[12,9,32,128]{3,2,1,0:T(8,128)S(1)} %get-tuple-element.36.refs_5_.refs_2_, ...), custom_call_target="tpu_custom_call" | custom-call | flops 3335000064 | bytes 1048576 | tf_op jit(solution)/shard_map/pallas_call | solution.py:668
Async XLA Ops:
  2.8 9.7 %collective-permute-start = (f32[104,128]{1,0:T(8,128)S(1)}, f32[104,128]{1,0:T(8,128)S(1)}, u32[]{:S(2)}, u32[]{:S(2)}) collective-permute-start(f32[104,128]{1,0:T(8,128)S(1)} %get-tuple-element.31), channel_id=1, source_target_pairs={{0,4},{4,8},{8,12},{12,16},{16,20},{20,24},{24,28},{28,0},{1,5},{5... | collective-permute-start | bytes 159752 | tf_op jit(solution)/shard_map/ppermute | solution.py:630
  5.8 6.7 %collective-permute-start.1 = (f32[104,128]{1,0:T(8,128)S(1)}, f32[104,128]{1,0:T(8,128)S(1)}, u32[]{:S(2)}, u32[]{:S(2)}) collective-permute-start(f32[104,128]{1,0:T(8,128)S(1)} %get-tuple-element.32), channel_id=1, source_target_pairs={{4,0},{8,4},{12,8},{16,12},{20,16},{24,20},{28,24},{0,28},{5,1},{9... | collective-permute-start | bytes 159752 | tf_op jit(solution)/shard_map/ppermute | solution.py:631
  9.0 8.4 %collective-permute-start.2 = (f32[26,32,128]{2,1,0:T(8,128)S(1)}, f32[26,32,128]{2,1,0:T(8,128)S(1)}, u32[]{:S(2)}, u32[]{:S(2)}) collective-permute-start(f32[26,32,128]{2,1,0:T(8,128)S(1)} %get-tuple-element.46), channel_id=1, source_target_pairs={{0,4},{1,2},{2,1},{3,7},{4,0},{5,6},{6,5},{7,3},{8,12},{9,10},{10,... | collective-permute-start | bytes 1277960 | tf_op jit(solution)/shard_map/ppermute | solution.py:634
  9.0 8.3 %collective-permute-start.3 = (f32[26,32,128]{2,1,0:T(8,128)S(1)}, f32[26,32,128]{2,1,0:T(8,128)S(1)}, u32[]{:S(2)}, u32[]{:S(2)}) collective-permute-start(f32[26,32,128]{2,1,0:T(8,128)S(1)} %get-tuple-element.47), channel_id=1, source_target_pairs={{0,1},{1,0},{2,3},{3,2},{4,5},{5,4},{6,7},{7,6},{8,9},{9,8},{10,11... | collective-permute-start | bytes 1277960 | tf_op jit(solution)/shard_map/ppermute | solution.py:634
  12.7 4.6 %collective-permute-start.4 = (f32[32,128]{1,0:T(8,128)S(1)}, f32[32,128]{1,0:T(8,128)S(1)}, u32[]{:S(2)}, u32[]{:S(2)}) collective-permute-start(f32[32,128]{1,0:T(8,128)S(1)} %get-tuple-element.48), channel_id=1, source_target_pairs={{0,4},{1,2},{2,1},{3,7},{4,0},{5,6},{6,5},{7,3},{8,12},{9,10},{10,... | collective-permute-start | bytes 49160 | tf_op jit(solution)/shard_map/ppermute | solution.py:634
  13.0 4.3 %collective-permute-start.5 = (f32[32,128]{1,0:T(8,128)S(1)}, f32[32,128]{1,0:T(8,128)S(1)}, u32[]{:S(2)}, u32[]{:S(2)}) collective-permute-start(f32[32,128]{1,0:T(8,128)S(1)} %get-tuple-element.49), channel_id=1, source_target_pairs={{0,1},{1,0},{2,3},{3,2},{4,5},{5,4},{6,7},{7,6},{8,9},{9,8},{10,11... | collective-permute-start | bytes 49160 | tf_op jit(solution)/shard_map/ppermute | solution.py:634

commit v16 on v15

--- a/solution.py
+++ b/solution.py
@@ -150,6 +150,17 @@
     after = jnp.where(inner, vertical_mix * m * pltpu.roll(m, K - 1, 0), 0.0)
     before = pltpu.roll(after, 1, 0)
     return after, before, 1.0 - after - before
+
+
+def levels_of(masks):
+    inner = lax.broadcasted_iota(jnp.int32, (K, W), 0) < K - 1
+    for i in range(0, len(masks), 4):
+        some = masks[i : i + 4]
+        nexts = [pltpu.roll(m, K - 1, 0) for m in some]
+        after = [jnp.where(inner, vertical_mix * m * n, 0.0) for m, n in zip(some, nexts)]
+        before = [pltpu.roll(a, 1, 0) for a in after]
+        for a, b in zip(after, before):
+            yield a, b, 1.0 - a - b
 
 
 def chunk(q):
@@ -282,14 +293,6 @@
                 emit(j - 1, q, forward + transposed + [at[1][2] - at[2][1]])
 
 
-def by_fours(start, stop, body):
-    def four(i, carry):
-        body([start + 4 * i + k for k in range(4)])
-        return carry
-
-    lax.fori_loop(0, (stop - start) // 4, four, 0)
-
-
 def raw_levels(raw, j):
     return lambda f, q: (raw.at[f][strided(q, j, R, 1), :], raw.at[f][strided(q, j, R, -1), :])
 
@@ -317,12 +320,9 @@
 
 
 def prepare(rows, raw, y_out, level_out, base_out):
-    def levels(js):
-        for j in js:
-            for k, value in enumerate(level_coefficients(rows[M, j])):
-                level_out[j, k] = value
-
-    by_fours(0, R, levels)
+    for j, got in enumerate(levels_of([rows[M, j] for j in range(R)])):
+        for k in range(3):
+            level_out[j, k] = got[k]
 
     def emit(j, q, values):
         for k in range(9):
@@ -330,21 +330,18 @@
 
     y_coefficients(2, R - 3, lambda f, j, q: rows.at[f, j][chunk(q)], emit)
 
-    def first(js):
-        def job(j):
-            def store(f, q, value):
-                base_out.at[f, j - 2][chunk(q)] = value
-
-            return dict(
-                store=store,
-                load=lambda f, d, q: rows.at[f, j + d][chunk(q)],
-                y=y_out.at[j - 2],
-                z=(level_out.at[j], raw_levels(raw, j)),
-            )
-
-        step_rows([job(j) for j in js])
-
-    by_fours(2, R - 2, first)
+    def job(j):
+        def store(f, q, value):
+            base_out.at[f, j - 2][chunk(q)] = value
+
+        return dict(
+            store=store,
+            load=lambda f, d, q: rows.at[f, j + d][chunk(q)],
+            y=y_out.at[j - 2],
+            z=(level_out.at[j], raw_levels(raw, j)),
+        )
+
+    step_rows([job(j) for j in range(2, R - 2)])
 
 
 def interior(*refs):
@@ -459,7 +456,7 @@
     rows, merged, y_in, level_in, x_in, c1_in, part1_in, c2_in, part2_in, edge_in = refs[:10]
     second, first, second_corners, first_corners = refs[10:14]
     outs = refs[14:18]
-    sides, corners, x_new, y_new, level_new, c1_new, merged1, beyond, halos = refs[18:]
+    sides, corners, x_new, y_new, level_new, c1_new, merged1, beyond, halos, halos_x = refs[18:]
     lane = lanes()
     place = lax.axis_index("ns")
     last = lax.axis_size("ns") - 1
@@ -467,14 +464,10 @@
     inside = {SOUTH: place > 0, NORTH: place < last}
     near = (-2, -1, 0, 1, R - 2, R - 1, R, R + 1)
     new_at = {j: i for i, j in enumerate(near)}
-    def unpack(b, carry):
-        for message, side in ((second, odd), (first, 1 - odd)):
-            here = jnp.where(side == NORTH, place < last, place > 0)
+    for message, side in ((second, odd), (first, 1 - odd)):
+        here = jnp.where(side == NORTH, place < last, place > 0)
+        for b in range(SIDE_BLOCKS):
             sides[side, b] = jnp.where(here, message[b], 0.0)
-        return carry
-
-    lax.fori_loop(0, SIDE_BLOCKS, unpack, 0, unroll=2)
-
     for message, side in ((second_corners, odd), (first_corners, 1 - odd)):
         here = jnp.where(side == NORTH, place < last, place > 0)
         corners[side] = jnp.where(here, message[...], 0.0)
@@ -507,20 +500,32 @@
     for low in (-2, R - 2):
         y_coefficients(low, low + 3, lambda f, j, q: row(f, j)[chunk(q)], emit)
 
-    for j in near:
-        if not 0 <= j < R:
-            got = x_coefficients(
-                row(U, j)[...], halo_beyond(U, j), row(M, j)[...], halo_beyond(M, j), lane
-            )
-            for k in range(9):
-                x_new[new_at[j], k] = got[k]
-            for k, value in enumerate(level_coefficients(row(M, j)[...])):
-                level_new[new_at[j], k] = value
-
     out_rows = [j for j in near if not 0 <= j < R]
+    for i, j in enumerate(out_rows):
+        for k, f in enumerate((U, M)):
+            halos_x[i, k] = halo_beyond(f, j)
     for f in range(4):
         for i, j in enumerate(out_rows):
             halos[i, f] = halo_beyond(f, j)
+
+    def issue(item):
+        i, q = item
+        u, m = (row(f, out_rows[i])[chunk(q)] for f in (U, M))
+        uh, mh = (halos_x.at[i, k][chunk(q)] for k in range(2))
+        return (
+            {d: shifted(u, uh, d, lane[:8]) for d in (-2, -1, 0, 1)},
+            {d: shifted(m, mh, d, lane[:8]) for d in (-2, -1, 0, 1, 2)},
+        )
+
+    def finish(item, got):
+        i, q = item
+        for k, value in enumerate(coefficients(*got)):
+            x_new.at[new_at[out_rows[i]], k][chunk(q)] = value
+
+    pipeline([(i, q) for i in range(4) for q in range(K // 8)], issue, finish)
+    for j, got in zip(out_rows, levels_of([row(M, j)[...] for j in out_rows])):
+        for k in range(3):
+            level_new[new_at[j], k] = got[k]
 
     def kept(k):
         return lambda f, q: halos.at[k, f][chunk(q)]
@@ -572,12 +577,9 @@
 
     step_rows([second_job(j) for j in (0, 2, 1, 3, R - 2, R - 4, R - 1, R - 3)])
 
-    def copy(j, carry):
+    for j in range(4, R - 4):
         for f in range(4):
             outs[f][pl.ds(j, K, stride=R), :] = c2_in[f, j - 4]
-        return carry
-
-    lax.fori_loop(4, R - 4, copy, 0, unroll=2)
 
 
 def vmem():
@@ -679,6 +681,7 @@
             pltpu.VMEM((4,) + row, F32),
             pltpu.VMEM((FIELDS,) + row, F32),
             pltpu.VMEM((4, 4) + row, F32),
+            pltpu.VMEM((4, 2) + row, F32),
         ],
         cost=2.9,
     )(

time: 20.5 us -> 20.2 us (0.985)
  Pallas kernels: 10.6 us -> 10.1 us
    pallas_call x1, Pallas kernels: 2.99 us -> 2.68 us  [local(): call(boundary, [vmem()] * 14, [(K * R, W)] * 4, [pltpu.VMEM((2, SIDE_BLOC...]
  transfers between devices with their start and end apart: 6 -> 6, of which waited for: 1 -> 1; matrix products, arithmetic and copies ran while one was open for 0% -> 0% of each run, Pallas kernels for 27% -> 26%
where the time goes in v16:
time: 20.2 us; the launch traced here: 20 us
  Pallas kernels  10.1 us (50%)
  starting transfers between devices  8.43 us (42%)
  waiting for transfers between devices  0.81 us (4%)
  between operations  0.69 us (3%)
    pallas_call x1, Pallas kernels, local(): call(interior, [vmem()] * 8, [(R, 9) + row, (4, R - 4, TALL, W), (4, 4) +...  3.51 us
    ppermute x1, starting transfers between devices, local(): lax.ppermute(to_west, 'ew', [((i + 1) % n_ew, i) for i in range(n_ew)])  3.1 us
    ppermute x1, starting transfers between devices, local(): lax.ppermute(to_east, 'ew', [(i, (i + 1) % n_ew) for i in range(n_ew)])  2.99 us
    pallas_call x1, Pallas kernels, local(): call(boundary, [vmem()] * 14, [(K * R, W)] * 4, [pltpu.VMEM((2, SIDE_BLOC...  2.68 us
    ppermute x4, starting transfers between devices, swap(): return lax.ppermute(message, ('ew', 'ns'), partners(odd, n_ew, n_ns))  2.33 us
    pallas_call x1, Pallas kernels, local(): call(pack_edges, [pl.BlockSpec(memory_space=pltpu.HBM)] * FIELDS, [(FIELD...  2.17 us
    pallas_call x1, Pallas kernels, local(): call(prepare, [vmem()] * 2, [(R - 4, 9) + row, (R, 3) + row, (4, R - 4) +...  1.51 us
    ppermute x4, waiting for transfers between devices, swap(): return lax.ppermute(message, ('ew', 'ns'), partners(odd, n_ew, n_ns))  0.8 us
  transfers between devices with their start and end apart: 6, of which 1 were waited for; matrix products, arithmetic and copies ran while one was open for 0% of the time, Pallas kernels for 26%

profile of v16, /device:TPU:0, one launch (start us, length us, event | category | flops | bytes accessed | tf_op | source)
XLA Modules:
  0.0 20.0 jit_solution(17226950570551507645)
XLA Ops:
  0.6 2.2 %shard_map.102 = (f32[7,16,32,128]{3,2,1,0:T(8,128)S(1)}, f32[4,544,128]{2,1,0:T(8,128)S(1)}, f32[7,32,128]{2,1,0:T(8,128)S(1)}, f32[104,128]{1,0:T(8,128)S(1)}, f32[104,128]{1,0:T(8,128)S(1)}) custom-call(f32[512,128]{1,0:T(8,128)} %bitcast.11, f32[512,128]{1,0:T(8,128)} %bitcast.12, f32[512,128]{1,0:T(8,128)} %bitcast.13, f32[512,128]{1,0:T(8,128)} %bitcast.14, ...), custom_call_target="tpu_custom_call" | custom-call | flops 2529999872 | bytes 1048576 | tf_op jit(solution)/shard_map/pallas_call | solution.py:619
  2.8 3.0 %collective-permute-start = (f32[104,128]{1,0:T(8,128)S(1)}, f32[104,128]{1,0:T(8,128)S(1)}, u32[]{:S(2)}, u32[]{:S(2)}) collective-permute-start(f32[104,128]{1,0:T(8,128)S(1)} %get-tuple-element.31), channel_id=1, source_target_pairs={{0,4},{4,8},{8,12},{12,16},{16,20},{20,24},{24,28},{28,0},{1,5},{5... | collective-permute-start | bytes 159752 | tf_op jit(solution)/shard_map/ppermute | solution.py:632
  5.8 3.1 %collective-permute-start.1 = (f32[104,128]{1,0:T(8,128)S(1)}, f32[104,128]{1,0:T(8,128)S(1)}, u32[]{:S(2)}, u32[]{:S(2)}) collective-permute-start(f32[104,128]{1,0:T(8,128)S(1)} %get-tuple-element.32), channel_id=1, source_target_pairs={{4,0},{8,4},{12,8},{16,12},{20,16},{24,20},{28,24},{0,28},{5,1},{9... | collective-permute-start | bytes 159752 | tf_op jit(solution)/shard_map/ppermute | solution.py:633
  8.9 0.1 shard_map.106
  9.0 0.1 collective-permute-start.2
  9.0 1.7 %collective-permute-start.3 = (f32[26,32,128]{2,1,0:T(8,128)S(1)}, f32[26,32,128]{2,1,0:T(8,128)S(1)}, u32[]{:S(2)}, u32[]{:S(2)}) collective-permute-start(f32[26,32,128]{2,1,0:T(8,128)S(1)} %get-tuple-element.47), channel_id=1, source_target_pairs={{0,1},{1,0},{2,3},{3,2},{4,5},{5,4},{6,7},{7,6},{8,9},{9,8},{10,11... | collective-permute-start | bytes 1277960 | tf_op jit(solution)/shard_map/ppermute | solution.py:636
  10.8 1.5 %shard_map.103 = (f32[12,9,32,128]{3,2,1,0:T(8,128)S(1)}, f32[16,3,32,128]{3,2,1,0:T(8,128)S(1)}, f32[4,12,32,128]{3,2,1,0:T(8,128)S(1)}) custom-call(f32[7,16,32,128]{3,2,1,0:T(8,128)S(1)} %get-tuple-element.29.rows.refs_0_, f32[4,544,128]{2,1,0:T(8,128)S(1)} %get-tuple-element.33.raw.refs_1_), custom_call_target="tpu_custom_call" | custom-call | flops 1955000064 | bytes 1048576 | tf_op jit(solution)/shard_map/pallas_call | solution.py:642
  12.3 0.0 collective-permute-done.from_west
  12.3 0.0 collective-permute-done.1.from_east
  12.3 0.2 shard_map.104
  12.5 0.3 %collective-permute-start.4 = (f32[32,128]{1,0:T(8,128)S(1)}, f32[32,128]{1,0:T(8,128)S(1)}, u32[]{:S(2)}, u32[]{:S(2)}) collective-permute-start(f32[32,128]{1,0:T(8,128)S(1)} %get-tuple-element.48), channel_id=1, source_target_pairs={{0,4},{1,2},{2,1},{3,7},{4,0},{5,6},{6,5},{7,3},{8,12},{9,10},{10,... | collective-permute-start | bytes 49160 | tf_op jit(solution)/shard_map/ppermute | solution.py:636
  12.8 0.2 collective-permute-start.5
  13.0 3.5 %shard_map.105 = (f32[16,9,32,128]{3,2,1,0:T(8,128)S(1)}, f32[4,12,48,128]{3,2,1,0:T(8,128)S(1)}, f32[4,4,32,128]{3,2,1,0:T(8,128)S(1)}, f32[4,8,32,128]{3,2,1,0...) custom-call(f32[7,16,32,128]{3,2,1,0:T(8,128)S(1)} %get-tuple-element.29.rows.refs_0_, ...), custom_call_target="tpu_custom_call" | custom-call | flops 5405000192 | bytes 1048576 | tf_op jit(solution)/shard_map/pallas_call | solution.py:658
  16.5 0.8 %collective-permute-done.4.refs_12_ = f32[32,128]{1,0:T(8,128)S(1)} collective-permute-done((f32[32,128]{1,0:T(8,128)S(1)}, f32[32,128]{1,0:T(8,128)S(1)}, u32[]{:S(2)}, u32[]{:S(2)}) %collective-permute-start.4) | collective-permute-done | bytes 16416 | tf_op jit(solution)/shard_map/ppermute | solution.py:636
  17.3 0.0 collective-permute-done.5.refs_13_
  17.3 0.0 collective-permute-done.2.refs_10_
  17.3 0.0 collective-permute-done.3.refs_11_
  17.3 2.7 %shard_map.107 = (f32[512,128]{1,0:T(8,128)}, f32[512,128]{1,0:T(8,128)}, f32[512,128]{1,0:T(8,128)}, f32[512,128]{1,0:T(8,128)}) custom-call(f32[7,16,32,128]{3,2,1,0:T(8,128)S(1)} %get-tuple-element.29.rows.refs_0_, f32[7,32,128]{2,1,0:T(8,128)S(1)} %get-tuple-element.35.refs_4_.refs_1_, f32[12,9,32,128]{3,2,1,0:T(8,128)S(1)} %get-tuple-element.36.refs_5_.refs_2_, ...), custom_call_target="tpu_custom_call" | custom-call | flops 3335000064 | bytes 1048576 | tf_op jit(solution)/shard_map/pallas_call | solution.py:670
Async XLA Ops:
  2.8 9.5 %collective-permute-start = (f32[104,128]{1,0:T(8,128)S(1)}, f32[104,128]{1,0:T(8,128)S(1)}, u32[]{:S(2)}, u32[]{:S(2)}) collective-permute-start(f32[104,128]{1,0:T(8,128)S(1)} %get-tuple-element.31), channel_id=1, source_target_pairs={{0,4},{4,8},{8,12},{12,16},{16,20},{20,24},{24,28},{28,0},{1,5},{5... | collective-permute-start | bytes 159752 | tf_op jit(solution)/shard_map/ppermute | solution.py:632
  5.8 6.5 %collective-permute-start.1 = (f32[104,128]{1,0:T(8,128)S(1)}, f32[104,128]{1,0:T(8,128)S(1)}, u32[]{:S(2)}, u32[]{:S(2)}) collective-permute-start(f32[104,128]{1,0:T(8,128)S(1)} %get-tuple-element.32), channel_id=1, source_target_pairs={{4,0},{8,4},{12,8},{16,12},{20,16},{24,20},{28,24},{0,28},{5,1},{9... | collective-permute-start | bytes 159752 | tf_op jit(solution)/shard_map/ppermute | solution.py:633
  9.0 8.4 %collective-permute-start.2 = (f32[26,32,128]{2,1,0:T(8,128)S(1)}, f32[26,32,128]{2,1,0:T(8,128)S(1)}, u32[]{:S(2)}, u32[]{:S(2)}) collective-permute-start(f32[26,32,128]{2,1,0:T(8,128)S(1)} %get-tuple-element.46), channel_id=1, source_target_pairs={{0,4},{1,2},{2,1},{3,7},{4,0},{5,6},{6,5},{7,3},{8,12},{9,10},{10,... | collective-permute-start | bytes 1277960 | tf_op jit(solution)/shard_map/ppermute | solution.py:636
  9.0 8.3 %collective-permute-start.3 = (f32[26,32,128]{2,1,0:T(8,128)S(1)}, f32[26,32,128]{2,1,0:T(8,128)S(1)}, u32[]{:S(2)}, u32[]{:S(2)}) collective-permute-start(f32[26,32,128]{2,1,0:T(8,128)S(1)} %get-tuple-element.47), channel_id=1, source_target_pairs={{0,1},{1,0},{2,3},{3,2},{4,5},{5,4},{6,7},{7,6},{8,9},{9,8},{10,11... | collective-permute-start | bytes 1277960 | tf_op jit(solution)/shard_map/ppermute | solution.py:636
  12.5 4.8 %collective-permute-start.4 = (f32[32,128]{1,0:T(8,128)S(1)}, f32[32,128]{1,0:T(8,128)S(1)}, u32[]{:S(2)}, u32[]{:S(2)}) collective-permute-start(f32[32,128]{1,0:T(8,128)S(1)} %get-tuple-element.48), channel_id=1, source_target_pairs={{0,4},{1,2},{2,1},{3,7},{4,0},{5,6},{6,5},{7,3},{8,12},{9,10},{10,... | collective-permute-start | bytes 49160 | tf_op jit(solution)/shard_map/ppermute | solution.py:636
  12.8 4.5 %collective-permute-start.5 = (f32[32,128]{1,0:T(8,128)S(1)}, f32[32,128]{1,0:T(8,128)S(1)}, u32[]{:S(2)}, u32[]{:S(2)}) collective-permute-start(f32[32,128]{1,0:T(8,128)S(1)} %get-tuple-element.49), channel_id=1, source_target_pairs={{0,1},{1,0},{2,3},{3,2},{4,5},{5,4},{6,7},{7,6},{8,9},{9,8},{10,11... | collective-permute-start | bytes 49160 | tf_op jit(solution)/shard_map/ppermute | solution.py:636
